TPU v7x, 32 devices: a whole 2x2x4 slice. The times are simulated.
32 devices in a mesh: dp: 8 (over z, core), expert: 4 (over y, x).
Axes of the slice: x: 2, y: 2, z: 4, core: 2. Of those that a mesh axis runs over, the one named last changes fastest.
Arguments:
- tokens: bfloat16 [64, 128, 768], P(('dp', 'expert')), may hold values from -6 to 6
- teacher: bfloat16 [64, 128, 768], P(('dp', 'expert')), may hold values from -6 to 6
- routes: int32 [64, 128, 1], P(('dp', 'expert')), may hold values from 0 to 3; in each aligned block of 128 rows (0 to 127, 128 to 255, ..., all dimensions but the last counted through in order) at most 64 rows name the same one
- piece_start: int32 [64], P(('dp', 'expert')), may hold values from 0 to 96
- valid_mask: int32 [64, 128], P(('dp', 'expert')), may hold values from 0 to 1, as said below
- lower_gain: bfloat16 [768], P(('dp', 'expert')), may hold values from 0.5 to 1.5
- lower_bias: bfloat16 [768], P(('dp', 'expert')), may hold values from -0.59765625 to 0.59765625
- lower_triple: bfloat16 [768, 2304], P(('dp', 'expert')), may hold values from -0.21875 to 0.21875
- lower_output: bfloat16 [768, 768], P(('dp', 'expert')), may hold values from -0.875 to 0.875
- feed_gain: bfloat16 [768], P(('dp', 'expert')), may hold values from 0.5 to 1.5
- feed_bias: bfloat16 [768], P(('dp', 'expert')), may hold values from -0.59765625 to 0.59765625
- feed_expand: bfloat16 [768, 3072], P(('dp', 'expert')), may hold values from -0.21875 to 0.21875
- feed_shrink: bfloat16 [3072, 768], P(('dp', 'expert')), may hold values from -0.21875 to 0.21875
- upper_gain: bfloat16 [768], P(('dp', 'expert')), may hold values from 0.5 to 1.5
- upper_bias: bfloat16 [768], P(('dp', 'expert')), may hold values from -0.59765625 to 0.59765625
- upper_triple: bfloat16 [768, 2304], P(('dp', 'expert')), may hold values from -0.21875 to 0.21875
- upper_output: bfloat16 [768, 768], P(('dp', 'expert')), may hold values from -0.875 to 0.875
- mixer_gain: bfloat16 [768], P(('dp', 'expert')), may hold values from 0.5 to 1.5
- mixer_bias: bfloat16 [768], P(('dp', 'expert')), may hold values from -0.59765625 to 0.59765625
- router: bfloat16 [768, 4], P(('dp', 'expert')), may hold values from -0.15625 to 0.15625
- expert_expand: bfloat16 [4, 768, 3072], P('expert', 'dp'), may hold values from -0.21875 to 0.21875
- expert_shrink: bfloat16 [4, 3072, 768], P('expert', 'dp'), may hold values from -0.21875 to 0.21875
Outputs:
- states: bfloat16 [64, 128, 768], P(('dp', 'expert'))
- tokens_delta: float32 [64, 128, 768], P(('dp', 'expert'))
- lower_gain_delta: float32 [768], P(('dp', 'expert'))
- lower_bias_delta: float32 [768], P(('dp', 'expert'))
- lower_triple_delta: float32 [768, 2304], P(('dp', 'expert'))
- lower_output_delta: float32 [768, 768], P(('dp', 'expert'))
- feed_gain_delta: float32 [768], P(('dp', 'expert'))
- feed_bias_delta: float32 [768], P(('dp', 'expert'))
- feed_expand_delta: float32 [768, 3072], P(('dp', 'expert'))
- feed_shrink_delta: float32 [3072, 768], P(('dp', 'expert'))
- upper_gain_delta: float32 [768], P(('dp', 'expert'))
- upper_bias_delta: float32 [768], P(('dp', 'expert'))
- upper_triple_delta: float32 [768, 2304], P(('dp', 'expert'))
- upper_output_delta: float32 [768, 768], P(('dp', 'expert'))
- mixer_gain_delta: float32 [768], P(('dp', 'expert'))
- mixer_bias_delta: float32 [768], P(('dp', 'expert'))
- router_delta: float32 [768, 4], P(('dp', 'expert'))
- expert_expand_delta: float32 [4, 768, 3072], P('expert', 'dp')
- expert_shrink_delta: float32 [4, 3072, 768], P('expert', 'dp')
- mean_loss: float32 [], replicated
Inputs may be any that keep to these rules, and one draw needn't show every extreme that they name: `routes`: in each sequence no expert is chosen by more than 64 tokens; in some sequence one is chosen by exactly 64. `valid_mask`: the first token of every sequence is valid.
All inputs are finite; a program needn't handle non-finite values.
Results may differ from a plain program's by a relative error of at most 0.013.
Values may be sent and summed in bfloat16 or wider, within the bound.
No kernel may reach another device: no remote copies, remote signals or barrier semaphores. Data moves between devices by JAX's collectives and lax.ppermute only.
A program may use at most 192 MiB of HBM per device.

v0:
```python
import jax
import jax.numpy as jnp
from jax import lax
from jax.sharding import PartitionSpec as P

H = 12
HD = 64


HIGH = lax.Precision.HIGHEST


def shortened(array):
    return jax.tree.map(lambda a: a.astype(jnp.bfloat16) if a.dtype == jnp.float32 else a, array)


def layer_norm(values, norm_gain, norm_bias):
    centered = values - jnp.mean(values, axis=-1, keepdims=True)
    spread = jnp.mean(centered * centered, axis=-1, keepdims=True)
    return centered * lax.rsqrt(spread + 1e-05) * norm_gain + norm_bias


def gelu_tanh(values):
    return jax.nn.gelu(values, approximate=True)


def norm_backward(stream, norm_gain, norm_bias, normed_grad):
    _, norm_back = jax.vjp(
        layer_norm, stream, norm_gain.astype(jnp.float32), norm_bias.astype(jnp.float32)
    )
    return norm_back(normed_grad)


def allowed_mask(start, length):
    position = jnp.arange(length, dtype=jnp.int32)
    inside = (position >= start) & (position < start + length // 4)
    return (position[:, None] >= position[None, :]) | inside[:, None] & inside[None, :]


def route_tables(route_row, experts, capacity):
    numbers = jnp.arange(experts, dtype=jnp.int32)
    chosen = (route_row[:, None] == numbers[None, :]).astype(jnp.int32)
    slot_index = jnp.sum((jnp.cumsum(chosen, axis=0) - 1) * chosen, axis=1)
    target = route_row * capacity + slot_index
    dispatch = (jnp.arange(experts * capacity, dtype=jnp.int32)[:, None] == target[None, :]).astype(
        jnp.bfloat16
    )
    return (chosen.astype(jnp.float32), dispatch)


def masked_scores(packed, allowed):
    scores = jnp.einsum(
        "qhd,khd->hqk", packed[:, 0], packed[:, 1], preferred_element_type=jnp.float32
    ) * HD ** (-0.5)
    return jnp.where(allowed[None], scores, -1e30)


def attend_forward(stream, norm_gain, norm_bias, triple, output, allowed):
    length, features = stream.shape
    normed = layer_norm(
        stream, norm_gain.astype(jnp.float32), norm_bias.astype(jnp.float32)
    ).astype(jnp.bfloat16)
    packed = (
        jnp.dot(normed, triple, preferred_element_type=jnp.float32)
        .astype(jnp.bfloat16)
        .reshape(length, 3, H, HD)
    )
    scores = masked_scores(packed, allowed)
    highest = jnp.max(scores, axis=-1, keepdims=True)
    exponent = jnp.exp(scores - highest)
    row_total = jnp.sum(exponent, axis=-1, keepdims=True)
    weights = (exponent / row_total).astype(jnp.bfloat16)
    logsum = highest + jnp.log(row_total)
    context = jnp.einsum("hqk,khd->qhd", weights, packed[:, 2], preferred_element_type=jnp.float32)
    context = context.astype(jnp.bfloat16).reshape(length, features)
    branch = jnp.dot(context, output, preferred_element_type=jnp.float32)
    return (stream + branch, (normed, packed, logsum, context))


def attend_backward(stream, norm_gain, norm_bias, triple, output, allowed, stored, upstream):
    normed, packed, logsum, context = stored
    length, features = stream.shape
    scale_q = HD ** (-0.5)
    branch_grad = upstream.astype(jnp.bfloat16)
    output_grad = jnp.einsum("ld,le->de", context, branch_grad, preferred_element_type=jnp.float32)
    context_grad = jnp.einsum("le,de->ld", branch_grad, output, preferred_element_type=jnp.float32)
    context_grad = context_grad.astype(jnp.bfloat16).reshape(length, H, HD)
    probs = jnp.exp(masked_scores(packed, allowed) - logsum)
    value_grad = jnp.einsum(
        "hqk,qhd->khd", probs.astype(jnp.bfloat16), context_grad, preferred_element_type=jnp.float32
    )
    prob_grad = jnp.einsum(
        "qhd,khd->hqk", context_grad, packed[:, 2], preferred_element_type=jnp.float32
    )
    score_grad = (probs * (prob_grad - jnp.sum(probs * prob_grad, axis=-1, keepdims=True))).astype(
        jnp.bfloat16
    )
    query_grad = (
        jnp.einsum("hqk,khd->qhd", score_grad, packed[:, 1], preferred_element_type=jnp.float32)
        * scale_q
    )
    key_grad = (
        jnp.einsum("hqk,qhd->khd", score_grad, packed[:, 0], preferred_element_type=jnp.float32)
        * scale_q
    )
    packed_grad = (
        jnp.stack([query_grad, key_grad, value_grad], axis=1)
        .reshape(length, 3 * features)
        .astype(jnp.bfloat16)
    )
    triple_grad = jnp.einsum("ld,le->de", normed, packed_grad, preferred_element_type=jnp.float32)
    normed_grad = jnp.einsum("le,de->ld", packed_grad, triple, preferred_element_type=jnp.float32)
    stream_grad, gain_grad, bias_grad = norm_backward(stream, norm_gain, norm_bias, normed_grad)
    return (upstream + stream_grad, (gain_grad, bias_grad, triple_grad, output_grad))


def feed_forward(stream, norm_gain, norm_bias, expand, shrink):
    normed = layer_norm(
        stream, norm_gain.astype(jnp.float32), norm_bias.astype(jnp.float32)
    ).astype(jnp.bfloat16)
    inner_pre = jnp.dot(normed, expand, preferred_element_type=jnp.float32)
    active = gelu_tanh(inner_pre).astype(jnp.bfloat16)
    return (
        stream + jnp.dot(active, shrink, preferred_element_type=jnp.float32),
        (normed, inner_pre),
    )


def feed_backward(stream, norm_gain, norm_bias, expand, shrink, stored, upstream):
    normed, inner_pre = stored
    branch_grad = upstream.astype(jnp.bfloat16)
    active = gelu_tanh(inner_pre).astype(jnp.bfloat16)
    shrink_grad = jnp.einsum("lf,ld->fd", active, branch_grad, preferred_element_type=jnp.float32)
    active_grad = jnp.einsum("ld,fd->lf", branch_grad, shrink, preferred_element_type=jnp.float32)
    _, gelu_back = jax.vjp(gelu_tanh, inner_pre)
    inner_grad = gelu_back(active_grad)[0].astype(jnp.bfloat16)
    expand_grad = jnp.einsum("ld,lf->df", normed, inner_grad, preferred_element_type=jnp.float32)
    normed_grad = jnp.einsum("lf,df->ld", inner_grad, expand, preferred_element_type=jnp.float32)
    stream_grad, gain_grad, bias_grad = norm_backward(stream, norm_gain, norm_bias, normed_grad)
    return (upstream + stream_grad, (gain_grad, bias_grad, expand_grad, shrink_grad))


def mixture_forward(stream, norm_gain, norm_bias, router, expand, shrink, chosen, dispatch, groups):
    length, features = stream.shape
    normed = layer_norm(
        stream, norm_gain.astype(jnp.float32), norm_bias.astype(jnp.float32)
    ).astype(jnp.bfloat16)
    logits = jnp.dot(normed, router, preferred_element_type=jnp.float32)
    gate_value = jax.nn.sigmoid(jnp.sum(logits * chosen, axis=1))
    expert_probs = jax.nn.softmax(logits, axis=1)
    buffer = jnp.dot(dispatch, normed, preferred_element_type=jnp.float32).astype(jnp.bfloat16)
    buffer = buffer.reshape(groups, expand.shape[0], -1, features)
    arrived = lax.all_to_all(buffer, "expert", split_axis=0, concat_axis=0, tiled=True)
    inner_pre = jnp.einsum("secd,edf->secf", arrived, expand, preferred_element_type=jnp.float32)
    active = gelu_tanh(inner_pre).astype(jnp.bfloat16)
    result = jnp.einsum(
        "secf,efd->secd", active, shrink, preferred_element_type=jnp.float32
    ).astype(jnp.bfloat16)
    returned, arrived = (
        lax.all_to_all(result, "expert", split_axis=0, concat_axis=0, tiled=True),
        arrived,
    )
    combined = jnp.einsum(
        "sl,sd->ld", dispatch, returned.reshape(-1, features), preferred_element_type=jnp.float32
    )
    return (
        stream + gate_value[:, None] * combined,
        (normed, gate_value, expert_probs, combined, arrived),
    )


def mixture_backward(
    stream,
    norm_gain,
    norm_bias,
    router,
    expand,
    shrink,
    chosen,
    dispatch,
    valid_row,
    expert_share,
    balance_scale,
    stored,
    upstream,
):
    normed, gate_value, expert_probs, combined, arrived = stored
    features = stream.shape[1]
    gate_grad = jnp.sum(upstream * combined, axis=1)
    combined_grad = (gate_value[:, None] * upstream).astype(jnp.bfloat16)
    outgoing = jnp.dot(dispatch, combined_grad, preferred_element_type=jnp.float32).astype(
        jnp.bfloat16
    )
    landed = lax.all_to_all(
        outgoing.reshape(arrived.shape), "expert", split_axis=0, concat_axis=0, tiled=True
    )
    inner_pre = jnp.einsum("secd,edf->secf", arrived, expand, preferred_element_type=jnp.float32)
    active = gelu_tanh(inner_pre).astype(jnp.bfloat16)
    shrink_grad = jnp.einsum("secf,secd->efd", active, landed, preferred_element_type=jnp.float32)
    active_grad = jnp.einsum("secd,efd->secf", landed, shrink, preferred_element_type=jnp.float32)
    _, gelu_back = jax.vjp(gelu_tanh, inner_pre)
    inner_grad = gelu_back(active_grad)[0].astype(jnp.bfloat16)
    expand_grad = jnp.einsum(
        "secd,secf->edf", arrived, inner_grad, preferred_element_type=jnp.float32
    )
    rows_grad = jnp.einsum(
        "secf,edf->secd", inner_grad, expand, preferred_element_type=jnp.float32
    ).astype(jnp.bfloat16)
    back_rows = lax.all_to_all(rows_grad, "expert", split_axis=0, concat_axis=0, tiled=True)
    routed_grad = jnp.einsum(
        "sl,sd->ld", dispatch, back_rows.reshape(-1, features), preferred_element_type=jnp.float32
    )
    logits_grad = chosen * (gate_grad * gate_value * (1.0 - gate_value))[:, None]
    logits_grad = logits_grad + balance_scale * valid_row[:, None] * expert_probs * (
        expert_share - jnp.sum(expert_probs * expert_share, axis=1, keepdims=True)
    )
    router_grad = jnp.einsum("ld,le->de", normed.astype(jnp.float32), logits_grad, precision=HIGH)
    normed_grad = routed_grad + jnp.einsum(
        "le,de->ld", logits_grad, router.astype(jnp.float32), precision=HIGH
    )
    stream_grad, gain_grad, bias_grad = norm_backward(stream, norm_gain, norm_bias, normed_grad)
    return (upstream + stream_grad, (gain_grad, bias_grad, router_grad), (expand_grad, shrink_grad))


def body(
    tokens,
    teacher,
    routes,
    piece_start,
    valid_mask,
    lower_gain,
    lower_bias,
    lower_triple,
    lower_output,
    feed_gain,
    feed_bias,
    feed_expand,
    feed_shrink,
    upper_gain,
    upper_bias,
    upper_triple,
    upper_output,
    mixer_gain,
    mixer_bias,
    router,
    expert_expand,
    expert_shrink,
):
    dense_shards = (
        lower_gain,
        lower_bias,
        lower_triple,
        lower_output,
        feed_gain,
        feed_bias,
        feed_expand,
        feed_shrink,
        upper_gain,
        upper_bias,
        upper_triple,
        upper_output,
        mixer_gain,
        mixer_bias,
        router,
    )
    micro_count = tokens.shape[0]
    length = tokens.shape[1]
    features = tokens.shape[2]
    experts = router.shape[1]
    capacity = max(2, 2 * length // experts)
    groups = lax.axis_size("expert")
    total_tokens = micro_count * length * lax.axis_size("dp") * groups
    valid_all = valid_mask.astype(jnp.float32)
    numbers = jnp.arange(experts, dtype=jnp.int32)
    chosen_all = (routes[..., 0][..., None] == numbers).astype(jnp.float32)
    counts, valid_total = lax.psum(
        (jnp.sum(valid_all[..., None] * chosen_all, axis=(0, 1)), jnp.sum(valid_all)),
        ("dp", "expert"),
    )
    expert_share = counts / valid_total
    loss_ratio = total_tokens / valid_total
    balance_scale = total_tokens * features * 0.1 * experts / valid_total
    gathered = (
        (
            lax.all_gather(dense_shards[0], ("dp", "expert"), axis=0, tiled=True),
            lax.all_gather(dense_shards[1], ("dp", "expert"), axis=0, tiled=True),
            lax.all_gather(dense_shards[2], ("dp", "expert"), axis=0, tiled=True),
            lax.all_gather(dense_shards[3], ("dp", "expert"), axis=0, tiled=True),
            lax.all_gather(dense_shards[4], ("dp", "expert"), axis=0, tiled=True),
            lax.all_gather(dense_shards[5], ("dp", "expert"), axis=0, tiled=True),
            lax.all_gather(dense_shards[6], ("dp", "expert"), axis=0, tiled=True),
            lax.all_gather(dense_shards[7], ("dp", "expert"), axis=0, tiled=True),
            lax.all_gather(dense_shards[8], ("dp", "expert"), axis=0, tiled=True),
            lax.all_gather(dense_shards[9], ("dp", "expert"), axis=0, tiled=True),
            lax.all_gather(dense_shards[10], ("dp", "expert"), axis=0, tiled=True),
            lax.all_gather(dense_shards[11], ("dp", "expert"), axis=0, tiled=True),
            lax.all_gather(dense_shards[12], ("dp", "expert"), axis=0, tiled=True),
            lax.all_gather(dense_shards[13], ("dp", "expert"), axis=0, tiled=True),
            lax.all_gather(dense_shards[14], ("dp", "expert"), axis=0, tiled=True),
        ),
        (
            lax.all_gather(expert_expand, "dp", axis=1, tiled=True),
            lax.all_gather(expert_shrink, "dp", axis=1, tiled=True),
        ),
    )
    saved = []
    outputs = []
    squared_local = jnp.zeros((), jnp.float32)
    for micro_index in range(micro_count):
        dense_full, expert_full = gathered
        allowed = allowed_mask(piece_start[micro_index], length)
        chosen, dispatch = route_tables(routes[micro_index, :, 0], experts, capacity)
        stream_in = tokens[micro_index].astype(jnp.float32)
        stream_one, stored_one = attend_forward(
            stream_in, dense_full[0], dense_full[1], dense_full[2], dense_full[3], allowed
        )
        stream_two, stored_two = feed_forward(
            stream_one, dense_full[4], dense_full[5], dense_full[6], dense_full[7]
        )
        stream_three, stored_three = attend_forward(
            stream_two, dense_full[8], dense_full[9], dense_full[10], dense_full[11], allowed
        )
        final, stored_four = mixture_forward(
            stream_three,
            dense_full[12],
            dense_full[13],
            dense_full[14],
            expert_full[0],
            expert_full[1],
            chosen,
            dispatch,
            groups,
        )
        valid_row = valid_all[micro_index]
        difference = final - teacher[micro_index].astype(jnp.float32)
        squared_local = squared_local + 0.5 * jnp.sum(valid_row[:, None] * difference * difference)
        upstream = loss_ratio * valid_row[:, None] * difference
        saved.append(
            (
                stream_in,
                stream_one,
                stream_two,
                stream_three,
                stored_one,
                stored_two,
                stored_three,
                stored_four,
                allowed,
                chosen,
                dispatch,
                valid_row,
                upstream,
            )
        )
        outputs.append(final.astype(jnp.bfloat16))
    dense_total = None
    expert_total = None
    token_grads = [None] * micro_count
    for micro_index in reversed(range(micro_count)):
        (
            stream_in,
            stream_one,
            stream_two,
            stream_three,
            stored_one,
            stored_two,
            stored_three,
            stored_four,
            allowed,
            chosen,
            dispatch,
            valid_row,
            upstream,
        ) = saved[micro_index]
        dense_full, expert_full = gathered
        grad_three, mixer_part, expert_part = mixture_backward(
            stream_three,
            dense_full[12],
            dense_full[13],
            dense_full[14],
            expert_full[0],
            expert_full[1],
            chosen,
            dispatch,
            valid_row,
            expert_share,
            balance_scale,
            stored_four,
            upstream,
        )
        grad_two, upper_part = attend_backward(
            stream_two,
            dense_full[8],
            dense_full[9],
            dense_full[10],
            dense_full[11],
            allowed,
            stored_three,
            grad_three,
        )
        grad_one, feed_part = feed_backward(
            stream_one,
            dense_full[4],
            dense_full[5],
            dense_full[6],
            dense_full[7],
            stored_two,
            grad_two,
        )
        grad_in, lower_part = attend_backward(
            stream_in,
            dense_full[0],
            dense_full[1],
            dense_full[2],
            dense_full[3],
            allowed,
            stored_one,
            grad_one,
        )
        token_grads[micro_index] = grad_in
        dense_part = lower_part + feed_part + upper_part + mixer_part
        if dense_total is None:
            dense_total = dense_part
            expert_total = expert_part
        else:
            dense_total = jax.tree.map(jnp.add, dense_total, dense_part)
            expert_total = jax.tree.map(jnp.add, expert_total, expert_part)
    dense_partial = jax.tree.map(
        lambda part: part.astype(jnp.float32),
        lax.psum_scatter(shortened(dense_total), "dp", scatter_dimension=0, tiled=True),
    )
    dense_grads = jax.tree.map(
        lambda part: part.astype(jnp.float32),
        lax.psum_scatter(shortened(dense_partial), "expert", scatter_dimension=0, tiled=True),
    )
    expert_grads = jax.tree.map(
        lambda part: part.astype(jnp.float32),
        lax.psum_scatter(shortened(expert_total), "dp", scatter_dimension=1, tiled=True),
    )
    squared_total = lax.psum(squared_local, ("dp", "expert"))
    mean_loss = loss_ratio * squared_total / (total_tokens * features)
    return (
        (jnp.stack(outputs), jnp.stack(token_grads))
        + tuple(dense_grads)
        + tuple(expert_grads)
        + (mean_loss,)
    )


def solution(mesh):
    placed = (
        P(("dp", "expert"), None, None),
        P(("dp", "expert"), None, None),
        P(("dp", "expert"), None, None),
        P(("dp", "expert")),
        P(("dp", "expert"), None),
        P(("dp", "expert")),
        P(("dp", "expert")),
        P(("dp", "expert"), None),
        P(("dp", "expert"), None),
        P(("dp", "expert")),
        P(("dp", "expert")),
        P(("dp", "expert"), None),
        P(("dp", "expert"), None),
        P(("dp", "expert")),
        P(("dp", "expert")),
        P(("dp", "expert"), None),
        P(("dp", "expert"), None),
        P(("dp", "expert")),
        P(("dp", "expert")),
        P(("dp", "expert"), None),
        P("expert", "dp", None),
        P("expert", "dp", None),
    )
    return jax.shard_map(
        body,
        mesh=mesh,
        in_specs=placed,
        out_specs=(
            P(("dp", "expert"), None, None),
            P(("dp", "expert"), None, None),
            P(("dp", "expert")),
            P(("dp", "expert")),
            P(("dp", "expert"), None),
            P(("dp", "expert"), None),
            P(("dp", "expert")),
            P(("dp", "expert")),
            P(("dp", "expert"), None),
            P(("dp", "expert"), None),
            P(("dp", "expert")),
            P(("dp", "expert")),
            P(("dp", "expert"), None),
            P(("dp", "expert"), None),
            P(("dp", "expert")),
            P(("dp", "expert")),
            P(("dp", "expert"), None),
            P("expert", "dp", None),
            P("expert", "dp", None),
            P(),
        ),
        check_vma=False,
    )
```

profile of v0, /device:TPU:0, one launch (start us, length us, event | category | flops | bytes accessed | tf_op | source)
XLA Modules:
  0.0 1195.2 jit_solution(7187353167507203987)
XLA Ops:
  16.6 42.3 %all-reduce.30 = (f32[4]{0:T(128)S(1)}, f32[]{:T(128)}) all-reduce(f32[4]{0:T(128)S(1)} %select_reduce_fusion, f32[]{:T(128)} %convert_reduce_fusion.2), channel_id=1, replica_groups=mesh['dp'=8,'expert'=4] {'dp','expert'}, use_global_device_ids=true, to_apply=%region_36.37 | all-reduce | flops 5 | bytes 40 | tf_op jit(solution)/shard_map/psum | solution.py:276
  76.3 41.1 %all-reduce.31 = (bf16[768]{0:T(1024)(128)(2,1)S(1)}, bf16[768]{0:T(1024)(128)(2,1)S(1)}, bf16[768]{0:T(1024)(128)(2,1)S(1)}, bf16[768]{0:T(1024)(128)(2,1)S(1)}...) all-reduce(bf16[768]{0:T(1024)(128)(2,1)S(1)} %dynamic-update-slice, ...), channel_id=1, replica_groups=mesh['dp'=8,'expert'=4] {'dp','expert'}, use_global_device_ids=true, to_apply=%add.1 | all-reduce | flops 6144 | bytes 24576
  121.2 66.7 %all-gather = bf16[32,24,4]{1,2,0:T(4,128)(2,1)S(1)} all-gather(bf16[1,24,4]{1,2,0:T(4,128)(2,1)} %bitcast.594), channel_id=1, replica_groups=mesh['dp'=8,'expert'=4] {'dp','expert'}, dimensions={0}, use_global_device_ids=true | all-gather | bytes 6336 | tf_op jit(solution)/shard_map/all_gather | solution.py:299
  190.4 3.8 convolution_convert_fusion.1
  211.2 49.2 %all-gather.16.cloned.1.call-done = bf16[3072,768]{1,0:T(8,128)(2,1)} async-done(((bf16[96,768]{1,0:T(8,128)(2,1)}), bf16[3072,768]{1,0:T(8,128)(2,1)}) %all-gather.16.cloned.1.call-update) | async-done | bytes 4718608 | tf_op jit(solution)/shard_map/all_gather | solution.py:292
  264.1 58.0 %all-gather.18.cloned.1.call-done = bf16[768,2304]{1,0:T(8,128)(2,1)} async-done(((bf16[24,2304]{1,0:T(8,128)(2,1)}), bf16[768,2304]{1,0:T(8,128)(2,1)}) %all-gather.18.cloned.1.call-update) | async-done | bytes 3538960 | tf_op jit(solution)/shard_map/all_gather | solution.py:295
  342.0 35.7 %all-gather.20.cloned.1.call-done = bf16[768,768]{1,0:T(8,128)(2,1)} async-done(((bf16[24,768]{1,0:T(8,128)(2,1)}), bf16[768,768]{1,0:T(8,128)(2,1)}) %all-gather.20.cloned.1.call-update) | async-done | bytes 1179664 | tf_op jit(solution)/shard_map/all_gather | solution.py:296
  386.5 4.1 all-to-all-start.2
  400.0 4.1 all-to-all-start
  404.2 25.9 %all-gather.22.cloned.1.call-done = bf16[1,768,3072]{2,1,0:T(8,128)(2,1)} async-done(((bf16[1,96,3072]{2,1,0:T(8,128)(2,1)}), bf16[1,768,3072]{2,1,0:T(8,128)(2,1)}) %all-gather.22.cloned.1.call-update) | async-done | bytes 4718608 | tf_op jit(solution)/shard_map/all_gather | solution.py:302
  430.1 5.5 fusion.23
  435.6 46.7 %all-gather.24.cloned.1.call-done = bf16[1,3072,768]{2,1,0:T(8,128)(2,1)} async-done(((bf16[1,384,768]{2,1,0:T(8,128)(2,1)}), bf16[1,3072,768]{2,1,0:T(8,128)(2,1)}) %all-gather.24.cloned.1.call-update) | async-done | bytes 4718608 | tf_op jit(solution)/shard_map/all_gather | solution.py:303
  482.2 6.0 fusion.95
  488.2 4.1 all-to-all-start.3
  492.4 3.9 fusion.20
  498.0 5.1 fusion.100
  503.1 4.1 all-to-all-start.1
  510.4 4.1 all-to-all-done.1
  514.5 3.6 fusion.166
  520.6 4.1 all-to-all-start.6
  531.2 4.3 all-to-all-start.4
  535.5 6.1 fusion.48
  542.8 4.5 fusion.105
  547.3 4.2 all-to-all-start.7
  551.5 6.1 fusion.53
  558.8 4.5 fusion.108
  563.3 4.2 all-to-all-start.5
  641.9 4.0 add_convert_fusion
  648.7 3.7 add_convert_fusion.1
  653.0 27.4 %reduce-scatter.41.cloned.1.call-done = bf16[96,768]{1,0:T(8,128)(2,1)} async-done(((bf16[768,768]{1,0:T(8,128)(2,1)}), bf16[96,768]{1,0:T(8,128)(2,1)}) %reduce-scatter.41.cloned.1.call-update) | async-done | bytes 147472 | tf_op jit(solution)/shard_map/reduce_scatter | solution.py:430
  680.4 44.2 %reduce-scatter.39.cloned.1.call-done = bf16[96,2304]{1,0:T(8,128)(2,1)} async-done(((bf16[768,2304]{1,0:T(8,128)(2,1)}), bf16[96,2304]{1,0:T(8,128)(2,1)}) %reduce-scatter.39.cloned.1.call-update) | async-done | bytes 442384 | tf_op jit(solution)/shard_map/reduce_scatter | solution.py:430
  724.7 8.0 fusion.70
  732.7 36.6 %reduce-scatter.29.cloned.1.call-done = bf16[96,2304]{1,0:T(8,128)(2,1)} async-done(((bf16[768,2304]{1,0:T(8,128)(2,1)}), bf16[96,2304]{1,0:T(8,128)(2,1)}) %reduce-scatter.29.cloned.1.call-update) | async-done | bytes 442384 | tf_op jit(solution)/shard_map/reduce_scatter | solution.py:430
  769.4 6.5 fusion.19
  779.7 4.7 fusion.18
  789.1 38.9 %psum.23 = f32[]{:T(128)} all-reduce(f32[]{:T(128)S(6)} %add.535), channel_id=1, replica_groups=mesh['dp'=8,'expert'=4] {'dp','expert'}, use_global_device_ids=true, to_apply=%region_112.113 | all-reduce | flops 1 | bytes 8 | tf_op jit(solution)/shard_map/psum | solution.py:440
  836.8 19.9 %reduce-scatter.35.cloned.1.call-done = bf16[384,768]{1,0:T(8,128)(2,1)} async-done(((bf16[3072,768]{1,0:T(8,128)(2,1)}), bf16[384,768]{1,0:T(8,128)(2,1)}) %reduce-scatter.35.cloned.1.call-update) | async-done | bytes 589840 | tf_op jit(solution)/shard_map/reduce_scatter | solution.py:430
  858.5 27.4 %all-reduce.32 = (bf16[768]{0:T(1024)(128)(2,1)S(1)}, bf16[768]{0:T(1024)(128)(2,1)S(1)}, bf16[768]{0:T(1024)(128)(2,1)S(1)}, bf16[768]{0:T(1024)(128)(2,1)S(1)}...) all-reduce(bf16[768]{0:T(1024)(128)(2,1)S(1)} %add_convert_fusion.1, ...), channel_id=2, replica_groups=mesh['dp'=8,'expert'=4] {'dp'}, use_global_device_ids=true, to_apply=%region_64.65.clone | all-reduce | flops 6144 | bytes 24576
  886.5 10.2 all-reduce.33
  900.2 12.7 %reduce-scatter.33.cloned.1.call-done = bf16[96,3072]{1,0:T(8,128)(2,1)} async-done(((bf16[768,3072]{1,0:T(8,128)(2,1)}), bf16[96,3072]{1,0:T(8,128)(2,1)}) %reduce-scatter.33.cloned.1.call-update) | async-done | bytes 589840 | tf_op jit(solution)/shard_map/reduce_scatter | solution.py:430
  917.5 20.0 %reduce-scatter.51.cloned.1.call-done = bf16[24,768]{1,0:T(8,128)(2,1)} async-done(((bf16[96,768]{1,0:T(8,128)(2,1)}), bf16[24,768]{1,0:T(8,128)(2,1)}) %reduce-scatter.51.cloned.1.call-update) | async-done | bytes 36880
  938.9 24.8 %reduce-scatter.57.cloned.1.call-done = bf16[24,768]{1,0:T(8,128)(2,1)} async-done(((bf16[96,768]{1,0:T(8,128)(2,1)}), bf16[24,768]{1,0:T(8,128)(2,1)}) %reduce-scatter.57.cloned.1.call-update) | async-done | bytes 36880
  965.1 25.9 %reduce-scatter.55.cloned.1.call-done = bf16[24,2304]{1,0:T(8,128)(2,1)} async-done(((bf16[96,2304]{1,0:T(8,128)(2,1)}), bf16[24,2304]{1,0:T(8,128)(2,1)}) %reduce-scatter.55.cloned.1.call-update) | async-done | bytes 110608
  992.5 25.5 %reduce-scatter.49.cloned.1.call-done = bf16[24,2304]{1,0:T(8,128)(2,1)} async-done(((bf16[96,2304]{1,0:T(8,128)(2,1)}), bf16[24,2304]{1,0:T(8,128)(2,1)}) %reduce-scatter.49.cloned.1.call-update) | async-done | bytes 110608
  1019.7 55.6 %reduce-scatter.45.cloned.1.call-done = bf16[1,384,768]{2,1,0:T(8,128)(2,1)} async-done(((bf16[1,3072,768]{2,1,0:T(8,128)(2,1)}), bf16[1,384,768]{2,1,0:T(8,128)(2,1)}) %reduce-scatter.45.cloned.1.call-update) | async-done | bytes 589840 | tf_op jit(solution)/shard_map/reduce_scatter | solution.py:438
  1077.4 53.6 %reduce-scatter.43.cloned.1.call-done = bf16[1,96,3072]{2,1,0:T(8,128)(2,1)} async-done(((bf16[1,768,3072]{2,1,0:T(8,128)(2,1)}), bf16[1,96,3072]{2,1,0:T(8,128)(2,1)}) %reduce-scatter.43.cloned.1.call-update) | async-done | bytes 589840 | tf_op jit(solution)/shard_map/reduce_scatter | solution.py:438
  1133.2 24.4 %reduce-scatter.37.cloned.1.call-done = bf16[96,768]{1,0:T(8,128)(2,1)} async-done(((bf16[384,768]{1,0:T(8,128)(2,1)}), bf16[96,768]{1,0:T(8,128)(2,1)}) %reduce-scatter.37.cloned.1.call-update) | async-done | bytes 147472 | tf_op jit(solution)/shard_map/reduce_scatter | solution.py:434
  1159.3 26.3 %reduce-scatter.53.cloned.1.call-done = bf16[24,3072]{1,0:T(8,128)(2,1)} async-done(((bf16[96,3072]{1,0:T(8,128)(2,1)}), bf16[24,3072]{1,0:T(8,128)(2,1)}) %reduce-scatter.53.cloned.1.call-update) | async-done | bytes 147472
  (732 shorter events, 218.3 us)
Async XLA Ops:
  7.2 182.6 %copy-start.155 = (s32[2,128,1]{1,2,0:T(1,128)S(1)}, s32[2,128,1]{1,2,0:T(1,128)}, u32[]{:S(2)}) copy-start(s32[2,128,1]{1,2,0:T(1,128)} %param.24) | copy-start | bytes 3076
  7.2 183.2 %all-gather.10.cloned.1.call-start = ((), (), s32[]{:S(2)}) async-start(), calls=%async_computation.23 | async-start | bytes 3649536 | tf_op jit(solution)/shard_map/all_gather | solution.py:287
  7.9 194.6 %all-gather.12.cloned.1.call-start = ((), (), s32[]{:S(2)}) async-start(), calls=%async_computation.24 | async-start | bytes 1216512 | tf_op jit(solution)/shard_map/all_gather | solution.py:288
  8.7 198.8 %all-gather.14.cloned.1.call-start = ((), (), s32[]{:S(2)}) async-start(), calls=%async_computation.25 | async-start | bytes 4866048 | tf_op jit(solution)/shard_map/all_gather | solution.py:291
  9.4 251.0 %all-gather.16.cloned.1.call-start = ((), (), s32[]{:S(2)}) async-start(), calls=%async_computation.26 | async-start | bytes 4866048 | tf_op jit(solution)/shard_map/all_gather | solution.py:292
  10.0 312.1 %all-gather.18.cloned.1.call-start = ((), (), s32[]{:S(2)}) async-start(), calls=%async_computation.27 | async-start | bytes 3649536 | tf_op jit(solution)/shard_map/all_gather | solution.py:295
  10.6 367.2 %all-gather.20.cloned.1.call-start = ((), (), s32[]{:S(2)}) async-start(), calls=%async_computation.28 | async-start | bytes 1216512 | tf_op jit(solution)/shard_map/all_gather | solution.py:296
  11.2 418.9 %all-gather.22.cloned.1.call-start = ((), (), s32[]{:S(2)}) async-start(), calls=%async_computation.29 | async-start | bytes 5308416 | tf_op jit(solution)/shard_map/all_gather | solution.py:302
  11.9 470.3 %all-gather.24.cloned.1.call-start = ((), (), s32[]{:S(2)}) async-start(), calls=%async_computation.30 | async-start | bytes 5308416 | tf_op jit(solution)/shard_map/all_gather | solution.py:303
  15.8 174.6 %copy-start.146 = (s32[128]{0:T(128)}, s32[128]{0:T(128)S(1)}, u32[]{:S(2)}) copy-start(s32[128]{0:T(128)S(1)} %get-tuple-element.137) | copy-start | bytes 1540
  15.8 174.6 %copy-start.150 = (s32[128]{0:T(128)}, s32[128]{0:T(128)S(1)}, u32[]{:S(2)}) copy-start(s32[128]{0:T(128)S(1)} %get-tuple-element.136) | copy-start | bytes 1540
  68.4 52.7 %copy-start.186 = (f32[128]{0:T(128)}, f32[128]{0:T(128)S(1)}, u32[]{:S(2)}) copy-start(f32[128]{0:T(128)S(1)} %get-tuple-element.53) | copy-start | bytes 1540
  68.4 52.7 %copy-start.188 = (f32[128]{0:T(128)}, f32[128]{0:T(128)S(1)}, u32[]{:S(2)}) copy-start(f32[128]{0:T(128)S(1)} %get-tuple-element.52) | copy-start | bytes 1540
  204.5 121.3 %copy-start.24 = (f32[128,768]{1,0:T(8,128)}, f32[128,768]{1,0:T(8,128)S(1)}, u32[]{:S(2)}) copy-start(f32[128,768]{1,0:T(8,128)S(1)} %get-tuple-element.143) | copy-start | bytes 1179652
  204.6 121.3 %copy-start.137 = (f32[128]{0:T(128)}, f32[128]{0:T(128)S(1)}, u32[]{:S(2)}) copy-start(f32[128]{0:T(128)S(1)} %broadcast_multiply_fusion.10) | copy-start | bytes 1540
  205.3 120.5 %copy-start.156 = (f32[128]{0:T(128)}, f32[128]{0:T(128)S(1)}, u32[]{:S(2)}) copy-start(f32[128]{0:T(128)S(1)} %fusion.262) | copy-start | bytes 1540
  207.3 53.1 %copy-start.14 = (f32[128,768]{1,0:T(8,128)}, f32[128,768]{1,0:T(8,128)S(1)}, u32[]{:S(2)}) copy-start(f32[128,768]{1,0:T(8,128)S(1)} %get-tuple-element.153) | copy-start | bytes 1179652
  211.1 52.7 %copy-start.34 = (f32[128,3072]{1,0:T(8,128)}, f32[128,3072]{1,0:T(8,128)S(1)}, u32[]{:S(2)}) copy-start(f32[128,3072]{1,0:T(8,128)S(1)} %fusion.276) | copy-start | bytes 4718596
  211.1 111.0 %copy-start.88 = (f32[768]{0:T(1024)S(1)}, f32[768]{0:T(1024)}, u32[]{:S(2)}) copy-start(f32[768]{0:T(1024)} %convert_element_type.510) | copy-start | bytes 9220
  263.9 62.0 %copy-start.11 = (f32[128,768]{1,0:T(8,128)}, f32[128,768]{1,0:T(8,128)S(1)}, u32[]{:S(2)}) copy-start(f32[128,768]{1,0:T(8,128)S(1)} %get-tuple-element.155) | copy-start | bytes 1179652
  263.9 61.9 %copy-start.120 = (f32[128]{0:T(128)}, f32[128]{0:T(128)S(1)}, u32[]{:S(2)}) copy-start(f32[128]{0:T(128)S(1)} %broadcast_multiply_fusion.5) | copy-start | bytes 1540
  264.1 61.8 %copy-start.194 = (f32[128]{0:T(128)}, f32[128]{0:T(128)S(1)}, u32[]{:S(2)}) copy-start(f32[128]{0:T(128)S(1)} %multiply_reduce_fusion.19) | copy-start | bytes 1540
  264.1 61.8 %copy-start.143 = (f32[128]{0:T(128)}, f32[128]{0:T(128)S(1)}, u32[]{:S(2)}) copy-start(f32[128]{0:T(128)S(1)} %fusion.267) | copy-start | bytes 1540
  386.5 13.5 %all-to-all-start.2 = ((bf16[4,1,64,768]{3,2,1,0:T(8,128)(2,1)}), bf16[4,1,64,768]{3,2,1,0:T(8,128)(2,1)}, u32[]{:S(2)}, u32[]{:S(2)}) async-start(bf16[4,1,64,768]{3,2,1,0:T(8,128)(2,1)} %bitcast.581), calls=%async_computation.2 | async-start | bytes 786432 | tf_op jit(solution)/shard_map/all_to_all | solution.py:153
  400.0 88.2 %all-to-all-start = ((bf16[4,1,64,768]{3,2,1,0:T(8,128)(2,1)}), bf16[4,1,64,768]{3,2,1,0:T(8,128)(2,1)}, u32[]{:S(2)}, u32[]{:S(2)}) async-start(bf16[4,1,64,768]{3,2,1,0:T(8,128)(2,1)} %bitcast.582), calls=%async_computation | async-start | bytes 786432 | tf_op jit(solution)/shard_map/all_to_all | solution.py:153
  488.2 14.8 %all-to-all-start.3 = ((bf16[4,1,64,768]{3,2,1,0:T(8,128)(2,1)}), bf16[4,1,64,768]{3,2,1,0:T(8,128)(2,1)}, u32[]{:S(2)}, u32[]{:S(2)}) async-start(bf16[4,1,64,768]{3,2,1,0:T(8,128)(2,1)} %fusion.95), calls=%async_computation.3 | async-start | bytes 786432 | tf_op jit(solution)/shard_map/all_to_all | solution.py:160
  503.1 11.5 all-to-all-start.1
  520.6 10.5 all-to-all-start.6
  531.2 16.2 %all-to-all-start.4 = ((bf16[4,1,64,768]{3,2,1,0:T(8,128)(2,1)}), bf16[4,1,64,768]{3,2,1,0:T(8,128)(2,1)}, u32[]{:S(2)}, u32[]{:S(2)}) async-start(bf16[4,1,64,768]{3,2,1,0:T(8,128)(2,1)} %bitcast.583), calls=%async_computation.4 | async-start | bytes 786432 | tf_op jit(solution)/shard_map/all_to_all | solution.py:194
  547.3 15.9 %all-to-all-start.7 = ((bf16[4,1,64,768]{3,2,1,0:T(8,128)(2,1)}), bf16[4,1,64,768]{3,2,1,0:T(8,128)(2,1)}, u32[]{:S(2)}, u32[]{:S(2)}) async-start(bf16[4,1,64,768]{3,2,1,0:T(8,128)(2,1)} %fusion.105), calls=%async_computation.7 | async-start | bytes 786432 | tf_op jit(solution)/shard_map/all_to_all | solution.py:209
  563.3 10.2 all-to-all-start.5
  567.5 85.0 %reduce-scatter.31.cloned.1.call-start = ((), (), s32[]{:S(2)}) async-start(), calls=%async_computation.32 | async-start | bytes 1327104 | tf_op jit(solution)/shard_map/reduce_scatter | solution.py:430
  615.6 64.7 %reduce-scatter.41.cloned.1.call-start = ((), (), s32[]{:S(2)}) async-start(), calls=%async_computation.37 | async-start | bytes 1327104 | tf_op jit(solution)/shard_map/reduce_scatter | solution.py:430
  617.7 106.9 %reduce-scatter.39.cloned.1.call-start = ((), (), s32[]{:S(2)}) async-start(), calls=%async_computation.36 | async-start | bytes 3981312 | tf_op jit(solution)/shard_map/reduce_scatter | solution.py:430
  622.2 147.1 %reduce-scatter.29.cloned.1.call-start = ((), (), s32[]{:S(2)}) async-start(), calls=%async_computation.31 | async-start | bytes 3981312 | tf_op jit(solution)/shard_map/reduce_scatter | solution.py:430
  637.8 192.6 %reduce-scatter.47.cloned.1.call-start = ((), (), s32[]{:S(2)}) async-start(), calls=%async_computation.40 | async-start | bytes 221184
  640.1 216.6 %reduce-scatter.35.cloned.1.call-start = ((), (), s32[]{:S(2)}) async-start(), calls=%async_computation.34 | async-start | bytes 5308416 | tf_op jit(solution)/shard_map/reduce_scatter | solution.py:430
  646.0 266.8 %reduce-scatter.33.cloned.1.call-start = ((), (), s32[]{:S(2)}) async-start(), calls=%async_computation.33 | async-start | bytes 5308416 | tf_op jit(solution)/shard_map/reduce_scatter | solution.py:430
  652.4 285.1 %reduce-scatter.51.cloned.1.call-start = ((), (), s32[]{:S(2)}) async-start(), calls=%async_computation.42 | async-start | bytes 184320
  653.0 310.7 %reduce-scatter.57.cloned.1.call-start = ((), (), s32[]{:S(2)}) async-start(), calls=%async_computation.45 | async-start | bytes 184320
  680.4 310.5 %reduce-scatter.55.cloned.1.call-start = ((), (), s32[]{:S(2)}) async-start(), calls=%async_computation.44 | async-start | bytes 552960
  724.7 293.4 %reduce-scatter.49.cloned.1.call-start = ((), (), s32[]{:S(2)}) async-start(), calls=%async_computation.41 | async-start | bytes 552960
  769.3 306.0 %reduce-scatter.45.cloned.1.call-start = ((), (), s32[]{:S(2)}) async-start(), calls=%async_computation.39 | async-start | bytes 5308416 | tf_op jit(solution)/shard_map/reduce_scatter | solution.py:438
  775.9 355.1 %reduce-scatter.43.cloned.1.call-start = ((), (), s32[]{:S(2)}) async-start(), calls=%async_computation.38 | async-start | bytes 5308416 | tf_op jit(solution)/shard_map/reduce_scatter | solution.py:438
  784.4 49.8 %copy-start.113 = (f32[128]{0:T(128)S(1)}, f32[128]{0:T(128)}, u32[]{:S(2)}) copy-start(f32[128]{0:T(128)} %copy-done.111) | copy-start | bytes 1540
  784.4 49.8 %copy-start.116 = (f32[128]{0:T(128)S(1)}, f32[128]{0:T(128)}, u32[]{:S(2)}) copy-start(f32[128]{0:T(128)} %copy-done.114) | copy-start | bytes 1540
  784.4 373.2 %reduce-scatter.37.cloned.1.call-start = ((), (), s32[]{:S(2)}) async-start(), calls=%async_computation.35 | async-start | bytes 737280 | tf_op jit(solution)/shard_map/reduce_scatter | solution.py:434
  856.7 328.9 %reduce-scatter.53.cloned.1.call-start = ((), (), s32[]{:S(2)}) async-start(), calls=%async_computation.43 | async-start | bytes 737280
  (199 other events, 624.9 us)
Sparse Core Ops, SparseCore 0:
  10.9 62.9 all-gather.9
  76.8 52.8 all-gather.11
  132.6 62.5 all-gather.13
  198.0 62.3 all-gather.15
  263.1 58.9 all-gather.17
  324.8 52.8 all-gather.19
  379.4 50.6 all-gather.21
  431.7 50.4 all-gather.23
  615.8 30.7 reduce-scatter.30
  649.2 31.1 reduce-scatter.40
  682.7 41.8 reduce-scatter.38
  726.9 42.2 reduce-scatter.28
  772.1 28.7 reduce-scatter.46
  803.2 53.4 reduce-scatter.34
  858.9 53.8 reduce-scatter.32
  915.7 21.7 reduce-scatter.50
  940.3 23.3 reduce-scatter.56
  966.6 24.2 reduce-scatter.54
  993.8 24.2 reduce-scatter.48
  1020.3 54.9 reduce-scatter.44
  1077.7 53.3 reduce-scatter.42
  1134.2 23.4 reduce-scatter.36
  1160.5 25.0 reduce-scatter.52
where the time goes:
time: 1200 us
  waiting for transfers between devices  628 us (52%)
  blocking collectives  226 us (19%)
  matrix products  178 us (15%)
  other arithmetic  57.6 us (5%)
  local copies, waits for them, and re-layouts  45.1 us (4%)
  starting transfers between devices  35 us (3%)
  between operations  24.6 us (2%)
    reduce_scatter x6, waiting for transfers between devices, body(): lax.psum_scatter(shortened(dense_total), 'dp', scatter_dimension=0, tiled...  141 us
    unnamed x29, waiting for transfers between devices  128 us
    reduce_scatter x2, waiting for transfers between devices, body(): lax.psum_scatter(shortened(expert_total), 'dp', scatter_dimension=1, tile...  109 us
    unnamed x3, blocking collectives  78.6 us
    all_gather x1, blocking collectives, body(): lax.all_gather(dense_shards[14], ('dp', 'expert'), axis=0, tiled=True)  66.7 us
    all_gather x1, waiting for transfers between devices, body(): lax.all_gather(dense_shards[10], ('dp', 'expert'), axis=0, tiled=True)  58 us
    all_gather x1, waiting for transfers between devices, body(): lax.all_gather(dense_shards[7], ('dp', 'expert'), axis=0, tiled=True)  49.2 us
    all_gather x1, waiting for transfers between devices, body(): lax.all_gather(expert_shrink, 'dp', axis=1, tiled=True)  46.7 us
  transfers between devices with their start and end apart: 31, of which 21 were waited for; matrix products, arithmetic and copies ran while one was open for 18% of the time, Pallas kernels for 0%

commit v1 on v0

v1 whole, which is shorter than its diff:
```python
import jax
import jax.numpy as jnp
from jax import lax
from jax.sharding import PartitionSpec as P

H = 12
HD = 64
HIGH = lax.Precision.HIGHEST
AXES = ("dp", "expert")
F32 = jnp.float32
BF16 = jnp.bfloat16


def place():
    depth = lax.axis_size("dp") // 2
    row = lax.axis_index("dp")
    return depth, lax.axis_size("expert"), row // 2, row % 2, lax.axis_index("expert")


def pairs(target):
    depth, across = lax.axis_size("dp") // 2, lax.axis_size("expert")
    out = []
    for z in range(depth):
        for c in range(2):
            for e in range(across):
                to = target(z, c, e)
                if to is not None and 0 <= to[0] < depth:
                    out.append(((z * 2 + c) * across + e, (to[0] * 2 + to[1]) * across + to[2]))
    return out


def hop(values, target):
    return lax.ppermute(values, AXES, pairs(target))


def swap_cores(values):
    return hop(values, lambda z, c, e: (z, 1 - c, e))


def first_side(values):
    return hop(values, lambda z, c, e: (z, c, e ^ (1 + c)))


def second_side(values):
    return hop(values, lambda z, c, e: (z, c, e ^ (2 - c)))


def gather_line(own):
    depth, _, z, _, _ = place()
    ups, downs = [own], [own]
    for _ in range(depth - 1):
        ups.append(hop(ups[-1], lambda z, c, e: (z + 1, c, e)))
        downs.append(hop(downs[-1], lambda z, c, e: (z - 1, c, e)))
    slots = []
    for j in range(depth):
        value = own
        for t in range(1, j + 1):
            value = jnp.where(z == j - t, downs[t], value)
        for t in range(1, depth - j):
            value = jnp.where(z == j + t, ups[t], value)
        slots.append(value)
    return jnp.stack(slots)


def gather_sides(line, buffer):
    depth, across, z, c, e = place()
    if across != 4:
        whole = lax.all_gather(line, "expert", axis=1)
        both = jnp.stack([whole, swap_cores(whole)])
        both = jnp.where(c == 0, both, both[::-1])
        return jnp.moveaxis(both, 0, 1)
    one = first_side(line)
    two, three = second_side(line), second_side(one)
    there = (e, e ^ (1 + c), e ^ (2 - c), e ^ 3)
    over = (e, e ^ (2 - c), e ^ (1 + c), e ^ 3)
    for part, mine, theirs in zip((line, one, two, three), there, over):
        buffer = lax.dynamic_update_slice(buffer, part[:, None, None], (0, c, mine, 0, 0))
        buffer = lax.dynamic_update_slice(
            buffer, swap_cores(part)[:, None, None], (0, 1 - c, theirs, 0, 0)
        )
    return buffer


def gather_dense(own):
    depth, across, _, _, _ = place()
    rows, columns = own.shape
    buffer = jnp.zeros((depth, 2, across, rows, columns), own.dtype)
    return gather_sides(gather_line(own), buffer).reshape(-1, columns)


def add(first, second):
    return (first.astype(F32) + second.astype(F32)).astype(BF16)


def scatter_line(line):
    depth, _, z, _, _ = place()
    total = lax.dynamic_index_in_dim(line, z, 0, False).astype(F32)
    for sign in (1, -1):
        come = None
        for k in range(depth - 1, 0, -1):
            at = jnp.clip(z + sign * k, 0, depth - 1)
            part = lax.dynamic_index_in_dim(line, at, 0, False)
            if come is not None:
                part = add(part, come)
            come = hop(
                part,
                lambda z, c, e: (z + sign, c, e) if 0 <= z + sign * k < depth else None,
            )
        total = total + come.astype(F32)
    return total


def scatter_dense(grad):
    depth, across, z, c, e = place()
    columns = grad.shape[1]
    grad = grad.reshape(depth, 2, across, -1, columns)
    mine = lax.dynamic_index_in_dim(grad, c, 1, False)
    other = swap_cores(lax.dynamic_index_in_dim(grad, 1 - c, 1, False))
    if across != 4:
        line = lax.psum_scatter(add(mine, other), "expert", scatter_dimension=1, tiled=True)
        return scatter_line(line[:, 0])
    pick = lambda a, at: lax.dynamic_index_in_dim(a, at, 1, False)
    half = lambda at: add(pick(mine, at), pick(other, at))
    near = add(half(e), second_side(half(e ^ (2 - c))))
    far = add(half(e ^ (1 + c)), second_side(half(e ^ 3)))
    return scatter_line(add(near, first_side(far)))


def total_over_devices(value):
    depth, across, _, _, _ = place()
    value = value + swap_cores(value)
    if across & (across - 1) or depth & (depth - 1):
        value = lax.psum(value, "expert")
        values = lax.all_gather(value, "dp")[::2]
        return jnp.sum(values, axis=0)
    step = 1
    while step < across:
        value = value + hop(value, lambda z, c, e: (z, c, e ^ step))
        step *= 2
    step = 1
    while step < depth:
        value = value + hop(value, lambda z, c, e: (z ^ step, c, e))
        step *= 2
    return value


def exchange(rows):
    return lax.all_to_all(rows, "expert", split_axis=0, concat_axis=0, tiled=True)


def dot(a, b):
    return jnp.dot(a, b, preferred_element_type=F32)


def dot_nt(a, b):
    return lax.dot_general(a, b, (((1,), (1,)), ((), ())), preferred_element_type=F32)


def dot_tn(a, b):
    return lax.dot_general(a, b, (((0,), (0,)), ((), ())), preferred_element_type=F32)


def norm(values, gain, bias):
    centered = values - jnp.mean(values, axis=-1, keepdims=True)
    spread = jnp.mean(centered * centered, axis=-1, keepdims=True)
    return centered * lax.rsqrt(spread + 1e-05) * gain + bias


def norm_backward(stream, gain, bias, grad):
    _, back = jax.vjp(norm, stream, gain, bias)
    return back(grad)


def gelu(values):
    return jax.nn.gelu(values, approximate=True)


def gelu_backward(values, grad):
    _, back = jax.vjp(gelu, values)
    return back(grad)[0]


def scores_of(packed, allowed):
    scores = jnp.einsum("mqhd,mkhd->mhqk", packed[:, :, 0], packed[:, :, 1], preferred_element_type=F32)
    return jnp.where(allowed[:, None], scores * HD ** (-0.5), -1e30)


def attend_forward(stream, gain, bias, triple, output, allowed):
    tokens, features = stream.shape
    groups, length, _ = allowed.shape
    normed = norm(stream, gain, bias).astype(BF16)
    packed = dot(normed, triple).astype(BF16).reshape(groups, length, 3, H, HD)
    scores = scores_of(packed, allowed)
    highest = jnp.max(scores, axis=-1, keepdims=True)
    exponent = jnp.exp(scores - highest)
    row_total = jnp.sum(exponent, axis=-1, keepdims=True)
    weights = (exponent / row_total).astype(BF16)
    logsum = highest + jnp.log(row_total)
    context = jnp.einsum("mhqk,mkhd->mqhd", weights, packed[:, :, 2], preferred_element_type=F32)
    context = context.astype(BF16).reshape(tokens, features)
    return stream + dot(context, output), (normed, packed, logsum, context)


def attend_backward(stream, gain, bias, triple, output, allowed, stored, upstream):
    normed, packed, logsum, context = stored
    tokens, features = stream.shape
    groups, length, _ = allowed.shape
    scale = HD ** (-0.5)
    branch = upstream.astype(BF16)
    output_grad = dot_tn(context, branch).astype(BF16)
    context_grad = dot_nt(branch, output).astype(BF16).reshape(groups, length, H, HD)
    probs = jnp.exp(scores_of(packed, allowed) - logsum)
    value_grad = jnp.einsum("mhqk,mqhd->mkhd", probs.astype(BF16), context_grad, preferred_element_type=F32)
    prob_grad = jnp.einsum("mqhd,mkhd->mhqk", context_grad, packed[:, :, 2], preferred_element_type=F32)
    score_grad = (probs * (prob_grad - jnp.sum(probs * prob_grad, axis=-1, keepdims=True))).astype(BF16)
    query_grad = jnp.einsum("mhqk,mkhd->mqhd", score_grad, packed[:, :, 1], preferred_element_type=F32) * scale
    key_grad = jnp.einsum("mhqk,mqhd->mkhd", score_grad, packed[:, :, 0], preferred_element_type=F32) * scale
    packed_grad = jnp.stack([query_grad, key_grad, value_grad], axis=2).astype(BF16)
    packed_grad = packed_grad.reshape(tokens, 3 * features)
    triple_grad = dot_tn(normed, packed_grad).astype(BF16)
    back, gain_grad, bias_grad = norm_backward(stream, gain, bias, dot_nt(packed_grad, triple))
    return upstream + back, gain_grad, bias_grad, triple_grad, output_grad


def feed_forward(stream, gain, bias, expand, shrink):
    normed = norm(stream, gain, bias).astype(BF16)
    inner = dot(normed, expand)
    active = gelu(inner).astype(BF16)
    return stream + dot(active, shrink), (normed, inner)


def feed_backward(stream, gain, bias, expand, shrink, stored, upstream):
    normed, inner = stored
    branch = upstream.astype(BF16)
    shrink_grad = dot_tn(gelu(inner).astype(BF16), branch).astype(BF16)
    inner_grad = gelu_backward(inner, dot_nt(branch, shrink)).astype(BF16)
    expand_grad = dot_tn(normed, inner_grad).astype(BF16)
    back, gain_grad, bias_grad = norm_backward(stream, gain, bias, dot_nt(inner_grad, expand))
    return upstream + back, gain_grad, bias_grad, expand_grad, shrink_grad


def body(
    tokens,
    teacher,
    routes,
    piece_start,
    valid_mask,
    lower_gain,
    lower_bias,
    lower_triple,
    lower_output,
    feed_gain,
    feed_bias,
    feed_expand,
    feed_shrink,
    upper_gain,
    upper_bias,
    upper_triple,
    upper_output,
    mixer_gain,
    mixer_bias,
    router,
    expert_expand,
    expert_shrink,
):
    count, length, features = tokens.shape
    local = count * length
    experts = router.shape[1]
    share_rows = router.shape[0]
    devices = lax.axis_size("dp") * lax.axis_size("expert")
    capacity = max(2, 2 * length // experts)
    total_tokens = local * devices
    valid = valid_mask.astype(F32)
    route = routes[..., 0]
    chosen = (route[..., None] == jnp.arange(experts, dtype=jnp.int32)).astype(F32)

    counts = jnp.concatenate([jnp.sum(valid[..., None] * chosen, axis=1), jnp.sum(valid, axis=1)[:, None]], axis=1)
    counts = jnp.pad(counts.astype(BF16), ((0, share_rows - count), (0, 0)))
    vectors = [lower_gain, lower_bias, feed_gain, feed_bias, upper_gain, upper_bias, mixer_gain, mixer_bias]
    extra = jnp.concatenate([jnp.stack(vectors, axis=1), router, counts], axis=1)
    extra_width = -(-extra.shape[1] // 128) * 128
    extra = jnp.pad(extra, ((0, 0), (0, extra_width - extra.shape[1])))

    lower = gather_dense(jnp.concatenate([lower_triple, lower_output, extra], axis=1))
    middle = gather_dense(jnp.concatenate([feed_expand, upper_triple, upper_output], axis=1))
    shrink_full = gather_dense(feed_shrink)
    expert_in = lax.all_gather(expert_expand[0], "dp", axis=0, tiled=True)
    expert_out = lax.all_gather(expert_shrink[0], "dp", axis=0, tiled=True)
    wide = 3 * features
    triple_one, output_one, extra_full = lower[:, :wide], lower[:, wide : wide + features], lower[:, wide + features :]
    inner_width = feed_expand.shape[1]
    expand_full = middle[:, :inner_width]
    triple_two = middle[:, inner_width : inner_width + wide]
    output_two = middle[:, inner_width + wide :]
    rows = extra_full[:, :8].astype(F32).T
    gains = [rows[k] for k in range(8)]
    router_full = extra_full[:, 8 : 8 + experts]
    sums = extra_full.reshape(devices, share_rows, -1)[:, :count, 8 + experts : 9 + 2 * experts]
    sums = jnp.sum(sums.astype(F32), axis=(0, 1))
    valid_total = sums[experts]
    expert_share = sums[:experts] / valid_total
    loss_ratio = total_tokens / valid_total
    balance_scale = total_tokens * features * 0.1 * experts / valid_total

    position = jnp.arange(length, dtype=jnp.int32)
    inside = (position >= piece_start[:, None]) & (position < piece_start[:, None] + length // 4)
    allowed = (position[:, None] >= position[None, :]) | (inside[:, :, None] & inside[:, None, :])

    earlier = (position[:, None] > position[None, :]).astype(BF16)
    before = jnp.einsum("qk,mke->mqe", earlier, chosen.astype(BF16), preferred_element_type=F32)
    slot = jnp.sum(before * chosen, axis=-1).astype(jnp.int32)
    target = route * (count * capacity) + jnp.arange(count, dtype=jnp.int32)[:, None] * capacity + slot
    places = jnp.arange(experts * count * capacity, dtype=jnp.int32)
    dispatch = (places[:, None] == target.reshape(-1)[None, :]).astype(BF16)
    chosen = chosen.reshape(local, experts)
    valid = valid.reshape(local, 1)

    stream_in = tokens.reshape(local, features).astype(F32)
    stream_one, stored_one = attend_forward(stream_in, gains[0], gains[1], triple_one, output_one, allowed)
    stream_two, stored_two = feed_forward(stream_one, gains[2], gains[3], expand_full, shrink_full)
    stream_three, stored_three = attend_forward(stream_two, gains[4], gains[5], triple_two, output_two, allowed)
    normed = norm(stream_three, gains[6], gains[7]).astype(BF16)
    arrived = exchange(dot(dispatch, normed).astype(BF16))
    logits = dot(normed, router_full)
    gate = jax.nn.sigmoid(jnp.sum(logits * chosen, axis=1, keepdims=True))
    expert_probs = jax.nn.softmax(logits, axis=1)
    inner = dot(arrived, expert_in)
    active = gelu(inner).astype(BF16)
    returned = exchange(dot(active, expert_out).astype(BF16))
    combined = dot_tn(dispatch, returned)
    final = stream_three + gate * combined
    difference = final - teacher.reshape(local, features).astype(F32)
    squared = 0.5 * jnp.sum(valid * difference * difference)
    upstream = loss_ratio * valid * difference

    gate_grad = jnp.sum(upstream * combined, axis=1, keepdims=True)
    landed = exchange(dot(dispatch, (gate * upstream).astype(BF16)).astype(BF16))
    inner_grad = gelu_backward(inner, dot_nt(landed, expert_out)).astype(BF16)
    rows_grad = exchange(dot_nt(inner_grad, expert_in).astype(BF16))
    expert_out_grad = dot_tn(active, landed).astype(BF16)
    expert_in_grad = dot_tn(arrived, inner_grad).astype(BF16)
    expert_out_grad = lax.psum_scatter(expert_out_grad, "dp", scatter_dimension=0, tiled=True)
    expert_in_grad = lax.psum_scatter(expert_in_grad, "dp", scatter_dimension=0, tiled=True)
    routed_grad = dot_tn(dispatch, rows_grad)
    logits_grad = chosen * (gate_grad * gate * (1.0 - gate)) + balance_scale * valid * expert_probs * (
        expert_share - jnp.sum(expert_probs * expert_share, axis=1, keepdims=True)
    )
    router_grad = lax.dot_general(normed.astype(F32), logits_grad, (((0,), (0,)), ((), ())), precision=HIGH)
    normed_grad = routed_grad + lax.dot_general(
        logits_grad, router_full.astype(F32), (((1,), (1,)), ((), ())), precision=HIGH
    )
    back, mixer_gain_grad, mixer_bias_grad = norm_backward(stream_three, gains[6], gains[7], normed_grad)
    grad_three = upstream + back

    grad_two, upper_gain_grad, upper_bias_grad, triple_two_grad, output_two_grad = attend_backward(
        stream_two, gains[4], gains[5], triple_two, output_two, allowed, stored_three, grad_three
    )
    upper_part = scatter_dense(jnp.concatenate([triple_two_grad, output_two_grad], axis=1))
    grad_one, feed_gain_grad, feed_bias_grad, expand_grad, shrink_grad = feed_backward(
        stream_one, gains[2], gains[3], expand_full, shrink_full, stored_two, grad_two
    )
    shrink_part = scatter_dense(shrink_grad)
    expand_part = scatter_dense(expand_grad)
    grad_in, lower_gain_grad, lower_bias_grad, triple_one_grad, output_one_grad = attend_backward(
        stream_in, gains[0], gains[1], triple_one, output_one, allowed, stored_one, grad_one
    )
    small = [
        lower_gain_grad,
        lower_bias_grad,
        feed_gain_grad,
        feed_bias_grad,
        upper_gain_grad,
        upper_bias_grad,
        mixer_gain_grad,
        mixer_bias_grad,
    ]
    small = jnp.concatenate([jnp.stack(small, axis=1), router_grad], axis=1).astype(BF16)
    small = jnp.pad(small, ((0, 0), (0, extra_width - small.shape[1])))
    lower_part = scatter_dense(jnp.concatenate([triple_one_grad, output_one_grad, small], axis=1))
    small = lower_part[:, wide + features :]

    squared_total = total_over_devices(jnp.full((8, 128), squared))[0, 0]
    mean_loss = loss_ratio * squared_total / (total_tokens * features)
    return (
        final.astype(BF16).reshape(tokens.shape),
        grad_in.reshape(tokens.shape),
        small[:, 0],
        small[:, 1],
        lower_part[:, :wide],
        lower_part[:, wide : wide + features],
        small[:, 2],
        small[:, 3],
        expand_part,
        shrink_part,
        small[:, 4],
        small[:, 5],
        upper_part[:, :wide],
        upper_part[:, wide:],
        small[:, 6],
        small[:, 7],
        small[:, 8 : 8 + experts],
        expert_in_grad.astype(F32)[None],
        expert_out_grad.astype(F32)[None],
        mean_loss,
    )


def solution(mesh):
    both = ("dp", "expert")
    token = P(both, None, None)
    vector = P(both)
    matrix = P(both, None)
    expert = P("expert", "dp", None)
    dense = (vector, vector, matrix, matrix, vector, vector, matrix, matrix)
    weights = dense + (vector, vector, matrix, matrix, vector, vector, matrix, expert, expert)
    return jax.shard_map(
        body,
        mesh=mesh,
        in_specs=(token, token, token, vector, matrix) + weights,
        out_specs=(token, token) + weights + (P(),),
        check_vma=False,
    )
```

time: 1200 us -> 648 us (0.54)
  waiting for transfers between devices: 628 us -> 175 us
  blocking collectives: 226 us -> 0 us
  starting transfers between devices: 35 us -> 182 us
  matrix products: 178 us -> 115 us
  local copies, waits for them, and re-layouts: 45.1 us -> 88.6 us
    reduce_scatter x9 -> x2, waiting for transfers between devices: 274 us -> 0.01 us  [the longest x1 0.01 us: body(): lax.psum_scatter(expert_out_grad, 'dp', scatter_dimension=0, tiled=True)]
    all_gather x8 -> x2, waiting for transfers between devices: 216 us -> 0.02 us  [the longest x1 0.02 us: body(): expert_out = lax.all_gather(expert_shrink[0], 'dp', axis=0, tiled=True)]
    ppermute x0 -> x84, starting transfers between devices: none -> 165 us  [hop(): return lax.ppermute(values, AXES, pairs(target))]
    ppermute x0 -> x84, waiting for transfers between devices: none -> 148 us  [hop(): return lax.ppermute(values, AXES, pairs(target))]
    unnamed x29 -> x4, waiting for transfers between devices: 128 us -> 0.73 us
    psum x2 -> x0, blocking collectives: 81.2 us -> none  [the longest x1 42.3 us: body(): lax.psum((jnp.sum(valid_all[..., None] * chosen_all, axis=(0, 1)), jnp.su...]
    unnamed x3 -> x0, blocking collectives: 78.6 us -> none
    all_gather x1 -> x0, blocking collectives: 66.7 us -> none  [body(): lax.all_gather(dense_shards[14], ('dp', 'expert'), axis=0, tiled=True)]
  transfers between devices with their start and end apart: 31 -> 92, of which waited for: 21 -> 27; matrix products, arithmetic and copies ran while one was open for 18% -> 33% of each run, Pallas kernels for 0% -> 0%
where the time goes in v1:
time: 648 us; the launch traced here: 637 us
  starting transfers between devices  182 us (28%)
  waiting for transfers between devices  175 us (27%)
  matrix products  115 us (18%)
  local copies, waits for them, and re-layouts  88.6 us (14%)
  other arithmetic  55.9 us (9%)
  between operations  21 us (3%)
    ppermute x84, starting transfers between devices, hop(): return lax.ppermute(values, AXES, pairs(target))  165 us
    ppermute x84, waiting for transfers between devices, hop(): return lax.ppermute(values, AXES, pairs(target))  148 us
    dot_general x11, matrix products, dot(): return jnp.dot(a, b, preferred_element_type=F32)  39 us
    dot_general x8, matrix products, dot_nt(): lax.dot_general(a, b, (((1,), (1,)), ((), ())), preferred_element_type=F32)  31 us
    dot_general x10, matrix products, dot_tn(): lax.dot_general(a, b, (((0,), (0,)), ((), ())), preferred_element_type=F32)  29.2 us
    all_to_all x4, waiting for transfers between devices, exchange(): lax.all_to_all(rows, 'expert', split_axis=0, concat_axis=0, tiled=True)  25.7 us
    unnamed x302, local copies, waits for them, and re-layouts  21.1 us
    convert_element_type x24, other arithmetic, add(): return (first.astype(F32) + second.astype(F32)).astype(BF16)  20.4 us
  transfers between devices with their start and end apart: 92, of which 27 were waited for; matrix products, arithmetic and copies ran while one was open for 33% of the time, Pallas kernels for 0%

profile of v1, /device:TPU:0, one launch (start us, length us, event | category | flops | bytes accessed | tf_op | source)
XLA Modules:
  0.0 637.0 jit_solution(4116355016371685116)
XLA Ops:
  8.0 4.9 collective-permute-start.26
  26.3 5.2 collective-permute-start
  42.8 5.3 collective-permute-start.13
  54.5 12.1 %collective-permute-done.27 = bf16[96,768]{1,0:T(8,128)(2,1)S(1)} collective-permute-done((bf16[96,768]{1,0:T(8,128)(2,1)S(1)}, bf16[96,768]{1,0:T(8,128)(2,1)S(1)}, u32[]{:S(2)}, u32[]{:S(2)}) %collective-permute-start.27) | collective-permute-done | bytes 147488 | tf_op jit(solution)/shard_map/ppermute | solution.py:33
  66.6 8.3 %collective-permute-start.1 = (bf16[24,3200]{1,0:T(8,128)(2,1)S(1)}, bf16[24,3200]{1,0:T(8,128)(2,1)S(1)}, u32[]{:S(2)}, u32[]{:S(2)}) collective-permute-start(bf16[24,3200]{1,0:T(8,128)(2,1)S(1)} %collective-permute-done), channel_id=1, source_target_pairs={{0,8},{1,9},{2,10},{3,11},{4,12},{5,13},{6,14},{7,15},{8,16},{9,17... | collective-permute-start | bytes 460808 | tf_op jit(solution)/shard_map/ppermute | solution.py:33
  75.0 4.4 collective-permute-start.28
  82.5 5.2 collective-permute-start.14
  89.0 4.6 collective-permute-start.2
  97.0 10.9 %collective-permute-done.5 = bf16[24,3200]{1,0:T(8,128)(2,1)S(1)} collective-permute-done((bf16[24,3200]{1,0:T(8,128)(2,1)S(1)}, bf16[24,3200]{1,0:T(8,128)(2,1)S(1)}, u32[]{:S(2)}, u32[]{:S(2)}) %collective-permute-start.5) | collective-permute-done | bytes 153632 | tf_op jit(solution)/shard_map/ppermute | solution.py:33
  112.5 11.4 %collective-permute-start.15 = (bf16[24,6144]{1,0:T(8,128)(2,1)S(1)}, bf16[24,6144]{1,0:T(8,128)(2,1)S(1)}, u32[]{:S(2)}, u32[]{:S(2)}) collective-permute-start(bf16[24,6144]{1,0:T(8,128)(2,1)S(1)} %collective-permute-done.14), channel_id=1, source_target_pairs={{0,8},{1,9},{2,10},{3,11},{4,12},{5,13},{6,14},{7,15},{8,16},{9,17... | collective-permute-start | bytes 884744 | tf_op jit(solution)/shard_map/ppermute | solution.py:33
  124.5 15.6 %collective-permute-done.18 = bf16[24,6144]{1,0:T(8,128)(2,1)S(1)} collective-permute-done((bf16[24,6144]{1,0:T(8,128)(2,1)S(1)}, bf16[24,6144]{1,0:T(8,128)(2,1)S(1)}, u32[]{:S(2)}, u32[]{:S(2)}) %collective-permute-start.18) | collective-permute-done | bytes 294944 | tf_op jit(solution)/shard_map/ppermute | solution.py:33
  158.1 18.6 %collective-permute-done.37 = bf16[4,96,768]{2,1,0:T(8,128)(2,1)S(1)} collective-permute-done((bf16[4,96,768]{2,1,0:T(8,128)(2,1)}, bf16[4,96,768]{2,1,0:T(8,128)(2,1)S(1)}, u32[]{:S(2)}, u32[]{:S(2)}) %collective-permute-start.37) | collective-permute-done | bytes 589856 | tf_op jit(solution)/shard_map/ppermute | solution.py:33
  179.0 20.5 %collective-permute-done.11 = bf16[4,24,3200]{2,1,0:T(8,128)(2,1)S(1)} collective-permute-done((bf16[4,24,3200]{2,1,0:T(8,128)(2,1)}, bf16[4,24,3200]{2,1,0:T(8,128)(2,1)S(1)}, u32[]{:S(2)}, u32[]{:S(2)}) %collective-permute-start.11) | collective-permute-done | bytes 614432 | tf_op jit(solution)/shard_map/ppermute | solution.py:33
  234.5 4.3 fusion.19
  241.3 4.2 convolution_convert_fusion.6
  247.9 4.0 reshape.605
  260.8 4.2 all-to-all-start
  266.8 10.0 %all-to-all-done = bf16[4,128,768]{2,1,0:T(8,128)(2,1)} async-done(((bf16[4,128,768]{2,1,0:T(8,128)(2,1)}), bf16[4,128,768]{2,1,0:T(8,128)(2,1)}, u32[]{:S(2)}, u32[]{:S(2)}) %all-to-all-start) | async-done | bytes 786464 | tf_op jit(solution)/shard_map/all_to_all | solution.py:148
  276.8 7.8 %fusion.15 = f32[512,3072]{1,0:T(8,128)} fusion(bf16[512,768]{1,0:T(8,128)(2,1)} %bitcast.88, bf16[1,768,3072]{2,1,0:T(8,128)(2,1)} %all-gather.5.cloned.1.call-done), kind=kOutput, calls=%fused_computation.26 | convolution fusion | flops 2415919104 | bytes 11796480 | tf_op jit(solution)/shard_map/dot_general | solution.py:152
  284.7 8.9 %fusion.39 = bf16[512,768]{1,0:T(8,128)(2,1)} fusion(bf16[1,3072,768]{2,1,0:T(8,128)(2,1)} %all-gather.7.cloned.1.call-done, f32[512,3072]{1,0:T(8,128)} %fusion.15), kind=kOutput, calls=%fused_computation.70 | convolution fusion | flops 2430468096 | bytes 11796480 | tf_op jit(solution)/shard_map/dot_general | solution.py:152
  293.6 4.2 all-to-all-start.1
  300.4 8.4 %all-to-all-done.1 = bf16[4,128,768]{2,1,0:T(8,128)(2,1)} async-done(((bf16[4,128,768]{2,1,0:T(8,128)(2,1)}), bf16[4,128,768]{2,1,0:T(8,128)(2,1)}, u32[]{:S(2)}, u32[]{:S(2)}) %all-to-all-start.1) | async-done | bytes 786464 | tf_op jit(solution)/shard_map/all_to_all | solution.py:148
  308.9 3.2 fusion.85
  314.2 4.4 all-to-all-start.2
  323.1 5.7 all-to-all-done.2
  328.9 8.6 %fusion.7 = bf16[512,3072]{1,0:T(8,128)(2,1)S(1)} fusion(f32[512,3072]{1,0:T(8,128)} %fusion.15, bf16[512,768]{1,0:T(8,128)(2,1)} %bitcast.99, bf16[1,3072,768]{2,1,0:T(8,128)(2,1)} %all-gather.7.cloned.1.call-done), kind=kOutput, calls=%fused_computation.10 | convolution fusion | flops 2447376384 | bytes 14942208 | tf_op jit(solution)/shard_map/dot_general | solution.py:156
  337.5 7.0 %fusion.36 = bf16[512,768]{1,0:T(8,128)(2,1)} fusion(bf16[512,3072]{1,0:T(8,128)(2,1)S(1)} %fusion.7, bf16[1,768,3072]{2,1,0:T(8,128)(2,1)} %all-gather.5.cloned.1.call-done), kind=kOutput, calls=%fused_computation.69 | convolution fusion | flops 2416312320 | bytes 8650752 | tf_op jit(solution)/shard_map/dot_general | solution.py:156
  344.5 3.5 all-to-all-start.3
  348.1 8.4 %convolution_convert_fusion = bf16[3072,768]{1,0:T(8,128)(2,1)} fusion(bf16[512,768]{1,0:T(8,128)(2,1)} %bitcast.99, f32[512,3072]{1,0:T(8,128)} %fusion.15), kind=kOutput, calls=%fused_computation.12 | convolution fusion | flops 2432434176 | bytes 11796480 | tf_op jit(solution)/shard_map/dot_general | solution.py:160
  376.3 3.9 multiply_reduce_fusion.3
  382.2 3.4 fusion.27
  406.7 4.3 convolution_convert_fusion.3
  431.1 3.4 collective-permute-done.79
  451.0 6.9 %convolution_convert_fusion.1 = bf16[768,3072]{1,0:T(8,128)(2,1)} fusion(bf16[512,768]{1,0:T(8,128)(2,1)} %bitcast.88, bf16[512,3072]{1,0:T(8,128)(2,1)} %copy-done.137), kind=kOutput, calls=%fused_computation.13 | convolution fusion | flops 2418278400 | bytes 8650752 | tf_op jit(solution)/shard_map/dot_general | solution.py:160
  474.0 4.8 collective-permute-done.61
  481.8 9.6 %collective-permute-done.71 = bf16[4,24,3072]{2,1,0:T(8,128)(2,1)S(1)} collective-permute-done((bf16[4,24,3072]{2,1,0:T(8,128)(2,1)S(1)}, bf16[4,24,3072]{2,1,0:T(8,128)(2,1)S(1)}, u32[]{:S(2)}, u32[]{:S(2)}) %collective-permute-start.71) | collective-permute-done | bytes 589856 | tf_op jit(solution)/shard_map/ppermute | solution.py:33
  494.5 12.1 %collective-permute-done.51 = bf16[4,24,3072]{2,1,0:T(8,128)(2,1)S(1)} collective-permute-done((bf16[4,24,3072]{2,1,0:T(8,128)(2,1)S(1)}, bf16[4,24,3072]{2,1,0:T(8,128)(2,1)S(1)}, u32[]{:S(2)}, u32[]{:S(2)}) %collective-permute-start.51) | collective-permute-done | bytes 589856 | tf_op jit(solution)/shard_map/ppermute | solution.py:33
  509.4 10.4 %collective-permute-done.41 = bf16[4,24,3200]{2,1,0:T(8,128)(2,1)S(1)} collective-permute-done((bf16[4,24,3200]{2,1,0:T(8,128)(2,1)S(1)}, bf16[4,24,3200]{2,1,0:T(8,128)(2,1)S(1)}, u32[]{:S(2)}, u32[]{:S(2)}) %collective-permute-start.41) | collective-permute-done | bytes 614432 | tf_op jit(solution)/shard_map/ppermute | solution.py:33
  529.6 3.7 collective-permute-start.63
  536.0 3.5 collective-permute-start.73
  542.5 3.5 collective-permute-start.53
  549.8 4.2 collective-permute-start.64
  556.8 4.4 collective-permute-start.74
  565.4 4.4 collective-permute-start.65
  574.9 17.1 %collective-permute-start.55 = (bf16[24,3072]{1,0:T(8,128)(2,1)S(1)}, bf16[24,3072]{1,0:T(8,128)(2,1)S(1)}, u32[]{:S(2)}, u32[]{:S(2)}) collective-permute-start(bf16[24,3072]{1,0:T(8,128)(2,1)S(1)} %get-tuple-element.171), channel_id=1, source_target_pairs={{0,8},{1,9},{2,10},{3,11},{4,12},{5,13},{6,14},{7,15},{8,16},{9,17... | collective-permute-start | bytes 442376 | tf_op jit(solution)/shard_map/ppermute | solution.py:33
  599.5 4.8 collective-permute-done.78
  604.3 5.2 collective-permute-start.45
  614.5 7.3 %collective-permute-done.48 = bf16[24,3200]{1,0:T(8,128)(2,1)S(1)} collective-permute-done((bf16[24,3200]{1,0:T(8,128)(2,1)S(1)}, bf16[24,3200]{1,0:T(8,128)(2,1)S(1)}, u32[]{:S(2)}, u32[]{:S(2)}) %collective-permute-start.48) | collective-permute-done | bytes 153632 | tf_op jit(solution)/shard_map/ppermute | solution.py:33
  (675 shorter events, 275.1 us)
Async XLA Ops:
  7.2 269.6 %all-gather.5.cloned.1.call-start = ((), (), s32[]{:S(2)}) async-start(), calls=%async_computation.8 | async-start | bytes 5308416 | tf_op jit(solution)/shard_map/all_gather | solution.py:287
  7.9 276.8 %all-gather.7.cloned.1.call-start = ((), (), s32[]{:S(2)}) async-start(), calls=%async_computation.9 | async-start | bytes 5308416 | tf_op jit(solution)/shard_map/all_gather | solution.py:288
  8.0 34.9 %collective-permute-start.26 = (bf16[96,768]{1,0:T(8,128)(2,1)}, bf16[96,768]{1,0:T(8,128)(2,1)S(1)}, u32[]{:S(2)}, u32[]{:S(2)}) collective-permute-start(bf16[96,768]{1,0:T(8,128)(2,1)} %param.34), channel_id=1, source_target_pairs={{0,8},{1,9},{2,10},{3,11},{4,12},{5,13},{6,14},{7,15},{8,16},{9,17... | collective-permute-start | bytes 442376 | tf_op jit(solution)/shard_map/ppermute | solution.py:33
  12.9 35.2 %collective-permute-start.29 = (bf16[96,768]{1,0:T(8,128)(2,1)}, bf16[96,768]{1,0:T(8,128)(2,1)S(1)}, u32[]{:S(2)}, u32[]{:S(2)}) collective-permute-start(bf16[96,768]{1,0:T(8,128)(2,1)} %param.34), channel_id=1, source_target_pairs={{8,0},{9,1},{10,2},{11,3},{12,4},{13,5},{14,6},{15,7},{16,8},{17,9... | collective-permute-start | bytes 442376 | tf_op jit(solution)/shard_map/ppermute | solution.py:33
  25.0 26.3 %collective-permute-start.3 = (bf16[24,3200]{1,0:T(8,128)(2,1)S(1)}, bf16[24,3200]{1,0:T(8,128)(2,1)S(1)}, u32[]{:S(2)}, u32[]{:S(2)}) collective-permute-start(bf16[24,3200]{1,0:T(8,128)(2,1)S(1)} %fusion.145), channel_id=1, source_target_pairs={{8,0},{9,1},{10,2},{11,3},{12,4},{13,5},{14,6},{15,7},{16,8},{17,9... | collective-permute-start | bytes 460808 | tf_op jit(solution)/shard_map/ppermute | solution.py:33
  26.3 26.9 %collective-permute-start = (bf16[24,3200]{1,0:T(8,128)(2,1)S(1)}, bf16[24,3200]{1,0:T(8,128)(2,1)S(1)}, u32[]{:S(2)}, u32[]{:S(2)}) collective-permute-start(bf16[24,3200]{1,0:T(8,128)(2,1)S(1)} %fusion.145), channel_id=1, source_target_pairs={{0,8},{1,9},{2,10},{3,11},{4,12},{5,13},{6,14},{7,15},{8,16},{9,17... | collective-permute-start | bytes 460808 | tf_op jit(solution)/shard_map/ppermute | solution.py:33
  34.2 45.2 %collective-permute-start.16 = (bf16[24,6144]{1,0:T(8,128)(2,1)S(1)}, bf16[24,6144]{1,0:T(8,128)(2,1)}, u32[]{:S(2)}, u32[]{:S(2)}) collective-permute-start(bf16[24,6144]{1,0:T(8,128)(2,1)S(1)} %constant_dynamic-update-slice_fusion), channel_id=1, source_target_pairs={{8,0},{9,1},{10,2},{11,3},{12,4},{13,5},{14,6},{15,7},{16,8},{17,9... | collective-permute-start | bytes 884744 | tf_op jit(solution)/shard_map/ppermute | solution.py:33
  42.8 38.4 %collective-permute-start.13 = (bf16[24,6144]{1,0:T(8,128)(2,1)S(1)}, bf16[24,6144]{1,0:T(8,128)(2,1)}, u32[]{:S(2)}, u32[]{:S(2)}) collective-permute-start(bf16[24,6144]{1,0:T(8,128)(2,1)S(1)} %constant_dynamic-update-slice_fusion), channel_id=1, source_target_pairs={{0,8},{1,9},{2,10},{3,11},{4,12},{5,13},{6,14},{7,15},{8,16},{9,17... | collective-permute-start | bytes 884744 | tf_op jit(solution)/shard_map/ppermute | solution.py:33
  51.4 23.6 %collective-permute-start.30 = (bf16[96,768]{1,0:T(8,128)(2,1)S(1)}, bf16[96,768]{1,0:T(8,128)(2,1)S(1)}, u32[]{:S(2)}, u32[]{:S(2)}) collective-permute-start(bf16[96,768]{1,0:T(8,128)(2,1)S(1)} %collective-permute-done.29), channel_id=1, source_target_pairs={{8,0},{9,1},{10,2},{11,3},{12,4},{13,5},{14,6},{15,7},{16,8},{17,9... | collective-permute-start | bytes 442376 | tf_op jit(solution)/shard_map/ppermute | solution.py:33
  53.2 29.3 %collective-permute-start.4 = (bf16[24,3200]{1,0:T(8,128)(2,1)S(1)}, bf16[24,3200]{1,0:T(8,128)(2,1)S(1)}, u32[]{:S(2)}, u32[]{:S(2)}) collective-permute-start(bf16[24,3200]{1,0:T(8,128)(2,1)S(1)} %collective-permute-done.3), channel_id=1, source_target_pairs={{8,0},{9,1},{10,2},{11,3},{12,4},{13,5},{14,6},{15,7},{16,8},{17,9... | collective-permute-start | bytes 460808 | tf_op jit(solution)/shard_map/ppermute | solution.py:33
  66.6 21.1 %collective-permute-start.1 = (bf16[24,3200]{1,0:T(8,128)(2,1)S(1)}, bf16[24,3200]{1,0:T(8,128)(2,1)S(1)}, u32[]{:S(2)}, u32[]{:S(2)}) collective-permute-start(bf16[24,3200]{1,0:T(8,128)(2,1)S(1)} %collective-permute-done), channel_id=1, source_target_pairs={{0,8},{1,9},{2,10},{3,11},{4,12},{5,13},{6,14},{7,15},{8,16},{9,17... | collective-permute-start | bytes 460808 | tf_op jit(solution)/shard_map/ppermute | solution.py:33
  81.2 29.9 %collective-permute-start.17 = (bf16[24,6144]{1,0:T(8,128)(2,1)}, bf16[24,6144]{1,0:T(8,128)(2,1)S(1)}, u32[]{:S(2)}, u32[]{:S(2)}) collective-permute-start(bf16[24,6144]{1,0:T(8,128)(2,1)} %collective-permute-done.16), channel_id=1, source_target_pairs={{8,0},{9,1},{10,2},{11,3},{12,4},{13,5},{14,6},{15,7},{16,8},{17,9... | collective-permute-start | bytes 884744 | tf_op jit(solution)/shard_map/ppermute | solution.py:33
  82.5 30.0 %collective-permute-start.14 = (bf16[24,6144]{1,0:T(8,128)(2,1)}, bf16[24,6144]{1,0:T(8,128)(2,1)S(1)}, u32[]{:S(2)}, u32[]{:S(2)}) collective-permute-start(bf16[24,6144]{1,0:T(8,128)(2,1)} %collective-permute-done.13), channel_id=1, source_target_pairs={{0,8},{1,9},{2,10},{3,11},{4,12},{5,13},{6,14},{7,15},{8,16},{9,17... | collective-permute-start | bytes 884744 | tf_op jit(solution)/shard_map/ppermute | solution.py:33
  94.6 55.6 %collective-permute-start.33 = (bf16[4,96,768]{2,1,0:T(8,128)(2,1)}, bf16[4,96,768]{2,1,0:T(8,128)(2,1)}, u32[]{:S(2)}, u32[]{:S(2)}) collective-permute-start(bf16[4,96,768]{2,1,0:T(8,128)(2,1)} %pad_maximum_fusion.4), channel_id=1, source_target_pairs={{0,1},{1,0},{2,3},{3,2},{4,6},{5,7},{6,4},{7,5},{8,9},{9,8},{10,11... | collective-permute-start | bytes 1769480 | tf_op jit(solution)/shard_map/ppermute | solution.py:33
  107.9 39.7 %collective-permute-start.32 = (bf16[4,96,768]{2,1,0:T(8,128)(2,1)}, bf16[4,96,768]{2,1,0:T(8,128)(2,1)}, u32[]{:S(2)}, u32[]{:S(2)}) collective-permute-start(bf16[4,96,768]{2,1,0:T(8,128)(2,1)} %pad_maximum_fusion.4), channel_id=1, source_target_pairs={{0,4},{1,5},{2,6},{3,7},{4,0},{5,1},{6,2},{7,3},{8,12},{9,13},{10,... | collective-permute-start | bytes 1769480 | tf_op jit(solution)/shard_map/ppermute | solution.py:33
  108.0 45.6 %collective-permute-start.35 = (bf16[4,96,768]{2,1,0:T(8,128)(2,1)}, bf16[4,96,768]{2,1,0:T(8,128)(2,1)}, u32[]{:S(2)}, u32[]{:S(2)}) collective-permute-start(bf16[4,96,768]{2,1,0:T(8,128)(2,1)} %pad_maximum_fusion.4), channel_id=1, source_target_pairs={{0,2},{1,3},{2,0},{3,1},{4,5},{5,4},{6,7},{7,6},{8,10},{9,11},{10,... | collective-permute-start | bytes 1769480 | tf_op jit(solution)/shard_map/ppermute | solution.py:33
  111.1 29.0 %collective-permute-start.18 = (bf16[24,6144]{1,0:T(8,128)(2,1)S(1)}, bf16[24,6144]{1,0:T(8,128)(2,1)S(1)}, u32[]{:S(2)}, u32[]{:S(2)}) collective-permute-start(bf16[24,6144]{1,0:T(8,128)(2,1)S(1)} %collective-permute-done.17), channel_id=1, source_target_pairs={{8,0},{9,1},{10,2},{11,3},{12,4},{13,5},{14,6},{15,7},{16,8},{17,9... | collective-permute-start | bytes 884744 | tf_op jit(solution)/shard_map/ppermute | solution.py:33
  112.5 29.2 %collective-permute-start.15 = (bf16[24,6144]{1,0:T(8,128)(2,1)S(1)}, bf16[24,6144]{1,0:T(8,128)(2,1)S(1)}, u32[]{:S(2)}, u32[]{:S(2)}) collective-permute-start(bf16[24,6144]{1,0:T(8,128)(2,1)S(1)} %collective-permute-done.14), channel_id=1, source_target_pairs={{0,8},{1,9},{2,10},{3,11},{4,12},{5,13},{6,14},{7,15},{8,16},{9,17... | collective-permute-start | bytes 884744 | tf_op jit(solution)/shard_map/ppermute | solution.py:33
  147.6 30.4 %collective-permute-start.9 = (bf16[4,24,3200]{2,1,0:T(8,128)(2,1)}, bf16[4,24,3200]{2,1,0:T(8,128)(2,1)S(1)}, u32[]{:S(2)}, u32[]{:S(2)}) collective-permute-start(bf16[4,24,3200]{2,1,0:T(8,128)(2,1)} %pad_maximum_fusion.3), channel_id=1, source_target_pairs={{0,2},{1,3},{2,0},{3,1},{4,5},{5,4},{6,7},{7,6},{8,10},{9,11},{10,... | collective-permute-start | bytes 1843208 | tf_op jit(solution)/shard_map/ppermute | solution.py:33
  150.3 49.8 %collective-permute-start.20 = (bf16[4,24,6144]{2,1,0:T(8,128)(2,1)S(1)}, bf16[4,24,6144]{2,1,0:T(8,128)(2,1)}, u32[]{:S(2)}, u32[]{:S(2)}) collective-permute-start(bf16[4,24,6144]{2,1,0:T(8,128)(2,1)S(1)} %copy-done.47), channel_id=1, source_target_pairs={{0,1},{1,0},{2,3},{3,2},{4,6},{5,7},{6,4},{7,5},{8,9},{9,8},{10,11... | collective-permute-start | bytes 3538952 | tf_op jit(solution)/shard_map/ppermute | solution.py:33
  152.1 24.6 %collective-permute-start.37 = (bf16[4,96,768]{2,1,0:T(8,128)(2,1)}, bf16[4,96,768]{2,1,0:T(8,128)(2,1)S(1)}, u32[]{:S(2)}, u32[]{:S(2)}) collective-permute-start(bf16[4,96,768]{2,1,0:T(8,128)(2,1)} %collective-permute-done.33), channel_id=1, source_target_pairs={{0,2},{1,3},{2,0},{3,1},{4,5},{5,4},{6,7},{7,6},{8,10},{9,11},{10,... | collective-permute-start | bytes 1769480 | tf_op jit(solution)/shard_map/ppermute | solution.py:33
  156.3 22.5 %collective-permute-start.8 = (bf16[4,24,3200]{2,1,0:T(8,128)(2,1)}, bf16[4,24,3200]{2,1,0:T(8,128)(2,1)S(1)}, u32[]{:S(2)}, u32[]{:S(2)}) collective-permute-start(bf16[4,24,3200]{2,1,0:T(8,128)(2,1)} %collective-permute-done.7), channel_id=1, source_target_pairs={{0,4},{1,5},{2,6},{3,7},{4,0},{5,1},{6,2},{7,3},{8,12},{9,13},{10,... | collective-permute-start | bytes 1843208 | tf_op jit(solution)/shard_map/ppermute | solution.py:33
  157.8 43.6 %collective-permute-start.19 = (bf16[4,24,6144]{2,1,0:T(8,128)(2,1)S(1)}, bf16[4,24,6144]{2,1,0:T(8,128)(2,1)S(1)}, u32[]{:S(2)}, u32[]{:S(2)}) collective-permute-start(bf16[4,24,6144]{2,1,0:T(8,128)(2,1)S(1)} %copy-done.47), channel_id=1, source_target_pairs={{0,4},{1,5},{2,6},{3,7},{4,0},{5,1},{6,2},{7,3},{8,12},{9,13},{10,... | collective-permute-start | bytes 3538952 | tf_op jit(solution)/shard_map/ppermute | solution.py:33
  176.6 24.8 %collective-permute-start.22 = (bf16[4,24,6144]{2,1,0:T(8,128)(2,1)S(1)}, bf16[4,24,6144]{2,1,0:T(8,128)(2,1)}, u32[]{:S(2)}, u32[]{:S(2)}) collective-permute-start(bf16[4,24,6144]{2,1,0:T(8,128)(2,1)S(1)} %copy-done.47), channel_id=1, source_target_pairs={{0,2},{1,3},{2,0},{3,1},{4,5},{5,4},{6,7},{7,6},{8,10},{9,11},{10,... | collective-permute-start | bytes 3538952 | tf_op jit(solution)/shard_map/ppermute | solution.py:33
  178.0 21.5 %collective-permute-start.11 = (bf16[4,24,3200]{2,1,0:T(8,128)(2,1)}, bf16[4,24,3200]{2,1,0:T(8,128)(2,1)S(1)}, u32[]{:S(2)}, u32[]{:S(2)}) collective-permute-start(bf16[4,24,3200]{2,1,0:T(8,128)(2,1)} %collective-permute-done.7), channel_id=1, source_target_pairs={{0,2},{1,3},{2,0},{3,1},{4,5},{5,4},{6,7},{7,6},{8,10},{9,11},{10,... | collective-permute-start | bytes 1843208 | tf_op jit(solution)/shard_map/ppermute | solution.py:33
  178.8 20.6 %collective-permute-start.10 = (bf16[4,24,3200]{2,1,0:T(8,128)(2,1)S(1)}, bf16[4,24,3200]{2,1,0:T(8,128)(2,1)S(1)}, u32[]{:S(2)}, u32[]{:S(2)}) collective-permute-start(bf16[4,24,3200]{2,1,0:T(8,128)(2,1)S(1)} %collective-permute-done.9), channel_id=1, source_target_pairs={{0,4},{1,5},{2,6},{3,7},{4,0},{5,1},{6,2},{7,3},{8,12},{9,13},{10,... | collective-permute-start | bytes 1843208 | tf_op jit(solution)/shard_map/ppermute | solution.py:33
  200.1 23.5 %collective-permute-start.24 = (bf16[4,24,6144]{2,1,0:T(8,128)(2,1)}, bf16[4,24,6144]{2,1,0:T(8,128)(2,1)}, u32[]{:S(2)}, u32[]{:S(2)}) collective-permute-start(bf16[4,24,6144]{2,1,0:T(8,128)(2,1)} %collective-permute-done.20), channel_id=1, source_target_pairs={{0,2},{1,3},{2,0},{3,1},{4,5},{5,4},{6,7},{7,6},{8,10},{9,11},{10,... | collective-permute-start | bytes 3538952 | tf_op jit(solution)/shard_map/ppermute | solution.py:33
  201.5 22.3 %collective-permute-start.21 = (bf16[4,24,6144]{2,1,0:T(8,128)(2,1)}, bf16[4,24,6144]{2,1,0:T(8,128)(2,1)}, u32[]{:S(2)}, u32[]{:S(2)}) collective-permute-start(bf16[4,24,6144]{2,1,0:T(8,128)(2,1)} %collective-permute-done.20), channel_id=1, source_target_pairs={{0,4},{1,5},{2,6},{3,7},{4,0},{5,1},{6,2},{7,3},{8,12},{9,13},{10,... | collective-permute-start | bytes 3538952 | tf_op jit(solution)/shard_map/ppermute | solution.py:33
  201.5 27.1 %collective-permute-start.23 = (bf16[4,24,6144]{2,1,0:T(8,128)(2,1)}, bf16[4,24,6144]{2,1,0:T(8,128)(2,1)}, u32[]{:S(2)}, u32[]{:S(2)}) collective-permute-start(bf16[4,24,6144]{2,1,0:T(8,128)(2,1)} %collective-permute-done.22), channel_id=1, source_target_pairs={{0,4},{1,5},{2,6},{3,7},{4,0},{5,1},{6,2},{7,3},{8,12},{9,13},{10,... | collective-permute-start | bytes 3538952 | tf_op jit(solution)/shard_map/ppermute | solution.py:33
  348.0 276.7 %reduce-scatter.5.cloned.1.call-start = ((), (), s32[]{:S(2)}) async-start(), calls=%async_computation.7 | async-start | bytes 5308416 | tf_op jit(solution)/shard_map/reduce_scatter | solution.py:342
  356.5 270.3 %reduce-scatter.3.cloned.1.call-start = ((), (), s32[]{:S(2)}) async-start(), calls=%async_computation.6 | async-start | bytes 5308416 | tf_op jit(solution)/shard_map/reduce_scatter | solution.py:343
  412.7 47.6 %collective-permute-start.59 = (bf16[4,4,96,768]{3,2,0,1:T(8,128)(2,1)}, bf16[4,4,96,768]{3,2,0,1:T(8,128)(2,1)}, u32[]{:S(2)}, u32[]{:S(2)}) collective-permute-start(bf16[4,4,96,768]{3,2,0,1:T(8,128)(2,1)} %copy_bitcast_fusion.1), channel_id=1, source_target_pairs={{0,4},{1,5},{2,6},{3,7},{4,0},{5,1},{6,2},{7,3},{8,12},{9,13},{10,... | collective-permute-start | bytes 7077896 | tf_op jit(solution)/shard_map/ppermute | solution.py:33
  418.2 46.4 %collective-permute-start.69 = (bf16[4,4,24,3072]{3,2,0,1:T(8,128)(2,1)}, bf16[4,4,24,3072]{3,2,0,1:T(8,128)(2,1)}, u32[]{:S(2)}, u32[]{:S(2)}) collective-permute-start(bf16[4,4,24,3072]{3,2,0,1:T(8,128)(2,1)} %copy_bitcast_fusion), channel_id=1, source_target_pairs={{0,4},{1,5},{2,6},{3,7},{4,0},{5,1},{6,2},{7,3},{8,12},{9,13},{10,... | collective-permute-start | bytes 7077896 | tf_op jit(solution)/shard_map/ppermute | solution.py:33
  423.2 45.1 %collective-permute-start.49 = (bf16[4,4,24,3072]{3,2,0,1:T(8,128)(2,1)}, bf16[4,4,24,3072]{3,2,0,1:T(8,128)(2,1)}, u32[]{:S(2)}, u32[]{:S(2)}) collective-permute-start(bf16[4,4,24,3072]{3,2,0,1:T(8,128)(2,1)} %copy_bitcast_fusion.2), channel_id=1, source_target_pairs={{0,4},{1,5},{2,6},{3,7},{4,0},{5,1},{6,2},{7,3},{8,12},{9,13},{10,... | collective-permute-start | bytes 7077896 | tf_op jit(solution)/shard_map/ppermute | solution.py:33
  429.8 40.5 %collective-permute-start.39 = (bf16[4,4,24,3200]{3,2,1,0:T(8,128)(2,1)}, bf16[4,4,24,3200]{3,2,1,0:T(8,128)(2,1)}, u32[]{:S(2)}, u32[]{:S(2)}) collective-permute-start(bf16[4,4,24,3200]{3,2,1,0:T(8,128)(2,1)} %dynamic-slice_bitcast_fusion), channel_id=1, source_target_pairs={{0,4},{1,5},{2,6},{3,7},{4,0},{5,1},{6,2},{7,3},{8,12},{9,13},{10,... | collective-permute-start | bytes 7372808 | tf_op jit(solution)/shard_map/ppermute | solution.py:33
  462.5 60.3 %collective-permute-start.60 = (bf16[4,96,768]{2,1,0:T(8,128)(2,1)S(1)}, bf16[4,96,768]{2,1,0:T(8,128)(2,1)S(1)}, u32[]{:S(2)}, u32[]{:S(2)}) collective-permute-start(bf16[4,96,768]{2,1,0:T(8,128)(2,1)S(1)} %get-tuple-element.144), channel_id=1, source_target_pairs={{0,2},{1,3},{2,0},{3,1},{4,5},{5,4},{6,7},{7,6},{8,10},{9,11},{10,... | collective-permute-start | bytes 1769480 | tf_op jit(solution)/shard_map/ppermute | solution.py:33
  466.6 60.0 %collective-permute-start.70 = (bf16[4,24,3072]{2,1,0:T(8,128)(2,1)S(1)}, bf16[4,24,3072]{2,1,0:T(8,128)(2,1)S(1)}, u32[]{:S(2)}, u32[]{:S(2)}) collective-permute-start(bf16[4,24,3072]{2,1,0:T(8,128)(2,1)S(1)} %get-tuple-element.142), channel_id=1, source_target_pairs={{0,2},{1,3},{2,0},{3,1},{4,5},{5,4},{6,7},{7,6},{8,10},{9,11},{10,... | collective-permute-start | bytes 1769480 | tf_op jit(solution)/shard_map/ppermute | solution.py:33
  468.3 23.1 %collective-permute-start.71 = (bf16[4,24,3072]{2,1,0:T(8,128)(2,1)S(1)}, bf16[4,24,3072]{2,1,0:T(8,128)(2,1)S(1)}, u32[]{:S(2)}, u32[]{:S(2)}) collective-permute-start(bf16[4,24,3072]{2,1,0:T(8,128)(2,1)S(1)} %get-tuple-element.143), channel_id=1, source_target_pairs={{0,2},{1,3},{2,0},{3,1},{4,5},{5,4},{6,7},{7,6},{8,10},{9,11},{10,... | collective-permute-start | bytes 1769480 | tf_op jit(solution)/shard_map/ppermute | solution.py:33
  470.4 64.7 %collective-permute-start.50 = (bf16[4,24,3072]{2,1,0:T(8,128)(2,1)S(1)}, bf16[4,24,3072]{2,1,0:T(8,128)(2,1)S(1)}, u32[]{:S(2)}, u32[]{:S(2)}) collective-permute-start(bf16[4,24,3072]{2,1,0:T(8,128)(2,1)S(1)} %get-tuple-element.146), channel_id=1, source_target_pairs={{0,2},{1,3},{2,0},{3,1},{4,5},{5,4},{6,7},{7,6},{8,10},{9,11},{10,... | collective-permute-start | bytes 1769480 | tf_op jit(solution)/shard_map/ppermute | solution.py:33
  478.8 27.8 %collective-permute-start.51 = (bf16[4,24,3072]{2,1,0:T(8,128)(2,1)S(1)}, bf16[4,24,3072]{2,1,0:T(8,128)(2,1)S(1)}, u32[]{:S(2)}, u32[]{:S(2)}) collective-permute-start(bf16[4,24,3072]{2,1,0:T(8,128)(2,1)S(1)} %get-tuple-element.147), channel_id=1, source_target_pairs={{0,2},{1,3},{2,0},{3,1},{4,5},{5,4},{6,7},{7,6},{8,10},{9,11},{10,... | collective-permute-start | bytes 1769480 | tf_op jit(solution)/shard_map/ppermute | solution.py:33
  491.4 28.4 %collective-permute-start.41 = (bf16[4,24,3200]{2,1,0:T(8,128)(2,1)S(1)}, bf16[4,24,3200]{2,1,0:T(8,128)(2,1)S(1)}, u32[]{:S(2)}, u32[]{:S(2)}) collective-permute-start(bf16[4,24,3200]{2,1,0:T(8,128)(2,1)S(1)} %get-tuple-element.141), channel_id=1, source_target_pairs={{0,2},{1,3},{2,0},{3,1},{4,5},{5,4},{6,7},{7,6},{8,10},{9,11},{10,... | collective-permute-start | bytes 1843208 | tf_op jit(solution)/shard_map/ppermute | solution.py:33
  547.7 22.1 %collective-permute-start.56 = (bf16[24,3072]{1,0:T(8,128)(2,1)S(1)}, bf16[24,3072]{1,0:T(8,128)(2,1)S(1)}, u32[]{:S(2)}, u32[]{:S(2)}) collective-permute-start(bf16[24,3072]{1,0:T(8,128)(2,1)S(1)} %get-tuple-element.174), channel_id=1, source_target_pairs={{24,16},{25,17},{26,18},{27,19},{28,20},{29,21},{30,22},{31,23}} | collective-permute-start | bytes 442376 | tf_op jit(solution)/shard_map/ppermute | solution.py:33
  548.5 25.0 %collective-permute-start.43 = (bf16[24,3200]{1,0:T(8,128)(2,1)S(1)}, bf16[24,3200]{1,0:T(8,128)(2,1)S(1)}, u32[]{:S(2)}, u32[]{:S(2)}) collective-permute-start(bf16[24,3200]{1,0:T(8,128)(2,1)S(1)} %get-tuple-element.161), channel_id=1, source_target_pairs={{0,8},{1,9},{2,10},{3,11},{4,12},{5,13},{6,14},{7,15}} | collective-permute-start | bytes 460808 | tf_op jit(solution)/shard_map/ppermute | solution.py:33
  554.1 40.1 %collective-permute-start.46 = (bf16[24,3200]{1,0:T(8,128)(2,1)S(1)}, bf16[24,3200]{1,0:T(8,128)(2,1)S(1)}, u32[]{:S(2)}, u32[]{:S(2)}) collective-permute-start(bf16[24,3200]{1,0:T(8,128)(2,1)S(1)} %get-tuple-element.162), channel_id=1, source_target_pairs={{24,16},{25,17},{26,18},{27,19},{28,20},{29,21},{30,22},{31,23}} | collective-permute-start | bytes 460808 | tf_op jit(solution)/shard_map/ppermute | solution.py:33
  565.4 48.3 %collective-permute-start.65 = (bf16[96,768]{1,0:T(8,128)(2,1)S(1)}, bf16[96,768]{1,0:T(8,128)(2,1)S(1)}, u32[]{:S(2)}, u32[]{:S(2)}) collective-permute-start(bf16[96,768]{1,0:T(8,128)(2,1)S(1)} %get-tuple-element.167), channel_id=1, source_target_pairs={{0,8},{1,9},{2,10},{3,11},{4,12},{5,13},{6,14},{7,15},{8,16},{9,17... | collective-permute-start | bytes 442376 | tf_op jit(solution)/shard_map/ppermute | solution.py:33
  569.8 22.3 %collective-permute-start.67 = (bf16[96,768]{1,0:T(8,128)(2,1)S(1)}, bf16[96,768]{1,0:T(8,128)(2,1)S(1)}, u32[]{:S(2)}, u32[]{:S(2)}) collective-permute-start(bf16[96,768]{1,0:T(8,128)(2,1)S(1)} %get-tuple-element.168), channel_id=1, source_target_pairs={{16,8},{17,9},{18,10},{19,11},{20,12},{21,13},{22,14},{23,15},{24,... | collective-permute-start | bytes 442376 | tf_op jit(solution)/shard_map/ppermute | solution.py:33
  570.5 27.6 %collective-permute-start.75 = (bf16[24,3072]{1,0:T(8,128)(2,1)S(1)}, bf16[24,3072]{1,0:T(8,128)(2,1)S(1)}, u32[]{:S(2)}, u32[]{:S(2)}) collective-permute-start(bf16[24,3072]{1,0:T(8,128)(2,1)S(1)} %get-tuple-element.163), channel_id=1, source_target_pairs={{0,8},{1,9},{2,10},{3,11},{4,12},{5,13},{6,14},{7,15},{8,16},{9,17... | collective-permute-start | bytes 442376 | tf_op jit(solution)/shard_map/ppermute | solution.py:33
  574.9 34.6 %collective-permute-start.55 = (bf16[24,3072]{1,0:T(8,128)(2,1)S(1)}, bf16[24,3072]{1,0:T(8,128)(2,1)S(1)}, u32[]{:S(2)}, u32[]{:S(2)}) collective-permute-start(bf16[24,3072]{1,0:T(8,128)(2,1)S(1)} %get-tuple-element.171), channel_id=1, source_target_pairs={{0,8},{1,9},{2,10},{3,11},{4,12},{5,13},{6,14},{7,15},{8,16},{9,17... | collective-permute-start | bytes 442376 | tf_op jit(solution)/shard_map/ppermute | solution.py:33
  (193 other events, 1550.8 us)
Sparse Core Ops, SparseCore 0:
  9.7 69.5 all-gather.4
  80.9 61.1 all-gather.6
  356.7 56.4 reduce-scatter.4
  458.1 55.2 reduce-scatter.2

commit v2 on v1

v2 whole, which is shorter than its diff:
```python
import math

import jax
import jax.numpy as jnp
from jax import lax
from jax.experimental import pallas as pl
from jax.experimental.pallas import tpu as pltpu
from jax.sharding import PartitionSpec as P

HD = 64
AXES = ("dp", "expert")
F32 = jnp.float32
BF16 = jnp.bfloat16


def place():
    depth = lax.axis_size("dp") // 2
    row = lax.axis_index("dp")
    return depth, lax.axis_size("expert"), row // 2, row % 2, lax.axis_index("expert")


def pairs(target):
    depth, across = lax.axis_size("dp") // 2, lax.axis_size("expert")
    out = []
    for z in range(depth):
        for c in range(2):
            for e in range(across):
                to = target(z, c, e)
                if to is not None and 0 <= to[0] < depth:
                    out.append(((z * 2 + c) * across + e, (to[0] * 2 + to[1]) * across + to[2]))
    return out


def hop(values, target):
    return lax.ppermute(values, AXES, pairs(target))


def swap_cores(values):
    return hop(values, lambda z, c, e: (z, 1 - c, e))


def first_side(values):
    return hop(values, lambda z, c, e: (z, c, e ^ (1 + c)))


def second_side(values):
    return hop(values, lambda z, c, e: (z, c, e ^ (2 - c)))


def after(value, *others):
    return lax.optimization_barrier((value, *others))[0]


def shift(values, by):
    depth = place()[0]
    return hop(values, lambda z, c, e: ((z + by) % depth, c, e))


def gather_line(own):
    return jnp.stack([own] + [shift(own, k) for k in range(1, place()[0])])


def gather_sides(line):
    if place()[1] != 4:
        return [lax.all_gather(line, "expert", axis=1)]
    one = first_side(line)
    return [line, one, second_side(line), second_side(one)]


def gather_cores(parts):
    parts = [*parts, *(swap_cores(p) for p in parts)]
    return [p.reshape(-1, p.shape[-1]) for p in parts]


def order(rows):
    depth, across, z, c, e = place()
    k = jnp.arange(depth, dtype=jnp.int32)
    layer = (z - k) % depth
    if across == 4:
        there = jnp.stack([e, e ^ (1 + c), e ^ (2 - c), e ^ 3])
        over = jnp.stack([e, e ^ (2 - c), e ^ (1 + c), e ^ 3])
    else:
        there = over = jnp.arange(across, dtype=jnp.int32)
    first = (layer * 2 + c)[None, :] * across + there[:, None]
    second = (layer * 2 + 1 - c)[None, :] * across + over[:, None]
    if across != 4:
        first, second = first.T, second.T
    return jnp.concatenate([first.reshape(-1), second.reshape(-1)]) * rows


def add(first, second):
    return (first.astype(F32) + second.astype(F32)).astype(BF16)


def scatter_line(line):
    return [line[0]] + [shift(line[k], -k) for k in range(1, place()[0])]


def total(parts):
    return sum(p.astype(F32) for p in parts[1:]) + parts[0].astype(F32)


def scatter_cores(mine, other):
    depth, across, _, _, _ = place()
    other = swap_cores(other)
    if across != 4:
        return [add(mine, other).reshape(depth, across, -1, mine.shape[1])]
    half = mine.shape[0] // 2
    return [add(mine[:half], other[:half]), add(mine[half:], other[half:])]


def scatter_far(parts):
    return [parts[0], second_side(parts[1])] if len(parts) == 2 else parts


def scatter_near(parts):
    depth = place()[0]
    if len(parts) == 1:
        return lax.psum_scatter(parts[0], "expert", scatter_dimension=1, tiled=True)[:, 0]
    half = parts[0].shape[0] // 2
    mine, come = parts
    line = add(add(mine[:half], come[:half]), first_side(add(mine[half:], come[half:])))
    return line.reshape(depth, -1, line.shape[1])


def total_hops():
    depth, across, _, _, _ = place()
    if across & (across - 1) or depth & (depth - 1):
        return None
    hops = [lambda z, c, e: (z, 1 - c, e)]
    step = 1
    while step < across:
        hops.append(lambda z, c, e, step=step: (z, c, e ^ step))
        step *= 2
    step = 1
    while step < depth:
        hops.append(lambda z, c, e, step=step: (z ^ step, c, e))
        step *= 2
    return hops


def exchange(blocks):
    return [blocks[0]] + [
        hop(blocks[k], lambda z, c, e: (z, c, e ^ k)) for k in range(1, len(blocks))
    ]


LIMIT = 60 * 1024 * 1024
LIGHT = 1000


def cost(flops, moved, light=1):
    return pl.CostEstimate(flops=flops // light, bytes_accessed=moved // light, transcendentals=0)


WHOLE = pl.BlockSpec(memory_space=pltpu.VMEM)
SCALAR = pl.BlockSpec(memory_space=pltpu.SMEM)


def dot(a, b):
    return jnp.dot(a, b, preferred_element_type=F32)


def dot_nt(a, b):
    return lax.dot_general(a, b, (((1,), (1,)), ((), ())), preferred_element_type=F32)


def dot_tn(a, b):
    return lax.dot_general(a, b, (((0,), (0,)), ((), ())), preferred_element_type=F32)


def call(kernel, outs, ins, flops, grid=(), in_specs=None, out_specs=None, scratch=(), light=1):
    moved = sum(a.size * a.dtype.itemsize for a in (*ins, *outs))
    return pl.pallas_call(
        kernel,
        out_shape=outs,
        grid=grid,
        in_specs=in_specs or [WHOLE] * len(ins),
        out_specs=out_specs or [WHOLE] * len(outs),
        scratch_shapes=scratch,
        compiler_params=pltpu.CompilerParams(vmem_limit_bytes=LIMIT),
        cost_estimate=cost(flops, moved, light),
    )(*ins)


ANYWHERE = pl.BlockSpec(memory_space=pl.ANY)


def start_parts(parts, whole, sems, first=0):
    copies, at = [], 0
    for k, part in enumerate(parts):
        rows = part.shape[0]
        copies.append(pltpu.make_async_copy(part.at[:, first : first + whole.shape[1]], whole.at[at : at + rows], sems.at[k]))
        at += rows
    for copy in copies:
        copy.start()

    def wait():
        for copy in copies:
            copy.wait()

    return wait


def start_blocks(parts, places, whole, sems):
    count = places.shape[0] // len(parts)
    copies = []
    for k, part in enumerate(parts):
        rows = part.shape[0] // count
        for b in range(count):
            at = pl.multiple_of(places[k * count + b], 16)
            copies.append(
                pltpu.make_async_copy(
                    part.at[b * rows : (b + 1) * rows], whole.at[pl.ds(at, rows)], sems.at[k * count + b]
                )
            )
    for copy in copies:
        copy.start()

    def wait():
        for copy in copies:
            copy.wait()

    return wait


def mixed(values, mix):
    return dot(values, mix).astype(BF16)


def unmixed(values, mix):
    high = values.astype(BF16)
    low = (values - high.astype(F32)).astype(BF16)
    return dot_nt(low, mix) + dot_nt(high, mix)


def shaped(shape, dtype):
    return jax.ShapeDtypeStruct(shape, dtype)


def normalize(x):
    centered = x - jnp.mean(x, axis=-1, keepdims=True)
    scale = lax.rsqrt(jnp.mean(centered * centered, axis=-1, keepdims=True) + 1e-05)
    return centered * scale, scale


def norm_back(x, gain, grad, gains_ref, upstream):
    unit, scale = normalize(x)
    gains_ref[0:1, :] = jnp.sum(grad * unit, axis=0, keepdims=True)
    gains_ref[1:2, :] = jnp.sum(grad, axis=0, keepdims=True)
    inner = grad * gain
    middle = jnp.mean(inner, axis=-1, keepdims=True)
    tilt = jnp.mean(inner * unit, axis=-1, keepdims=True)
    return upstream + scale * (inner - middle - unit * tilt)


ROOT = math.sqrt(2.0 / math.pi)


def gelu(x):
    return 0.5 * x * (1.0 + jnp.tanh(ROOT * (x + 0.044715 * (x * x * x))))


def gelu_both(x):
    square = x * x
    slope = jnp.tanh(ROOT * x * (1.0 + 0.044715 * square))
    half = 0.5 * (1.0 + slope)
    return x * half, half + 0.5 * x * (1.0 - slope * slope) * (ROOT * (1.0 + 0.134145 * square))


def allowed_pair(start, length):
    row = lax.broadcasted_iota(jnp.int32, (2 * length, length), 0)
    row = jnp.where(row >= length, row - length, row)
    column = lax.broadcasted_iota(jnp.int32, (2 * length, length), 1)
    piece = length // 4
    inside = (row >= start) & (row < start + piece) & (column >= start) & (column < start + piece)
    return (column <= row) | inside


def apart(pair):
    low = lax.broadcasted_iota(jnp.int32, pair.shape, 1) < HD
    zero = jnp.zeros_like(pair)
    return jnp.concatenate([jnp.where(low, pair, zero), jnp.where(low, zero, pair)], axis=0)


def together(stacked):
    half = stacked.shape[0] // 2
    low = lax.broadcasted_iota(jnp.int32, (half, stacked.shape[1]), 1) < HD
    return jnp.where(low, stacked[:half], stacked[half:])


def softmax_pair(queries, keys, allowed):
    scores = jnp.where(allowed, dot_nt(queries, keys) * HD ** (-0.5), -1e30)
    exponent = jnp.exp(scores - jnp.max(scores, axis=-1, keepdims=True))
    return exponent / jnp.sum(exponent, axis=-1, keepdims=True)


def attend_forward(at, stream, rows, parts, first, mix, start, length):
    tokens, features = stream.shape
    wide = 3 * features
    width = parts[0].shape[1] - first
    count = len(parts)

    def kernel(*refs):
        start_ref, stream_ref, mix_ref = refs[:3]
        part_refs = refs[3 : 3 + count]
        out_ref, normed_ref, packed_ref, context_ref = refs[-6:-2]
        rows_ref, weights_ref, sems = refs[-7 if rows is None else 3 + count], refs[-2], refs[-1]
        wait = start_parts(part_refs, weights_ref, sems, first)
        x = stream_ref[...].astype(F32)
        unit = normalize(x)[0]
        mix = mix_ref[...]
        wait()
        if rows is None:
            rows_ref[...] = lax.dot_general(
                weights_ref[:, wide + features :], mix, (((0,), (1,)), ((), ())), preferred_element_type=F32
            )
        normed = (unit * rows_ref[at : at + 1, :] + rows_ref[at + 1 : at + 2, :]).astype(BF16)
        normed = mixed(normed, mix)
        normed_ref[...] = normed
        for j in range(3):
            columns = slice(j * features, (j + 1) * features)
            packed_ref[:, columns] = dot(normed, weights_ref[:, columns]).astype(BF16)
        for s in range(tokens // length):
            allowed = allowed_pair(start_ref[s], length)
            here = slice(s * length, (s + 1) * length)
            for p in range(features // (2 * HD)):
                at_q, at_k, at_v = (slice(j * features + p * 2 * HD, j * features + (p + 1) * 2 * HD) for j in range(3))
                probs = softmax_pair(apart(packed_ref[here, at_q]), packed_ref[here, at_k], allowed)
                context_ref[here, at_q] = together(dot(probs.astype(BF16), packed_ref[here, at_v])).astype(BF16)
        context = mixed(context_ref[...], mix)
        context_ref[...] = context
        out_ref[...] = x + dot(context, weights_ref[:, wide : wide + features])

    outs = [
        shaped((tokens, features), F32),
        shaped((tokens, features), BF16),
        shaped((tokens, wide), BF16),
        shaped((tokens, features), BF16),
    ]
    ins = [start, stream, mix, *parts]
    specs = [SCALAR, WHOLE, WHOLE] + [ANYWHERE] * count
    if rows is None:
        outs = [shaped((width - wide - features, features), F32)] + outs
    else:
        ins, specs = ins + [rows], specs + [WHOLE]
    scratch = [
        pltpu.VMEM((features, width), BF16),
        pltpu.SemaphoreType.DMA((count,)),
    ]
    return call(kernel, outs, ins, 10 * tokens * features * features, (), specs, None, scratch)


def attend_backward(at, stream, rows, parts, first, mix, start, length, stored, upstream, extra=()):
    normed, packed, context = stored
    tokens, features = stream.shape
    wide = 3 * features
    width = parts[0].shape[1] - first
    small = width - wide - features if extra else 0
    count = len(parts)

    def kernel(*refs):
        start_ref = refs[0]
        part_refs = refs[1 : 1 + count]
        mix_ref, stream_ref, rows_ref, normed_ref, packed_ref, context_ref, up_ref = refs[1 + count : 8 + count]
        extra_refs = refs[8 + count : 8 + count + len(extra)]
        out_ref, mine_ref, other_ref, gains_ref, delta_ref, weights_ref, sems = refs[8 + count + len(extra) :]
        wait = start_parts(part_refs, weights_ref, sems, first)

        def put(columns, values):
            mine_ref[:, columns] = values[: features // 2].astype(BF16)
            other_ref[:, columns] = values[features // 2 :].astype(BF16)

        upstream = up_ref[...]
        branch = upstream.astype(BF16)
        mix = mix_ref[...]
        put(slice(wide, wide + features), dot_tn(context_ref[...], branch))
        wait()
        context_grad = dot_nt(branch, weights_ref[:, wide : wide + features]).astype(BF16)
        context_grad = dot_nt(context_grad, mix).astype(BF16)
        scale = HD ** (-0.5)
        for s in range(tokens // length):
            allowed = allowed_pair(start_ref[s], length)
            here = slice(s * length, (s + 1) * length)
            for p in range(features // (2 * HD)):
                at_q, at_k, at_v = (slice(j * features + p * 2 * HD, j * features + (p + 1) * 2 * HD) for j in range(3))
                queries, keys, values = apart(packed_ref[here, at_q]), packed_ref[here, at_k], packed_ref[here, at_v]
                probs = softmax_pair(queries, keys, allowed)
                out_grad = apart(context_grad[here, at_q])
                delta_ref[here, at_v] = dot_tn(probs.astype(BF16), out_grad).astype(BF16)
                prob_grad = dot_nt(out_grad, values)
                middle = jnp.sum(probs * prob_grad, axis=-1, keepdims=True)
                score_grad = (probs * (prob_grad - middle)).astype(BF16)
                delta_ref[here, at_q] = (together(dot(score_grad, keys)) * scale).astype(BF16)
                delta_ref[here, at_k] = (dot_tn(score_grad, queries) * scale).astype(BF16)
        turned = normed_ref[...].T
        normed_grad = jnp.zeros((tokens, features), F32)
        for j in range(3):
            columns = slice(j * features, (j + 1) * features)
            put(columns, dot(turned, delta_ref[:, columns]))
            normed_grad += dot_nt(delta_ref[:, columns], weights_ref[:, columns])
        out_ref[...] = norm_back(
            stream_ref[...].astype(F32), rows_ref[at : at + 1, :], unmixed(normed_grad, mix), gains_ref, upstream
        )
        if extra:
            mixer_ref, upper_ref, feed_ref = extra_refs
            lines = [gains_ref[0:2, :], feed_ref[0:2, :], upper_ref[0:2, :], mixer_ref[6:, :]]
            lines = dot(jnp.concatenate(lines, axis=0).astype(BF16), mix)
            put(slice(wide + features, width), lines.T)

    outs = [
        shaped((tokens, features), F32),
        shaped((features // 2, wide + features + small), BF16),
        shaped((features // 2, wide + features + small), BF16),
        shaped((8, features), F32),
    ]
    ins = [start, *parts, mix, stream, rows, normed, packed, context, upstream, *extra]
    specs = [SCALAR] + [ANYWHERE] * count + [WHOLE] * (7 + len(extra))
    scratch = [
        pltpu.VMEM((tokens, wide), BF16),
        pltpu.VMEM((features, width), BF16),
        pltpu.SemaphoreType.DMA((count,)),
    ]
    return call(kernel, outs, ins, 22 * tokens * features * features, (), specs, None, scratch, LIGHT)


def feed_forward(stream, rows, expand, shrink, places, mix, depth):
    tokens, features = stream.shape
    inner_width = sum(p.shape[0] for p in shrink)
    step = inner_width // depth
    count, blocks = len(expand), places.shape[0]

    def kernel(*refs):
        places_ref = refs[0]
        expand_refs, shrink_refs = refs[1 : 1 + count], refs[1 + count : -10]
        mix_ref, stream_ref, rows_ref, out_ref, normed_ref, inner_ref = refs[-10:-4]
        expand_ref, shrink_ref, expand_sems, shrink_sems = refs[-4:]
        j = pl.program_id(0)

        @pl.when(j == 0)
        def _():
            wait_expand = start_parts(expand_refs, expand_ref, expand_sems)
            wait_shrink = start_blocks(shrink_refs, places_ref, shrink_ref, shrink_sems)
            x = stream_ref[...]
            normed = (normalize(x)[0] * rows_ref[2:3, :] + rows_ref[3:4, :]).astype(BF16)
            normed_ref[...] = mixed(normed, mix_ref[...])
            out_ref[...] = x
            wait_expand()
            wait_shrink()

        here = pl.ds(pl.multiple_of(j * step, 128), step)
        inner = dot(normed_ref[...], expand_ref[:, here])
        inner_ref[...] = inner
        out_ref[...] += dot(gelu(inner).astype(BF16), shrink_ref[here, :])

    fixed = lambda a: pl.BlockSpec(a.shape, lambda j: (0, 0))
    outs = [
        shaped((tokens, features), F32),
        shaped((tokens, features), BF16),
        shaped((tokens, inner_width), F32),
    ]
    return call(
        kernel,
        outs,
        [places, *expand, *shrink, mix, stream, rows],
        4 * tokens * features * inner_width,
        (depth,),
        [SCALAR] + [ANYWHERE] * (count + len(shrink)) + [fixed(mix), fixed(stream), fixed(rows)],
        [fixed(outs[0]), fixed(outs[1]), pl.BlockSpec((tokens, step), lambda j: (0, j))],
        [
            pltpu.VMEM((features, inner_width), BF16),
            pltpu.VMEM((inner_width, features), BF16),
            pltpu.SemaphoreType.DMA((count,)),
            pltpu.SemaphoreType.DMA((blocks,)),
        ],
    )


def feed_backward(stream, rows, expand, shrink, places, mix, depth, stored, upstream):
    normed, inner = stored
    tokens, features = stream.shape
    inner_width = sum(p.shape[0] for p in shrink)
    step = inner_width // depth
    count, blocks = len(expand), places.shape[0]
    pieces = max(1, blocks // depth)
    piece = step // pieces
    side, half = max(1, pieces // 2), min(piece, step // 2)

    def kernel(places_ref, *refs):
        expand_refs, shrink_refs = refs[:count], refs[count:-19]
        mix_ref, stream_ref, rows_ref, normed_ref, inner_ref, up_ref = refs[-19:-13]
        out_ref, mine_ref, other_ref, near_ref, over_ref, gains_ref = refs[-13:-7]
        total_ref, turned_ref, active_ref, expand_ref, shrink_ref, expand_sems, shrink_sems = refs[-7:]
        j = pl.program_id(0)

        @pl.when(j == 0)
        def _():
            wait_shrink = start_blocks(shrink_refs, places_ref, shrink_ref, shrink_sems)
            wait_expand = start_parts(expand_refs, expand_ref, expand_sems)
            turned_ref[...] = normed_ref[...].T
            total_ref[...] = jnp.zeros_like(total_ref)
            wait_shrink()
            wait_expand()

        here = pl.ds(pl.multiple_of(j * step, 128), step)
        branch = up_ref[...].astype(BF16)
        active, slope = gelu_both(inner_ref[...])
        active_ref[...] = active.astype(BF16).T
        for p in range(pieces):
            start = 0
            if pieces > 1:
                layer = lax.rem(places_ref[0] // step - j + depth, depth)
                start = pl.multiple_of(places_ref[p * depth + layer] - j * step, 16)
            part = active_ref[pl.ds(start, piece), :]
            grad = dot(part, branch).astype(BF16)
            if pieces == 1:
                near_ref[0, 0] = grad[: step // 2]
                over_ref[0, 0] = grad[step // 2 :]
            elif p < pieces // 2:
                near_ref[p, 0] = grad
            else:
                over_ref[p - pieces // 2, 0] = grad
        inner_grad = (dot_nt(branch, shrink_ref[here, :]) * slope).astype(BF16)
        expand_grad = dot(turned_ref[...], inner_grad).astype(BF16)
        mine_ref[...] = expand_grad[: features // 2]
        other_ref[...] = expand_grad[features // 2 :]
        total_ref[...] += dot_nt(inner_grad, expand_ref[:, here])

        @pl.when(j == depth - 1)
        def _():
            grad = unmixed(total_ref[...], mix_ref[...])
            out_ref[...] = norm_back(stream_ref[...], rows_ref[2:3, :], grad, gains_ref, up_ref[...])

    def layer(j, places_ref):
        if pieces == 1:
            return (0, j, 0, 0)
        return (0, lax.rem(places_ref[0] // step - j + depth, depth), 0, 0)

    fixed = lambda a: pl.BlockSpec(a.shape, lambda j, places_ref: (0, 0))
    columns = lambda height: pl.BlockSpec((height, step), lambda j, places_ref: (0, j))
    outs = [
        shaped((tokens, features), F32),
        shaped((features // 2, inner_width), BF16),
        shaped((features // 2, inner_width), BF16),
        shaped((side, depth, half, features), BF16),
        shaped((side, depth, half, features), BF16),
        shaped((8, features), F32),
    ]
    ins = [places, *expand, *shrink, mix, stream, rows, normed, inner, upstream]
    flops = 8 * tokens * features * inner_width
    out, mine, other, near, over, gains = pl.pallas_call(
        kernel,
        out_shape=outs,
        grid_spec=pltpu.PrefetchScalarGridSpec(
            num_scalar_prefetch=1,
            grid=(depth,),
            in_specs=[ANYWHERE] * (count + len(shrink))
            + [fixed(mix), fixed(stream), fixed(rows), fixed(normed), columns(tokens), fixed(upstream)],
            out_specs=[
                fixed(outs[0]),
                columns(features // 2),
                columns(features // 2),
                pl.BlockSpec((side, 1, half, features), layer),
                pl.BlockSpec((side, 1, half, features), layer),
                fixed(outs[5]),
            ],
            scratch_shapes=[
                pltpu.VMEM((tokens, features), F32),
                pltpu.VMEM((features, tokens), BF16),
                pltpu.VMEM((step, tokens), BF16),
                pltpu.VMEM((features, inner_width), BF16),
                pltpu.VMEM((inner_width, features), BF16),
                pltpu.SemaphoreType.DMA((count,)),
                pltpu.SemaphoreType.DMA((blocks,)),
            ],
        ),
        compiler_params=pltpu.CompilerParams(vmem_limit_bytes=LIMIT),
        cost_estimate=cost(flops, sum(a.size * a.dtype.itemsize for a in (*ins, *outs)), LIGHT),
    )(*ins)
    if pieces == 1:
        shrink_grad = [jnp.concatenate([near, over], axis=2).reshape(inner_width, features)]
    else:
        shrink_grad = [near.reshape(-1, features), over.reshape(-1, features)]
    return out, (mine, other), shrink_grad, gains


LANE = 8


def gate_of(logits, meta):
    lane = lax.broadcasted_iota(jnp.int32, logits.shape, 1)
    chosen = lane == meta[:, 0:1] + LANE
    return jax.nn.sigmoid(jnp.sum(jnp.where(chosen, logits, 0.0), axis=-1, keepdims=True)), chosen


def put_blocks(refs, columns, values):
    rows = values.shape[0] // len(refs)
    for k, ref in enumerate(refs):
        ref[:, columns] = values[k * rows : (k + 1) * rows]


def mixer_before(stream, rows, facts, teacher, meta, target, slots, experts):
    tokens, features = stream.shape

    def kernel(stream_ref, rows_ref, facts_ref, teacher_ref, meta_ref, target_ref, *refs):
        normed_ref, logits_ref = refs[:2]
        ahead_refs, back_refs = refs[2 : 2 + experts], refs[2 + experts :]
        x = stream_ref[...]
        normed = (normalize(x)[0] * rows_ref[6:7, :] + rows_ref[7:8, :]).astype(BF16)
        normed_ref[...] = normed
        dispatch = lax.broadcasted_iota(jnp.int32, (slots, tokens), 0) == target_ref[...]
        dispatch = dispatch.astype(F32).astype(BF16)
        put_blocks(ahead_refs, slice(None), dot(dispatch, normed).astype(BF16))
        logits = dot_nt(normed, rows_ref[...].astype(BF16))
        logits_ref[...] = logits
        meta = meta_ref[...]
        gate = gate_of(logits, meta)[0]
        factor = facts_ref[1:2, 0:1] * meta[:, 2:3].astype(F32) * gate
        offset = (factor * (x - teacher_ref[...].astype(F32))).astype(BF16)
        slope = factor * gate
        high = slope.astype(BF16)
        low = (slope - high.astype(F32)).astype(BF16)
        lane = lax.broadcasted_iota(jnp.int32, (tokens, 128), 1)
        slope = jnp.where(lane == 0, high.astype(F32), jnp.where(lane == 1, low.astype(F32), 0.0)).astype(BF16)
        put_blocks(back_refs, slice(0, features), dot(dispatch, offset).astype(BF16))
        put_blocks(back_refs, slice(features, None), dot(dispatch, slope).astype(BF16))

    outs = [
        shaped((tokens, features), BF16),
        shaped((tokens, rows.shape[0]), F32),
    ]
    outs += [shaped((slots // experts, features), BF16)] * experts
    outs += [shaped((slots // experts, features + 128), BF16)] * experts
    ins = [stream, rows, facts, teacher, meta, target]
    normed, logits, *blocks = call(kernel, outs, ins, 4 * slots * tokens * features)
    return normed, logits, blocks[:experts], blocks[experts:]


def expert_forward(blocks, expand, shrink, depth):
    experts = len(blocks)
    rows, features = blocks[0].shape
    slots = experts * rows
    inner_width = shrink.shape[0]
    step = inner_width // depth

    def kernel(*refs):
        block_refs, (expand_ref, shrink_ref) = refs[:experts], refs[experts : experts + 2]
        out_refs = refs[experts + 2 : 2 * experts + 2]
        arrived_ref, inner_ref, total_ref = refs[2 * experts + 2 :]
        j = pl.program_id(0)

        @pl.when(j == 0)
        def _():
            for k in range(experts):
                arrived_ref[k * rows : (k + 1) * rows, :] = block_refs[k][...]

        inner = dot(arrived_ref[...], expand_ref[...])
        inner_ref[...] = inner
        part = dot(gelu(inner).astype(BF16), shrink_ref[...])

        @pl.when(j == 0)
        def _():
            total_ref[...] = part

        @pl.when(j > 0)
        def _():
            total_ref[...] += part

        @pl.when(j == depth - 1)
        def _():
            put_blocks(out_refs, slice(None), total_ref[...].astype(BF16))

    fixed = lambda a: pl.BlockSpec(a.shape, lambda j: (0, 0))
    outs = [shaped((rows, features), BF16)] * experts
    outs += [shaped((slots, features), BF16), shaped((slots, inner_width), F32)]
    *result, arrived, inner = call(
        kernel,
        outs,
        [*blocks, expand, shrink],
        4 * slots * features * inner_width,
        (depth,),
        [fixed(b) for b in blocks]
        + [
            pl.BlockSpec((features, step), lambda j: (0, j)),
            pl.BlockSpec((step, features), lambda j: (j, 0)),
        ],
        [fixed(o) for o in outs[:-1]] + [pl.BlockSpec((slots, step), lambda j: (0, j))],
        [pltpu.VMEM((slots, features), F32)],
    )
    return result, arrived, inner


def expert_backward(back, result, inner, expand, shrink, depth):
    experts = len(back)
    rows, features = result[0].shape
    slots = experts * rows
    inner_width = shrink.shape[0]
    step = inner_width // depth

    def kernel(*refs):
        back_refs, result_refs = refs[:experts], refs[experts : 2 * experts]
        inner_ref, expand_ref, shrink_ref = refs[2 * experts : 2 * experts + 3]
        out_refs = refs[2 * experts + 3 : 3 * experts + 3]
        landed_ref, active_ref, inner_grad_ref, total_ref = refs[3 * experts + 3 :]
        j = pl.program_id(0)

        @pl.when(j == 0)
        def _():
            for k in range(experts):
                terms = back_refs[k][:, features:].astype(F32)
                slope = terms[:, 0:1] + terms[:, 1:2]
                landed = back_refs[k][:, :features].astype(F32) + slope * result_refs[k][...].astype(F32)
                landed_ref[k * rows : (k + 1) * rows, :] = landed.astype(BF16)
            total_ref[...] = jnp.zeros_like(total_ref)

        active, slope = gelu_both(inner_ref[...])
        active_ref[...] = active.astype(BF16)
        inner_grad = (dot_nt(landed_ref[...], shrink_ref[...]) * slope).astype(BF16)
        inner_grad_ref[...] = inner_grad
        total_ref[...] += dot_nt(inner_grad, expand_ref[...])

        @pl.when(j == depth - 1)
        def _():
            put_blocks(out_refs, slice(None), total_ref[...].astype(BF16))

    fixed = lambda a: pl.BlockSpec(a.shape, lambda j: (0, 0))
    columns = lambda height: pl.BlockSpec((height, step), lambda j: (0, j))
    outs = [shaped((rows, features), BF16)] * experts
    outs += [
        shaped((slots, features), BF16),
        shaped((slots, inner_width), BF16),
        shaped((slots, inner_width), BF16),
    ]
    *rows_grad, landed, active, inner_grad = call(
        kernel,
        outs,
        [*back, *result, inner, expand, shrink],
        4 * slots * features * inner_width,
        (depth,),
        [fixed(b) for b in (*back, *result)]
        + [
            columns(slots),
            columns(features),
            pl.BlockSpec((step, features), lambda j: (j, 0)),
        ],
        [fixed(o) for o in outs[:-2]] + [columns(slots), columns(slots)],
        [pltpu.VMEM((slots, features), F32)],
    )
    return rows_grad, landed, active, inner_grad


def expert_grads(arrived, active, landed, inner_grad, owners):
    slots, features = landed.shape
    inner_width = active.shape[1]
    shrink_rows, expand_rows = inner_width // owners, features // owners
    steps = inner_width // features
    each = owners // steps if owners % steps == 0 else 1

    def shrink_kernel(active_ref, landed_ref, out_ref):
        grad = dot_tn(active_ref[...], landed_ref[...]).astype(BF16)
        for k in range(each):
            out_ref[k] = grad[k * shrink_rows : (k + 1) * shrink_rows]

    [grads] = call(
        shrink_kernel,
        [shaped((owners, 2 * shrink_rows, features), BF16)],
        [active, landed],
        2 * slots * features * inner_width,
        (owners // each,),
        [pl.BlockSpec((slots, each * shrink_rows), lambda j: (0, j)), pl.BlockSpec(landed.shape, lambda j: (0, 0))],
        [pl.BlockSpec((each, shrink_rows, features), lambda j: (j, 0, 0))],
        light=LIGHT,
    )

    def expand_kernel(arrived_ref, inner_grad_ref, grads_ref, out_ref, turned_ref):
        @pl.when(pl.program_id(0) == 0)
        def _():
            turned_ref[...] = arrived_ref[...].T

        grad = dot(turned_ref[...], inner_grad_ref[...]).astype(BF16)
        for k in range(owners):
            out_ref[k] = grad[k * expand_rows : (k + 1) * expand_rows]

    first = shrink_rows // expand_rows
    moved = 2 * slots * (features + inner_width) + 2 * features * inner_width
    return pl.pallas_call(
        expand_kernel,
        out_shape=shaped(grads.shape, BF16),
        grid=(steps,),
        in_specs=[
            pl.BlockSpec(arrived.shape, lambda j: (0, 0)),
            pl.BlockSpec((slots, features), lambda j: (0, j)),
            ANYWHERE,
        ],
        out_specs=pl.BlockSpec((owners, expand_rows, features), lambda j: (0, first + j, 0)),
        scratch_shapes=[pltpu.VMEM((features, slots), BF16)],
        input_output_aliases={2: 0},
        compiler_params=pltpu.CompilerParams(vmem_limit_bytes=LIMIT),
        cost_estimate=cost(2 * slots * features * inner_width, moved, LIGHT),
    )(arrived, inner_grad, grads)


def mixer_after(stream, rows, facts, teacher, meta, normed, logits, returned, rows_grad, experts):
    tokens, features = stream.shape
    block = returned[0].shape[0]
    slots = experts * block

    def kernel(*refs):
        stream_ref, rows_ref, facts_ref, teacher_ref, meta_ref, normed_ref, logits_ref = refs[:7]
        returned_refs, rows_grad_refs = refs[7 : 7 + experts], refs[7 + experts : 7 + 2 * experts]
        states_ref, grad_ref, small_ref, squared_ref = refs[7 + 2 * experts :]
        x = stream_ref[...]
        meta = meta_ref[...]
        combine = lax.broadcasted_iota(jnp.int32, (tokens, slots), 1) == meta[:, 1:2]
        combine = combine.astype(F32).astype(BF16)
        combined = dot(combine, jnp.concatenate([r[...] for r in returned_refs], axis=0))
        logits = logits_ref[...]
        gate, chosen = gate_of(logits, meta)
        final = x + gate * combined
        states_ref[...] = final.astype(BF16)
        valid = meta[:, 2:3].astype(F32)
        difference = final - teacher_ref[...].astype(F32)
        masked = valid * difference
        squared = 0.5 * jnp.sum(jnp.sum(masked * difference, axis=-1, keepdims=True), axis=0, keepdims=True)
        squared_ref[...] = jnp.broadcast_to(squared, squared_ref.shape)
        upstream = facts_ref[1:2, 0:1] * masked
        gate_grad = jnp.sum(upstream * combined, axis=-1, keepdims=True)
        lane = lax.broadcasted_iota(jnp.int32, logits.shape, 1)
        real = (lane >= LANE) & (lane < LANE + experts)
        shown = jnp.where(real, logits, -1e30)
        exponent = jnp.exp(shown - jnp.max(shown, axis=-1, keepdims=True))
        probs = exponent / jnp.sum(exponent, axis=-1, keepdims=True)
        share = facts_ref[0:1, :]
        tilt = jnp.sum(probs * share, axis=-1, keepdims=True)
        logits_grad = facts_ref[2:3, 0:1] * valid * probs * (share - tilt)
        logits_grad = jnp.where(real, logits_grad, 0.0)
        logits_grad += jnp.where(chosen, gate_grad * gate * (1.0 - gate), 0.0)
        first = logits_grad.astype(BF16)
        left = logits_grad - first.astype(F32)
        second = left.astype(BF16)
        third = (left - second.astype(F32)).astype(BF16)
        weights = rows_ref[...].astype(BF16)
        normed = normed_ref[...]
        normed_grad = dot(combine, jnp.concatenate([r[...] for r in rows_grad_refs], axis=0))
        normed_grad += dot(third, weights) + dot(second, weights) + dot(first, weights)
        small_ref[...] = dot_tn(third, normed) + dot_tn(second, normed) + dot_tn(first, normed)
        grad_ref[...] = norm_back(x, rows_ref[6:7, :], normed_grad, small_ref.at[6:8], upstream)

    outs = [
        shaped((tokens, features), BF16),
        shaped((tokens, features), F32),
        shaped(rows.shape, F32),
        shaped((8, 128), F32),
    ]
    ins = [stream, rows, facts, teacher, meta, normed, logits, *returned, *rows_grad]
    return call(kernel, outs, ins, 4 * slots * tokens * features)


def body(
    tokens,
    teacher,
    routes,
    piece_start,
    valid_mask,
    lower_gain,
    lower_bias,
    lower_triple,
    lower_output,
    feed_gain,
    feed_bias,
    feed_expand,
    feed_shrink,
    upper_gain,
    upper_bias,
    upper_triple,
    upper_output,
    mixer_gain,
    mixer_bias,
    router,
    expert_expand,
    expert_shrink,
):
    count, length, features = tokens.shape
    local = count * length
    experts = router.shape[1]
    share_rows = router.shape[0]
    devices = lax.axis_size("dp") * lax.axis_size("expert")
    capacity = max(2, 2 * length // experts)
    total_tokens = local * devices
    valid = valid_mask.astype(F32)
    route = routes[..., 0]
    chosen = (route[..., None] == jnp.arange(experts, dtype=jnp.int32)).astype(F32)

    counts = jnp.concatenate([jnp.sum(valid[..., None] * chosen, axis=1), jnp.sum(valid, axis=1)[:, None]], axis=1)
    counts = jnp.pad(counts.astype(BF16), ((0, share_rows - count), (0, 0)))
    vectors = [lower_gain, lower_bias, feed_gain, feed_bias, upper_gain, upper_bias, mixer_gain, mixer_bias]
    extra = jnp.concatenate([jnp.stack(vectors, axis=1), router, counts], axis=1)
    extra_width = -(-extra.shape[1] // 128) * 128
    extra = jnp.pad(extra, ((0, 0), (0, extra_width - extra.shape[1])))

    wide = 3 * features
    depth = lax.axis_size("dp") // 2

    row_order = (order(share_rows)[:, None] + jnp.arange(share_rows, dtype=jnp.int32)).reshape(1, features)
    mix = (jnp.arange(features, dtype=jnp.int32)[:, None] == row_order).astype(BF16)
    shrink_rows = feed_shrink.shape[0]
    inner_width = feed_expand.shape[1]
    lower = gather_line(jnp.concatenate([lower_triple, lower_output, extra], axis=1))
    expand_full = gather_line(after(feed_expand, lower))
    shrink_full = gather_line(after(feed_shrink, lower))
    upper = jnp.concatenate([upper_triple, upper_output], axis=1)
    upper = gather_line(after(upper, expand_full, shrink_full))
    early = [expand_full, shrink_full]
    expert_in = lax.all_gather(after(expert_expand[0], *early), "dp", axis=0, tiled=True)
    expert_out = lax.all_gather(after(expert_shrink[0], *early), "dp", axis=0, tiled=True)
    lower = gather_cores(gather_sides(lower))

    position = jnp.arange(length, dtype=jnp.int32)
    earlier = (position[:, None] > position[None, :]).astype(BF16)
    before = jnp.einsum("qk,mke->mqe", earlier, chosen.astype(BF16), preferred_element_type=F32)
    slot = jnp.sum(before * chosen, axis=-1).astype(jnp.int32)
    target = (route ^ lax.axis_index("expert")) * (count * capacity) + jnp.arange(count, dtype=jnp.int32)[:, None] * capacity + slot
    slots = experts * count * capacity
    meta = jnp.stack([route.reshape(-1), target.reshape(-1), valid_mask.reshape(-1)], axis=1)
    target = target.reshape(1, local)

    stream_in = tokens.reshape(local, features)
    labels = teacher.reshape(local, features)
    rows, stream_one, *stored_one = attend_forward(0, stream_in, None, lower, 0, mix, piece_start, length)
    lane = jnp.arange(features, dtype=jnp.int32)
    sums = rows[LANE + experts : LANE + 2 * experts + 1]
    sums = jnp.sum(jnp.where(lane % share_rows < count, sums, 0.0), axis=1)
    valid_total = sums[experts]
    loss_ratio = total_tokens / valid_total
    balance_scale = total_tokens * features * 0.1 * experts / valid_total
    share = jnp.pad(sums[:experts] / valid_total, (LANE, extra_width - LANE - experts))
    facts = jnp.stack([share, jnp.full_like(share, loss_ratio), jnp.full_like(share, balance_scale)])
    facts = jnp.pad(facts, ((0, 5), (0, 0)))

    expand_full, shrink_full = gather_sides(expand_full), gather_sides(shrink_full)
    expand_full = gather_cores([after(p, stream_one) for p in expand_full])
    shrink_full = gather_cores([after(p, stream_one) for p in shrink_full])
    places = order(shrink_rows)
    if shrink_rows % 16:
        whole = jnp.concatenate(shrink_full, axis=0).reshape(devices, shrink_rows, features)
        shrink_full = [jnp.zeros_like(whole).at[places // shrink_rows].set(whole).reshape(-1, features)]
        places = jnp.zeros((1,), jnp.int32)
    stream_two, *stored_two = feed_forward(stream_one, rows, expand_full, shrink_full, places, mix, depth)
    upper = gather_sides(upper)
    upper = gather_cores([after(p, stream_two) for p in upper])
    stream_three, *stored_three = attend_forward(4, stream_two, rows, upper, 0, mix, piece_start, length)
    normed, logits, ahead, back = mixer_before(
        stream_three, rows, facts, labels, meta, target, slots, experts
    )
    ahead = exchange(ahead)
    back = exchange([after(b, *ahead) for b in back])
    result, arrived, inner = expert_forward(ahead, expert_in, expert_out, depth)
    returned = exchange(result)
    rows_grad, landed, active, inner_grad = expert_backward(back, result, inner, expert_in, expert_out, depth)
    rows_grad = exchange(rows_grad)
    owners = lax.axis_size("dp")
    expert_grad = expert_grads(arrived, active, landed, inner_grad, owners)
    rows_grad = [after(r, expert_grad) for r in rows_grad]
    expert_grad = lax.psum_scatter(expert_grad, "dp", scatter_dimension=0, tiled=True)[0]
    states, grad_three, mixer_small, squared = mixer_after(
        stream_three, rows, facts, labels, meta, normed, logits, returned, rows_grad, experts
    )
    grad_two, *upper_grad, upper_small = attend_backward(
        4, stream_two, rows, upper, 0, mix, piece_start, length, stored_three, grad_three
    )
    at_once = lax.optimization_barrier
    hops = total_hops()

    def hop_loss(value, first, last):
        for target in hops[first:last] if hops else ():
            value = value + hop(value, target)
        return value

    upper_part = scatter_cores(*upper_grad)

    grad_two, *upper_part = at_once((grad_two, *upper_part))
    upper_part = scatter_far(upper_part)
    squared = hop_loss(squared, 0, 1)
    grad_one, expand_grad, shrink_grad, feed_small = feed_backward(
        stream_one, rows, expand_full, shrink_full, places, mix, depth, stored_two, grad_two
    )
    if shrink_rows % 16:
        blocks = order(shrink_rows) // shrink_rows
        pick = (blocks[:, None] == jnp.arange(devices, dtype=jnp.int32)).astype(BF16)
        shrink_grad = dot(pick, shrink_grad[0].reshape(devices, -1)).astype(BF16).reshape(2, -1, features)
        shrink_grad = [shrink_grad[0], shrink_grad[1]]

    upper_part, squared, grad_one, expand_grad, shrink_grad = at_once(
        (upper_part, squared, grad_one, expand_grad, shrink_grad)
    )
    upper_part = scatter_near(upper_part)
    squared = hop_loss(squared, 1, 2)
    expand_part, shrink_part = scatter_cores(*expand_grad), scatter_cores(*shrink_grad)

    upper_part, squared, expand_part, shrink_part, grad_one = at_once(
        (upper_part, squared, expand_part, shrink_part, grad_one)
    )
    upper_part = scatter_line(upper_part)
    expand_part, shrink_part = scatter_far(expand_part), scatter_far(shrink_part)
    grad_in, *lower_grad, _ = attend_backward(
        0, stream_in, rows, lower, 0, mix, piece_start, length, stored_one, grad_one, (mixer_small, upper_small, feed_small)
    )

    upper_part, expand_part, shrink_part, grad_in, lower_grad, squared = at_once(
        (upper_part, expand_part, shrink_part, grad_in, lower_grad, squared)
    )
    upper_part = total(upper_part)
    lower_part = scatter_cores(*lower_grad)
    expand_part, shrink_part = scatter_near(expand_part), scatter_near(shrink_part)
    squared = hop_loss(squared, 2, 3)

    lower_part, expand_part, shrink_part, squared = at_once((lower_part, expand_part, shrink_part, squared))
    lower_part = scatter_far(lower_part)
    expand_part = scatter_line(expand_part)
    squared = hop_loss(squared, 3, 4)

    lower_part, expand_part, shrink_part, squared = at_once((lower_part, expand_part, shrink_part, squared))
    expand_part = total(expand_part)
    lower_part = scatter_near(lower_part)
    shrink_part = scatter_line(shrink_part)
    squared = hop_loss(squared, 4, None)

    lower_part, shrink_part, squared = at_once((lower_part, shrink_part, squared))
    lower_part, shrink_part = total(scatter_line(lower_part)), total(shrink_part)
    if hops is None:
        squared = lax.psum(squared, AXES)
    small = lower_part[:, wide + features :]
    owned = expert_shrink.shape[1]
    expert_in_grad = expert_grad[owned:].reshape(-1, expert_expand.shape[1], features)
    expert_in_grad = jnp.moveaxis(expert_in_grad, 0, 1).reshape(expert_expand.shape[1:])

    squared_total = squared[0, 0]
    mean_loss = loss_ratio * squared_total / (total_tokens * features)
    return (
        states.reshape(tokens.shape),
        grad_in.reshape(tokens.shape),
        small[:, 0],
        small[:, 1],
        lower_part[:, :wide],
        lower_part[:, wide : wide + features],
        small[:, 2],
        small[:, 3],
        expand_part,
        shrink_part,
        small[:, 4],
        small[:, 5],
        upper_part[:, :wide],
        upper_part[:, wide:],
        small[:, 6],
        small[:, 7],
        small[:, 8 : 8 + experts],
        expert_in_grad.astype(F32)[None],
        expert_grad[:owned].astype(F32)[None],
        mean_loss,
    )


def solution(mesh):
    both = ("dp", "expert")
    token = P(both, None, None)
    vector = P(both)
    matrix = P(both, None)
    expert = P("expert", "dp", None)
    dense = (vector, vector, matrix, matrix, vector, vector, matrix, matrix)
    weights = dense + (vector, vector, matrix, matrix, vector, vector, matrix, expert, expert)
    return jax.shard_map(
        body,
        mesh=mesh,
        in_specs=(token, token, token, vector, matrix) + weights,
        out_specs=(token, token) + weights + (P(),),
        check_vma=False,
    )
```

time: 648 us -> 454 us (0.70)
  Pallas kernels: 0 us -> 140 us
  matrix products: 115 us -> 0.15 us
  starting transfers between devices: 182 us -> 87.9 us
  local copies, waits for them, and re-layouts: 88.6 us -> 23.1 us
  other arithmetic: 55.9 us -> 27.5 us
  waiting for transfers between devices: 175 us -> 149 us
    pallas_call x0 -> x12, Pallas kernels: none -> 140 us  [the longest x10 115 us: call(): pl.pallas_call(kernel, out_shape=outs, grid=grid, in_specs=in_specs or [W...]
    dot_general x43 -> x0, matrix products: 114 us -> none  [the longest x11 39 us: dot(): return jnp.dot(a, b, preferred_element_type=F32)]
    ppermute x84 -> x81, starting transfers between devices: 165 us -> 87.7 us  [hop(): return lax.ppermute(values, AXES, pairs(target))]
    all_to_all x4 -> x0, waiting for transfers between devices: 25.7 us -> none  [exchange(): lax.all_to_all(rows, 'expert', split_axis=0, concat_axis=0, tiled=True)]
    dynamic_update_slice x21 -> x0, local copies, waits for them, and re-layouts: 19.2 us -> none  [the longest x9 9.69 us: gather_sides(): lax.dynamic_update_slice(buffer, part[:, None, None], (0, c, mine, 0, 0))]
    all_to_all x4 -> x0, starting transfers between devices: 16.3 us -> none  [exchange(): lax.all_to_all(rows, 'expert', split_axis=0, concat_axis=0, tiled=True)]
    unnamed x302 -> x90, local copies, waits for them, and re-layouts: 21.1 us -> 7.78 us
    reshape x4 -> x0, local copies, waits for them, and re-layouts: 8.03 us -> none  [the longest x2 4.36 us: attend_forward(): packed = dot(normed, triple).astype(BF16).reshape(groups, length, 3, H, HD)]
  transfers between devices with their start and end apart: 92 -> 84, of which waited for: 27 -> 31; matrix products, arithmetic and copies ran while one was open for 33% -> 7% of each run, Pallas kernels for 0% -> 23%
where the time goes in v2:
time: 454 us; the launch traced here: 446 us
  waiting for transfers between devices  149 us (33%)
  Pallas kernels  140 us (31%)
  starting transfers between devices  87.9 us (19%)
  other arithmetic  27.5 us (6%)
  local copies, waits for them, and re-layouts  23.1 us (5%)
  between operations  18.1 us (4%)
    ppermute x81, waiting for transfers between devices, hop(): return lax.ppermute(values, AXES, pairs(target))  149 us
    pallas_call x10, Pallas kernels, call(): pl.pallas_call(kernel, out_shape=outs, grid=grid, in_specs=in_specs or [W...  115 us
    ppermute x81, starting transfers between devices, hop(): return lax.ppermute(values, AXES, pairs(target))  87.7 us
    pallas_call x1, Pallas kernels, feed_backward(): pl.pallas_call(kernel, out_shape=outs, grid_spec=pltpu.PrefetchScalarGrid...  18.8 us
    convert_element_type x12, other arithmetic, add(): return (first.astype(F32) + second.astype(F32)).astype(BF16)  12.5 us
  transfers between devices with their start and end apart: 84, of which 31 were waited for; matrix products, arithmetic and copies ran while one was open for 7% of the time, Pallas kernels for 23%

profile of v2, /device:TPU:0, one launch (start us, length us, event | category | flops | bytes accessed | tf_op | source)
XLA Modules:
  0.0 446.4 jit_solution(1866181653407684822)
XLA Ops:
  17.6 4.1 collective-permute-start.1
  25.5 7.6 %collective-permute-done.1 = bf16[24,3200]{1,0:T(8,128)(2,1)S(1)} collective-permute-done((bf16[24,3200]{1,0:T(8,128)(2,1)S(1)}, bf16[24,3200]{1,0:T(8,128)(2,1)S(1)}, u32[]{:S(2)}, u32[]{:S(2)}) %collective-permute-start.1) | collective-permute-done | bytes 153632 | tf_op jit(solution)/shard_map/ppermute | solution.py:35
  36.1 2.3 collective-permute-start.4
  43.9 8.9 %collective-permute-done.4 = bf16[24,3072]{1,0:T(8,128)(2,1)S(1)} collective-permute-done((bf16[24,3072]{1,0:T(8,128)(2,1)S(1)}, bf16[24,3072]{1,0:T(8,128)(2,1)S(1)}, u32[]{:S(2)}, u32[]{:S(2)}) %collective-permute-start.4) | collective-permute-done | bytes 147488 | tf_op jit(solution)/shard_map/ppermute | solution.py:35
  52.9 11.6 %collective-permute-done.21 = bf16[96,768]{1,0:T(8,128)(2,1)S(1)} collective-permute-done((bf16[96,768]{1,0:T(8,128)(2,1)S(1)}, bf16[96,768]{1,0:T(8,128)(2,1)S(1)}, u32[]{:S(2)}, u32[]{:S(2)}) %collective-permute-start.21) | collective-permute-done | bytes 147488 | tf_op jit(solution)/shard_map/ppermute | solution.py:35
  68.8 8.1 %collective-permute-done.32 = bf16[24,3072]{1,0:T(8,128)(2,1)S(1)} collective-permute-done((bf16[24,3072]{1,0:T(8,128)(2,1)S(1)}, bf16[24,3072]{1,0:T(8,128)(2,1)S(1)}, u32[]{:S(2)}, u32[]{:S(2)}) %collective-permute-start.32) | collective-permute-done | bytes 147488 | tf_op jit(solution)/shard_map/ppermute | solution.py:35
  76.9 5.4 %collective-permute-done.6 = bf16[4,24,3200]{2,1,0:T(8,128)(2,1)S(1)} collective-permute-done((bf16[4,24,3200]{2,1,0:T(8,128)(2,1)S(1)}, bf16[4,24,3200]{2,1,0:T(8,128)(2,1)S(1)}, u32[]{:S(2)}, u32[]{:S(2)}) %collective-permute-start.6) | collective-permute-done | bytes 614432 | tf_op jit(solution)/shard_map/ppermute | solution.py:35
  82.6 6.6 %collective-permute-done.31 = bf16[24,3072]{1,0:T(8,128)(2,1)S(1)} collective-permute-done((bf16[24,3072]{1,0:T(8,128)(2,1)S(1)}, bf16[24,3072]{1,0:T(8,128)(2,1)S(1)}, u32[]{:S(2)}, u32[]{:S(2)}) %collective-permute-start.31) | collective-permute-done | bytes 147488 | tf_op jit(solution)/shard_map/ppermute | solution.py:35
  92.0 4.5 %collective-permute-done.8 = bf16[4,24,3200]{2,1,0:T(8,128)(2,1)} collective-permute-done((bf16[4,24,3200]{2,1,0:T(8,128)(2,1)S(1)}, bf16[4,24,3200]{2,1,0:T(8,128)(2,1)}, u32[]{:S(2)}, u32[]{:S(2)}) %collective-permute-start.8) | collective-permute-done | bytes 614432 | tf_op jit(solution)/shard_map/ppermute | solution.py:35
  99.7 9.6 %collective-permute-done.13 = bf16[4,24,3072]{2,1,0:T(8,128)(2,1)} collective-permute-done((bf16[4,24,3072]{2,1,0:T(8,128)(2,1)S(1)}, bf16[4,24,3072]{2,1,0:T(8,128)(2,1)}, u32[]{:S(2)}, u32[]{:S(2)}) %collective-permute-start.13) | collective-permute-done | bytes 589856 | tf_op jit(solution)/shard_map/ppermute | solution.py:35
  114.7 8.9 %shard_map.365 = (f32[128,768]{1,0:T(8,128)}, f32[256,768]{1,0:T(8,128)}, bf16[256,768]{1,0:T(8,128)(2,1)}, bf16[256,2304]{1,0:T(8,128)(2,1)}, bf16[256,768]{1,0:T(8,128)(2,1)}) custom-call(s32[2]{0:T(128)} %refs_0_.7, bf16[256,768]{1,0:T(8,128)(2,1)} %bitcast.181, bf16[768,768]{1,0:T(8,128)(2,1)} %fusion.refs_2_.refs_17_.refs_9_.refs_16_, ...), custom_call_target="tpu_custom_call" | custom-call | flops 1509949440 | bytes 9633800 | tf_op jit(solution)/shard_map/pallas_call | solution.py:174
  125.7 6.2 %collective-permute-done.15 = bf16[4,24,3072]{2,1,0:T(8,128)(2,1)} collective-permute-done((bf16[4,24,3072]{2,1,0:T(8,128)(2,1)}, bf16[4,24,3072]{2,1,0:T(8,128)(2,1)}, u32[]{:S(2)}, u32[]{:S(2)}) %collective-permute-start.15) | collective-permute-done | bytes 589856 | tf_op jit(solution)/shard_map/ppermute | solution.py:35
  132.4 5.8 %collective-permute-done.25 = bf16[4,96,768]{2,1,0:T(8,128)(2,1)} collective-permute-done((bf16[4,96,768]{2,1,0:T(8,128)(2,1)}, bf16[4,96,768]{2,1,0:T(8,128)(2,1)}, u32[]{:S(2)}, u32[]{:S(2)}) %collective-permute-start.25) | collective-permute-done | bytes 589856 | tf_op jit(solution)/shard_map/ppermute | solution.py:35
  144.0 11.3 %shard_map.366 = (f32[256,768]{1,0:T(8,128)}, bf16[256,768]{1,0:T(8,128)(2,1)}, f32[256,3072]{1,0:T(8,128)}) custom-call(s32[32]{0:T(128)} %get-tuple-element.388.refs_0_.places_ref, bf16[96,3072]{1,0:T(8,128)(2,1)} %bitcast.142, bf16[96,3072]{1,0:T(8,128)(2,1)} %bitcast.32.refs_2_.refs_1_, bf16[96,3072]{1,0:T(8,128)(2,1)} %bitcast.33.refs_3_.refs_2_, ...), custom_call_target="tpu_custom_call" | custom-call | flops 2415919104 | bytes 16121984 | tf_op jit(solution)/shard_map/pallas_call | solution.py:174
  162.8 8.1 %shard_map.367 = (f32[256,768]{1,0:T(8,128)}, bf16[256,768]{1,0:T(8,128)(2,1)}, bf16[256,2304]{1,0:T(8,128)(2,1)}, bf16[256,768]{1,0:T(8,128)(2,1)}) custom-call(s32[2]{0:T(128)} %refs_0_.7, f32[256,768]{1,0:T(8,128)} %get-tuple-element.158.refs_1_.refs_10_, bf16[768,768]{1,0:T(8,128)(2,1)} %fusion.refs_2_.refs_17_.refs_9_.refs_16_, ...), custom_call_target="tpu_custom_call" | custom-call | flops 1509949440 | bytes 9830408 | tf_op jit(solution)/shard_map/pallas_call | solution.py:174
  170.9 3.6 shard_map.368
  175.3 2.7 collective-permute-start.42
  178.0 4.5 %collective-permute-done.40.refs_1_ = bf16[128,768]{1,0:T(8,128)(2,1)S(1)} collective-permute-done((bf16[128,768]{1,0:T(8,128)(2,1)}, bf16[128,768]{1,0:T(8,128)(2,1)S(1)}, u32[]{:S(2)}, u32[]{:S(2)}) %collective-permute-start.40) | collective-permute-done | bytes 196640 | tf_op jit(solution)/shard_map/ppermute | solution.py:35
  182.5 3.5 collective-permute-done.42.refs_3_
  189.5 11.1 %shard_map.369 = (bf16[128,768]{1,0:T(8,128)(2,1)}, bf16[128,768]{1,0:T(8,128)(2,1)}, bf16[128,768]{1,0:T(8,128)(2,1)}, bf16[128,768]{1,0:T(8,128)(2,1)}, bf16[512,768]{1,0:T(8,128)(2,1)}, /*index=5*/f32[512,3072]{1,0:T(8,128)}) custom-call(bf16[128,768]{1,0:T(8,128)(2,1)} %get-tuple-element.167.refs_0_, bf16[128,768]{1,0:T(8,128)(2,1)} %copy-done.41, ...), custom_call_target="tpu_custom_call" | custom-call | flops 4831838208 | bytes 18087936 | tf_op jit(solution)/shard_map/pallas_call | solution.py:174
  201.4 14.6 %shard_map.370 = (bf16[128,768]{1,0:T(8,128)(2,1)}, bf16[128,768]{1,0:T(8,128)(2,1)}, bf16[128,768]{1,0:T(8,128)(2,1)}, bf16[128,768]{1,0:T(8,128)(2,1)}, bf16[5...) custom-call(bf16[128,896]{1,0:T(8,128)(2,1)} %get-tuple-element.178.refs_0_, ...), custom_call_target="tpu_custom_call" | custom-call | flops 4831838208 | bytes 25296896 | tf_op jit(solution)/shard_map/pallas_call | solution.py:174
  221.9 3.1 collective-permute-done.51.refs_14_
  226.8 19.3 %shard_map.371.grads_ref = bf16[8,768,768]{2,1,0:T(8,128)(2,1)} custom-call(bf16[512,3072]{1,0:T(8,128)(2,1)} %get-tuple-element.189.active_ref, bf16[512,768]{1,0:T(8,128)(2,1)} %get-tuple-element.190.landed_ref), custom_call_target="tpu_custom_call" | custom-call | flops 2415919 | bytes 13369 | tf_op jit(solution)/shard_map/pallas_call | solution.py:174
  246.1 6.7 %shard_map.372 = bf16[8,768,768]{2,1,0:T(8,128)(2,1)} custom-call(bf16[512,768]{1,0:T(8,128)(2,1)} %get-tuple-element.187.arrived_ref, bf16[512,3072]{1,0:T(8,128)(2,1)} %get-tuple-element.188.inner_grad_ref, bf16[8,768,768]{2,1,0:T(8,128)(2,1)} %shard_map.371.grads_ref), custom_call_target="tpu_custom_call", output_to_operand_aliasing={{}: (2, {})} | custom-call | flops 2415919 | bytes 8650 | tf_op jit(solution)/shard_map/pallas_call | solution.py:786
  253.7 5.6 %shard_map.373 = (bf16[256,768]{1,0:T(8,128)(2,1)}, f32[256,768]{1,0:T(8,128)}, f32[128,768]{1,0:T(8,128)}, f32[8,128]{1,0:T(8,128)}) custom-call(f32[256,768]{1,0:T(8,128)} %get-tuple-element.164.stream_ref.refs_0_, f32[128,768]{1,0:T(8,128)} %get-tuple-element.157.refs_19_.refs_11_.rows_ref.refs_1_.refs_18_, f32[8,128]{1,0:T(8,128)} %pad.19.facts_ref.refs_2_, ...), custom_call_target="tpu_custom_call" | custom-call | flops 402653184 | bytes 5254144 | tf_op jit(solution)/shard_map/pallas_call | solution.py:174
  259.3 15.2 %shard_map.374 = (f32[256,768]{1,0:T(8,128)}, bf16[384,3072]{1,0:T(8,128)(2,1)}, bf16[384,3072]{1,0:T(8,128)(2,1)}, f32[8,768]{1,0:T(8,128)}) custom-call(s32[2]{0:T(128)} %refs_0_.7, bf16[96,3072]{1,0:T(8,128)(2,1)} %bitcast.147, bf16[96,3072]{1,0:T(8,128)(2,1)} %bitcast.56.refs_4_.refs_2_, bf16[96,3072]{1,0:T(8,128)(2,1)} %bitcast.57.refs_5_.refs_3_, ...), custom_call_target="tpu_custom_call" | custom-call | flops 3321888 | bytes 15360 | tf_op jit(solution)/shard_map/pallas_call | solution.py:174
  274.7 4.8 %collective-permute-done.52 = bf16[384,3072]{1,0:T(8,128)(2,1)} collective-permute-done((bf16[384,3072]{1,0:T(8,128)(2,1)}, bf16[384,3072]{1,0:T(8,128)(2,1)}, u32[]{:S(2)}, u32[]{:S(2)}) %collective-permute-start.52) | collective-permute-done | bytes 2359328 | tf_op jit(solution)/shard_map/ppermute | solution.py:35
  279.5 3.6 add_convert_fusion.6
  285.6 18.8 %shard_map.375 = (f32[256,768]{1,0:T(8,128)}, bf16[384,3072]{1,0:T(8,128)(2,1)}, bf16[384,3072]{1,0:T(8,128)(2,1)}, bf16[4,4,96,768]{3,2,1,0:T(8,128)(2,1)}, bf1...) custom-call(s32[32]{0:T(128)} %get-tuple-element.388.refs_0_.places_ref, bf16[96,3072]{1,0:T(8,128)(2,1)} %bitcast.143, ...), custom_call_target="tpu_custom_call" | custom-call | flops 4831838 | bytes 26370 | tf_op jit(solution)/shard_map/pallas_call | solution.py:551
  307.3 7.9 %collective-permute-done.56 = f32[8,128]{1,0:T(8,128)S(1)} collective-permute-done((f32[8,128]{1,0:T(8,128)S(1)}, f32[8,128]{1,0:T(8,128)S(1)}, u32[]{:S(2)}, u32[]{:S(2)}) %collective-permute-start.56) | collective-permute-done | bytes 4128 | tf_op jit(solution)/shard_map/ppermute | solution.py:35
  323.2 2.5 collective-permute-start.61
  325.7 2.9 collective-permute-start.60
  328.5 3.0 collective-permute-start.59
  331.6 17.0 %shard_map.376 = (f32[256,768]{1,0:T(8,128)}, bf16[384,3200]{1,0:T(8,128)(2,1)}, bf16[384,3200]{1,0:T(8,128)(2,1)}, f32[8,768]{1,0:T(8,128)}) custom-call(s32[2]{0:T(128)} %refs_0_.7, bf16[96,3200]{1,0:T(8,128)(2,1)} %bitcast.141, bf16[96,3200]{1,0:T(8,128)(2,1)} %bitcast.149, bf16[96,3200]{1,0:T(8,128)(2,1)} %bitcast.151, ...), custom_call_target="tpu_custom_call" | custom-call | flops 3321888 | bytes 15802 | tf_op jit(solution)/shard_map/pallas_call | solution.py:174
  355.6 2.9 collective-permute-done.67
  358.6 2.9 collective-permute-done.66
  362.9 4.9 %collective-permute-done.65 = bf16[96,3072]{1,0:T(8,128)(2,1)S(1)} collective-permute-done((bf16[96,3072]{1,0:T(8,128)(2,1)S(1)}, bf16[96,3072]{1,0:T(8,128)(2,1)S(1)}, u32[]{:S(2)}, u32[]{:S(2)}) %collective-permute-start.65) | collective-permute-done | bytes 589856 | tf_op jit(solution)/shard_map/ppermute | solution.py:35
  369.6 2.5 collective-permute-start.72
  372.8 4.4 collective-permute-start.70
  380.7 4.0 collective-permute-done.71
  384.6 7.6 %collective-permute-done.70 = bf16[24,3072]{1,0:T(8,128)(2,1)S(1)} collective-permute-done((bf16[24,3072]{1,0:T(8,128)(2,1)S(1)}, bf16[24,3072]{1,0:T(8,128)(2,1)S(1)}, u32[]{:S(2)}, u32[]{:S(2)}) %collective-permute-start.70) | collective-permute-done | bytes 147488 | tf_op jit(solution)/shard_map/ppermute | solution.py:35
  392.2 4.3 collective-permute-start.77
  403.7 7.9 %collective-permute-done.73 = bf16[96,3200]{1,0:T(8,128)(2,1)S(1)} collective-permute-done((bf16[96,3200]{1,0:T(8,128)(2,1)S(1)}, bf16[96,3200]{1,0:T(8,128)(2,1)S(1)}, u32[]{:S(2)}, u32[]{:S(2)}) %collective-permute-start.73) | collective-permute-done | bytes 614432 | tf_op jit(solution)/shard_map/ppermute | solution.py:35
  413.0 2.8 collective-permute-start.78
  417.6 2.7 collective-permute-done.78
  420.2 4.3 collective-permute-done.80
  424.6 5.9 %collective-permute-done.79 = bf16[24,3200]{1,0:T(8,128)(2,1)S(1)} collective-permute-done((bf16[24,3200]{1,0:T(8,128)(2,1)S(1)}, bf16[24,3200]{1,0:T(8,128)(2,1)S(1)}, u32[]{:S(2)}, u32[]{:S(2)}) %collective-permute-start.79) | collective-permute-done | bytes 153632 | tf_op jit(solution)/shard_map/ppermute | solution.py:35
  433.5 2.4 slice_convert_fusion
  (308 shorter events, 109.7 us)
Async XLA Ops:
  7.2 182.3 %all-gather.3.cloned.1.call-start = ((), (), s32[]{:S(2)}) async-start(), calls=%async_computation.1 | async-start | bytes 5308416 | tf_op jit(solution)/shard_map/all_gather | solution.py:914
  17.6 15.5 %collective-permute-start.1 = (bf16[24,3200]{1,0:T(8,128)(2,1)S(1)}, bf16[24,3200]{1,0:T(8,128)(2,1)S(1)}, u32[]{:S(2)}, u32[]{:S(2)}) collective-permute-start(bf16[24,3200]{1,0:T(8,128)(2,1)S(1)} %get-tuple-element.386), channel_id=1, source_target_pairs={{0,16},{1,17},{2,18},{3,19},{4,20},{5,21},{6,22},{7,23},{8,24},{9,... | collective-permute-start | bytes 460808 | tf_op jit(solution)/shard_map/ppermute | solution.py:35
  36.1 16.7 %collective-permute-start.4 = (bf16[24,3072]{1,0:T(8,128)(2,1)S(1)}, bf16[24,3072]{1,0:T(8,128)(2,1)S(1)}, u32[]{:S(2)}, u32[]{:S(2)}) collective-permute-start(bf16[24,3072]{1,0:T(8,128)(2,1)S(1)} %copy-done.27), channel_id=1, source_target_pairs={{0,16},{1,17},{2,18},{3,19},{4,20},{5,21},{6,22},{7,23},{8,24},{9,... | collective-permute-start | bytes 442376 | tf_op jit(solution)/shard_map/ppermute | solution.py:35
  38.4 14.4 %collective-permute-start.3 = (bf16[24,3072]{1,0:T(8,128)(2,1)S(1)}, bf16[24,3072]{1,0:T(8,128)(2,1)S(1)}, u32[]{:S(2)}, u32[]{:S(2)}) collective-permute-start(bf16[24,3072]{1,0:T(8,128)(2,1)S(1)} %copy-done.27), channel_id=1, source_target_pairs={{0,8},{1,9},{2,10},{3,11},{4,12},{5,13},{6,14},{7,15},{8,16},{9,17... | collective-permute-start | bytes 442376 | tf_op jit(solution)/shard_map/ppermute | solution.py:35
  42.2 22.2 %collective-permute-start.21 = (bf16[96,768]{1,0:T(8,128)(2,1)S(1)}, bf16[96,768]{1,0:T(8,128)(2,1)S(1)}, u32[]{:S(2)}, u32[]{:S(2)}) collective-permute-start(bf16[96,768]{1,0:T(8,128)(2,1)S(1)} %copy-done.28), channel_id=1, source_target_pairs={{0,16},{1,17},{2,18},{3,19},{4,20},{5,21},{6,22},{7,23},{8,24},{9,... | collective-permute-start | bytes 442376 | tf_op jit(solution)/shard_map/ppermute | solution.py:35
  42.3 22.2 %collective-permute-start.20 = (bf16[96,768]{1,0:T(8,128)(2,1)S(1)}, bf16[96,768]{1,0:T(8,128)(2,1)S(1)}, u32[]{:S(2)}, u32[]{:S(2)}) collective-permute-start(bf16[96,768]{1,0:T(8,128)(2,1)S(1)} %copy-done.28), channel_id=1, source_target_pairs={{0,8},{1,9},{2,10},{3,11},{4,12},{5,13},{6,14},{7,15},{8,16},{9,17... | collective-permute-start | bytes 442376 | tf_op jit(solution)/shard_map/ppermute | solution.py:35
  64.6 124.9 %all-gather.5.cloned.1.call-start = ((), (), s32[]{:S(2)}) async-start(), calls=%async_computation.2 | async-start | bytes 5308416 | tf_op jit(solution)/shard_map/all_gather | solution.py:915
  65.4 368.1 %reduce-scatter.2.cloned.1.call-start = ((), (), s32[]{:S(2)}) async-start(), calls=%async_computation.3 | async-start | bytes 10616832 | tf_op jit(solution)/shard_map/reduce_scatter | solution.py:964
  65.4 16.8 %collective-permute-start.6 = (bf16[4,24,3200]{2,1,0:T(8,128)(2,1)S(1)}, bf16[4,24,3200]{2,1,0:T(8,128)(2,1)S(1)}, u32[]{:S(2)}, u32[]{:S(2)}) collective-permute-start(bf16[4,24,3200]{2,1,0:T(8,128)(2,1)S(1)} %pad_maximum_fusion), channel_id=1, source_target_pairs={{0,1},{1,0},{2,3},{3,2},{4,6},{5,7},{6,4},{7,5},{8,9},{9,8},{10,11... | collective-permute-start | bytes 1843208 | tf_op jit(solution)/shard_map/ppermute | solution.py:35
  67.0 24.2 %collective-permute-start.7 = (bf16[4,24,3200]{2,1,0:T(8,128)(2,1)S(1)}, bf16[4,24,3200]{2,1,0:T(8,128)(2,1)S(1)}, u32[]{:S(2)}, u32[]{:S(2)}) collective-permute-start(bf16[4,24,3200]{2,1,0:T(8,128)(2,1)S(1)} %pad_maximum_fusion), channel_id=1, source_target_pairs={{0,2},{1,3},{2,0},{3,1},{4,5},{5,4},{6,7},{7,6},{8,10},{9,11},{10,... | collective-permute-start | bytes 1843208 | tf_op jit(solution)/shard_map/ppermute | solution.py:35
  68.6 22.9 %collective-permute-start.9 = (bf16[4,24,3200]{2,1,0:T(8,128)(2,1)S(1)}, bf16[4,24,3200]{2,1,0:T(8,128)(2,1)}, u32[]{:S(2)}, u32[]{:S(2)}) collective-permute-start(bf16[4,24,3200]{2,1,0:T(8,128)(2,1)S(1)} %pad_maximum_fusion), channel_id=1, source_target_pairs={{0,4},{1,5},{2,6},{3,7},{4,0},{5,1},{6,2},{7,3},{8,12},{9,13},{10,... | collective-permute-start | bytes 1843208 | tf_op jit(solution)/shard_map/ppermute | solution.py:35
  68.7 20.5 %collective-permute-start.31 = (bf16[24,3072]{1,0:T(8,128)(2,1)S(1)}, bf16[24,3072]{1,0:T(8,128)(2,1)S(1)}, u32[]{:S(2)}, u32[]{:S(2)}) collective-permute-start(bf16[24,3072]{1,0:T(8,128)(2,1)S(1)} %pad_maximum_fusion.4), channel_id=1, source_target_pairs={{0,16},{1,17},{2,18},{3,19},{4,20},{5,21},{6,22},{7,23},{8,24},{9,... | collective-permute-start | bytes 442376 | tf_op jit(solution)/shard_map/ppermute | solution.py:35
  82.2 14.3 %collective-permute-start.8 = (bf16[4,24,3200]{2,1,0:T(8,128)(2,1)S(1)}, bf16[4,24,3200]{2,1,0:T(8,128)(2,1)}, u32[]{:S(2)}, u32[]{:S(2)}) collective-permute-start(bf16[4,24,3200]{2,1,0:T(8,128)(2,1)S(1)} %collective-permute-done.6), channel_id=1, source_target_pairs={{0,2},{1,3},{2,0},{3,1},{4,5},{5,4},{6,7},{7,6},{8,10},{9,11},{10,... | collective-permute-start | bytes 1843208 | tf_op jit(solution)/shard_map/ppermute | solution.py:35
  89.7 19.5 %collective-permute-start.13 = (bf16[4,24,3072]{2,1,0:T(8,128)(2,1)S(1)}, bf16[4,24,3072]{2,1,0:T(8,128)(2,1)}, u32[]{:S(2)}, u32[]{:S(2)}) collective-permute-start(bf16[4,24,3072]{2,1,0:T(8,128)(2,1)S(1)} %pad_maximum_fusion.1), channel_id=1, source_target_pairs={{0,1},{1,0},{2,3},{3,2},{4,6},{5,7},{6,4},{7,5},{8,9},{9,8},{10,11... | collective-permute-start | bytes 1769480 | tf_op jit(solution)/shard_map/ppermute | solution.py:35
  91.2 18.9 %collective-permute-start.11 = (bf16[4,24,3200]{2,1,0:T(8,128)(2,1)S(1)}, bf16[4,24,3200]{2,1,0:T(8,128)(2,1)}, u32[]{:S(2)}, u32[]{:S(2)}) collective-permute-start(bf16[4,24,3200]{2,1,0:T(8,128)(2,1)S(1)} %collective-permute-done.7), channel_id=1, source_target_pairs={{0,4},{1,5},{2,6},{3,7},{4,0},{5,1},{6,2},{7,3},{8,12},{9,13},{10,... | collective-permute-start | bytes 1843208 | tf_op jit(solution)/shard_map/ppermute | solution.py:35
  91.5 20.8 %collective-permute-start.10 = (bf16[4,24,3200]{2,1,0:T(8,128)(2,1)S(1)}, bf16[4,24,3200]{2,1,0:T(8,128)(2,1)}, u32[]{:S(2)}, u32[]{:S(2)}) collective-permute-start(bf16[4,24,3200]{2,1,0:T(8,128)(2,1)S(1)} %collective-permute-done.6), channel_id=1, source_target_pairs={{0,4},{1,5},{2,6},{3,7},{4,0},{5,1},{6,2},{7,3},{8,12},{9,13},{10,... | collective-permute-start | bytes 1843208 | tf_op jit(solution)/shard_map/ppermute | solution.py:35
  96.5 15.9 %collective-permute-start.12 = (bf16[4,24,3200]{2,1,0:T(8,128)(2,1)}, bf16[4,24,3200]{2,1,0:T(8,128)(2,1)}, u32[]{:S(2)}, u32[]{:S(2)}) collective-permute-start(bf16[4,24,3200]{2,1,0:T(8,128)(2,1)} %collective-permute-done.8), channel_id=1, source_target_pairs={{0,4},{1,5},{2,6},{3,7},{4,0},{5,1},{6,2},{7,3},{8,12},{9,13},{10,... | collective-permute-start | bytes 1843208 | tf_op jit(solution)/shard_map/ppermute | solution.py:35
  99.1 26.0 %collective-permute-start.24 = (bf16[4,96,768]{2,1,0:T(8,128)(2,1)S(1)}, bf16[4,96,768]{2,1,0:T(8,128)(2,1)}, u32[]{:S(2)}, u32[]{:S(2)}) collective-permute-start(bf16[4,96,768]{2,1,0:T(8,128)(2,1)S(1)} %pad_maximum_fusion.2), channel_id=1, source_target_pairs={{0,2},{1,3},{2,0},{3,1},{4,5},{5,4},{6,7},{7,6},{8,10},{9,11},{10,... | collective-permute-start | bytes 1769480 | tf_op jit(solution)/shard_map/ppermute | solution.py:35
  109.2 15.9 %collective-permute-start.14 = (bf16[4,24,3072]{2,1,0:T(8,128)(2,1)S(1)}, bf16[4,24,3072]{2,1,0:T(8,128)(2,1)}, u32[]{:S(2)}, u32[]{:S(2)}) collective-permute-start(bf16[4,24,3072]{2,1,0:T(8,128)(2,1)S(1)} %pad_maximum_fusion.1), channel_id=1, source_target_pairs={{0,2},{1,3},{2,0},{3,1},{4,5},{5,4},{6,7},{7,6},{8,10},{9,11},{10,... | collective-permute-start | bytes 1769480 | tf_op jit(solution)/shard_map/ppermute | solution.py:35
  110.1 21.8 %collective-permute-start.15 = (bf16[4,24,3072]{2,1,0:T(8,128)(2,1)}, bf16[4,24,3072]{2,1,0:T(8,128)(2,1)}, u32[]{:S(2)}, u32[]{:S(2)}) collective-permute-start(bf16[4,24,3072]{2,1,0:T(8,128)(2,1)} %collective-permute-done.13), channel_id=1, source_target_pairs={{0,2},{1,3},{2,0},{3,1},{4,5},{5,4},{6,7},{7,6},{8,10},{9,11},{10,... | collective-permute-start | bytes 1769480 | tf_op jit(solution)/shard_map/ppermute | solution.py:35
  112.3 19.6 %collective-permute-start.33 = (bf16[4,24,3072]{2,1,0:T(8,128)(2,1)S(1)}, bf16[4,24,3072]{2,1,0:T(8,128)(2,1)}, u32[]{:S(2)}, u32[]{:S(2)}) collective-permute-start(bf16[4,24,3072]{2,1,0:T(8,128)(2,1)S(1)} %pad_maximum_fusion.3), channel_id=1, source_target_pairs={{0,1},{1,0},{2,3},{3,2},{4,6},{5,7},{6,4},{7,5},{8,9},{9,8},{10,11... | collective-permute-start | bytes 1769480 | tf_op jit(solution)/shard_map/ppermute | solution.py:35
  112.4 25.8 %collective-permute-start.25 = (bf16[4,96,768]{2,1,0:T(8,128)(2,1)}, bf16[4,96,768]{2,1,0:T(8,128)(2,1)}, u32[]{:S(2)}, u32[]{:S(2)}) collective-permute-start(bf16[4,96,768]{2,1,0:T(8,128)(2,1)} %collective-permute-done.23), channel_id=1, source_target_pairs={{0,2},{1,3},{2,0},{3,1},{4,5},{5,4},{6,7},{7,6},{8,10},{9,11},{10,... | collective-permute-start | bytes 1769480 | tf_op jit(solution)/shard_map/ppermute | solution.py:35
  125.1 13.2 %collective-permute-start.16 = (bf16[4,24,3072]{2,1,0:T(8,128)(2,1)S(1)}, bf16[4,24,3072]{2,1,0:T(8,128)(2,1)S(1)}, u32[]{:S(2)}, u32[]{:S(2)}) collective-permute-start(bf16[4,24,3072]{2,1,0:T(8,128)(2,1)S(1)} %pad_maximum_fusion.1), channel_id=1, source_target_pairs={{0,4},{1,5},{2,6},{3,7},{4,0},{5,1},{6,2},{7,3},{8,12},{9,13},{10,... | collective-permute-start | bytes 1769480 | tf_op jit(solution)/shard_map/ppermute | solution.py:35
  125.2 13.8 %collective-permute-start.17 = (bf16[4,24,3072]{2,1,0:T(8,128)(2,1)}, bf16[4,24,3072]{2,1,0:T(8,128)(2,1)S(1)}, u32[]{:S(2)}, u32[]{:S(2)}) collective-permute-start(bf16[4,24,3072]{2,1,0:T(8,128)(2,1)} %collective-permute-done.13), channel_id=1, source_target_pairs={{0,4},{1,5},{2,6},{3,7},{4,0},{5,1},{6,2},{7,3},{8,12},{9,13},{10,... | collective-permute-start | bytes 1769480 | tf_op jit(solution)/shard_map/ppermute | solution.py:35
  139.6 16.3 %collective-permute-start.34 = (bf16[4,24,3072]{2,1,0:T(8,128)(2,1)S(1)}, bf16[4,24,3072]{2,1,0:T(8,128)(2,1)}, u32[]{:S(2)}, u32[]{:S(2)}) collective-permute-start(bf16[4,24,3072]{2,1,0:T(8,128)(2,1)S(1)} %pad_maximum_fusion.3), channel_id=1, source_target_pairs={{0,2},{1,3},{2,0},{3,1},{4,5},{5,4},{6,7},{7,6},{8,10},{9,11},{10,... | collective-permute-start | bytes 1769480 | tf_op jit(solution)/shard_map/ppermute | solution.py:35
  140.4 15.4 %collective-permute-start.35 = (bf16[4,24,3072]{2,1,0:T(8,128)(2,1)}, bf16[4,24,3072]{2,1,0:T(8,128)(2,1)S(1)}, u32[]{:S(2)}, u32[]{:S(2)}) collective-permute-start(bf16[4,24,3072]{2,1,0:T(8,128)(2,1)} %collective-permute-done.33), channel_id=1, source_target_pairs={{0,2},{1,3},{2,0},{3,1},{4,5},{5,4},{6,7},{7,6},{8,10},{9,11},{10,... | collective-permute-start | bytes 1769480 | tf_op jit(solution)/shard_map/ppermute | solution.py:35
  186.0 14.6 %collective-permute-start.46 = (bf16[128,896]{1,0:T(8,128)(2,1)}, bf16[128,896]{1,0:T(8,128)(2,1)S(1)}, u32[]{:S(2)}, u32[]{:S(2)}) collective-permute-start(bf16[128,896]{1,0:T(8,128)(2,1)} %get-tuple-element.180), channel_id=1, source_target_pairs={{0,1},{1,0},{2,3},{3,2},{4,5},{5,4},{6,7},{7,6},{8,9},{9,8},{10,11... | collective-permute-start | bytes 688136 | tf_op jit(solution)/shard_map/ppermute | solution.py:35
  187.6 13.0 %collective-permute-start.47 = (bf16[128,896]{1,0:T(8,128)(2,1)}, bf16[128,896]{1,0:T(8,128)(2,1)S(1)}, u32[]{:S(2)}, u32[]{:S(2)}) collective-permute-start(bf16[128,896]{1,0:T(8,128)(2,1)} %get-tuple-element.182), channel_id=1, source_target_pairs={{0,2},{1,3},{2,0},{3,1},{4,6},{5,7},{6,4},{7,5},{8,10},{9,11},{10,... | collective-permute-start | bytes 688136 | tf_op jit(solution)/shard_map/ppermute | solution.py:35
  217.9 34.9 %collective-permute-start.50 = (bf16[128,768]{1,0:T(8,128)(2,1)}, bf16[128,768]{1,0:T(8,128)(2,1)S(1)}, u32[]{:S(2)}, u32[]{:S(2)}) collective-permute-start(bf16[128,768]{1,0:T(8,128)(2,1)} %get-tuple-element.194), channel_id=1, source_target_pairs={{0,2},{1,3},{2,0},{3,1},{4,6},{5,7},{6,4},{7,5},{8,10},{9,11},{10,... | collective-permute-start | bytes 589832 | tf_op jit(solution)/shard_map/ppermute | solution.py:35
  219.2 33.6 %collective-permute-start.49 = (bf16[128,768]{1,0:T(8,128)(2,1)}, bf16[128,768]{1,0:T(8,128)(2,1)S(1)}, u32[]{:S(2)}, u32[]{:S(2)}) collective-permute-start(bf16[128,768]{1,0:T(8,128)(2,1)} %get-tuple-element.192), channel_id=1, source_target_pairs={{0,1},{1,0},{2,3},{3,2},{4,5},{5,4},{6,7},{7,6},{8,9},{9,8},{10,11... | collective-permute-start | bytes 589832 | tf_op jit(solution)/shard_map/ppermute | solution.py:35
  219.6 33.2 %collective-permute-start.43 = (bf16[128,768]{1,0:T(8,128)(2,1)S(1)}, bf16[128,768]{1,0:T(8,128)(2,1)S(1)}, u32[]{:S(2)}, u32[]{:S(2)}) collective-permute-start(bf16[128,768]{1,0:T(8,128)(2,1)S(1)} %copy-done.40), channel_id=1, source_target_pairs={{0,1},{1,0},{2,3},{3,2},{4,5},{5,4},{6,7},{7,6},{8,9},{9,8},{10,11... | collective-permute-start | bytes 589832 | tf_op jit(solution)/shard_map/ppermute | solution.py:35
  221.2 31.6 %collective-permute-start.44 = (bf16[128,768]{1,0:T(8,128)(2,1)S(1)}, bf16[128,768]{1,0:T(8,128)(2,1)S(1)}, u32[]{:S(2)}, u32[]{:S(2)}) collective-permute-start(bf16[128,768]{1,0:T(8,128)(2,1)S(1)} %copy-done.39), channel_id=1, source_target_pairs={{0,2},{1,3},{2,0},{3,1},{4,6},{5,7},{6,4},{7,5},{8,10},{9,11},{10,... | collective-permute-start | bytes 589832 | tf_op jit(solution)/shard_map/ppermute | solution.py:35
  225.0 27.8 %collective-permute-start.45 = (bf16[128,768]{1,0:T(8,128)(2,1)S(1)}, bf16[128,768]{1,0:T(8,128)(2,1)S(1)}, u32[]{:S(2)}, u32[]{:S(2)}) collective-permute-start(bf16[128,768]{1,0:T(8,128)(2,1)S(1)} %copy-done.38), channel_id=1, source_target_pairs={{0,3},{1,2},{2,1},{3,0},{4,7},{5,6},{6,5},{7,4},{8,11},{9,10},{10,... | collective-permute-start | bytes 589832 | tf_op jit(solution)/shard_map/ppermute | solution.py:35
  283.1 21.3 %collective-permute-start.53 = (bf16[192,3072]{1,0:T(8,128)(2,1)}, bf16[192,3072]{1,0:T(8,128)(2,1)S(1)}, u32[]{:S(2)}, u32[]{:S(2)}) collective-permute-start(bf16[192,3072]{1,0:T(8,128)(2,1)} %get-tuple-element.207), channel_id=1, source_target_pairs={{0,2},{1,3},{2,0},{3,1},{4,5},{5,4},{6,7},{7,6},{8,10},{9,11},{10,... | collective-permute-start | bytes 3538952 | tf_op jit(solution)/shard_map/ppermute | solution.py:35
  304.8 13.2 %collective-permute-start.57 = (bf16[384,3072]{1,0:T(8,128)(2,1)}, bf16[384,3072]{1,0:T(8,128)(2,1)S(1)}, u32[]{:S(2)}, u32[]{:S(2)}) collective-permute-start(bf16[384,3072]{1,0:T(8,128)(2,1)} %get-tuple-element.221), channel_id=1, source_target_pairs={{0,4},{1,5},{2,6},{3,7},{4,0},{5,1},{6,2},{7,3},{8,12},{9,13},{10,... | collective-permute-start | bytes 7077896 | tf_op jit(solution)/shard_map/ppermute | solution.py:35
  321.1 27.5 %collective-permute-start.62 = (bf16[192,3072]{1,0:T(8,128)(2,1)}, bf16[192,3072]{1,0:T(8,128)(2,1)}, u32[]{:S(2)}, u32[]{:S(2)}) collective-permute-start(bf16[192,3072]{1,0:T(8,128)(2,1)} %get-tuple-element.227), channel_id=1, source_target_pairs={{0,2},{1,3},{2,0},{3,1},{4,5},{5,4},{6,7},{7,6},{8,10},{9,11},{10,... | collective-permute-start | bytes 3538952 | tf_op jit(solution)/shard_map/ppermute | solution.py:35
  321.8 28.4 %collective-permute-start.63 = (bf16[768,768]{1,0:T(8,128)(2,1)S(1)}, bf16[768,768]{1,0:T(8,128)(2,1)}, u32[]{:S(2)}, u32[]{:S(2)}) collective-permute-start(bf16[768,768]{1,0:T(8,128)(2,1)S(1)} %get-tuple-element.229), channel_id=1, source_target_pairs={{0,2},{1,3},{2,0},{3,1},{4,5},{5,4},{6,7},{7,6},{8,10},{9,11},{10,... | collective-permute-start | bytes 3538952 | tf_op jit(solution)/shard_map/ppermute | solution.py:35
  323.2 25.4 %collective-permute-start.61 = (bf16[24,3072]{1,0:T(8,128)(2,1)S(1)}, bf16[24,3072]{1,0:T(8,128)(2,1)}, u32[]{:S(2)}, u32[]{:S(2)}) collective-permute-start(bf16[24,3072]{1,0:T(8,128)(2,1)S(1)} %get-tuple-element.381), channel_id=1, source_target_pairs={{0,8},{1,9},{2,10},{3,11},{4,12},{5,13},{6,14},{7,15},{8,16},{9,17... | collective-permute-start | bytes 442376 | tf_op jit(solution)/shard_map/ppermute | solution.py:35
  325.7 22.9 %collective-permute-start.60 = (bf16[24,3072]{1,0:T(8,128)(2,1)S(1)}, bf16[24,3072]{1,0:T(8,128)(2,1)}, u32[]{:S(2)}, u32[]{:S(2)}) collective-permute-start(bf16[24,3072]{1,0:T(8,128)(2,1)S(1)} %get-tuple-element.382), channel_id=1, source_target_pairs={{0,16},{1,17},{2,18},{3,19},{4,20},{5,21},{6,22},{7,23},{8,24},{9,... | collective-permute-start | bytes 442376 | tf_op jit(solution)/shard_map/ppermute | solution.py:35
  328.5 20.0 %collective-permute-start.59 = (bf16[24,3072]{1,0:T(8,128)(2,1)S(1)}, bf16[24,3072]{1,0:T(8,128)(2,1)}, u32[]{:S(2)}, u32[]{:S(2)}) collective-permute-start(bf16[24,3072]{1,0:T(8,128)(2,1)S(1)} %get-tuple-element.383), channel_id=1, source_target_pairs={{0,24},{1,25},{2,26},{3,27},{4,28},{5,29},{6,30},{7,31},{8,0},{9,1... | collective-permute-start | bytes 442376 | tf_op jit(solution)/shard_map/ppermute | solution.py:35
  350.3 18.8 %collective-permute-start.64 = (bf16[384,3200]{1,0:T(8,128)(2,1)}, bf16[384,3200]{1,0:T(8,128)(2,1)S(1)}, u32[]{:S(2)}, u32[]{:S(2)}) collective-permute-start(bf16[384,3200]{1,0:T(8,128)(2,1)} %get-tuple-element.243), channel_id=1, source_target_pairs={{0,4},{1,5},{2,6},{3,7},{4,0},{5,1},{6,2},{7,3},{8,12},{9,13},{10,... | collective-permute-start | bytes 7372808 | tf_op jit(solution)/shard_map/ppermute | solution.py:35
  353.2 14.5 %collective-permute-start.65 = (bf16[96,3072]{1,0:T(8,128)(2,1)S(1)}, bf16[96,3072]{1,0:T(8,128)(2,1)S(1)}, u32[]{:S(2)}, u32[]{:S(2)}) collective-permute-start(bf16[96,3072]{1,0:T(8,128)(2,1)S(1)} %add_convert_fusion.15), channel_id=1, source_target_pairs={{0,1},{1,0},{2,3},{3,2},{4,6},{5,7},{6,4},{7,5},{8,9},{9,8},{10,11... | collective-permute-start | bytes 1769480 | tf_op jit(solution)/shard_map/ppermute | solution.py:35
  372.2 20.0 %collective-permute-start.68 = (bf16[192,3200]{1,0:T(8,128)(2,1)S(1)}, bf16[192,3200]{1,0:T(8,128)(2,1)S(1)}, u32[]{:S(2)}, u32[]{:S(2)}) collective-permute-start(bf16[192,3200]{1,0:T(8,128)(2,1)S(1)} %get-tuple-element.250), channel_id=1, source_target_pairs={{0,2},{1,3},{2,0},{3,1},{4,5},{5,4},{6,7},{7,6},{8,10},{9,11},{10,... | collective-permute-start | bytes 3686408 | tf_op jit(solution)/shard_map/ppermute | solution.py:35
  372.8 19.4 %collective-permute-start.70 = (bf16[24,3072]{1,0:T(8,128)(2,1)S(1)}, bf16[24,3072]{1,0:T(8,128)(2,1)S(1)}, u32[]{:S(2)}, u32[]{:S(2)}) collective-permute-start(bf16[24,3072]{1,0:T(8,128)(2,1)S(1)} %get-tuple-element.378), channel_id=1, source_target_pairs={{0,16},{1,17},{2,18},{3,19},{4,20},{5,21},{6,22},{7,23},{8,24},{9,... | collective-permute-start | bytes 442376 | tf_op jit(solution)/shard_map/ppermute | solution.py:35
  377.2 15.0 %collective-permute-start.69 = (bf16[24,3072]{1,0:T(8,128)(2,1)S(1)}, bf16[24,3072]{1,0:T(8,128)(2,1)S(1)}, u32[]{:S(2)}, u32[]{:S(2)}) collective-permute-start(bf16[24,3072]{1,0:T(8,128)(2,1)S(1)} %get-tuple-element.379), channel_id=1, source_target_pairs={{0,24},{1,25},{2,26},{3,27},{4,28},{5,29},{6,30},{7,31},{8,0},{9,1... | collective-permute-start | bytes 442376 | tf_op jit(solution)/shard_map/ppermute | solution.py:35
  396.5 15.3 %collective-permute-start.76 = (bf16[96,768]{1,0:T(8,128)(2,1)S(1)}, bf16[96,768]{1,0:T(8,128)(2,1)S(1)}, u32[]{:S(2)}, u32[]{:S(2)}) collective-permute-start(bf16[96,768]{1,0:T(8,128)(2,1)S(1)} %get-tuple-element.373), channel_id=1, source_target_pairs={{0,8},{1,9},{2,10},{3,11},{4,12},{5,13},{6,14},{7,15},{8,16},{9,17... | collective-permute-start | bytes 442376 | tf_op jit(solution)/shard_map/ppermute | solution.py:35
  398.8 13.0 %collective-permute-start.75 = (bf16[96,768]{1,0:T(8,128)(2,1)S(1)}, bf16[96,768]{1,0:T(8,128)(2,1)S(1)}, u32[]{:S(2)}, u32[]{:S(2)}) collective-permute-start(bf16[96,768]{1,0:T(8,128)(2,1)S(1)} %get-tuple-element.374), channel_id=1, source_target_pairs={{0,16},{1,17},{2,18},{3,19},{4,20},{5,21},{6,22},{7,23},{8,24},{9,... | collective-permute-start | bytes 442376 | tf_op jit(solution)/shard_map/ppermute | solution.py:35
  415.8 14.7 %collective-permute-start.79 = (bf16[24,3200]{1,0:T(8,128)(2,1)S(1)}, bf16[24,3200]{1,0:T(8,128)(2,1)S(1)}, u32[]{:S(2)}, u32[]{:S(2)}) collective-permute-start(bf16[24,3200]{1,0:T(8,128)(2,1)S(1)} %get-tuple-element.372), channel_id=1, source_target_pairs={{0,16},{1,17},{2,18},{3,19},{4,20},{5,21},{6,22},{7,23},{8,24},{9,... | collective-permute-start | bytes 460808 | tf_op jit(solution)/shard_map/ppermute | solution.py:35
  (80 other events, 850.2 us)
Sparse Core Ops, SparseCore 0:
  64.7 57.2 all-gather.2
  123.7 49.9 all-gather.4
  274.8 115.3 reduce-scatter.1

commit v3 on v2

--- a/solution.py
+++ b/solution.py
@@ -47,6 +47,9 @@
     return hop(values, lambda z, c, e: (z, c, e ^ (2 - c)))
 
 
+at_once = lax.optimization_barrier
+
+
 def after(value, *others):
     return lax.optimization_barrier((value, *others))[0]
 
@@ -56,20 +59,37 @@
     return hop(values, lambda z, c, e: ((z + by) % depth, c, e))
 
 
-def gather_line(own):
-    return jnp.stack([own] + [shift(own, k) for k in range(1, place()[0])])
-
-
-def gather_sides(line):
+def pull_line(own):
+    return [shift(own, k) for k in range(1, place()[0])]
+
+
+def gather_lines(own):
+    depth, _, z, c, _ = place()
+    both = lax.all_gather(own, "dp", axis=0, tiled=True).reshape(depth, 2, *own.shape)
+    zero = jnp.zeros_like(z)
+    at = lambda k, core: lax.dynamic_slice(both, ((z - k) % depth, core, zero, zero), (1, 1, *own.shape))[0]
+    return [jnp.concatenate([at(k, core) for k in range(depth)]) for core in (c, 1 - c)]
+
+
+def pull_near(line):
+    return first_side(line) if place()[1] == 4 else line
+
+
+def pull_far(line, near, over=None):
     if place()[1] != 4:
-        return [lax.all_gather(line, "expert", axis=1)]
-    one = first_side(line)
-    return [line, one, second_side(line), second_side(one)]
-
-
-def gather_cores(parts):
-    parts = [*parts, *(swap_cores(p) for p in parts)]
-    return [p.reshape(-1, p.shape[-1]) for p in parts]
+        whole = lax.all_gather(line, "expert", axis=1)
+        return [whole], None, [swap_cores(whole)]
+    pair = jnp.stack([line, near])
+    side = [swap_cores(pair)] if over is None else [over, swap_cores(near)]
+    return [pair], second_side(pair), side
+
+
+def pull_over(far):
+    return None if far is None else swap_cores(far)
+
+
+def in_order(pair, far, pair_over, far_over):
+    return [p.reshape(-1, p.shape[-1]) for p in (*pair, far, *pair_over, far_over) if p is not None]
 
 
 def order(rows):
@@ -101,8 +121,11 @@
 
 
 def scatter_cores(mine, other):
+    return sum_cores(mine, swap_cores(other))
+
+
+def sum_cores(mine, other):
     depth, across, _, _, _ = place()
-    other = swap_cores(other)
     if across != 4:
         return [add(mine, other).reshape(depth, across, -1, mine.shape[1])]
     half = mine.shape[0] // 2
@@ -203,16 +226,14 @@
 
 
 def start_blocks(parts, places, whole, sems):
-    count = places.shape[0] // len(parts)
+    rows = whole.shape[0] // places.shape[0]
     copies = []
-    for k, part in enumerate(parts):
-        rows = part.shape[0] // count
-        for b in range(count):
-            at = pl.multiple_of(places[k * count + b], 16)
+    for part in parts:
+        for b in range(part.shape[0] // rows):
+            k = len(copies)
+            at = pl.multiple_of(places[k], 16)
             copies.append(
-                pltpu.make_async_copy(
-                    part.at[b * rows : (b + 1) * rows], whole.at[pl.ds(at, rows)], sems.at[k * count + b]
-                )
+                pltpu.make_async_copy(part.at[b * rows : (b + 1) * rows], whole.at[pl.ds(at, rows)], sems.at[k])
             )
     for copy in copies:
         copy.start()
@@ -348,7 +369,7 @@
         pltpu.VMEM((features, width), BF16),
         pltpu.SemaphoreType.DMA((count,)),
     ]
-    return call(kernel, outs, ins, 10 * tokens * features * features, (), specs, None, scratch)
+    return call(kernel, outs, ins, 10 * tokens * features * features, (), specs, None, scratch, LIGHT)
 
 
 def attend_backward(at, stream, rows, parts, first, mix, start, length, stored, upstream, extra=()):
@@ -473,46 +494,36 @@
             pltpu.SemaphoreType.DMA((count,)),
             pltpu.SemaphoreType.DMA((blocks,)),
         ],
-    )
-
-
-def feed_backward(stream, rows, expand, shrink, places, mix, depth, stored, upstream):
-    normed, inner = stored
-    tokens, features = stream.shape
-    inner_width = sum(p.shape[0] for p in shrink)
+        LIGHT,
+    )
+
+
+def feed_backward_shrink(shrink, places, depth, inner, upstream):
+    tokens, features = upstream.shape
+    inner_width = inner.shape[1]
     step = inner_width // depth
-    count, blocks = len(expand), places.shape[0]
+    count, blocks = len(shrink), places.shape[0]
     pieces = max(1, blocks // depth)
     piece = step // pieces
     side, half = max(1, pieces // 2), min(piece, step // 2)
 
     def kernel(places_ref, *refs):
-        expand_refs, shrink_refs = refs[:count], refs[count:-19]
-        mix_ref, stream_ref, rows_ref, normed_ref, inner_ref, up_ref = refs[-19:-13]
-        out_ref, mine_ref, other_ref, near_ref, over_ref, gains_ref = refs[-13:-7]
-        total_ref, turned_ref, active_ref, expand_ref, shrink_ref, expand_sems, shrink_sems = refs[-7:]
+        shrink_refs = refs[:count]
+        inner_ref, up_ref, inner_grad_ref, near_ref, over_ref, active_ref, shrink_ref, sems = refs[count:]
         j = pl.program_id(0)
 
         @pl.when(j == 0)
         def _():
-            wait_shrink = start_blocks(shrink_refs, places_ref, shrink_ref, shrink_sems)
-            wait_expand = start_parts(expand_refs, expand_ref, expand_sems)
-            turned_ref[...] = normed_ref[...].T
-            total_ref[...] = jnp.zeros_like(total_ref)
-            wait_shrink()
-            wait_expand()
-
-        here = pl.ds(pl.multiple_of(j * step, 128), step)
+            start_blocks(shrink_refs, places_ref, shrink_ref, sems)()
+
         branch = up_ref[...].astype(BF16)
         active, slope = gelu_both(inner_ref[...])
         active_ref[...] = active.astype(BF16).T
         for p in range(pieces):
             start = 0
             if pieces > 1:
-                layer = lax.rem(places_ref[0] // step - j + depth, depth)
-                start = pl.multiple_of(places_ref[p * depth + layer] - j * step, 16)
-            part = active_ref[pl.ds(start, piece), :]
-            grad = dot(part, branch).astype(BF16)
+                start = pl.multiple_of(places_ref[p * depth + chunk_at(j, places_ref)] - j * step, 16)
+            grad = dot(active_ref[pl.ds(start, piece), :], branch).astype(BF16)
             if pieces == 1:
                 near_ref[0, 0] = grad[: step // 2]
                 over_ref[0, 0] = grad[step // 2 :]
@@ -520,68 +531,105 @@
                 near_ref[p, 0] = grad
             else:
                 over_ref[p - pieces // 2, 0] = grad
-        inner_grad = (dot_nt(branch, shrink_ref[here, :]) * slope).astype(BF16)
-        expand_grad = dot(turned_ref[...], inner_grad).astype(BF16)
-        mine_ref[...] = expand_grad[: features // 2]
-        other_ref[...] = expand_grad[features // 2 :]
-        total_ref[...] += dot_nt(inner_grad, expand_ref[:, here])
-
-        @pl.when(j == depth - 1)
-        def _():
-            grad = unmixed(total_ref[...], mix_ref[...])
-            out_ref[...] = norm_back(stream_ref[...], rows_ref[2:3, :], grad, gains_ref, up_ref[...])
+        here = pl.ds(pl.multiple_of(j * step, 128), step)
+        inner_grad_ref[...] = (dot_nt(branch, shrink_ref[here, :]) * slope).astype(BF16)
+
+    def chunk_at(j, places_ref):
+        return lax.rem(places_ref[0] // step - j + depth, depth)
 
     def layer(j, places_ref):
-        if pieces == 1:
-            return (0, j, 0, 0)
-        return (0, lax.rem(places_ref[0] // step - j + depth, depth), 0, 0)
-
-    fixed = lambda a: pl.BlockSpec(a.shape, lambda j, places_ref: (0, 0))
-    columns = lambda height: pl.BlockSpec((height, step), lambda j, places_ref: (0, j))
+        return (0, j if pieces == 1 else chunk_at(j, places_ref), 0, 0)
+
+    columns = pl.BlockSpec((tokens, step), lambda j, places_ref: (0, j))
     outs = [
-        shaped((tokens, features), F32),
-        shaped((features // 2, inner_width), BF16),
-        shaped((features // 2, inner_width), BF16),
+        shaped((tokens, inner_width), BF16),
         shaped((side, depth, half, features), BF16),
         shaped((side, depth, half, features), BF16),
-        shaped((8, features), F32),
     ]
-    ins = [places, *expand, *shrink, mix, stream, rows, normed, inner, upstream]
-    flops = 8 * tokens * features * inner_width
-    out, mine, other, near, over, gains = pl.pallas_call(
+    ins = [places, *shrink, inner, upstream]
+    moved = sum(a.size * a.dtype.itemsize for a in (*ins, *outs))
+    inner_grad, near, over = pl.pallas_call(
         kernel,
         out_shape=outs,
         grid_spec=pltpu.PrefetchScalarGridSpec(
             num_scalar_prefetch=1,
             grid=(depth,),
-            in_specs=[ANYWHERE] * (count + len(shrink))
-            + [fixed(mix), fixed(stream), fixed(rows), fixed(normed), columns(tokens), fixed(upstream)],
-            out_specs=[
-                fixed(outs[0]),
-                columns(features // 2),
-                columns(features // 2),
-                pl.BlockSpec((side, 1, half, features), layer),
-                pl.BlockSpec((side, 1, half, features), layer),
-                fixed(outs[5]),
-            ],
+            in_specs=[ANYWHERE] * count
+            + [columns, pl.BlockSpec(upstream.shape, lambda j, places_ref: (0, 0))],
+            out_specs=[columns] + [pl.BlockSpec((side, 1, half, features), layer)] * 2,
             scratch_shapes=[
-                pltpu.VMEM((tokens, features), F32),
-                pltpu.VMEM((features, tokens), BF16),
                 pltpu.VMEM((step, tokens), BF16),
-                pltpu.VMEM((features, inner_width), BF16),
                 pltpu.VMEM((inner_width, features), BF16),
-                pltpu.SemaphoreType.DMA((count,)),
                 pltpu.SemaphoreType.DMA((blocks,)),
             ],
         ),
         compiler_params=pltpu.CompilerParams(vmem_limit_bytes=LIMIT),
-        cost_estimate=cost(flops, sum(a.size * a.dtype.itemsize for a in (*ins, *outs)), LIGHT),
+        cost_estimate=cost(4 * tokens * features * inner_width, moved, LIGHT),
     )(*ins)
     if pieces == 1:
         shrink_grad = [jnp.concatenate([near, over], axis=2).reshape(inner_width, features)]
     else:
         shrink_grad = [near.reshape(-1, features), over.reshape(-1, features)]
-    return out, (mine, other), shrink_grad, gains
+    return inner_grad, shrink_grad
+
+
+def feed_backward_expand(stream, rows, expand, mix, depth, normed, inner_grad, upstream):
+    tokens, features = stream.shape
+    inner_width = inner_grad.shape[1]
+    step = inner_width // depth
+    count = len(expand)
+
+    def kernel(*refs):
+        expand_refs = refs[:count]
+        mix_ref, stream_ref, rows_ref, normed_ref, inner_grad_ref, up_ref = refs[count : count + 6]
+        out_ref, mine_ref, other_ref, gains_ref, total_ref, turned_ref, expand_ref, sems = refs[count + 6 :]
+        j = pl.program_id(0)
+
+        @pl.when(j == 0)
+        def _():
+            wait = start_parts(expand_refs, expand_ref, sems)
+            turned_ref[...] = normed_ref[...].T
+            total_ref[...] = jnp.zeros_like(total_ref)
+            wait()
+
+        inner_grad = inner_grad_ref[...]
+        expand_grad = dot(turned_ref[...], inner_grad).astype(BF16)
+        mine_ref[...] = expand_grad[: features // 2]
+        other_ref[...] = expand_grad[features // 2 :]
+        here = pl.ds(pl.multiple_of(j * step, 128), step)
+        total_ref[...] += dot_nt(inner_grad, expand_ref[:, here])
+
+        @pl.when(j == depth - 1)
+        def _():
+            grad = unmixed(total_ref[...], mix_ref[...])
+            out_ref[...] = norm_back(stream_ref[...], rows_ref[2:3, :], grad, gains_ref, up_ref[...])
+
+    fixed = lambda a: pl.BlockSpec(a.shape, lambda j: (0, 0))
+    columns = lambda height: pl.BlockSpec((height, step), lambda j: (0, j))
+    outs = [
+        shaped((tokens, features), F32),
+        shaped((features // 2, inner_width), BF16),
+        shaped((features // 2, inner_width), BF16),
+        shaped((8, features), F32),
+    ]
+    out, mine, other, gains = call(
+        kernel,
+        outs,
+        [*expand, mix, stream, rows, normed, inner_grad, upstream],
+        4 * tokens * features * inner_width,
+        (depth,),
+        [ANYWHERE] * count
+        + [fixed(mix), fixed(stream), fixed(rows), fixed(normed), columns(tokens), fixed(upstream)],
+        [fixed(outs[0]), columns(features // 2), columns(features // 2), fixed(outs[3])],
+        [
+            pltpu.VMEM((tokens, features), F32),
+            pltpu.VMEM((features, tokens), BF16),
+            pltpu.VMEM((features, inner_width), BF16),
+            pltpu.SemaphoreType.DMA((count,)),
+        ],
+        LIGHT,
+    )
+    return out, (mine, other), gains
 
 
 LANE = 8
@@ -636,11 +684,24 @@
     return normed, logits, blocks[:experts], blocks[experts:]
 
 
-def expert_forward(blocks, expand, shrink, depth):
+def expert_specs(weights, step):
+    owners, height, features = weights.shape
+    shrink_rows = height // 2
+    expand_rows = features // owners
+    each = step // shrink_rows
+    first = shrink_rows // expand_rows
+    expand = pl.BlockSpec(
+        (owners, expand_rows, step), lambda j: (0, first + j * step // features, j * step % features // step)
+    )
+    return expand, pl.BlockSpec((each, shrink_rows, features), lambda j: (j, 0, 0))
+
+
+def expert_forward(blocks, weights, depth):
     experts = len(blocks)
     rows, features = blocks[0].shape
     slots = experts * rows
-    inner_width = shrink.shape[0]
+    owners, height, _ = weights.shape
+    inner_width = owners * height // 2
     step = inner_width // depth
 
     def kernel(*refs):
@@ -654,9 +715,9 @@
             for k in range(experts):
                 arrived_ref[k * rows : (k + 1) * rows, :] = block_refs[k][...]
 
-        inner = dot(arrived_ref[...], expand_ref[...])
+        inner = dot(arrived_ref[...], expand_ref[...].reshape(features, step))
         inner_ref[...] = inner
-        part = dot(gelu(inner).astype(BF16), shrink_ref[...])
+        part = dot(gelu(inner).astype(BF16), shrink_ref[...].reshape(step, features))
 
         @pl.when(j == 0)
         def _():
@@ -676,32 +737,29 @@
     *result, arrived, inner = call(
         kernel,
         outs,
-        [*blocks, expand, shrink],
+        [*blocks, weights, weights],
         4 * slots * features * inner_width,
         (depth,),
-        [fixed(b) for b in blocks]
-        + [
-            pl.BlockSpec((features, step), lambda j: (0, j)),
-            pl.BlockSpec((step, features), lambda j: (j, 0)),
-        ],
+        [fixed(b) for b in blocks] + [*expert_specs(weights, step)],
         [fixed(o) for o in outs[:-1]] + [pl.BlockSpec((slots, step), lambda j: (0, j))],
         [pltpu.VMEM((slots, features), F32)],
     )
     return result, arrived, inner
 
 
-def expert_backward(back, result, inner, expand, shrink, depth):
+def expert_backward(back, result, inner, weights, depth):
     experts = len(back)
     rows, features = result[0].shape
     slots = experts * rows
-    inner_width = shrink.shape[0]
+    owners, height, _ = weights.shape
+    inner_width = owners * height // 2
     step = inner_width // depth
 
     def kernel(*refs):
         back_refs, result_refs = refs[:experts], refs[experts : 2 * experts]
         inner_ref, expand_ref, shrink_ref = refs[2 * experts : 2 * experts + 3]
         out_refs = refs[2 * experts + 3 : 3 * experts + 3]
-        landed_ref, active_ref, inner_grad_ref, total_ref = refs[3 * experts + 3 :]
+        inner_grad_ref, grads_ref, landed_ref, total_ref = refs[3 * experts + 3 :]
         j = pl.program_id(0)
 
         @pl.when(j == 0)
@@ -714,10 +772,11 @@
             total_ref[...] = jnp.zeros_like(total_ref)
 
         active, slope = gelu_both(inner_ref[...])
-        active_ref[...] = active.astype(BF16)
-        inner_grad = (dot_nt(landed_ref[...], shrink_ref[...]) * slope).astype(BF16)
+        landed = landed_ref[...]
+        inner_grad = (dot_nt(landed, shrink_ref[...].reshape(step, features)) * slope).astype(BF16)
         inner_grad_ref[...] = inner_grad
-        total_ref[...] += dot_nt(inner_grad, expand_ref[...])
+        grads_ref[...] = dot_tn(active.astype(BF16), landed).astype(BF16)
+        total_ref[...] += dot_nt(inner_grad, expand_ref[...].reshape(features, step))
 
         @pl.when(j == depth - 1)
         def _():
@@ -726,78 +785,50 @@
     fixed = lambda a: pl.BlockSpec(a.shape, lambda j: (0, 0))
     columns = lambda height: pl.BlockSpec((height, step), lambda j: (0, j))
     outs = [shaped((rows, features), BF16)] * experts
-    outs += [
-        shaped((slots, features), BF16),
-        shaped((slots, inner_width), BF16),
-        shaped((slots, inner_width), BF16),
-    ]
-    *rows_grad, landed, active, inner_grad = call(
+    outs += [shaped((slots, inner_width), BF16), shaped((inner_width, features), BF16)]
+    *rows_grad, inner_grad, grads = call(
         kernel,
         outs,
-        [*back, *result, inner, expand, shrink],
-        4 * slots * features * inner_width,
+        [*back, *result, inner, weights, weights],
+        6 * slots * features * inner_width,
         (depth,),
         [fixed(b) for b in (*back, *result)]
         + [
             columns(slots),
-            columns(features),
-            pl.BlockSpec((step, features), lambda j: (j, 0)),
+            *expert_specs(weights, step),
         ],
-        [fixed(o) for o in outs[:-2]] + [columns(slots), columns(slots)],
-        [pltpu.VMEM((slots, features), F32)],
-    )
-    return rows_grad, landed, active, inner_grad
-
-
-def expert_grads(arrived, active, landed, inner_grad, owners):
-    slots, features = landed.shape
-    inner_width = active.shape[1]
-    shrink_rows, expand_rows = inner_width // owners, features // owners
-    steps = inner_width // features
-    each = owners // steps if owners % steps == 0 else 1
-
-    def shrink_kernel(active_ref, landed_ref, out_ref):
-        grad = dot_tn(active_ref[...], landed_ref[...]).astype(BF16)
-        for k in range(each):
-            out_ref[k] = grad[k * shrink_rows : (k + 1) * shrink_rows]
-
-    [grads] = call(
-        shrink_kernel,
-        [shaped((owners, 2 * shrink_rows, features), BF16)],
-        [active, landed],
-        2 * slots * features * inner_width,
-        (owners // each,),
-        [pl.BlockSpec((slots, each * shrink_rows), lambda j: (0, j)), pl.BlockSpec(landed.shape, lambda j: (0, 0))],
-        [pl.BlockSpec((each, shrink_rows, features), lambda j: (j, 0, 0))],
-        light=LIGHT,
-    )
-
-    def expand_kernel(arrived_ref, inner_grad_ref, grads_ref, out_ref, turned_ref):
+        [fixed(o) for o in outs[:-2]]
+        + [columns(slots), pl.BlockSpec((step, features), lambda j: (j, 0))],
+        [pltpu.VMEM((slots, features), BF16), pltpu.VMEM((slots, features), F32)],
+        LIGHT,
+    )
+    return rows_grad, inner_grad, grads
+
+
+def expert_expand_grad(arrived, inner_grad):
+    slots, features = arrived.shape
+    inner_width = inner_grad.shape[1]
+
+    def kernel(arrived_ref, inner_grad_ref, out_ref, turned_ref):
         @pl.when(pl.program_id(0) == 0)
         def _():
             turned_ref[...] = arrived_ref[...].T
 
-        grad = dot(turned_ref[...], inner_grad_ref[...]).astype(BF16)
-        for k in range(owners):
-            out_ref[k] = grad[k * expand_rows : (k + 1) * expand_rows]
-
-    first = shrink_rows // expand_rows
-    moved = 2 * slots * (features + inner_width) + 2 * features * inner_width
-    return pl.pallas_call(
-        expand_kernel,
-        out_shape=shaped(grads.shape, BF16),
-        grid=(steps,),
-        in_specs=[
-            pl.BlockSpec(arrived.shape, lambda j: (0, 0)),
-            pl.BlockSpec((slots, features), lambda j: (0, j)),
-            ANYWHERE,
-        ],
-        out_specs=pl.BlockSpec((owners, expand_rows, features), lambda j: (0, first + j, 0)),
-        scratch_shapes=[pltpu.VMEM((features, slots), BF16)],
-        input_output_aliases={2: 0},
-        compiler_params=pltpu.CompilerParams(vmem_limit_bytes=LIMIT),
-        cost_estimate=cost(2 * slots * features * inner_width, moved, LIGHT),
-    )(arrived, inner_grad, grads)
+        out_ref[...] = dot(turned_ref[...], inner_grad_ref[...]).astype(BF16)
+
+    columns = lambda height: pl.BlockSpec((height, features), lambda j: (0, j))
+    [grad] = call(
+        kernel,
+        [shaped((features, inner_width), BF16)],
+        [arrived, inner_grad],
+        2 * slots * features * inner_width,
+        (inner_width // features,),
+        [pl.BlockSpec(arrived.shape, lambda j: (0, 0)), columns(slots)],
+        [columns(features)],
+        [pltpu.VMEM((features, slots), BF16)],
+        LIGHT,
+    )
+    return grad
 
 
 def mixer_after(stream, rows, facts, teacher, meta, normed, logits, returned, rows_grad, experts):
@@ -905,15 +936,9 @@
     mix = (jnp.arange(features, dtype=jnp.int32)[:, None] == row_order).astype(BF16)
     shrink_rows = feed_shrink.shape[0]
     inner_width = feed_expand.shape[1]
-    lower = gather_line(jnp.concatenate([lower_triple, lower_output, extra], axis=1))
-    expand_full = gather_line(after(feed_expand, lower))
-    shrink_full = gather_line(after(feed_shrink, lower))
-    upper = jnp.concatenate([upper_triple, upper_output], axis=1)
-    upper = gather_line(after(upper, expand_full, shrink_full))
-    early = [expand_full, shrink_full]
-    expert_in = lax.all_gather(after(expert_expand[0], *early), "dp", axis=0, tiled=True)
-    expert_out = lax.all_gather(after(expert_shrink[0], *early), "dp", axis=0, tiled=True)
-    lower = gather_cores(gather_sides(lower))
+    inner_width = feed_expand.shape[1]
+    lower_own = jnp.concatenate([lower_triple, lower_output, extra], axis=1)
+    upper_own = jnp.concatenate([upper_triple, upper_output], axis=1)
 
     position = jnp.arange(length, dtype=jnp.int32)
     earlier = (position[:, None] > position[None, :]).astype(BF16)
@@ -926,7 +951,40 @@
 
     stream_in = tokens.reshape(local, features)
     labels = teacher.reshape(local, features)
+    places = order(shrink_rows)
+    pieces = expert_expand[0].reshape(-1, inner_width // features, features)
+    experts_own = jnp.concatenate([expert_shrink[0], jnp.moveaxis(pieces, 1, 0).reshape(-1, features)])
+
+    shrink_line, shrink_over = gather_lines(feed_shrink)
+    wide_line, wide_over = gather_lines(jnp.concatenate([feed_expand, upper_own], axis=1))
+    lower = pull_line(lower_own)
+
+    lower, experts_own, mix, meta, target, places = at_once((lower, experts_own, mix, meta, target, places))
+    experts_full = lax.all_gather(experts_own, "dp")
+    lower = jnp.stack([lower_own, *lower])
+    near = pull_near(lower)
+
+    lower, near, shrink_line, shrink_over = at_once((lower, near, shrink_line, shrink_over))
+    lower = pull_far(lower, near)
+    shrink_near = pull_near(shrink_line)
+
+    lower, shrink_line, shrink_near = at_once((lower, shrink_line, shrink_near))
+    lower_over = pull_over(lower[1])
+
+    lower, lower_over, wide_line, wide_over = at_once((lower, lower_over, wide_line, wide_over))
+    lower = in_order(*lower, lower_over)
+    shrink_full = pull_far(shrink_line, shrink_near, shrink_over)
+    expand_line, expand_over = wide_line[..., :inner_width], wide_over[..., :inner_width]
+    upper_line, upper_over = wide_line[..., inner_width:], wide_over[..., inner_width:]
+    expand_near = pull_near(expand_line)
     rows, stream_one, *stored_one = attend_forward(0, stream_in, None, lower, 0, mix, piece_start, length)
+
+    shrink_full, expand_line, expand_near, rows, stream_one = at_once(
+        (shrink_full, expand_line, expand_near, rows, stream_one)
+    )
+    shrink_full = in_order(*shrink_full, pull_over(shrink_full[1]))
+    expand_full = pull_far(expand_line, expand_near, expand_over)
+    upper_near = pull_near(upper_line)
     lane = jnp.arange(features, dtype=jnp.int32)
     sums = rows[LANE + experts : LANE + 2 * experts + 1]
     sums = jnp.sum(jnp.where(lane % share_rows < count, sums, 0.0), axis=1)
@@ -937,38 +995,40 @@
     facts = jnp.stack([share, jnp.full_like(share, loss_ratio), jnp.full_like(share, balance_scale)])
     facts = jnp.pad(facts, ((0, 5), (0, 0)))
 
-    expand_full, shrink_full = gather_sides(expand_full), gather_sides(shrink_full)
-    expand_full = gather_cores([after(p, stream_one) for p in expand_full])
-    shrink_full = gather_cores([after(p, stream_one) for p in shrink_full])
-    places = order(shrink_rows)
+    shrink_full, expand_full, upper_line, upper_near, stream_one, facts = at_once(
+        (shrink_full, expand_full, upper_line, upper_near, stream_one, facts)
+    )
+    expand_full = in_order(*expand_full, pull_over(expand_full[1]))
+
+    expand_full, upper_line, upper_near, stream_one = at_once((expand_full, upper_line, upper_near, stream_one))
+    upper = pull_far(upper_line, upper_near, upper_over)
+
     if shrink_rows % 16:
         whole = jnp.concatenate(shrink_full, axis=0).reshape(devices, shrink_rows, features)
         shrink_full = [jnp.zeros_like(whole).at[places // shrink_rows].set(whole).reshape(-1, features)]
         places = jnp.zeros((1,), jnp.int32)
     stream_two, *stored_two = feed_forward(stream_one, rows, expand_full, shrink_full, places, mix, depth)
-    upper = gather_sides(upper)
-    upper = gather_cores([after(p, stream_two) for p in upper])
+
+    upper, stream_two = at_once((upper, stream_two))
+    upper = in_order(*upper, pull_over(upper[1]))
     stream_three, *stored_three = attend_forward(4, stream_two, rows, upper, 0, mix, piece_start, length)
     normed, logits, ahead, back = mixer_before(
         stream_three, rows, facts, labels, meta, target, slots, experts
     )
     ahead = exchange(ahead)
     back = exchange([after(b, *ahead) for b in back])
-    result, arrived, inner = expert_forward(ahead, expert_in, expert_out, depth)
+    result, arrived, inner = expert_forward(ahead, experts_full, depth)
     returned = exchange(result)
-    rows_grad, landed, active, inner_grad = expert_backward(back, result, inner, expert_in, expert_out, depth)
+    rows_grad, inner_grad, expert_out_grad = expert_backward(back, result, inner, experts_full, depth)
+    returned, rows_grad, inner_grad, expert_out_grad = at_once((returned, rows_grad, inner_grad, expert_out_grad))
+    expert_out_grad = lax.psum_scatter(expert_out_grad, "dp", scatter_dimension=0, tiled=True)
     rows_grad = exchange(rows_grad)
-    owners = lax.axis_size("dp")
-    expert_grad = expert_grads(arrived, active, landed, inner_grad, owners)
-    rows_grad = [after(r, expert_grad) for r in rows_grad]
-    expert_grad = lax.psum_scatter(expert_grad, "dp", scatter_dimension=0, tiled=True)[0]
     states, grad_three, mixer_small, squared = mixer_after(
         stream_three, rows, facts, labels, meta, normed, logits, returned, rows_grad, experts
     )
     grad_two, *upper_grad, upper_small = attend_backward(
         4, stream_two, rows, upper, 0, mix, piece_start, length, stored_three, grad_three
     )
-    at_once = lax.optimization_barrier
     hops = total_hops()
 
     def hop_loss(value, first, last):
@@ -976,32 +1036,47 @@
             value = value + hop(value, target)
         return value
 
-    upper_part = scatter_cores(*upper_grad)
+    inner_grad = after(inner_grad, grad_two)
+    upper_mine, upper_other = upper_grad
+    upper_other = swap_cores(upper_other)
+    expert_in_grad = expert_expand_grad(arrived, inner_grad)
+
+    upper_mine, upper_other, expert_in_grad, grad_two = at_once((upper_mine, upper_other, expert_in_grad, grad_two))
+    expert_in_grad = lax.psum_scatter(expert_in_grad, "dp", scatter_dimension=0, tiled=True)
+    upper_part = sum_cores(upper_mine, upper_other)
 
     grad_two, *upper_part = at_once((grad_two, *upper_part))
     upper_part = scatter_far(upper_part)
     squared = hop_loss(squared, 0, 1)
-    grad_one, expand_grad, shrink_grad, feed_small = feed_backward(
-        stream_one, rows, expand_full, shrink_full, places, mix, depth, stored_two, grad_two
-    )
+    feed_normed, inner_pre = stored_two
+    inner_grad, shrink_grad = feed_backward_shrink(shrink_full, places, depth, inner_pre, grad_two)
     if shrink_rows % 16:
         blocks = order(shrink_rows) // shrink_rows
         pick = (blocks[:, None] == jnp.arange(devices, dtype=jnp.int32)).astype(BF16)
         shrink_grad = dot(pick, shrink_grad[0].reshape(devices, -1)).astype(BF16).reshape(2, -1, features)
         shrink_grad = [shrink_grad[0], shrink_grad[1]]
 
-    upper_part, squared, grad_one, expand_grad, shrink_grad = at_once(
-        (upper_part, squared, grad_one, expand_grad, shrink_grad)
-    )
+    upper_part, squared, inner_grad, shrink_grad = at_once((upper_part, squared, inner_grad, shrink_grad))
     upper_part = scatter_near(upper_part)
     squared = hop_loss(squared, 1, 2)
-    expand_part, shrink_part = scatter_cores(*expand_grad), scatter_cores(*shrink_grad)
-
-    upper_part, squared, expand_part, shrink_part, grad_one = at_once(
-        (upper_part, squared, expand_part, shrink_part, grad_one)
-    )
+    shrink_mine, shrink_other = shrink_grad
+    shrink_other = swap_cores(shrink_other)
+    grad_one, expand_grad, feed_small = feed_backward_expand(
+        stream_one, rows, expand_full, mix, depth, feed_normed, inner_grad, grad_two
+    )
+
+    upper_part, squared, shrink_mine, shrink_other, expand_grad, grad_one = at_once(
+        (upper_part, squared, shrink_mine, shrink_other, expand_grad, grad_one)
+    )
+    shrink_part = scatter_far(sum_cores(shrink_mine, shrink_other))
+    expand_part = scatter_cores(*expand_grad)
+
+    upper_part, expand_part, shrink_part, grad_one, squared = at_once(
+        (upper_part, expand_part, shrink_part, grad_one, squared)
+    )
+    expand_part = scatter_far(expand_part)
+    shrink_part = scatter_near(shrink_part)
     upper_part = scatter_line(upper_part)
-    expand_part, shrink_part = scatter_far(expand_part), scatter_far(shrink_part)
     grad_in, *lower_grad, _ = attend_backward(
         0, stream_in, rows, lower, 0, mix, piece_start, length, stored_one, grad_one, (mixer_small, upper_small, feed_small)
     )
@@ -1009,31 +1084,34 @@
     upper_part, expand_part, shrink_part, grad_in, lower_grad, squared = at_once(
         (upper_part, expand_part, shrink_part, grad_in, lower_grad, squared)
     )
-    upper_part = total(upper_part)
     lower_part = scatter_cores(*lower_grad)
-    expand_part, shrink_part = scatter_near(expand_part), scatter_near(shrink_part)
-    squared = hop_loss(squared, 2, 3)
-
-    lower_part, expand_part, shrink_part, squared = at_once((lower_part, expand_part, shrink_part, squared))
+    expand_part = scatter_near(expand_part)
+    shrink_part = scatter_line(shrink_part)
+
+    lower_part, expand_part, shrink_part, upper_part, squared = at_once(
+        (lower_part, expand_part, shrink_part, upper_part, squared)
+    )
     lower_part = scatter_far(lower_part)
     expand_part = scatter_line(expand_part)
+    upper_part = total(upper_part)
+    squared = hop_loss(squared, 2, 3)
+
+    lower_part, expand_part, shrink_part, upper_part, squared = at_once(
+        (lower_part, expand_part, shrink_part, upper_part, squared)
+    )
+    lower_part = scatter_near(lower_part)
     squared = hop_loss(squared, 3, 4)
-
-    lower_part, expand_part, shrink_part, squared = at_once((lower_part, expand_part, shrink_part, squared))
-    expand_part = total(expand_part)
-    lower_part = scatter_near(lower_part)
-    shrink_part = scatter_line(shrink_part)
+    shrink_part = total(shrink_part)
+    expert_out_grad, expert_in_grad = expert_out_grad.astype(F32), expert_in_grad.astype(F32)
+
+    lower_part, expand_part, shrink_part, upper_part, squared, expert_in_grad, expert_out_grad = at_once(
+        (lower_part, expand_part, shrink_part, upper_part, squared, expert_in_grad, expert_out_grad)
+    )
     squared = hop_loss(squared, 4, None)
-
-    lower_part, shrink_part, squared = at_once((lower_part, shrink_part, squared))
-    lower_part, shrink_part = total(scatter_line(lower_part)), total(shrink_part)
+    lower_part, expand_part = total(scatter_line(lower_part)), total(expand_part)
     if hops is None:
         squared = lax.psum(squared, AXES)
     small = lower_part[:, wide + features :]
-    owned = expert_shrink.shape[1]
-    expert_in_grad = expert_grad[owned:].reshape(-1, expert_expand.shape[1], features)
-    expert_in_grad = jnp.moveaxis(expert_in_grad, 0, 1).reshape(expert_expand.shape[1:])
-
     squared_total = squared[0, 0]
     mean_loss = loss_ratio * squared_total / (total_tokens * features)
     return (
@@ -1054,8 +1132,8 @@
         small[:, 6],
         small[:, 7],
         small[:, 8 : 8 + experts],
-        expert_in_grad.astype(F32)[None],
-        expert_grad[:owned].astype(F32)[None],
+        expert_in_grad[None],
+        expert_out_grad[None],
         mean_loss,
     )
 

time: 454 us -> 420 us (0.925)
  waiting for transfers between devices: 149 us -> 120 us
  Pallas kernels: 140 us -> 127 us
  other arithmetic: 27.5 us -> 39.6 us
  starting transfers between devices: 87.9 us -> 77.7 us
  local copies, waits for them, and re-layouts: 23.1 us -> 28.6 us
    ppermute x81 -> x60, waiting for transfers between devices: 149 us -> 118 us  [hop(): return lax.ppermute(values, AXES, pairs(target))]
    pallas_call x2 -> x1, Pallas kernels: 25.5 us -> 11.9 us  [feed_backward_shrink(): pl.pallas_call(kernel, out_shape=outs, grid_spec=pltpu.PrefetchScalarGrid...]
    ppermute x81 -> x60, starting transfers between devices: 87.7 us -> 77.4 us  [hop(): return lax.ppermute(values, AXES, pairs(target))]
    concatenate x1 -> x4, other arithmetic: 0.01 us -> 5.2 us  [the longest x2 2.3 us: gather_lines(): jnp.concatenate([at(k, core) for k in range(depth)])]
    pallas_call x10 -> x11, Pallas kernels: 115 us -> 115 us  [call(): pl.pallas_call(kernel, out_shape=outs, grid=grid, in_specs=in_specs or [W...]
  transfers between devices with their start and end apart: 84 -> 65, of which waited for: 31 -> 29; matrix products, arithmetic and copies ran while one was open for 7% -> 14% of each run, Pallas kernels for 23% -> 31%
where the time goes in v3:
time: 420 us; the launch traced here: 412 us
  Pallas kernels  127 us (30%)
  waiting for transfers between devices  120 us (29%)
  starting transfers between devices  77.7 us (18%)
  other arithmetic  39.6 us (9%)
  local copies, waits for them, and re-layouts  28.6 us (7%)
  between operations  18.3 us (4%)
    ppermute x60, waiting for transfers between devices, hop(): return lax.ppermute(values, AXES, pairs(target))  118 us
    pallas_call x11, Pallas kernels, call(): pl.pallas_call(kernel, out_shape=outs, grid=grid, in_specs=in_specs or [W...  115 us
    ppermute x60, starting transfers between devices, hop(): return lax.ppermute(values, AXES, pairs(target))  77.4 us
    convert_element_type x12, other arithmetic, add(): return (first.astype(F32) + second.astype(F32)).astype(BF16)  16.5 us
    pallas_call x1, Pallas kernels, feed_backward_shrink(): pl.pallas_call(kernel, out_shape=outs, grid_spec=pltpu.PrefetchScalarGrid...  11.9 us
  transfers between devices with their start and end apart: 65, of which 29 were waited for; matrix products, arithmetic and copies ran while one was open for 14% of the time, Pallas kernels for 31%

profile of v3, /device:TPU:0, one launch (start us, length us, event | category | flops | bytes accessed | tf_op | source)
XLA Modules:
  0.0 412.1 jit_solution(13988234650685518117)
XLA Ops:
  19.2 4.1 collective-permute-start.1
  24.9 2.2 collective-permute-start.2
  32.8 9.2 %collective-permute-done.1 = bf16[24,3200]{1,0:T(8,128)(2,1)S(1)} collective-permute-done((bf16[24,3200]{1,0:T(8,128)(2,1)S(1)}, bf16[24,3200]{1,0:T(8,128)(2,1)S(1)}, u32[]{:S(2)}, u32[]{:S(2)}) %collective-permute-start.1) | collective-permute-done | bytes 153632 | tf_op jit(solution)/shard_map/ppermute | solution.py:35
  48.1 4.4 %collective-permute-done.3 = bf16[4,24,3200]{2,1,0:T(8,128)(2,1)S(1)} collective-permute-done((bf16[4,24,3200]{2,1,0:T(8,128)(2,1)S(1)}, bf16[4,24,3200]{2,1,0:T(8,128)(2,1)S(1)}, u32[]{:S(2)}, u32[]{:S(2)}) %collective-permute-start.3) | collective-permute-done | bytes 614432 | tf_op jit(solution)/shard_map/ppermute | solution.py:35
  56.0 14.9 %collective-permute-done.6 = bf16[4,96,768]{2,1,0:T(8,128)(2,1)} collective-permute-done((bf16[4,96,768]{2,1,0:T(8,128)(2,1)S(1)}, bf16[4,96,768]{2,1,0:T(8,128)(2,1)}, u32[]{:S(2)}, u32[]{:S(2)}) %collective-permute-start.6) | collective-permute-done | bytes 589856 | tf_op jit(solution)/shard_map/ppermute | solution.py:35
  70.9 5.0 %collective-permute-done.4 = bf16[2,4,24,3200]{3,2,1,0:T(8,128)(2,1)} collective-permute-done((bf16[2,4,24,3200]{3,2,1,0:T(8,128)(2,1)S(1)}, bf16[2,4,24,3200]{3,2,1,0:T(8,128)(2,1)}, u32[]{:S(2)}, u32[]{:S(2)}) %collective-permute-start.4) | collective-permute-done | bytes 1228832 | tf_op jit(solution)/shard_map/ppermute | solution.py:35
  85.6 9.9 %shard_map.365 = (f32[128,768]{1,0:T(8,128)}, f32[256,768]{1,0:T(8,128)}, bf16[256,768]{1,0:T(8,128)(2,1)}, bf16[256,2304]{1,0:T(8,128)(2,1)}, bf16[256,768]{1,0:T(8,128)(2,1)}) custom-call(s32[2]{0:T(128)} %refs_0_.7, bf16[256,768]{1,0:T(8,128)(2,1)} %bitcast.202, bf16[768,768]{1,0:T(8,128)(2,1)} %fusion.refs_2_.refs_11_.refs_6_.refs_5_, ...), custom_call_target="tpu_custom_call" | custom-call | flops 1509949 | bytes 9633 | tf_op jit(solution)/shard_map/pallas_call | solution.py:197
  95.5 4.7 %collective-permute-done.7 = bf16[2,4,96,768]{3,2,1,0:T(8,128)(2,1)} collective-permute-done((bf16[2,4,96,768]{3,2,1,0:T(8,128)(2,1)S(1)}, bf16[2,4,96,768]{3,2,1,0:T(8,128)(2,1)}, u32[]{:S(2)}, u32[]{:S(2)}) %collective-permute-start.7) | collective-permute-done | bytes 1179680 | tf_op jit(solution)/shard_map/ppermute | solution.py:35
  101.6 2.5 collective-permute-start.12
  110.2 8.4 %collective-permute-done.12 = bf16[2,4,24,3072]{3,2,1,0:T(8,128)(2,1)S(1)} collective-permute-done((bf16[2,4,24,3072]{3,2,1,0:T(8,128)(2,1)S(1)}, bf16[2,4,24,3072]{3,2,1,0:T(8,128)(2,1)S(1)}, u32[]{:S(2)}, u32[]{:S(2)}) %collective-permute-start.12) | collective-permute-done | bytes 1179680 | tf_op jit(solution)/shard_map/ppermute | solution.py:35
  118.8 2.8 collective-permute-done.15
  125.8 11.5 %shard_map.366 = (f32[256,768]{1,0:T(8,128)}, bf16[256,768]{1,0:T(8,128)(2,1)}, f32[256,3072]{1,0:T(8,128)}) custom-call(s32[32]{0:T(128)} %get-tuple-element.254.refs_0_.places_ref, bf16[192,3072]{1,0:T(8,128)(2,1)} %bitcast.166, bf16[192,3072]{1,0:T(8,128)(2,1)} %bitcast.180, bf16[96,3072]{1,0:T(8,128)(2,1)} %bitcast.172, ...), custom_call_target="tpu_custom_call" | custom-call | flops 2415919 | bytes 16121 | tf_op jit(solution)/shard_map/pallas_call | solution.py:197
  137.3 3.1 collective-permute-done.16
  141.2 2.3 collective-permute-done.18
  144.5 8.2 %shard_map.367 = (f32[256,768]{1,0:T(8,128)}, bf16[256,768]{1,0:T(8,128)(2,1)}, bf16[256,2304]{1,0:T(8,128)(2,1)}, bf16[256,768]{1,0:T(8,128)(2,1)}) custom-call(s32[2]{0:T(128)} %refs_0_.7, f32[256,768]{1,0:T(8,128)} %get-tuple-element.267.refs_1_.refs_7_, bf16[768,768]{1,0:T(8,128)(2,1)} %fusion.refs_2_.refs_11_.refs_6_.refs_5_, ...), custom_call_target="tpu_custom_call" | custom-call | flops 1509949 | bytes 9830 | tf_op jit(solution)/shard_map/pallas_call | solution.py:197
  152.7 3.6 shard_map.368
  159.8 4.5 %collective-permute-done.19.refs_1_ = bf16[128,768]{1,0:T(8,128)(2,1)S(1)} collective-permute-done((bf16[128,768]{1,0:T(8,128)(2,1)}, bf16[128,768]{1,0:T(8,128)(2,1)S(1)}, u32[]{:S(2)}, u32[]{:S(2)}) %collective-permute-start.19) | collective-permute-done | bytes 196640 | tf_op jit(solution)/shard_map/ppermute | solution.py:35
  164.3 3.9 collective-permute-done.20.refs_2_
  172.3 11.1 %shard_map.369 = (bf16[128,768]{1,0:T(8,128)(2,1)}, bf16[128,768]{1,0:T(8,128)(2,1)}, bf16[128,768]{1,0:T(8,128)(2,1)}, bf16[128,768]{1,0:T(8,128)(2,1)}, bf16[512,768]{1,0:T(8,128)(2,1)}, /*index=5*/f32[512,3072]{1,0:T(8,128)}) custom-call(bf16[128,768]{1,0:T(8,128)(2,1)} %get-tuple-element.278.refs_0_, bf16[128,768]{1,0:T(8,128)(2,1)} %copy-done.24, ...), custom_call_target="tpu_custom_call" | custom-call | flops 4831838208 | bytes 27525120 | tf_op jit(solution)/shard_map/pallas_call | solution.py:197
  187.7 15.4 %shard_map.370 = (bf16[128,768]{1,0:T(8,128)(2,1)}, bf16[128,768]{1,0:T(8,128)(2,1)}, bf16[128,768]{1,0:T(8,128)(2,1)}, bf16[128,768]{1,0:T(8,128)(2,1)}, bf16[5...) custom-call(bf16[128,896]{1,0:T(8,128)(2,1)} %get-tuple-element.288.refs_0_, bf16[128,896]{1,0:T(8,128)(2,1)} %copy-done.21, ...), custom_call_target="tpu_custom_call" | custom-call | flops 7247757 | bytes 35520 | tf_op jit(solution)/shard_map/pallas_call | solution.py:197
  207.8 3.4 collective-permute-done.28.refs_12_
  211.2 3.0 collective-permute-done.29.refs_13_
  215.0 5.6 %shard_map.371 = (bf16[256,768]{1,0:T(8,128)(2,1)}, f32[256,768]{1,0:T(8,128)}, f32[128,768]{1,0:T(8,128)}, f32[8,128]{1,0:T(8,128)}) custom-call(f32[256,768]{1,0:T(8,128)} %get-tuple-element.272.stream_ref.refs_0_, f32[128,768]{1,0:T(8,128)} %get-tuple-element.244.refs_13_.refs_8_.rows_ref.refs_1_.refs_7_, f32[8,128]{1,0:T(8,128)} %pad.19.facts_ref.refs_2_, ...), custom_call_target="tpu_custom_call" | custom-call | flops 402653184 | bytes 5254144 | tf_op jit(solution)/shard_map/pallas_call | solution.py:197
  220.6 15.4 %shard_map.372 = (f32[256,768]{1,0:T(8,128)}, bf16[384,3072]{1,0:T(8,128)(2,1)}, bf16[384,3072]{1,0:T(8,128)(2,1)}, f32[8,768]{1,0:T(8,128)}) custom-call(s32[2]{0:T(128)} %refs_0_.7, bf16[192,3072]{1,0:T(8,128)(2,1)} %bitcast.169, bf16[192,3072]{1,0:T(8,128)(2,1)} %bitcast.74.refs_4_.refs_2_, bf16[96,3072]{1,0:T(8,128)(2,1)} %bitcast.175, ...), custom_call_target="tpu_custom_call" | custom-call | flops 3321888 | bytes 15360 | tf_op jit(solution)/shard_map/pallas_call | solution.py:197
  236.1 7.0 %shard_map.373 = bf16[768,3072]{1,0:T(8,128)(2,1)} custom-call(bf16[512,768]{1,0:T(8,128)(2,1)} %get-tuple-element.317.arrived_ref, bf16[512,3072]{1,0:T(8,128)(2,1)} %get-tuple-element.320.inner_grad_ref), custom_call_target="tpu_custom_call" | custom-call | flops 2415919 | bytes 8650 | tf_op jit(solution)/shard_map/pallas_call | solution.py:197
  243.1 3.6 add_convert_fusion.6
  248.8 11.9 %shard_map.374 = (bf16[256,3072]{1,0:T(8,128)(2,1)}, bf16[4,4,96,768]{3,2,1,0:T(8,128)(2,1)}, bf16[4,4,96,768]{3,2,1,0:T(8,128)(2,1)}) custom-call(s32[32]{0:T(128)} %get-tuple-element.254.refs_0_.places_ref, bf16[768,768]{1,0:T(8,128)(2,1)} %bitcast.165, bf16[768,768]{1,0:T(8,128)(2,1)} %bitcast.58.refs_7_.refs_1_, bf16[384,768]{1,0:T(8,128)(2,1)} %bitcast.171, ...), custom_call_target="tpu_custom_call" | custom-call | flops 2415919 | bytes 14942 | tf_op jit(solution)/shard_map/pallas_call | solution.py:551
  260.7 2.3 collective-permute-done.32
  265.3 10.8 %shard_map.375 = (f32[256,768]{1,0:T(8,128)}, bf16[384,3072]{1,0:T(8,128)(2,1)}, bf16[384,3072]{1,0:T(8,128)(2,1)}, f32[8,768]{1,0:T(8,128)}) custom-call(bf16[192,3072]{1,0:T(8,128)(2,1)} %bitcast.167, bf16[192,3072]{1,0:T(8,128)(2,1)} %bitcast.181, bf16[96,3072]{1,0:T(8,128)(2,1)} %bitcast.173, bf16[96,3072]{1,0:T(8,128)(2,1)} %bitcast.69.refs_4_.refs_3_, ...), custom_call_target="tpu_custom_call" | custom-call | flops 2415919 | bytes 15360 | tf_op jit(solution)/shard_map/pallas_call | solution.py:197
  277.2 3.0 add_convert_fusion.2
  281.9 2.5 add_convert_fusion.4
  284.4 12.1 %collective-permute-done.38 = bf16[768,768]{1,0:T(8,128)(2,1)S(1)} collective-permute-done((bf16[768,768]{1,0:T(8,128)(2,1)S(1)}, bf16[768,768]{1,0:T(8,128)(2,1)S(1)}, u32[]{:S(2)}, u32[]{:S(2)}) %collective-permute-start.38) | collective-permute-done | bytes 1179680 | tf_op jit(solution)/shard_map/ppermute | solution.py:35
  300.4 4.3 %collective-permute-start.41 = (bf16[24,3072]{1,0:T(8,128)(2,1)}, bf16[24,3072]{1,0:T(8,128)(2,1)S(1)}, u32[]{:S(2)}, u32[]{:S(2)}) collective-permute-start(bf16[24,3072]{1,0:T(8,128)(2,1)} %get-tuple-element.539), channel_id=1, source_target_pairs={{0,8},{1,9},{2,10},{3,11},{4,12},{5,13},{6,14},{7,15},{8,16},{9,17... | collective-permute-start | bytes 442376 | tf_op jit(solution)/shard_map/ppermute | solution.py:35
  304.9 3.1 collective-permute-start.39
  308.1 16.9 %shard_map.376 = (f32[256,768]{1,0:T(8,128)}, bf16[384,3200]{1,0:T(8,128)(2,1)}, bf16[384,3200]{1,0:T(8,128)(2,1)}, f32[8,768]{1,0:T(8,128)}) custom-call(s32[2]{0:T(128)} %refs_0_.7, bf16[192,3200]{1,0:T(8,128)(2,1)} %bitcast.163, bf16[192,3200]{1,0:T(8,128)(2,1)} %bitcast.54.refs_4_.refs_2_, bf16[192,3200]{1,0:T(8,128)(2,1)} %bitcast.177, ...), custom_call_target="tpu_custom_call" | custom-call | flops 3321888 | bytes 15802 | tf_op jit(solution)/shard_map/pallas_call | solution.py:197
  328.8 2.9 collective-permute-start.48
  331.7 2.3 collective-permute-start.47
  334.1 3.7 collective-permute-done.45
  341.3 8.5 %collective-permute-done.47 = bf16[96,768]{1,0:T(8,128)(2,1)S(1)} collective-permute-done((bf16[96,768]{1,0:T(8,128)(2,1)S(1)}, bf16[96,768]{1,0:T(8,128)(2,1)S(1)}, u32[]{:S(2)}, u32[]{:S(2)}) %collective-permute-start.47) | collective-permute-done | bytes 147488 | tf_op jit(solution)/shard_map/ppermute | solution.py:35
  353.2 5.1 %collective-permute-start.52 = (bf16[24,3072]{1,0:T(8,128)(2,1)S(1)}, bf16[24,3072]{1,0:T(8,128)(2,1)S(1)}, u32[]{:S(2)}, u32[]{:S(2)}) collective-permute-start(bf16[24,3072]{1,0:T(8,128)(2,1)S(1)} %get-tuple-element.531), channel_id=1, source_target_pairs={{0,8},{1,9},{2,10},{3,11},{4,12},{5,13},{6,14},{7,15},{8,16},{9,17... | collective-permute-start | bytes 442376 | tf_op jit(solution)/shard_map/ppermute | solution.py:35
  360.9 2.3 collective-permute-done.52
  363.2 5.6 %collective-permute-done.51 = bf16[24,3072]{1,0:T(8,128)(2,1)S(1)} collective-permute-done((bf16[24,3072]{1,0:T(8,128)(2,1)S(1)}, bf16[24,3072]{1,0:T(8,128)(2,1)S(1)}, u32[]{:S(2)}, u32[]{:S(2)}) %collective-permute-start.51) | collective-permute-done | bytes 147488 | tf_op jit(solution)/shard_map/ppermute | solution.py:35
  370.6 2.2 convert_element_type.358
  372.7 2.2 convert_element_type.357
  375.0 4.5 %collective-permute-start.55 = (f32[8,128]{1,0:T(8,128)S(1)}, f32[8,128]{1,0:T(8,128)S(1)}, u32[]{:S(2)}, u32[]{:S(2)}) collective-permute-start(f32[8,128]{1,0:T(8,128)S(1)} %add.429), channel_id=1, source_target_pairs={{0,8},{1,9},{2,10},{3,11},{4,12},{5,13},{6,14},{7,15},{8,0},{9,1},... | collective-permute-start | bytes 12296 | tf_op jit(solution)/shard_map/ppermute | solution.py:35
  384.6 3.4 collective-permute-start.56
  393.4 2.8 collective-permute-done.58
  396.2 4.8 %collective-permute-done.57 = bf16[24,3200]{1,0:T(8,128)(2,1)S(1)} collective-permute-done((bf16[24,3200]{1,0:T(8,128)(2,1)S(1)}, bf16[24,3200]{1,0:T(8,128)(2,1)S(1)}, u32[]{:S(2)}, u32[]{:S(2)}) %collective-permute-start.57) | collective-permute-done | bytes 153632 | tf_op jit(solution)/shard_map/ppermute | solution.py:35
  (312 shorter events, 106.7 us)
Async XLA Ops:
  7.2 38.5 %all-gather.5.cloned.1.call-start = ((), (), s32[]{:S(2)}) async-start(), calls=%async_computation.2 | async-start | bytes 1327104 | tf_op jit(solution)/shard_map/all_gather | solution.py:68
  8.0 71.0 %all-gather.7.cloned.1.call-start = ((), (), s32[]{:S(2)}) async-start(), calls=%async_computation.3 | async-start | bytes 2654208 | tf_op jit(solution)/shard_map/all_gather | solution.py:68
  9.8 162.6 %all-gather.9.cloned.1.call-start = ((), (), s32[]{:S(2)}) async-start(), calls=%async_computation.6 | async-start | bytes 10616832 | tf_op jit(solution)/shard_map/all_gather | solution.py:963
  19.2 22.9 %collective-permute-start.1 = (bf16[24,3200]{1,0:T(8,128)(2,1)S(1)}, bf16[24,3200]{1,0:T(8,128)(2,1)S(1)}, u32[]{:S(2)}, u32[]{:S(2)}) collective-permute-start(bf16[24,3200]{1,0:T(8,128)(2,1)S(1)} %get-tuple-element.544), channel_id=1, source_target_pairs={{0,16},{1,17},{2,18},{3,19},{4,20},{5,21},{6,22},{7,23},{8,24},{9,... | collective-permute-start | bytes 460808 | tf_op jit(solution)/shard_map/ppermute | solution.py:35
  23.3 18.8 %collective-permute-start = (bf16[24,3200]{1,0:T(8,128)(2,1)S(1)}, bf16[24,3200]{1,0:T(8,128)(2,1)S(1)}, u32[]{:S(2)}, u32[]{:S(2)}) collective-permute-start(bf16[24,3200]{1,0:T(8,128)(2,1)S(1)} %get-tuple-element.544), channel_id=1, source_target_pairs={{0,8},{1,9},{2,10},{3,11},{4,12},{5,13},{6,14},{7,15},{8,16},{9,17... | collective-permute-start | bytes 460808 | tf_op jit(solution)/shard_map/ppermute | solution.py:35
  24.9 17.2 %collective-permute-start.2 = (bf16[24,3200]{1,0:T(8,128)(2,1)S(1)}, bf16[24,3200]{1,0:T(8,128)(2,1)S(1)}, u32[]{:S(2)}, u32[]{:S(2)}) collective-permute-start(bf16[24,3200]{1,0:T(8,128)(2,1)S(1)} %get-tuple-element.544), channel_id=1, source_target_pairs={{0,24},{1,25},{2,26},{3,27},{4,28},{5,29},{6,30},{7,31},{8,0},{9,1... | collective-permute-start | bytes 460808 | tf_op jit(solution)/shard_map/ppermute | solution.py:35
  42.1 328.4 %reduce-scatter.5.cloned.1.call-start = ((), (), s32[]{:S(2)}) async-start(), calls=%async_computation.5 | async-start | bytes 5308416 | tf_op jit(solution)/shard_map/reduce_scatter | solution.py:1024
  42.3 10.2 %collective-permute-start.3 = (bf16[4,24,3200]{2,1,0:T(8,128)(2,1)S(1)}, bf16[4,24,3200]{2,1,0:T(8,128)(2,1)S(1)}, u32[]{:S(2)}, u32[]{:S(2)}) collective-permute-start(bf16[4,24,3200]{2,1,0:T(8,128)(2,1)S(1)} %pad_maximum_fusion.7), channel_id=1, source_target_pairs={{0,1},{1,0},{2,3},{3,2},{4,6},{5,7},{6,4},{7,5},{8,9},{9,8},{10,11... | collective-permute-start | bytes 1843208 | tf_op jit(solution)/shard_map/ppermute | solution.py:35
  52.6 18.2 %collective-permute-start.5 = (bf16[2,4,24,3200]{3,2,1,0:T(8,128)(2,1)S(1)}, bf16[2,4,24,3200]{3,2,1,0:T(8,128)(2,1)S(1)}, u32[]{:S(2)}, u32[]{:S(2)}) collective-permute-start(bf16[2,4,24,3200]{3,2,1,0:T(8,128)(2,1)S(1)} %pad_maximum_fusion), channel_id=1, source_target_pairs={{0,4},{1,5},{2,6},{3,7},{4,0},{5,1},{6,2},{7,3},{8,12},{9,13},{10,... | collective-permute-start | bytes 3686408 | tf_op jit(solution)/shard_map/ppermute | solution.py:35
  52.7 23.2 %collective-permute-start.4 = (bf16[2,4,24,3200]{3,2,1,0:T(8,128)(2,1)S(1)}, bf16[2,4,24,3200]{3,2,1,0:T(8,128)(2,1)}, u32[]{:S(2)}, u32[]{:S(2)}) collective-permute-start(bf16[2,4,24,3200]{3,2,1,0:T(8,128)(2,1)S(1)} %pad_maximum_fusion), channel_id=1, source_target_pairs={{0,2},{1,3},{2,0},{3,1},{4,5},{5,4},{6,7},{7,6},{8,10},{9,11},{10,... | collective-permute-start | bytes 3686408 | tf_op jit(solution)/shard_map/ppermute | solution.py:35
  54.5 16.4 %collective-permute-start.6 = (bf16[4,96,768]{2,1,0:T(8,128)(2,1)S(1)}, bf16[4,96,768]{2,1,0:T(8,128)(2,1)}, u32[]{:S(2)}, u32[]{:S(2)}) collective-permute-start(bf16[4,96,768]{2,1,0:T(8,128)(2,1)S(1)} %get-tuple-element.222), channel_id=1, source_target_pairs={{0,1},{1,0},{2,3},{3,2},{4,6},{5,7},{6,4},{7,5},{8,9},{9,8},{10,11... | collective-permute-start | bytes 1769480 | tf_op jit(solution)/shard_map/ppermute | solution.py:35
  75.9 19.5 %collective-permute-start.8 = (bf16[4,96,768]{2,1,0:T(8,128)(2,1)}, bf16[4,96,768]{2,1,0:T(8,128)(2,1)S(1)}, u32[]{:S(2)}, u32[]{:S(2)}) collective-permute-start(bf16[4,96,768]{2,1,0:T(8,128)(2,1)} %collective-permute-done.6), channel_id=1, source_target_pairs={{0,4},{1,5},{2,6},{3,7},{4,0},{5,1},{6,2},{7,3},{8,12},{9,13},{10,... | collective-permute-start | bytes 1769480 | tf_op jit(solution)/shard_map/ppermute | solution.py:35
  77.1 23.0 %collective-permute-start.7 = (bf16[2,4,96,768]{3,2,1,0:T(8,128)(2,1)S(1)}, bf16[2,4,96,768]{3,2,1,0:T(8,128)(2,1)}, u32[]{:S(2)}, u32[]{:S(2)}) collective-permute-start(bf16[2,4,96,768]{3,2,1,0:T(8,128)(2,1)S(1)} %pad_maximum_fusion.2), channel_id=1, source_target_pairs={{0,2},{1,3},{2,0},{3,1},{4,5},{5,4},{6,7},{7,6},{8,10},{9,11},{10,... | collective-permute-start | bytes 3538952 | tf_op jit(solution)/shard_map/ppermute | solution.py:35
  83.5 16.7 %collective-permute-start.10 = (bf16[4,24,3072]{2,1,0:T(8,128)(2,1)}, bf16[4,24,3072]{2,1,0:T(8,128)(2,1)}, u32[]{:S(2)}, u32[]{:S(2)}) collective-permute-start(bf16[4,24,3072]{2,1,0:T(8,128)(2,1)} %get-tuple-element.240), channel_id=1, source_target_pairs={{0,1},{1,0},{2,3},{3,2},{4,6},{5,7},{6,4},{7,5},{8,9},{9,8},{10,11... | collective-permute-start | bytes 1769480 | tf_op jit(solution)/shard_map/ppermute | solution.py:35
  84.7 25.6 %collective-permute-start.14 = (bf16[4,24,3072]{2,1,0:T(8,128)(2,1)}, bf16[4,24,3072]{2,1,0:T(8,128)(2,1)}, u32[]{:S(2)}, u32[]{:S(2)}) collective-permute-start(bf16[4,24,3072]{2,1,0:T(8,128)(2,1)} %get-tuple-element.252), channel_id=1, source_target_pairs={{0,1},{1,0},{2,3},{3,2},{4,6},{5,7},{6,4},{7,5},{8,9},{9,8},{10,11... | collective-permute-start | bytes 1769480 | tf_op jit(solution)/shard_map/ppermute | solution.py:35
  101.6 17.0 %collective-permute-start.12 = (bf16[2,4,24,3072]{3,2,1,0:T(8,128)(2,1)S(1)}, bf16[2,4,24,3072]{3,2,1,0:T(8,128)(2,1)S(1)}, u32[]{:S(2)}, u32[]{:S(2)}) collective-permute-start(bf16[2,4,24,3072]{3,2,1,0:T(8,128)(2,1)S(1)} %pad_maximum_fusion.5), channel_id=1, source_target_pairs={{0,2},{1,3},{2,0},{3,1},{4,5},{5,4},{6,7},{7,6},{8,10},{9,11},{10,... | collective-permute-start | bytes 3538952 | tf_op jit(solution)/shard_map/ppermute | solution.py:35
  104.2 14.5 %collective-permute-start.11 = (bf16[2,4,96,768]{3,2,1,0:T(8,128)(2,1)}, bf16[2,4,96,768]{3,2,1,0:T(8,128)(2,1)S(1)}, u32[]{:S(2)}, u32[]{:S(2)}) collective-permute-start(bf16[2,4,96,768]{3,2,1,0:T(8,128)(2,1)} %collective-permute-done.7), channel_id=1, source_target_pairs={{0,4},{1,5},{2,6},{3,7},{4,0},{5,1},{6,2},{7,3},{8,12},{9,13},{10,... | collective-permute-start | bytes 3538952 | tf_op jit(solution)/shard_map/ppermute | solution.py:35
  124.0 16.4 %collective-permute-start.16 = (bf16[2,4,24,3072]{3,2,1,0:T(8,128)(2,1)S(1)}, bf16[2,4,24,3072]{3,2,1,0:T(8,128)(2,1)}, u32[]{:S(2)}, u32[]{:S(2)}) collective-permute-start(bf16[2,4,24,3072]{3,2,1,0:T(8,128)(2,1)S(1)} %pad_maximum_fusion.6), channel_id=1, source_target_pairs={{0,2},{1,3},{2,0},{3,1},{4,5},{5,4},{6,7},{7,6},{8,10},{9,11},{10,... | collective-permute-start | bytes 3538952 | tf_op jit(solution)/shard_map/ppermute | solution.py:35
  125.8 11.5 %collective-permute-start.17 = (bf16[4,24,3072]{2,1,0:T(8,128)(2,1)}, bf16[4,24,3072]{2,1,0:T(8,128)(2,1)S(1)}, u32[]{:S(2)}, u32[]{:S(2)}) collective-permute-start(bf16[4,24,3072]{2,1,0:T(8,128)(2,1)} %collective-permute-done.14), channel_id=1, source_target_pairs={{0,4},{1,5},{2,6},{3,7},{4,0},{5,1},{6,2},{7,3},{8,12},{9,13},{10,... | collective-permute-start | bytes 1769480 | tf_op jit(solution)/shard_map/ppermute | solution.py:35
  157.8 10.5 %collective-permute-start.20 = (bf16[128,768]{1,0:T(8,128)(2,1)}, bf16[128,768]{1,0:T(8,128)(2,1)S(1)}, u32[]{:S(2)}, u32[]{:S(2)}) collective-permute-start(bf16[128,768]{1,0:T(8,128)(2,1)} %get-tuple-element.280), channel_id=1, source_target_pairs={{0,2},{1,3},{2,0},{3,1},{4,6},{5,7},{6,4},{7,5},{8,10},{9,11},{10,... | collective-permute-start | bytes 589832 | tf_op jit(solution)/shard_map/ppermute | solution.py:35
  168.8 17.0 %collective-permute-start.25 = (bf16[128,896]{1,0:T(8,128)(2,1)}, bf16[128,896]{1,0:T(8,128)(2,1)S(1)}, u32[]{:S(2)}, u32[]{:S(2)}) collective-permute-start(bf16[128,896]{1,0:T(8,128)(2,1)} %get-tuple-element.290), channel_id=1, source_target_pairs={{0,1},{1,0},{2,3},{3,2},{4,5},{5,4},{6,7},{7,6},{8,9},{9,8},{10,11... | collective-permute-start | bytes 688136 | tf_op jit(solution)/shard_map/ppermute | solution.py:35
  170.3 16.7 %collective-permute-start.26 = (bf16[128,896]{1,0:T(8,128)(2,1)}, bf16[128,896]{1,0:T(8,128)(2,1)S(1)}, u32[]{:S(2)}, u32[]{:S(2)}) collective-permute-start(bf16[128,896]{1,0:T(8,128)(2,1)} %get-tuple-element.292), channel_id=1, source_target_pairs={{0,2},{1,3},{2,0},{3,1},{4,6},{5,7},{6,4},{7,5},{8,10},{9,11},{10,... | collective-permute-start | bytes 688136 | tf_op jit(solution)/shard_map/ppermute | solution.py:35
  171.2 15.8 %collective-permute-start.27 = (bf16[128,896]{1,0:T(8,128)(2,1)}, bf16[128,896]{1,0:T(8,128)(2,1)S(1)}, u32[]{:S(2)}, u32[]{:S(2)}) collective-permute-start(bf16[128,896]{1,0:T(8,128)(2,1)} %get-tuple-element.294), channel_id=1, source_target_pairs={{0,3},{1,2},{2,1},{3,0},{4,7},{5,6},{6,5},{7,4},{8,11},{9,10},{10,... | collective-permute-start | bytes 688136 | tf_op jit(solution)/shard_map/ppermute | solution.py:35
  183.5 19.7 %collective-permute-start.22 = (bf16[128,768]{1,0:T(8,128)(2,1)}, bf16[128,768]{1,0:T(8,128)(2,1)S(1)}, u32[]{:S(2)}, u32[]{:S(2)}) collective-permute-start(bf16[128,768]{1,0:T(8,128)(2,1)} %get-tuple-element.284.refs_5_), channel_id=1, source_target_pairs={{0,1},{1,0},{2,3},{3,2},{4,5},{5,4},{6,7},{7,6},{8,9},{9,8},{10,11... | collective-permute-start | bytes 589832 | tf_op jit(solution)/shard_map/ppermute | solution.py:35
  184.9 18.2 %collective-permute-start.23 = (bf16[128,768]{1,0:T(8,128)(2,1)}, bf16[128,768]{1,0:T(8,128)(2,1)S(1)}, u32[]{:S(2)}, u32[]{:S(2)}) collective-permute-start(bf16[128,768]{1,0:T(8,128)(2,1)} %get-tuple-element.285.refs_6_), channel_id=1, source_target_pairs={{0,2},{1,3},{2,0},{3,1},{4,6},{5,7},{6,4},{7,5},{8,10},{9,11},{10,... | collective-permute-start | bytes 589832 | tf_op jit(solution)/shard_map/ppermute | solution.py:35
  185.8 17.4 %collective-permute-start.24 = (bf16[128,768]{1,0:T(8,128)(2,1)}, bf16[128,768]{1,0:T(8,128)(2,1)S(1)}, u32[]{:S(2)}, u32[]{:S(2)}) collective-permute-start(bf16[128,768]{1,0:T(8,128)(2,1)} %get-tuple-element.286.refs_7_), channel_id=1, source_target_pairs={{0,3},{1,2},{2,1},{3,0},{4,7},{5,6},{6,5},{7,4},{8,11},{9,10},{10,... | collective-permute-start | bytes 589832 | tf_op jit(solution)/shard_map/ppermute | solution.py:35
  204.0 168.8 %reduce-scatter.3.cloned.1.call-start = ((), (), s32[]{:S(2)}) async-start(), calls=%async_computation.4 | async-start | bytes 5308416 | tf_op jit(solution)/shard_map/reduce_scatter | solution.py:1045
  246.7 16.4 %collective-permute-start.32 = (bf16[192,3072]{1,0:T(8,128)(2,1)}, bf16[192,3072]{1,0:T(8,128)(2,1)S(1)}, u32[]{:S(2)}, u32[]{:S(2)}) collective-permute-start(bf16[192,3072]{1,0:T(8,128)(2,1)} %get-tuple-element.325), channel_id=1, source_target_pairs={{0,2},{1,3},{2,0},{3,1},{4,5},{5,4},{6,7},{7,6},{8,10},{9,11},{10,... | collective-permute-start | bytes 3538952 | tf_op jit(solution)/shard_map/ppermute | solution.py:35
  263.1 13.8 %collective-permute-start.36 = (bf16[1536,768]{1,0:T(8,128)(2,1)}, bf16[1536,768]{1,0:T(8,128)(2,1)}, u32[]{:S(2)}, u32[]{:S(2)}) collective-permute-start(bf16[1536,768]{1,0:T(8,128)(2,1)} %bitcast.230), channel_id=1, source_target_pairs={{0,4},{1,5},{2,6},{3,7},{4,0},{5,1},{6,2},{7,3},{8,12},{9,13},{10,... | collective-permute-start | bytes 7077896 | tf_op jit(solution)/shard_map/ppermute | solution.py:35
  263.2 13.5 %collective-permute-start.34 = (bf16[96,3072]{1,0:T(8,128)(2,1)S(1)}, bf16[96,3072]{1,0:T(8,128)(2,1)S(1)}, u32[]{:S(2)}, u32[]{:S(2)}) collective-permute-start(bf16[96,3072]{1,0:T(8,128)(2,1)S(1)} %add_convert_fusion.18), channel_id=1, source_target_pairs={{0,1},{1,0},{2,3},{3,2},{4,6},{5,7},{6,4},{7,5},{8,9},{9,8},{10,11... | collective-permute-start | bytes 1769480 | tf_op jit(solution)/shard_map/ppermute | solution.py:35
  264.0 12.0 %collective-permute-start.35 = (f32[8,128]{1,0:T(8,128)S(1)}, f32[8,128]{1,0:T(8,128)S(1)}, u32[]{:S(2)}, u32[]{:S(2)}) collective-permute-start(f32[8,128]{1,0:T(8,128)S(1)} %add.409), channel_id=1, source_target_pairs={{0,1},{1,0},{2,3},{3,2},{4,5},{5,4},{6,7},{7,6},{8,9},{9,8},{10,11... | collective-permute-start | bytes 12296 | tf_op jit(solution)/shard_map/ppermute | solution.py:35
  280.2 16.3 %collective-permute-start.38 = (bf16[768,768]{1,0:T(8,128)(2,1)S(1)}, bf16[768,768]{1,0:T(8,128)(2,1)S(1)}, u32[]{:S(2)}, u32[]{:S(2)}) collective-permute-start(bf16[768,768]{1,0:T(8,128)(2,1)S(1)} %get-tuple-element.502), channel_id=1, source_target_pairs={{0,2},{1,3},{2,0},{3,1},{4,5},{5,4},{6,7},{7,6},{8,10},{9,11},{10,... | collective-permute-start | bytes 3538952 | tf_op jit(solution)/shard_map/ppermute | solution.py:35
  296.5 30.0 %collective-permute-start.42 = (bf16[192,3072]{1,0:T(8,128)(2,1)S(1)}, bf16[192,3072]{1,0:T(8,128)(2,1)}, u32[]{:S(2)}, u32[]{:S(2)}) collective-permute-start(bf16[192,3072]{1,0:T(8,128)(2,1)S(1)} %get-tuple-element.351), channel_id=1, source_target_pairs={{0,2},{1,3},{2,0},{3,1},{4,5},{5,4},{6,7},{7,6},{8,10},{9,11},{10,... | collective-permute-start | bytes 3538952 | tf_op jit(solution)/shard_map/ppermute | solution.py:35
  298.3 26.7 %collective-permute-start.43 = (bf16[384,768]{1,0:T(8,128)(2,1)}, bf16[384,768]{1,0:T(8,128)(2,1)}, u32[]{:S(2)}, u32[]{:S(2)}) collective-permute-start(bf16[384,768]{1,0:T(8,128)(2,1)} %add_convert_fusion.15), channel_id=1, source_target_pairs={{0,1},{1,0},{2,3},{3,2},{4,6},{5,7},{6,4},{7,5},{8,9},{9,8},{10,11... | collective-permute-start | bytes 1769480 | tf_op jit(solution)/shard_map/ppermute | solution.py:35
  300.4 26.1 %collective-permute-start.41 = (bf16[24,3072]{1,0:T(8,128)(2,1)}, bf16[24,3072]{1,0:T(8,128)(2,1)S(1)}, u32[]{:S(2)}, u32[]{:S(2)}) collective-permute-start(bf16[24,3072]{1,0:T(8,128)(2,1)} %get-tuple-element.539), channel_id=1, source_target_pairs={{0,8},{1,9},{2,10},{3,11},{4,12},{5,13},{6,14},{7,15},{8,16},{9,17... | collective-permute-start | bytes 442376 | tf_op jit(solution)/shard_map/ppermute | solution.py:35
  304.7 21.8 %collective-permute-start.40 = (bf16[24,3072]{1,0:T(8,128)(2,1)}, bf16[24,3072]{1,0:T(8,128)(2,1)S(1)}, u32[]{:S(2)}, u32[]{:S(2)}) collective-permute-start(bf16[24,3072]{1,0:T(8,128)(2,1)} %get-tuple-element.540), channel_id=1, source_target_pairs={{0,16},{1,17},{2,18},{3,19},{4,20},{5,21},{6,22},{7,23},{8,24},{9,... | collective-permute-start | bytes 442376 | tf_op jit(solution)/shard_map/ppermute | solution.py:35
  304.9 21.6 %collective-permute-start.39 = (bf16[24,3072]{1,0:T(8,128)(2,1)}, bf16[24,3072]{1,0:T(8,128)(2,1)S(1)}, u32[]{:S(2)}, u32[]{:S(2)}) collective-permute-start(bf16[24,3072]{1,0:T(8,128)(2,1)} %get-tuple-element.541), channel_id=1, source_target_pairs={{0,24},{1,25},{2,26},{3,27},{4,28},{5,29},{6,30},{7,31},{8,0},{9,1... | collective-permute-start | bytes 442376 | tf_op jit(solution)/shard_map/ppermute | solution.py:35
  326.5 12.6 %collective-permute-start.44 = (bf16[384,3200]{1,0:T(8,128)(2,1)}, bf16[384,3200]{1,0:T(8,128)(2,1)S(1)}, u32[]{:S(2)}, u32[]{:S(2)}) collective-permute-start(bf16[384,3200]{1,0:T(8,128)(2,1)} %get-tuple-element.367), channel_id=1, source_target_pairs={{0,4},{1,5},{2,6},{3,7},{4,0},{5,1},{6,2},{7,3},{8,12},{9,13},{10,... | collective-permute-start | bytes 7372808 | tf_op jit(solution)/shard_map/ppermute | solution.py:35
  327.9 9.9 %collective-permute-start.45 = (bf16[96,3072]{1,0:T(8,128)(2,1)S(1)}, bf16[96,3072]{1,0:T(8,128)(2,1)S(1)}, u32[]{:S(2)}, u32[]{:S(2)}) collective-permute-start(bf16[96,3072]{1,0:T(8,128)(2,1)S(1)} %add_convert_fusion.12), channel_id=1, source_target_pairs={{0,1},{1,0},{2,3},{3,2},{4,6},{5,7},{6,4},{7,5},{8,9},{9,8},{10,11... | collective-permute-start | bytes 1769480 | tf_op jit(solution)/shard_map/ppermute | solution.py:35
  328.8 12.5 %collective-permute-start.48 = (bf16[96,768]{1,0:T(8,128)(2,1)S(1)}, bf16[96,768]{1,0:T(8,128)(2,1)S(1)}, u32[]{:S(2)}, u32[]{:S(2)}) collective-permute-start(bf16[96,768]{1,0:T(8,128)(2,1)S(1)} %get-tuple-element.535), channel_id=1, source_target_pairs={{0,8},{1,9},{2,10},{3,11},{4,12},{5,13},{6,14},{7,15},{8,16},{9,17... | collective-permute-start | bytes 442376 | tf_op jit(solution)/shard_map/ppermute | solution.py:35
  331.7 18.1 %collective-permute-start.47 = (bf16[96,768]{1,0:T(8,128)(2,1)S(1)}, bf16[96,768]{1,0:T(8,128)(2,1)S(1)}, u32[]{:S(2)}, u32[]{:S(2)}) collective-permute-start(bf16[96,768]{1,0:T(8,128)(2,1)S(1)} %get-tuple-element.536), channel_id=1, source_target_pairs={{0,16},{1,17},{2,18},{3,19},{4,20},{5,21},{6,22},{7,23},{8,24},{9,... | collective-permute-start | bytes 442376 | tf_op jit(solution)/shard_map/ppermute | solution.py:35
  334.0 15.8 %collective-permute-start.46 = (bf16[96,768]{1,0:T(8,128)(2,1)S(1)}, bf16[96,768]{1,0:T(8,128)(2,1)S(1)}, u32[]{:S(2)}, u32[]{:S(2)}) collective-permute-start(bf16[96,768]{1,0:T(8,128)(2,1)S(1)} %get-tuple-element.537), channel_id=1, source_target_pairs={{0,24},{1,25},{2,26},{3,27},{4,28},{5,29},{6,30},{7,31},{8,0},{9,1... | collective-permute-start | bytes 442376 | tf_op jit(solution)/shard_map/ppermute | solution.py:35
  350.5 10.3 %collective-permute-start.53 = (f32[8,128]{1,0:T(8,128)S(1)}, f32[8,128]{1,0:T(8,128)S(1)}, u32[]{:S(2)}, u32[]{:S(2)}) collective-permute-start(f32[8,128]{1,0:T(8,128)S(1)} %copy-done.53), channel_id=1, source_target_pairs={{0,2},{1,3},{2,0},{3,1},{4,6},{5,7},{6,4},{7,5},{8,10},{9,11},{10,... | collective-permute-start | bytes 12296 | tf_op jit(solution)/shard_map/ppermute | solution.py:35
  351.8 16.9 %collective-permute-start.49 = (bf16[192,3200]{1,0:T(8,128)(2,1)S(1)}, bf16[192,3200]{1,0:T(8,128)(2,1)S(1)}, u32[]{:S(2)}, u32[]{:S(2)}) collective-permute-start(bf16[192,3200]{1,0:T(8,128)(2,1)S(1)} %get-tuple-element.377), channel_id=1, source_target_pairs={{0,2},{1,3},{2,0},{3,1},{4,5},{5,4},{6,7},{7,6},{8,10},{9,11},{10,... | collective-permute-start | bytes 3686408 | tf_op jit(solution)/shard_map/ppermute | solution.py:35
  353.2 9.9 %collective-permute-start.52 = (bf16[24,3072]{1,0:T(8,128)(2,1)S(1)}, bf16[24,3072]{1,0:T(8,128)(2,1)S(1)}, u32[]{:S(2)}, u32[]{:S(2)}) collective-permute-start(bf16[24,3072]{1,0:T(8,128)(2,1)S(1)} %get-tuple-element.531), channel_id=1, source_target_pairs={{0,8},{1,9},{2,10},{3,11},{4,12},{5,13},{6,14},{7,15},{8,16},{9,17... | collective-permute-start | bytes 442376 | tf_op jit(solution)/shard_map/ppermute | solution.py:35
  358.4 10.4 %collective-permute-start.51 = (bf16[24,3072]{1,0:T(8,128)(2,1)S(1)}, bf16[24,3072]{1,0:T(8,128)(2,1)S(1)}, u32[]{:S(2)}, u32[]{:S(2)}) collective-permute-start(bf16[24,3072]{1,0:T(8,128)(2,1)S(1)} %get-tuple-element.532), channel_id=1, source_target_pairs={{0,16},{1,17},{2,18},{3,19},{4,20},{5,21},{6,22},{7,23},{8,24},{9,... | collective-permute-start | bytes 442376 | tf_op jit(solution)/shard_map/ppermute | solution.py:35
  369.6 11.5 %collective-permute-start.54 = (bf16[96,3200]{1,0:T(8,128)(2,1)S(1)}, bf16[96,3200]{1,0:T(8,128)(2,1)}, u32[]{:S(2)}, u32[]{:S(2)}) collective-permute-start(bf16[96,3200]{1,0:T(8,128)(2,1)S(1)} %add_convert_fusion.9), channel_id=1, source_target_pairs={{0,1},{1,0},{2,3},{3,2},{4,6},{5,7},{6,4},{7,5},{8,9},{9,8},{10,11... | collective-permute-start | bytes 1843208 | tf_op jit(solution)/shard_map/ppermute | solution.py:35
  388.1 12.9 %collective-permute-start.57 = (bf16[24,3200]{1,0:T(8,128)(2,1)S(1)}, bf16[24,3200]{1,0:T(8,128)(2,1)S(1)}, u32[]{:S(2)}, u32[]{:S(2)}) collective-permute-start(bf16[24,3200]{1,0:T(8,128)(2,1)S(1)} %get-tuple-element.530), channel_id=1, source_target_pairs={{0,16},{1,17},{2,18},{3,19},{4,20},{5,21},{6,22},{7,23},{8,24},{9,... | collective-permute-start | bytes 460808 | tf_op jit(solution)/shard_map/ppermute | solution.py:35
  (77 other events, 508.2 us)
Sparse Core Ops, SparseCore 0:
  9.7 35.9 all-gather.4
  47.9 30.1 all-gather.6
  79.7 89.8 all-gather.8
  203.4 56.4 reduce-scatter.4
  277.3 73.1 reduce-scatter.2

commit v4 on v3

--- a/solution.py
+++ b/solution.py
@@ -169,6 +169,7 @@
 
 
 LIMIT = 60 * 1024 * 1024
+LANE = 8
 LIGHT = 1000
 
 
@@ -314,6 +315,40 @@
     scores = jnp.where(allowed, dot_nt(queries, keys) * HD ** (-0.5), -1e30)
     exponent = jnp.exp(scores - jnp.max(scores, axis=-1, keepdims=True))
     return exponent / jnp.sum(exponent, axis=-1, keepdims=True)
+
+
+def pack_lower(triple, output, vectors, router, route, valid):
+    share = triple.shape[0]
+    experts = router.shape[0]
+    wide, features = triple.shape[1], output.shape[1]
+
+    def kernel(triple_ref, output_ref, *refs):
+        vector_refs = refs[:LANE]
+        router_ref, route_ref, valid_ref, out_ref, turned_ref = refs[LANE:]
+        turned_ref[...] = jnp.zeros_like(turned_ref)
+        for k in range(LANE):
+            turned_ref[k : k + 1, :share] = vector_refs[k][...].astype(F32)
+        turned_ref[LANE : LANE + experts, :share] = router_ref[...].astype(F32)
+        valid = valid_ref[...].astype(F32)
+        route = route_ref[...]
+        lane = lax.broadcasted_iota(jnp.int32, (valid.shape[0], 128), 1) - LANE - experts
+        counts = jnp.where(lane == experts, jnp.sum(valid, axis=-1, keepdims=True), 0.0)
+        for e in range(experts):
+            count = jnp.sum(jnp.where(route == e, valid, 0.0), axis=-1, keepdims=True)
+            counts += jnp.where(lane == e, count, 0.0)
+        counts = jnp.concatenate([counts, jnp.zeros((share - counts.shape[0], 128), F32)], axis=0)
+        out_ref[:, :wide] = triple_ref[...]
+        out_ref[:, wide : wide + features] = output_ref[...]
+        out_ref[:, wide + features :] = (turned_ref[...].T[:share] + counts).astype(BF16)
+
+    [packed] = call(
+        kernel,
+        [shaped((share, wide + features + 128), BF16)],
+        [triple, output, *(v.reshape(1, share) for v in vectors), router, route, valid],
+        1,
+        scratch=[pltpu.VMEM((128, 128), F32)],
+    )
+    return packed
 
 
 def attend_forward(at, stream, rows, parts, first, mix, start, length):
@@ -630,9 +665,6 @@
         LIGHT,
     )
     return out, (mine, other), gains
-
-
-LANE = 8
 
 
 def gate_of(logits, meta):
@@ -922,12 +954,8 @@
     route = routes[..., 0]
     chosen = (route[..., None] == jnp.arange(experts, dtype=jnp.int32)).astype(F32)
 
-    counts = jnp.concatenate([jnp.sum(valid[..., None] * chosen, axis=1), jnp.sum(valid, axis=1)[:, None]], axis=1)
-    counts = jnp.pad(counts.astype(BF16), ((0, share_rows - count), (0, 0)))
     vectors = [lower_gain, lower_bias, feed_gain, feed_bias, upper_gain, upper_bias, mixer_gain, mixer_bias]
-    extra = jnp.concatenate([jnp.stack(vectors, axis=1), router, counts], axis=1)
-    extra_width = -(-extra.shape[1] // 128) * 128
-    extra = jnp.pad(extra, ((0, 0), (0, extra_width - extra.shape[1])))
+    extra_width = 128
 
     wide = 3 * features
     depth = lax.axis_size("dp") // 2
@@ -937,7 +965,7 @@
     shrink_rows = feed_shrink.shape[0]
     inner_width = feed_expand.shape[1]
     inner_width = feed_expand.shape[1]
-    lower_own = jnp.concatenate([lower_triple, lower_output, extra], axis=1)
+    lower_own = pack_lower(lower_triple, lower_output, vectors, router.T, route, valid_mask)
     upper_own = jnp.concatenate([upper_triple, upper_output], axis=1)
 
     position = jnp.arange(length, dtype=jnp.int32)
@@ -1070,6 +1098,7 @@
     )
     shrink_part = scatter_far(sum_cores(shrink_mine, shrink_other))
     expand_part = scatter_cores(*expand_grad)
+    squared = hop_loss(squared, 2, 3)
 
     upper_part, expand_part, shrink_part, grad_one, squared = at_once(
         (upper_part, expand_part, shrink_part, grad_one, squared)
@@ -1093,21 +1122,17 @@
     )
     lower_part = scatter_far(lower_part)
     expand_part = scatter_line(expand_part)
-    upper_part = total(upper_part)
-    squared = hop_loss(squared, 2, 3)
-
-    lower_part, expand_part, shrink_part, upper_part, squared = at_once(
-        (lower_part, expand_part, shrink_part, upper_part, squared)
-    )
-    lower_part = scatter_near(lower_part)
     squared = hop_loss(squared, 3, 4)
-    shrink_part = total(shrink_part)
+    upper_part, shrink_part = total(upper_part), total(shrink_part)
     expert_out_grad, expert_in_grad = expert_out_grad.astype(F32), expert_in_grad.astype(F32)
 
     lower_part, expand_part, shrink_part, upper_part, squared, expert_in_grad, expert_out_grad = at_once(
         (lower_part, expand_part, shrink_part, upper_part, squared, expert_in_grad, expert_out_grad)
     )
+    lower_part = scatter_near(lower_part)
     squared = hop_loss(squared, 4, None)
+
+    lower_part, expand_part, squared = at_once((lower_part, expand_part, squared))
     lower_part, expand_part = total(scatter_line(lower_part)), total(expand_part)
     if hops is None:
         squared = lax.psum(squared, AXES)

time: 420 us -> 408 us (0.971)
  starting transfers between devices: 77.7 us -> 62.9 us
  waiting for transfers between devices: 120 us -> 130 us
  local copies, waits for them, and re-layouts: 28.6 us -> 21.1 us
    ppermute x60, starting transfers between devices: 77.4 us -> 62.6 us  [hop(): return lax.ppermute(values, AXES, pairs(target))]
    another operation x8 -> x0, local copies, waits for them, and re-layouts: 5.97 us -> none  [body(): jnp.stack(vectors, axis=1)]
    all_gather x2, waiting for transfers between devices: 1.67 us -> 6.26 us  [gather_lines(): lax.all_gather(own, 'dp', axis=0, tiled=True).reshape(depth, 2, *own.shape)]
    pallas_call x11 -> x12, Pallas kernels: 115 us -> 118 us  [call(): pl.pallas_call(kernel, out_shape=outs, grid=grid, in_specs=in_specs or [W...]
  transfers between devices with their start and end apart: 65 -> 65, of which waited for: 29 -> 30; matrix products, arithmetic and copies ran while one was open for 14% -> 12% of each run, Pallas kernels for 31% -> 32%
where the time goes in v4:
time: 408 us; the launch traced here: 401 us
  waiting for transfers between devices  130 us (32%)
  Pallas kernels  129 us (32%)
  starting transfers between devices  62.9 us (15%)
  other arithmetic  39.3 us (10%)
  local copies, waits for them, and re-layouts  21.1 us (5%)
  between operations  18.1 us (4%)
    ppermute x60, waiting for transfers between devices, hop(): return lax.ppermute(values, AXES, pairs(target))  122 us
    pallas_call x12, Pallas kernels, call(): pl.pallas_call(kernel, out_shape=outs, grid=grid, in_specs=in_specs or [W...  118 us
    ppermute x60, starting transfers between devices, hop(): return lax.ppermute(values, AXES, pairs(target))  62.6 us
    convert_element_type x12, other arithmetic, add(): return (first.astype(F32) + second.astype(F32)).astype(BF16)  19.2 us
    pallas_call x1, Pallas kernels, feed_backward_shrink(): pl.pallas_call(kernel, out_shape=outs, grid_spec=pltpu.PrefetchScalarGrid...  11.8 us
    unnamed x81, local copies, waits for them, and re-layouts  8.36 us
  transfers between devices with their start and end apart: 65, of which 30 were waited for; matrix products, arithmetic and copies ran while one was open for 12% of the time, Pallas kernels for 32%

profile of v4, /device:TPU:0, one launch (start us, length us, event | category | flops | bytes accessed | tf_op | source)
XLA Modules:
  0.0 400.7 jit_solution(4139747217459746067)
XLA Ops:
  11.6 5.0 %collective-permute-start.2 = (bf16[24,3200]{1,0:T(8,128)(2,1)}, bf16[24,3200]{1,0:T(8,128)(2,1)S(1)}, u32[]{:S(2)}, u32[]{:S(2)}) collective-permute-start(bf16[24,3200]{1,0:T(8,128)(2,1)} %shard_map.365), channel_id=1, source_target_pairs={{0,24},{1,25},{2,26},{3,27},{4,28},{5,29},{6,30},{7,31},{8,0},{9,1... | collective-permute-start | bytes 460808 | tf_op jit(solution)/shard_map/ppermute | solution.py:35
  23.4 13.5 %collective-permute-done.1 = bf16[24,3200]{1,0:T(8,128)(2,1)S(1)} collective-permute-done((bf16[24,3200]{1,0:T(8,128)(2,1)}, bf16[24,3200]{1,0:T(8,128)(2,1)S(1)}, u32[]{:S(2)}, u32[]{:S(2)}) %collective-permute-start.1) | collective-permute-done | bytes 153632 | tf_op jit(solution)/shard_map/ppermute | solution.py:35
  38.6 3.4 all-gather.5.cloned.1.call-done
  44.4 2.9 collective-permute-done.3
  50.6 14.9 %collective-permute-done.6 = bf16[4,96,768]{2,1,0:T(8,128)(2,1)} collective-permute-done((bf16[4,96,768]{2,1,0:T(8,128)(2,1)S(1)}, bf16[4,96,768]{2,1,0:T(8,128)(2,1)}, u32[]{:S(2)}, u32[]{:S(2)}) %collective-permute-start.6) | collective-permute-done | bytes 589856 | tf_op jit(solution)/shard_map/ppermute | solution.py:35
  65.5 5.3 %collective-permute-done.4 = bf16[2,4,24,3200]{3,2,1,0:T(8,128)(2,1)} collective-permute-done((bf16[2,4,24,3200]{3,2,1,0:T(8,128)(2,1)S(1)}, bf16[2,4,24,3200]{3,2,1,0:T(8,128)(2,1)}, u32[]{:S(2)}, u32[]{:S(2)}) %collective-permute-start.4) | collective-permute-done | bytes 1228832 | tf_op jit(solution)/shard_map/ppermute | solution.py:35
  73.5 2.9 all-gather.7.cloned.1.call-done
  83.0 9.8 %shard_map.366 = (f32[128,768]{1,0:T(8,128)}, f32[256,768]{1,0:T(8,128)}, bf16[256,768]{1,0:T(8,128)(2,1)}, bf16[256,2304]{1,0:T(8,128)(2,1)}, bf16[256,768]{1,0:T(8,128)(2,1)}) custom-call(s32[2]{0:T(128)} %refs_0_.7, bf16[256,768]{1,0:T(8,128)(2,1)} %bitcast.199, bf16[768,768]{1,0:T(8,128)(2,1)} %fusion.refs_2_.refs_11_.refs_6_.refs_5_, ...), custom_call_target="tpu_custom_call" | custom-call | flops 1509949 | bytes 9633 | tf_op jit(solution)/shard_map/pallas_call | solution.py:198
  103.3 10.2 %collective-permute-done.12 = bf16[2,4,24,3072]{3,2,1,0:T(8,128)(2,1)S(1)} collective-permute-done((bf16[2,4,24,3072]{3,2,1,0:T(8,128)(2,1)S(1)}, bf16[2,4,24,3072]{3,2,1,0:T(8,128)(2,1)S(1)}, u32[]{:S(2)}, u32[]{:S(2)}) %collective-permute-start.12) | collective-permute-done | bytes 1179680 | tf_op jit(solution)/shard_map/ppermute | solution.py:35
  113.6 2.8 collective-permute-done.15
  120.4 11.6 %shard_map.367 = (f32[256,768]{1,0:T(8,128)}, bf16[256,768]{1,0:T(8,128)(2,1)}, f32[256,3072]{1,0:T(8,128)}) custom-call(s32[32]{0:T(128)} %get-tuple-element.249.refs_0_.places_ref, bf16[192,3072]{1,0:T(8,128)(2,1)} %bitcast.163, bf16[192,3072]{1,0:T(8,128)(2,1)} %bitcast.177, bf16[96,3072]{1,0:T(8,128)(2,1)} %bitcast.169, ...), custom_call_target="tpu_custom_call" | custom-call | flops 2415919 | bytes 16121 | tf_op jit(solution)/shard_map/pallas_call | solution.py:198
  132.0 3.2 collective-permute-done.16
  136.0 2.3 collective-permute-done.18
  139.3 8.2 %shard_map.368 = (f32[256,768]{1,0:T(8,128)}, bf16[256,768]{1,0:T(8,128)(2,1)}, bf16[256,2304]{1,0:T(8,128)(2,1)}, bf16[256,768]{1,0:T(8,128)(2,1)}) custom-call(s32[2]{0:T(128)} %refs_0_.7, f32[256,768]{1,0:T(8,128)} %get-tuple-element.262.refs_1_.refs_7_, bf16[768,768]{1,0:T(8,128)(2,1)} %fusion.refs_2_.refs_11_.refs_6_.refs_5_, ...), custom_call_target="tpu_custom_call" | custom-call | flops 1509949 | bytes 9830 | tf_op jit(solution)/shard_map/pallas_call | solution.py:198
  147.5 3.7 shard_map.369
  154.6 4.5 %collective-permute-done.19.refs_1_ = bf16[128,768]{1,0:T(8,128)(2,1)S(1)} collective-permute-done((bf16[128,768]{1,0:T(8,128)(2,1)}, bf16[128,768]{1,0:T(8,128)(2,1)S(1)}, u32[]{:S(2)}, u32[]{:S(2)}) %collective-permute-start.19) | collective-permute-done | bytes 196640 | tf_op jit(solution)/shard_map/ppermute | solution.py:35
  159.1 3.5 collective-permute-done.20.refs_2_
  167.6 11.2 %shard_map.370 = (bf16[128,768]{1,0:T(8,128)(2,1)}, bf16[128,768]{1,0:T(8,128)(2,1)}, bf16[128,768]{1,0:T(8,128)(2,1)}, bf16[128,768]{1,0:T(8,128)(2,1)}, bf16[512,768]{1,0:T(8,128)(2,1)}, /*index=5*/f32[512,3072]{1,0:T(8,128)}) custom-call(bf16[128,768]{1,0:T(8,128)(2,1)} %get-tuple-element.273.refs_0_, bf16[128,768]{1,0:T(8,128)(2,1)} %copy-done.25, ...), custom_call_target="tpu_custom_call" | custom-call | flops 4831838208 | bytes 27525120 | tf_op jit(solution)/shard_map/pallas_call | solution.py:198
  183.1 15.5 %shard_map.371 = (bf16[128,768]{1,0:T(8,128)(2,1)}, bf16[128,768]{1,0:T(8,128)(2,1)}, bf16[128,768]{1,0:T(8,128)(2,1)}, bf16[128,768]{1,0:T(8,128)(2,1)}, bf16[5...) custom-call(bf16[128,896]{1,0:T(8,128)(2,1)} %get-tuple-element.283.refs_0_, bf16[128,896]{1,0:T(8,128)(2,1)} %copy-done.22, ...), custom_call_target="tpu_custom_call" | custom-call | flops 7247757 | bytes 35520 | tf_op jit(solution)/shard_map/pallas_call | solution.py:198
  203.2 4.3 %collective-permute-done.28.refs_12_ = bf16[128,768]{1,0:T(8,128)(2,1)S(1)} collective-permute-done((bf16[128,768]{1,0:T(8,128)(2,1)S(1)}, bf16[128,768]{1,0:T(8,128)(2,1)S(1)}, u32[]{:S(2)}, u32[]{:S(2)}) %collective-permute-start.28) | collective-permute-done | bytes 196640 | tf_op jit(solution)/shard_map/ppermute | solution.py:35
  207.6 3.8 collective-permute-done.29.refs_13_
  212.2 5.6 %shard_map.372 = (bf16[256,768]{1,0:T(8,128)(2,1)}, f32[256,768]{1,0:T(8,128)}, f32[128,768]{1,0:T(8,128)}, f32[8,128]{1,0:T(8,128)}) custom-call(f32[256,768]{1,0:T(8,128)} %get-tuple-element.267.stream_ref.refs_0_, f32[128,768]{1,0:T(8,128)} %get-tuple-element.239.refs_13_.refs_8_.rows_ref.refs_1_.refs_7_, f32[8,128]{1,0:T(8,128)} %pad.9.facts_ref.refs_2_, ...), custom_call_target="tpu_custom_call" | custom-call | flops 402653184 | bytes 5254144 | tf_op jit(solution)/shard_map/pallas_call | solution.py:198
  217.8 15.3 %shard_map.373 = (f32[256,768]{1,0:T(8,128)}, bf16[384,3072]{1,0:T(8,128)(2,1)}, bf16[384,3072]{1,0:T(8,128)(2,1)}, f32[8,768]{1,0:T(8,128)}) custom-call(s32[2]{0:T(128)} %refs_0_.7, bf16[192,3072]{1,0:T(8,128)(2,1)} %bitcast.166, bf16[192,3072]{1,0:T(8,128)(2,1)} %bitcast.74.refs_4_.refs_2_, bf16[96,3072]{1,0:T(8,128)(2,1)} %bitcast.172, ...), custom_call_target="tpu_custom_call" | custom-call | flops 3321888 | bytes 15360 | tf_op jit(solution)/shard_map/pallas_call | solution.py:198
  233.2 7.0 %shard_map.374 = bf16[768,3072]{1,0:T(8,128)(2,1)} custom-call(bf16[512,768]{1,0:T(8,128)(2,1)} %get-tuple-element.312.arrived_ref, bf16[512,3072]{1,0:T(8,128)(2,1)} %get-tuple-element.315.inner_grad_ref), custom_call_target="tpu_custom_call" | custom-call | flops 2415919 | bytes 8650 | tf_op jit(solution)/shard_map/pallas_call | solution.py:198
  240.2 3.6 add_convert_fusion.6
  246.6 11.8 %shard_map.375 = (bf16[256,3072]{1,0:T(8,128)(2,1)}, bf16[4,4,96,768]{3,2,1,0:T(8,128)(2,1)}, bf16[4,4,96,768]{3,2,1,0:T(8,128)(2,1)}) custom-call(s32[32]{0:T(128)} %get-tuple-element.249.refs_0_.places_ref, bf16[768,768]{1,0:T(8,128)(2,1)} %bitcast.162, bf16[768,768]{1,0:T(8,128)(2,1)} %bitcast.58.refs_7_.refs_1_, bf16[384,768]{1,0:T(8,128)(2,1)} %bitcast.168, ...), custom_call_target="tpu_custom_call" | custom-call | flops 2415919 | bytes 14942 | tf_op jit(solution)/shard_map/pallas_call | solution.py:586
  261.3 2.2 add_convert_fusion.18
  265.4 10.9 %shard_map.376 = (f32[256,768]{1,0:T(8,128)}, bf16[384,3072]{1,0:T(8,128)(2,1)}, bf16[384,3072]{1,0:T(8,128)(2,1)}, f32[8,768]{1,0:T(8,128)}) custom-call(bf16[192,3072]{1,0:T(8,128)(2,1)} %bitcast.164, bf16[192,3072]{1,0:T(8,128)(2,1)} %bitcast.178, bf16[96,3072]{1,0:T(8,128)(2,1)} %bitcast.170, bf16[96,3072]{1,0:T(8,128)(2,1)} %bitcast.69.refs_4_.refs_3_, ...), custom_call_target="tpu_custom_call" | custom-call | flops 2415919 | bytes 15360 | tf_op jit(solution)/shard_map/pallas_call | solution.py:198
  279.4 2.4 add_convert_fusion.2
  283.9 14.3 %collective-permute-done.39 = f32[8,128]{1,0:T(8,128)S(1)} collective-permute-done((f32[8,128]{1,0:T(8,128)S(1)}, f32[8,128]{1,0:T(8,128)S(1)}, u32[]{:S(2)}, u32[]{:S(2)}) %collective-permute-start.39) | collective-permute-done | bytes 4128 | tf_op jit(solution)/shard_map/ppermute | solution.py:35
  298.1 1.9 add_convert_fusion.4
  302.9 2.3 collective-permute-start.41
  305.2 3.1 collective-permute-start.40
  308.3 17.0 %shard_map.377 = (f32[256,768]{1,0:T(8,128)}, bf16[384,3200]{1,0:T(8,128)(2,1)}, bf16[384,3200]{1,0:T(8,128)(2,1)}, f32[8,768]{1,0:T(8,128)}) custom-call(s32[2]{0:T(128)} %refs_0_.7, bf16[192,3200]{1,0:T(8,128)(2,1)} %bitcast.160, bf16[192,3200]{1,0:T(8,128)(2,1)} %bitcast.54.refs_4_.refs_2_, bf16[192,3200]{1,0:T(8,128)(2,1)} %bitcast.174, ...), custom_call_target="tpu_custom_call" | custom-call | flops 3321888 | bytes 15802 | tf_op jit(solution)/shard_map/pallas_call | solution.py:198
  329.1 2.2 convert_element_type.340
  332.2 3.0 collective-permute-start.47
  335.2 3.0 collective-permute-done.46
  339.7 2.2 convert_element_type.339
  341.9 3.0 add_convert_fusion
  345.4 3.0 collective-permute-start.54
  350.6 2.8 collective-permute-start.51
  354.3 3.9 collective-permute-done.53
  358.3 3.9 collective-permute-done.52
  362.2 3.0 collective-permute-done.50
  367.9 2.9 collective-permute-done.56
  370.8 4.7 %collective-permute-done.55 = bf16[96,3200]{1,0:T(8,128)(2,1)S(1)} collective-permute-done((bf16[96,3200]{1,0:T(8,128)(2,1)S(1)}, bf16[96,3200]{1,0:T(8,128)(2,1)S(1)}, u32[]{:S(2)}, u32[]{:S(2)}) %collective-permute-start.55) | collective-permute-done | bytes 614432 | tf_op jit(solution)/shard_map/ppermute | solution.py:35
  382.1 2.6 collective-permute-done.59
  384.7 4.9 %collective-permute-done.58 = bf16[24,3200]{1,0:T(8,128)(2,1)S(1)} collective-permute-done((bf16[24,3200]{1,0:T(8,128)(2,1)S(1)}, bf16[24,3200]{1,0:T(8,128)(2,1)S(1)}, u32[]{:S(2)}, u32[]{:S(2)}) %collective-permute-start.58) | collective-permute-done | bytes 153632 | tf_op jit(solution)/shard_map/ppermute | solution.py:35
  (257 shorter events, 97.8 us)
Async XLA Ops:
  7.2 34.8 %all-gather.5.cloned.1.call-start = ((), (), s32[]{:S(2)}) async-start(), calls=%async_computation.2 | async-start | bytes 1327104 | tf_op jit(solution)/shard_map/all_gather | solution.py:68
  8.0 68.4 %all-gather.7.cloned.1.call-start = ((), (), s32[]{:S(2)}) async-start(), calls=%async_computation.3 | async-start | bytes 2654208 | tf_op jit(solution)/shard_map/all_gather | solution.py:68
  9.8 157.8 %all-gather.9.cloned.1.call-start = ((), (), s32[]{:S(2)}) async-start(), calls=%async_computation.6 | async-start | bytes 10616832 | tf_op jit(solution)/shard_map/all_gather | solution.py:991
  11.6 11.7 %collective-permute-start.2 = (bf16[24,3200]{1,0:T(8,128)(2,1)}, bf16[24,3200]{1,0:T(8,128)(2,1)S(1)}, u32[]{:S(2)}, u32[]{:S(2)}) collective-permute-start(bf16[24,3200]{1,0:T(8,128)(2,1)} %shard_map.365), channel_id=1, source_target_pairs={{0,24},{1,25},{2,26},{3,27},{4,28},{5,29},{6,30},{7,31},{8,0},{9,1... | collective-permute-start | bytes 460808 | tf_op jit(solution)/shard_map/ppermute | solution.py:35
  16.7 20.2 %collective-permute-start.1 = (bf16[24,3200]{1,0:T(8,128)(2,1)}, bf16[24,3200]{1,0:T(8,128)(2,1)S(1)}, u32[]{:S(2)}, u32[]{:S(2)}) collective-permute-start(bf16[24,3200]{1,0:T(8,128)(2,1)} %shard_map.365), channel_id=1, source_target_pairs={{0,16},{1,17},{2,18},{3,19},{4,20},{5,21},{6,22},{7,23},{8,24},{9,... | collective-permute-start | bytes 460808 | tf_op jit(solution)/shard_map/ppermute | solution.py:35
  16.7 20.2 %collective-permute-start = (bf16[24,3200]{1,0:T(8,128)(2,1)}, bf16[24,3200]{1,0:T(8,128)(2,1)S(1)}, u32[]{:S(2)}, u32[]{:S(2)}) collective-permute-start(bf16[24,3200]{1,0:T(8,128)(2,1)} %shard_map.365), channel_id=1, source_target_pairs={{0,8},{1,9},{2,10},{3,11},{4,12},{5,13},{6,14},{7,15},{8,16},{9,17... | collective-permute-start | bytes 460808 | tf_op jit(solution)/shard_map/ppermute | solution.py:35
  36.9 292.2 %reduce-scatter.5.cloned.1.call-start = ((), (), s32[]{:S(2)}) async-start(), calls=%async_computation.5 | async-start | bytes 5308416 | tf_op jit(solution)/shard_map/reduce_scatter | solution.py:1052
  37.1 10.2 %collective-permute-start.3 = (bf16[4,24,3200]{2,1,0:T(8,128)(2,1)S(1)}, bf16[4,24,3200]{2,1,0:T(8,128)(2,1)S(1)}, u32[]{:S(2)}, u32[]{:S(2)}) collective-permute-start(bf16[4,24,3200]{2,1,0:T(8,128)(2,1)S(1)} %pad_maximum_fusion.7), channel_id=1, source_target_pairs={{0,1},{1,0},{2,3},{3,2},{4,6},{5,7},{6,4},{7,5},{8,9},{9,8},{10,11... | collective-permute-start | bytes 1843208 | tf_op jit(solution)/shard_map/ppermute | solution.py:35
  47.4 18.0 %collective-permute-start.5 = (bf16[2,4,24,3200]{3,2,1,0:T(8,128)(2,1)S(1)}, bf16[2,4,24,3200]{3,2,1,0:T(8,128)(2,1)S(1)}, u32[]{:S(2)}, u32[]{:S(2)}) collective-permute-start(bf16[2,4,24,3200]{3,2,1,0:T(8,128)(2,1)S(1)} %pad_maximum_fusion), channel_id=1, source_target_pairs={{0,4},{1,5},{2,6},{3,7},{4,0},{5,1},{6,2},{7,3},{8,12},{9,13},{10,... | collective-permute-start | bytes 3686408 | tf_op jit(solution)/shard_map/ppermute | solution.py:35
  47.5 23.2 %collective-permute-start.4 = (bf16[2,4,24,3200]{3,2,1,0:T(8,128)(2,1)S(1)}, bf16[2,4,24,3200]{3,2,1,0:T(8,128)(2,1)}, u32[]{:S(2)}, u32[]{:S(2)}) collective-permute-start(bf16[2,4,24,3200]{3,2,1,0:T(8,128)(2,1)S(1)} %pad_maximum_fusion), channel_id=1, source_target_pairs={{0,2},{1,3},{2,0},{3,1},{4,5},{5,4},{6,7},{7,6},{8,10},{9,11},{10,... | collective-permute-start | bytes 3686408 | tf_op jit(solution)/shard_map/ppermute | solution.py:35
  49.1 16.4 %collective-permute-start.6 = (bf16[4,96,768]{2,1,0:T(8,128)(2,1)S(1)}, bf16[4,96,768]{2,1,0:T(8,128)(2,1)}, u32[]{:S(2)}, u32[]{:S(2)}) collective-permute-start(bf16[4,96,768]{2,1,0:T(8,128)(2,1)S(1)} %get-tuple-element.217), channel_id=1, source_target_pairs={{0,1},{1,0},{2,3},{3,2},{4,6},{5,7},{6,4},{7,5},{8,9},{9,8},{10,11... | collective-permute-start | bytes 1769480 | tf_op jit(solution)/shard_map/ppermute | solution.py:35
  70.7 22.1 %collective-permute-start.8 = (bf16[4,96,768]{2,1,0:T(8,128)(2,1)}, bf16[4,96,768]{2,1,0:T(8,128)(2,1)S(1)}, u32[]{:S(2)}, u32[]{:S(2)}) collective-permute-start(bf16[4,96,768]{2,1,0:T(8,128)(2,1)} %collective-permute-done.6), channel_id=1, source_target_pairs={{0,4},{1,5},{2,6},{3,7},{4,0},{5,1},{6,2},{7,3},{8,12},{9,13},{10,... | collective-permute-start | bytes 1769480 | tf_op jit(solution)/shard_map/ppermute | solution.py:35
  71.9 20.9 %collective-permute-start.7 = (bf16[2,4,96,768]{3,2,1,0:T(8,128)(2,1)S(1)}, bf16[2,4,96,768]{3,2,1,0:T(8,128)(2,1)}, u32[]{:S(2)}, u32[]{:S(2)}) collective-permute-start(bf16[2,4,96,768]{3,2,1,0:T(8,128)(2,1)S(1)} %pad_maximum_fusion.2), channel_id=1, source_target_pairs={{0,2},{1,3},{2,0},{3,1},{4,5},{5,4},{6,7},{7,6},{8,10},{9,11},{10,... | collective-permute-start | bytes 3538952 | tf_op jit(solution)/shard_map/ppermute | solution.py:35
  80.9 13.3 %collective-permute-start.10 = (bf16[4,24,3072]{2,1,0:T(8,128)(2,1)}, bf16[4,24,3072]{2,1,0:T(8,128)(2,1)}, u32[]{:S(2)}, u32[]{:S(2)}) collective-permute-start(bf16[4,24,3072]{2,1,0:T(8,128)(2,1)} %get-tuple-element.235), channel_id=1, source_target_pairs={{0,1},{1,0},{2,3},{3,2},{4,6},{5,7},{6,4},{7,5},{8,9},{9,8},{10,11... | collective-permute-start | bytes 1769480 | tf_op jit(solution)/shard_map/ppermute | solution.py:35
  82.2 21.1 %collective-permute-start.14 = (bf16[4,24,3072]{2,1,0:T(8,128)(2,1)}, bf16[4,24,3072]{2,1,0:T(8,128)(2,1)}, u32[]{:S(2)}, u32[]{:S(2)}) collective-permute-start(bf16[4,24,3072]{2,1,0:T(8,128)(2,1)} %get-tuple-element.247), channel_id=1, source_target_pairs={{0,1},{1,0},{2,3},{3,2},{4,6},{5,7},{6,4},{7,5},{8,9},{9,8},{10,11... | collective-permute-start | bytes 1769480 | tf_op jit(solution)/shard_map/ppermute | solution.py:35
  95.6 17.8 %collective-permute-start.12 = (bf16[2,4,24,3072]{3,2,1,0:T(8,128)(2,1)S(1)}, bf16[2,4,24,3072]{3,2,1,0:T(8,128)(2,1)S(1)}, u32[]{:S(2)}, u32[]{:S(2)}) collective-permute-start(bf16[2,4,24,3072]{3,2,1,0:T(8,128)(2,1)S(1)} %pad_maximum_fusion.5), channel_id=1, source_target_pairs={{0,2},{1,3},{2,0},{3,1},{4,5},{5,4},{6,7},{7,6},{8,10},{9,11},{10,... | collective-permute-start | bytes 3538952 | tf_op jit(solution)/shard_map/ppermute | solution.py:35
  97.2 16.3 %collective-permute-start.11 = (bf16[2,4,96,768]{3,2,1,0:T(8,128)(2,1)}, bf16[2,4,96,768]{3,2,1,0:T(8,128)(2,1)S(1)}, u32[]{:S(2)}, u32[]{:S(2)}) collective-permute-start(bf16[2,4,96,768]{3,2,1,0:T(8,128)(2,1)} %collective-permute-done.7), channel_id=1, source_target_pairs={{0,4},{1,5},{2,6},{3,7},{4,0},{5,1},{6,2},{7,3},{8,12},{9,13},{10,... | collective-permute-start | bytes 3538952 | tf_op jit(solution)/shard_map/ppermute | solution.py:35
  118.8 16.4 %collective-permute-start.16 = (bf16[2,4,24,3072]{3,2,1,0:T(8,128)(2,1)S(1)}, bf16[2,4,24,3072]{3,2,1,0:T(8,128)(2,1)}, u32[]{:S(2)}, u32[]{:S(2)}) collective-permute-start(bf16[2,4,24,3072]{3,2,1,0:T(8,128)(2,1)S(1)} %pad_maximum_fusion.6), channel_id=1, source_target_pairs={{0,2},{1,3},{2,0},{3,1},{4,5},{5,4},{6,7},{7,6},{8,10},{9,11},{10,... | collective-permute-start | bytes 3538952 | tf_op jit(solution)/shard_map/ppermute | solution.py:35
  120.4 11.6 %collective-permute-start.17 = (bf16[4,24,3072]{2,1,0:T(8,128)(2,1)}, bf16[4,24,3072]{2,1,0:T(8,128)(2,1)S(1)}, u32[]{:S(2)}, u32[]{:S(2)}) collective-permute-start(bf16[4,24,3072]{2,1,0:T(8,128)(2,1)} %collective-permute-done.14), channel_id=1, source_target_pairs={{0,4},{1,5},{2,6},{3,7},{4,0},{5,1},{6,2},{7,3},{8,12},{9,13},{10,... | collective-permute-start | bytes 1769480 | tf_op jit(solution)/shard_map/ppermute | solution.py:35
  152.4 10.2 %collective-permute-start.20 = (bf16[128,768]{1,0:T(8,128)(2,1)}, bf16[128,768]{1,0:T(8,128)(2,1)S(1)}, u32[]{:S(2)}, u32[]{:S(2)}) collective-permute-start(bf16[128,768]{1,0:T(8,128)(2,1)} %get-tuple-element.275), channel_id=1, source_target_pairs={{0,2},{1,3},{2,0},{3,1},{4,6},{5,7},{6,4},{7,5},{8,10},{9,11},{10,... | collective-permute-start | bytes 589832 | tf_op jit(solution)/shard_map/ppermute | solution.py:35
  163.5 18.3 %collective-permute-start.25 = (bf16[128,896]{1,0:T(8,128)(2,1)}, bf16[128,896]{1,0:T(8,128)(2,1)S(1)}, u32[]{:S(2)}, u32[]{:S(2)}) collective-permute-start(bf16[128,896]{1,0:T(8,128)(2,1)} %get-tuple-element.285), channel_id=1, source_target_pairs={{0,1},{1,0},{2,3},{3,2},{4,5},{5,4},{6,7},{7,6},{8,9},{9,8},{10,11... | collective-permute-start | bytes 688136 | tf_op jit(solution)/shard_map/ppermute | solution.py:35
  164.7 17.6 %collective-permute-start.26 = (bf16[128,896]{1,0:T(8,128)(2,1)}, bf16[128,896]{1,0:T(8,128)(2,1)S(1)}, u32[]{:S(2)}, u32[]{:S(2)}) collective-permute-start(bf16[128,896]{1,0:T(8,128)(2,1)} %get-tuple-element.287), channel_id=1, source_target_pairs={{0,2},{1,3},{2,0},{3,1},{4,6},{5,7},{6,4},{7,5},{8,10},{9,11},{10,... | collective-permute-start | bytes 688136 | tf_op jit(solution)/shard_map/ppermute | solution.py:35
  165.8 16.5 %collective-permute-start.27 = (bf16[128,896]{1,0:T(8,128)(2,1)}, bf16[128,896]{1,0:T(8,128)(2,1)S(1)}, u32[]{:S(2)}, u32[]{:S(2)}) collective-permute-start(bf16[128,896]{1,0:T(8,128)(2,1)} %get-tuple-element.289), channel_id=1, source_target_pairs={{0,3},{1,2},{2,1},{3,0},{4,7},{5,6},{6,5},{7,4},{8,11},{9,10},{10,... | collective-permute-start | bytes 688136 | tf_op jit(solution)/shard_map/ppermute | solution.py:35
  178.8 19.8 %collective-permute-start.22 = (bf16[128,768]{1,0:T(8,128)(2,1)}, bf16[128,768]{1,0:T(8,128)(2,1)S(1)}, u32[]{:S(2)}, u32[]{:S(2)}) collective-permute-start(bf16[128,768]{1,0:T(8,128)(2,1)} %get-tuple-element.279.refs_5_), channel_id=1, source_target_pairs={{0,1},{1,0},{2,3},{3,2},{4,5},{5,4},{6,7},{7,6},{8,9},{9,8},{10,11... | collective-permute-start | bytes 589832 | tf_op jit(solution)/shard_map/ppermute | solution.py:35
  180.3 18.3 %collective-permute-start.23 = (bf16[128,768]{1,0:T(8,128)(2,1)}, bf16[128,768]{1,0:T(8,128)(2,1)S(1)}, u32[]{:S(2)}, u32[]{:S(2)}) collective-permute-start(bf16[128,768]{1,0:T(8,128)(2,1)} %get-tuple-element.280.refs_6_), channel_id=1, source_target_pairs={{0,2},{1,3},{2,0},{3,1},{4,6},{5,7},{6,4},{7,5},{8,10},{9,11},{10,... | collective-permute-start | bytes 589832 | tf_op jit(solution)/shard_map/ppermute | solution.py:35
  181.8 16.8 %collective-permute-start.24 = (bf16[128,768]{1,0:T(8,128)(2,1)}, bf16[128,768]{1,0:T(8,128)(2,1)S(1)}, u32[]{:S(2)}, u32[]{:S(2)}) collective-permute-start(bf16[128,768]{1,0:T(8,128)(2,1)} %get-tuple-element.281.refs_7_), channel_id=1, source_target_pairs={{0,3},{1,2},{2,1},{3,0},{4,7},{5,6},{6,5},{7,4},{8,11},{9,10},{10,... | collective-permute-start | bytes 589832 | tf_op jit(solution)/shard_map/ppermute | solution.py:35
  199.4 140.3 %reduce-scatter.3.cloned.1.call-start = ((), (), s32[]{:S(2)}) async-start(), calls=%async_computation.4 | async-start | bytes 5308416 | tf_op jit(solution)/shard_map/reduce_scatter | solution.py:1073
  243.8 16.4 %collective-permute-start.32 = (bf16[192,3072]{1,0:T(8,128)(2,1)}, bf16[192,3072]{1,0:T(8,128)(2,1)S(1)}, u32[]{:S(2)}, u32[]{:S(2)}) collective-permute-start(bf16[192,3072]{1,0:T(8,128)(2,1)} %get-tuple-element.320), channel_id=1, source_target_pairs={{0,2},{1,3},{2,0},{3,1},{4,5},{5,4},{6,7},{7,6},{8,10},{9,11},{10,... | collective-permute-start | bytes 3538952 | tf_op jit(solution)/shard_map/ppermute | solution.py:35
  261.3 16.7 %collective-permute-start.36 = (bf16[1536,768]{1,0:T(8,128)(2,1)}, bf16[1536,768]{1,0:T(8,128)(2,1)S(1)}, u32[]{:S(2)}, u32[]{:S(2)}) collective-permute-start(bf16[1536,768]{1,0:T(8,128)(2,1)} %bitcast.229), channel_id=1, source_target_pairs={{0,4},{1,5},{2,6},{3,7},{4,0},{5,1},{6,2},{7,3},{8,12},{9,13},{10,... | collective-permute-start | bytes 7077896 | tf_op jit(solution)/shard_map/ppermute | solution.py:35
  263.4 12.9 %collective-permute-start.34 = (bf16[96,3072]{1,0:T(8,128)(2,1)}, bf16[96,3072]{1,0:T(8,128)(2,1)}, u32[]{:S(2)}, u32[]{:S(2)}) collective-permute-start(bf16[96,3072]{1,0:T(8,128)(2,1)} %add_convert_fusion.18), channel_id=1, source_target_pairs={{0,1},{1,0},{2,3},{3,2},{4,6},{5,7},{6,4},{7,5},{8,9},{9,8},{10,11... | collective-permute-start | bytes 1769480 | tf_op jit(solution)/shard_map/ppermute | solution.py:35
  264.4 11.9 %collective-permute-start.35 = (f32[8,128]{1,0:T(8,128)S(1)}, f32[8,128]{1,0:T(8,128)S(1)}, u32[]{:S(2)}, u32[]{:S(2)}) collective-permute-start(f32[8,128]{1,0:T(8,128)S(1)} %add.405), channel_id=1, source_target_pairs={{0,1},{1,0},{2,3},{3,2},{4,5},{5,4},{6,7},{7,6},{8,9},{9,8},{10,11... | collective-permute-start | bytes 12296 | tf_op jit(solution)/shard_map/ppermute | solution.py:35
  279.4 18.7 %collective-permute-start.37 = (bf16[384,3072]{1,0:T(8,128)(2,1)}, bf16[384,3072]{1,0:T(8,128)(2,1)S(1)}, u32[]{:S(2)}, u32[]{:S(2)}) collective-permute-start(bf16[384,3072]{1,0:T(8,128)(2,1)} %get-tuple-element.339), channel_id=1, source_target_pairs={{0,4},{1,5},{2,6},{3,7},{4,0},{5,1},{6,2},{7,3},{8,12},{9,13},{10,... | collective-permute-start | bytes 7077896 | tf_op jit(solution)/shard_map/ppermute | solution.py:35
  281.8 18.3 %collective-permute-start.38 = (bf16[768,768]{1,0:T(8,128)(2,1)S(1)}, bf16[768,768]{1,0:T(8,128)(2,1)S(1)}, u32[]{:S(2)}, u32[]{:S(2)}) collective-permute-start(bf16[768,768]{1,0:T(8,128)(2,1)S(1)} %get-tuple-element.492), channel_id=1, source_target_pairs={{0,2},{1,3},{2,0},{3,1},{4,5},{5,4},{6,7},{7,6},{8,10},{9,11},{10,... | collective-permute-start | bytes 3538952 | tf_op jit(solution)/shard_map/ppermute | solution.py:35
  283.4 14.7 %collective-permute-start.39 = (f32[8,128]{1,0:T(8,128)S(1)}, f32[8,128]{1,0:T(8,128)S(1)}, u32[]{:S(2)}, u32[]{:S(2)}) collective-permute-start(f32[8,128]{1,0:T(8,128)S(1)} %add.409), channel_id=1, source_target_pairs={{0,2},{1,3},{2,0},{3,1},{4,6},{5,7},{6,4},{7,5},{8,10},{9,11},{10,... | collective-permute-start | bytes 12296 | tf_op jit(solution)/shard_map/ppermute | solution.py:35
  300.0 26.8 %collective-permute-start.43 = (bf16[192,3072]{1,0:T(8,128)(2,1)}, bf16[192,3072]{1,0:T(8,128)(2,1)}, u32[]{:S(2)}, u32[]{:S(2)}) collective-permute-start(bf16[192,3072]{1,0:T(8,128)(2,1)} %get-tuple-element.346), channel_id=1, source_target_pairs={{0,2},{1,3},{2,0},{3,1},{4,5},{5,4},{6,7},{7,6},{8,10},{9,11},{10,... | collective-permute-start | bytes 3538952 | tf_op jit(solution)/shard_map/ppermute | solution.py:35
  301.7 23.6 %collective-permute-start.44 = (bf16[384,768]{1,0:T(8,128)(2,1)S(1)}, bf16[384,768]{1,0:T(8,128)(2,1)}, u32[]{:S(2)}, u32[]{:S(2)}) collective-permute-start(bf16[384,768]{1,0:T(8,128)(2,1)S(1)} %add_convert_fusion.15), channel_id=1, source_target_pairs={{0,1},{1,0},{2,3},{3,2},{4,6},{5,7},{6,4},{7,5},{8,9},{9,8},{10,11... | collective-permute-start | bytes 1769480 | tf_op jit(solution)/shard_map/ppermute | solution.py:35
  302.3 24.5 %collective-permute-start.42 = (bf16[24,3072]{1,0:T(8,128)(2,1)S(1)}, bf16[24,3072]{1,0:T(8,128)(2,1)S(1)}, u32[]{:S(2)}, u32[]{:S(2)}) collective-permute-start(bf16[24,3072]{1,0:T(8,128)(2,1)S(1)} %get-tuple-element.529), channel_id=1, source_target_pairs={{0,8},{1,9},{2,10},{3,11},{4,12},{5,13},{6,14},{7,15},{8,16},{9,17... | collective-permute-start | bytes 442376 | tf_op jit(solution)/shard_map/ppermute | solution.py:35
  302.9 23.9 %collective-permute-start.41 = (bf16[24,3072]{1,0:T(8,128)(2,1)S(1)}, bf16[24,3072]{1,0:T(8,128)(2,1)S(1)}, u32[]{:S(2)}, u32[]{:S(2)}) collective-permute-start(bf16[24,3072]{1,0:T(8,128)(2,1)S(1)} %get-tuple-element.530), channel_id=1, source_target_pairs={{0,16},{1,17},{2,18},{3,19},{4,20},{5,21},{6,22},{7,23},{8,24},{9,... | collective-permute-start | bytes 442376 | tf_op jit(solution)/shard_map/ppermute | solution.py:35
  305.2 21.6 %collective-permute-start.40 = (bf16[24,3072]{1,0:T(8,128)(2,1)S(1)}, bf16[24,3072]{1,0:T(8,128)(2,1)S(1)}, u32[]{:S(2)}, u32[]{:S(2)}) collective-permute-start(bf16[24,3072]{1,0:T(8,128)(2,1)S(1)} %get-tuple-element.531), channel_id=1, source_target_pairs={{0,24},{1,25},{2,26},{3,27},{4,28},{5,29},{6,30},{7,31},{8,0},{9,1... | collective-permute-start | bytes 442376 | tf_op jit(solution)/shard_map/ppermute | solution.py:35
  326.8 15.0 %collective-permute-start.45 = (bf16[384,3200]{1,0:T(8,128)(2,1)}, bf16[384,3200]{1,0:T(8,128)(2,1)}, u32[]{:S(2)}, u32[]{:S(2)}) collective-permute-start(bf16[384,3200]{1,0:T(8,128)(2,1)} %get-tuple-element.362), channel_id=1, source_target_pairs={{0,4},{1,5},{2,6},{3,7},{4,0},{5,1},{6,2},{7,3},{8,12},{9,13},{10,... | collective-permute-start | bytes 7372808 | tf_op jit(solution)/shard_map/ppermute | solution.py:35
  331.3 13.5 %collective-permute-start.49 = (bf16[96,768]{1,0:T(8,128)(2,1)S(1)}, bf16[96,768]{1,0:T(8,128)(2,1)S(1)}, u32[]{:S(2)}, u32[]{:S(2)}) collective-permute-start(bf16[96,768]{1,0:T(8,128)(2,1)S(1)} %get-tuple-element.525), channel_id=1, source_target_pairs={{0,8},{1,9},{2,10},{3,11},{4,12},{5,13},{6,14},{7,15},{8,16},{9,17... | collective-permute-start | bytes 442376 | tf_op jit(solution)/shard_map/ppermute | solution.py:35
  331.4 14.0 %collective-permute-start.48 = (bf16[96,768]{1,0:T(8,128)(2,1)S(1)}, bf16[96,768]{1,0:T(8,128)(2,1)S(1)}, u32[]{:S(2)}, u32[]{:S(2)}) collective-permute-start(bf16[96,768]{1,0:T(8,128)(2,1)S(1)} %get-tuple-element.526), channel_id=1, source_target_pairs={{0,16},{1,17},{2,18},{3,19},{4,20},{5,21},{6,22},{7,23},{8,24},{9,... | collective-permute-start | bytes 442376 | tf_op jit(solution)/shard_map/ppermute | solution.py:35
  332.2 13.2 %collective-permute-start.47 = (bf16[96,768]{1,0:T(8,128)(2,1)S(1)}, bf16[96,768]{1,0:T(8,128)(2,1)S(1)}, u32[]{:S(2)}, u32[]{:S(2)}) collective-permute-start(bf16[96,768]{1,0:T(8,128)(2,1)S(1)} %get-tuple-element.527), channel_id=1, source_target_pairs={{0,24},{1,25},{2,26},{3,27},{4,28},{5,29},{6,30},{7,31},{8,0},{9,1... | collective-permute-start | bytes 442376 | tf_op jit(solution)/shard_map/ppermute | solution.py:35
  348.4 16.7 %collective-permute-start.50 = (bf16[192,3200]{1,0:T(8,128)(2,1)S(1)}, bf16[192,3200]{1,0:T(8,128)(2,1)S(1)}, u32[]{:S(2)}, u32[]{:S(2)}) collective-permute-start(bf16[192,3200]{1,0:T(8,128)(2,1)S(1)} %get-tuple-element.372), channel_id=1, source_target_pairs={{0,2},{1,3},{2,0},{3,1},{4,5},{5,4},{6,7},{7,6},{8,10},{9,11},{10,... | collective-permute-start | bytes 3686408 | tf_op jit(solution)/shard_map/ppermute | solution.py:35
  349.6 12.6 %collective-permute-start.52 = (bf16[24,3072]{1,0:T(8,128)(2,1)S(1)}, bf16[24,3072]{1,0:T(8,128)(2,1)S(1)}, u32[]{:S(2)}, u32[]{:S(2)}) collective-permute-start(bf16[24,3072]{1,0:T(8,128)(2,1)S(1)} %get-tuple-element.522), channel_id=1, source_target_pairs={{0,16},{1,17},{2,18},{3,19},{4,20},{5,21},{6,22},{7,23},{8,24},{9,... | collective-permute-start | bytes 442376 | tf_op jit(solution)/shard_map/ppermute | solution.py:35
  350.6 11.6 %collective-permute-start.51 = (bf16[24,3072]{1,0:T(8,128)(2,1)S(1)}, bf16[24,3072]{1,0:T(8,128)(2,1)S(1)}, u32[]{:S(2)}, u32[]{:S(2)}) collective-permute-start(bf16[24,3072]{1,0:T(8,128)(2,1)S(1)} %get-tuple-element.523), channel_id=1, source_target_pairs={{0,24},{1,25},{2,26},{3,27},{4,28},{5,29},{6,30},{7,31},{8,0},{9,1... | collective-permute-start | bytes 442376 | tf_op jit(solution)/shard_map/ppermute | solution.py:35
  365.3 10.2 %collective-permute-start.55 = (bf16[96,3200]{1,0:T(8,128)(2,1)S(1)}, bf16[96,3200]{1,0:T(8,128)(2,1)S(1)}, u32[]{:S(2)}, u32[]{:S(2)}) collective-permute-start(bf16[96,3200]{1,0:T(8,128)(2,1)S(1)} %add_convert_fusion.9), channel_id=1, source_target_pairs={{0,1},{1,0},{2,3},{3,2},{4,6},{5,7},{6,4},{7,5},{8,9},{9,8},{10,11... | collective-permute-start | bytes 1843208 | tf_op jit(solution)/shard_map/ppermute | solution.py:35
  377.9 11.7 %collective-permute-start.58 = (bf16[24,3200]{1,0:T(8,128)(2,1)S(1)}, bf16[24,3200]{1,0:T(8,128)(2,1)S(1)}, u32[]{:S(2)}, u32[]{:S(2)}) collective-permute-start(bf16[24,3200]{1,0:T(8,128)(2,1)S(1)} %get-tuple-element.520), channel_id=1, source_target_pairs={{0,16},{1,17},{2,18},{3,19},{4,20},{5,21},{6,22},{7,23},{8,24},{9,... | collective-permute-start | bytes 460808 | tf_op jit(solution)/shard_map/ppermute | solution.py:35
  (57 other events, 314.8 us)
Sparse Core Ops, SparseCore 0:
  9.7 32.2 all-gather.4
  44.2 32.1 all-gather.6
  78.0 89.4 all-gather.8
  198.8 56.3 reduce-scatter.4
  257.4 57.5 reduce-scatter.2

commit v5 on v4

--- a/solution.py
+++ b/solution.py
@@ -1117,8 +1117,8 @@
     expand_part = scatter_near(expand_part)
     shrink_part = scatter_line(shrink_part)
 
-    lower_part, expand_part, shrink_part, upper_part, squared = at_once(
-        (lower_part, expand_part, shrink_part, upper_part, squared)
+    lower_part, expand_part, shrink_part, upper_part, squared, expert_out_grad, expert_in_grad = at_once(
+        (lower_part, expand_part, shrink_part, upper_part, squared, expert_out_grad, expert_in_grad)
     )
     lower_part = scatter_far(lower_part)
     expand_part = scatter_line(expand_part)

time: 408 us -> 405 us (level)
  other arithmetic: 39.3 us -> 33.2 us
    convert_element_type x12, other arithmetic: 19.2 us -> 13 us  [add(): return (first.astype(F32) + second.astype(F32)).astype(BF16)]
    unnamed x81 -> x83, local copies, waits for them, and re-layouts: 8.36 us -> 7.39 us
  transfers between devices with their start and end apart: 65 -> 65, of which waited for: 30 -> 29; matrix products, arithmetic and copies ran while one was open for 12% -> 11% of each run, Pallas kernels for 32% -> 33%
where the time goes in v5:
time: 405 us; the launch traced here: 397 us
  waiting for transfers between devices  130 us (32%)
  Pallas kernels  130 us (32%)
  starting transfers between devices  64.8 us (16%)
  other arithmetic  33.2 us (8%)
  local copies, waits for them, and re-layouts  21.5 us (5%)
  between operations  18.2 us (4%)
    ppermute x60, waiting for transfers between devices, hop(): return lax.ppermute(values, AXES, pairs(target))  122 us
    pallas_call x12, Pallas kernels, call(): pl.pallas_call(kernel, out_shape=outs, grid=grid, in_specs=in_specs or [W...  118 us
    ppermute x60, starting transfers between devices, hop(): return lax.ppermute(values, AXES, pairs(target))  64.4 us
    convert_element_type x12, other arithmetic, add(): return (first.astype(F32) + second.astype(F32)).astype(BF16)  13 us
    pallas_call x1, Pallas kernels, feed_backward_shrink(): pl.pallas_call(kernel, out_shape=outs, grid_spec=pltpu.PrefetchScalarGrid...  11.9 us
  transfers between devices with their start and end apart: 65, of which 29 were waited for; matrix products, arithmetic and copies ran while one was open for 11% of the time, Pallas kernels for 33%

profile of v5, /device:TPU:0, one launch (start us, length us, event | category | flops | bytes accessed | tf_op | source)
XLA Modules:
  0.0 397.2 jit_solution(15849891237307285467)
XLA Ops:
  8.0 1.8 pad_maximum_fusion.10
  9.9 1.8 shard_map.365
  11.6 5.0 %collective-permute-start.2 = (bf16[24,3200]{1,0:T(8,128)(2,1)}, bf16[24,3200]{1,0:T(8,128)(2,1)S(1)}, u32[]{:S(2)}, u32[]{:S(2)}) collective-permute-start(bf16[24,3200]{1,0:T(8,128)(2,1)} %shard_map.365), channel_id=1, source_target_pairs={{0,24},{1,25},{2,26},{3,27},{4,28},{5,29},{6,30},{7,31},{8,0},{9,1... | collective-permute-start | bytes 460808 | tf_op jit(solution)/shard_map/ppermute | solution.py:35
  23.4 13.5 %collective-permute-done.1 = bf16[24,3200]{1,0:T(8,128)(2,1)S(1)} collective-permute-done((bf16[24,3200]{1,0:T(8,128)(2,1)}, bf16[24,3200]{1,0:T(8,128)(2,1)S(1)}, u32[]{:S(2)}, u32[]{:S(2)}) %collective-permute-start.1) | collective-permute-done | bytes 153632 | tf_op jit(solution)/shard_map/ppermute | solution.py:35
  38.6 3.4 all-gather.5.cloned.1.call-done
  44.4 2.9 collective-permute-done.3
  50.6 14.9 %collective-permute-done.6 = bf16[4,96,768]{2,1,0:T(8,128)(2,1)} collective-permute-done((bf16[4,96,768]{2,1,0:T(8,128)(2,1)S(1)}, bf16[4,96,768]{2,1,0:T(8,128)(2,1)}, u32[]{:S(2)}, u32[]{:S(2)}) %collective-permute-start.6) | collective-permute-done | bytes 589856 | tf_op jit(solution)/shard_map/ppermute | solution.py:35
  65.5 5.3 %collective-permute-done.4 = bf16[2,4,24,3200]{3,2,1,0:T(8,128)(2,1)} collective-permute-done((bf16[2,4,24,3200]{3,2,1,0:T(8,128)(2,1)S(1)}, bf16[2,4,24,3200]{3,2,1,0:T(8,128)(2,1)}, u32[]{:S(2)}, u32[]{:S(2)}) %collective-permute-start.4) | collective-permute-done | bytes 1228832 | tf_op jit(solution)/shard_map/ppermute | solution.py:35
  73.5 2.9 all-gather.7.cloned.1.call-done
  76.4 1.7 dynamic-slice_bitcast_fusion.3
  83.0 9.8 %shard_map.366 = (f32[128,768]{1,0:T(8,128)}, f32[256,768]{1,0:T(8,128)}, bf16[256,768]{1,0:T(8,128)(2,1)}, bf16[256,2304]{1,0:T(8,128)(2,1)}, bf16[256,768]{1,0:T(8,128)(2,1)}) custom-call(s32[2]{0:T(128)} %refs_0_.7, bf16[256,768]{1,0:T(8,128)(2,1)} %bitcast.199, bf16[768,768]{1,0:T(8,128)(2,1)} %fusion.refs_2_.refs_11_.refs_6_.refs_5_, ...), custom_call_target="tpu_custom_call" | custom-call | flops 1509949 | bytes 9633 | tf_op jit(solution)/shard_map/pallas_call | solution.py:198
  103.3 10.2 %collective-permute-done.12 = bf16[2,4,24,3072]{3,2,1,0:T(8,128)(2,1)S(1)} collective-permute-done((bf16[2,4,24,3072]{3,2,1,0:T(8,128)(2,1)S(1)}, bf16[2,4,24,3072]{3,2,1,0:T(8,128)(2,1)S(1)}, u32[]{:S(2)}, u32[]{:S(2)}) %collective-permute-start.12) | collective-permute-done | bytes 1179680 | tf_op jit(solution)/shard_map/ppermute | solution.py:35
  113.6 2.8 collective-permute-done.15
  120.4 11.5 %shard_map.367 = (f32[256,768]{1,0:T(8,128)}, bf16[256,768]{1,0:T(8,128)(2,1)}, f32[256,3072]{1,0:T(8,128)}) custom-call(s32[32]{0:T(128)} %get-tuple-element.251.refs_0_.places_ref, bf16[192,3072]{1,0:T(8,128)(2,1)} %bitcast.163, bf16[192,3072]{1,0:T(8,128)(2,1)} %bitcast.177, bf16[96,3072]{1,0:T(8,128)(2,1)} %bitcast.169, ...), custom_call_target="tpu_custom_call" | custom-call | flops 2415919 | bytes 16121 | tf_op jit(solution)/shard_map/pallas_call | solution.py:198
  132.0 3.2 collective-permute-done.16
  136.0 2.3 collective-permute-done.18
  139.4 8.2 %shard_map.368 = (f32[256,768]{1,0:T(8,128)}, bf16[256,768]{1,0:T(8,128)(2,1)}, bf16[256,2304]{1,0:T(8,128)(2,1)}, bf16[256,768]{1,0:T(8,128)(2,1)}) custom-call(s32[2]{0:T(128)} %refs_0_.7, f32[256,768]{1,0:T(8,128)} %get-tuple-element.264.refs_1_.refs_7_, bf16[768,768]{1,0:T(8,128)(2,1)} %fusion.refs_2_.refs_11_.refs_6_.refs_5_, ...), custom_call_target="tpu_custom_call" | custom-call | flops 1509949 | bytes 9830 | tf_op jit(solution)/shard_map/pallas_call | solution.py:198
  147.6 3.6 shard_map.369
  154.7 4.5 %collective-permute-done.19.refs_1_ = bf16[128,768]{1,0:T(8,128)(2,1)S(1)} collective-permute-done((bf16[128,768]{1,0:T(8,128)(2,1)}, bf16[128,768]{1,0:T(8,128)(2,1)S(1)}, u32[]{:S(2)}, u32[]{:S(2)}) %collective-permute-start.19) | collective-permute-done | bytes 196640 | tf_op jit(solution)/shard_map/ppermute | solution.py:35
  159.2 3.5 collective-permute-done.20.refs_2_
  167.6 11.2 %shard_map.370 = (bf16[128,768]{1,0:T(8,128)(2,1)}, bf16[128,768]{1,0:T(8,128)(2,1)}, bf16[128,768]{1,0:T(8,128)(2,1)}, bf16[128,768]{1,0:T(8,128)(2,1)}, bf16[512,768]{1,0:T(8,128)(2,1)}, /*index=5*/f32[512,3072]{1,0:T(8,128)}) custom-call(bf16[128,768]{1,0:T(8,128)(2,1)} %get-tuple-element.275.refs_0_, bf16[128,768]{1,0:T(8,128)(2,1)} %copy-done.26, ...), custom_call_target="tpu_custom_call" | custom-call | flops 4831838208 | bytes 27525120 | tf_op jit(solution)/shard_map/pallas_call | solution.py:198
  183.0 15.4 %shard_map.371 = (bf16[128,768]{1,0:T(8,128)(2,1)}, bf16[128,768]{1,0:T(8,128)(2,1)}, bf16[128,768]{1,0:T(8,128)(2,1)}, bf16[128,768]{1,0:T(8,128)(2,1)}, bf16[5...) custom-call(bf16[128,896]{1,0:T(8,128)(2,1)} %get-tuple-element.285.refs_0_, bf16[128,896]{1,0:T(8,128)(2,1)} %copy-done.23, ...), custom_call_target="tpu_custom_call" | custom-call | flops 7247757 | bytes 35520 | tf_op jit(solution)/shard_map/pallas_call | solution.py:198
  203.1 4.3 %collective-permute-done.28.refs_12_ = bf16[128,768]{1,0:T(8,128)(2,1)S(1)} collective-permute-done((bf16[128,768]{1,0:T(8,128)(2,1)S(1)}, bf16[128,768]{1,0:T(8,128)(2,1)S(1)}, u32[]{:S(2)}, u32[]{:S(2)}) %collective-permute-start.28) | collective-permute-done | bytes 196640 | tf_op jit(solution)/shard_map/ppermute | solution.py:35
  207.4 3.8 collective-permute-done.29.refs_13_
  212.0 5.6 %shard_map.372 = (bf16[256,768]{1,0:T(8,128)(2,1)}, f32[256,768]{1,0:T(8,128)}, f32[128,768]{1,0:T(8,128)}, f32[8,128]{1,0:T(8,128)}) custom-call(f32[256,768]{1,0:T(8,128)} %get-tuple-element.269.stream_ref.refs_0_, f32[128,768]{1,0:T(8,128)} %get-tuple-element.241.refs_13_.refs_8_.rows_ref.refs_1_.refs_7_, f32[8,128]{1,0:T(8,128)} %pad.9.facts_ref.refs_2_, ...), custom_call_target="tpu_custom_call" | custom-call | flops 402653184 | bytes 5254144 | tf_op jit(solution)/shard_map/pallas_call | solution.py:198
  217.6 15.3 %shard_map.373 = (f32[256,768]{1,0:T(8,128)}, bf16[384,3072]{1,0:T(8,128)(2,1)}, bf16[384,3072]{1,0:T(8,128)(2,1)}, f32[8,768]{1,0:T(8,128)}) custom-call(s32[2]{0:T(128)} %refs_0_.7, bf16[192,3072]{1,0:T(8,128)(2,1)} %bitcast.166, bf16[192,3072]{1,0:T(8,128)(2,1)} %bitcast.74.refs_4_.refs_2_, bf16[96,3072]{1,0:T(8,128)(2,1)} %bitcast.172, ...), custom_call_target="tpu_custom_call" | custom-call | flops 3321888 | bytes 15360 | tf_op jit(solution)/shard_map/pallas_call | solution.py:198
  233.0 7.2 %shard_map.374 = bf16[768,3072]{1,0:T(8,128)(2,1)} custom-call(bf16[512,768]{1,0:T(8,128)(2,1)} %get-tuple-element.314.arrived_ref, bf16[512,3072]{1,0:T(8,128)(2,1)} %get-tuple-element.317.inner_grad_ref), custom_call_target="tpu_custom_call" | custom-call | flops 2415919 | bytes 8650 | tf_op jit(solution)/shard_map/pallas_call | solution.py:198
  240.2 3.6 add_convert_fusion.6
  246.5 11.9 %shard_map.375 = (bf16[256,3072]{1,0:T(8,128)(2,1)}, bf16[4,4,96,768]{3,2,1,0:T(8,128)(2,1)}, bf16[4,4,96,768]{3,2,1,0:T(8,128)(2,1)}) custom-call(s32[32]{0:T(128)} %get-tuple-element.251.refs_0_.places_ref, bf16[768,768]{1,0:T(8,128)(2,1)} %bitcast.162, bf16[768,768]{1,0:T(8,128)(2,1)} %bitcast.58.refs_7_.refs_1_, bf16[384,768]{1,0:T(8,128)(2,1)} %bitcast.168, ...), custom_call_target="tpu_custom_call" | custom-call | flops 2415919 | bytes 14942 | tf_op jit(solution)/shard_map/pallas_call | solution.py:586
  258.4 1.9 collective-permute-done.32
  262.5 11.2 %shard_map.376 = (f32[256,768]{1,0:T(8,128)}, bf16[384,3072]{1,0:T(8,128)(2,1)}, bf16[384,3072]{1,0:T(8,128)(2,1)}, f32[8,768]{1,0:T(8,128)}) custom-call(bf16[192,3072]{1,0:T(8,128)(2,1)} %bitcast.164, bf16[192,3072]{1,0:T(8,128)(2,1)} %bitcast.178, bf16[96,3072]{1,0:T(8,128)(2,1)} %bitcast.170, bf16[96,3072]{1,0:T(8,128)(2,1)} %bitcast.69.refs_4_.refs_3_, ...), custom_call_target="tpu_custom_call" | custom-call | flops 2415919 | bytes 15360 | tf_op jit(solution)/shard_map/pallas_call | solution.py:198
  275.5 2.3 add_convert_fusion.2
  279.9 14.3 %collective-permute-done.39 = f32[8,128]{1,0:T(8,128)S(1)} collective-permute-done((f32[8,128]{1,0:T(8,128)S(1)}, f32[8,128]{1,0:T(8,128)S(1)}, u32[]{:S(2)}, u32[]{:S(2)}) %collective-permute-start.39) | collective-permute-done | bytes 4128 | tf_op jit(solution)/shard_map/ppermute | solution.py:35
  299.2 2.2 collective-permute-start.41
  301.3 3.2 collective-permute-start.40
  304.5 17.0 %shard_map.377 = (f32[256,768]{1,0:T(8,128)}, bf16[384,3200]{1,0:T(8,128)(2,1)}, bf16[384,3200]{1,0:T(8,128)(2,1)}, f32[8,768]{1,0:T(8,128)}) custom-call(s32[2]{0:T(128)} %refs_0_.7, bf16[192,3200]{1,0:T(8,128)(2,1)} %bitcast.160, bf16[192,3200]{1,0:T(8,128)(2,1)} %bitcast.54.refs_4_.refs_2_, bf16[192,3200]{1,0:T(8,128)(2,1)} %bitcast.174, ...), custom_call_target="tpu_custom_call" | custom-call | flops 3321888 | bytes 15802 | tf_op jit(solution)/shard_map/pallas_call | solution.py:198
  327.3 2.6 collective-permute-start.48
  330.1 4.2 %collective-permute-done.46 = bf16[96,3072]{1,0:T(8,128)(2,1)S(1)} collective-permute-done((bf16[96,3072]{1,0:T(8,128)(2,1)S(1)}, bf16[96,3072]{1,0:T(8,128)(2,1)S(1)}, u32[]{:S(2)}, u32[]{:S(2)}) %collective-permute-start.46) | collective-permute-done | bytes 589856 | tf_op jit(solution)/shard_map/ppermute | solution.py:35
  336.2 3.9 collective-permute-done.48
  340.1 3.7 collective-permute-start.54
  346.2 2.9 collective-permute-start.51
  350.3 1.9 convert_add_fusion.3
  354.4 4.8 %collective-permute-done.52 = bf16[24,3072]{1,0:T(8,128)(2,1)S(1)} collective-permute-done((bf16[24,3072]{1,0:T(8,128)(2,1)S(1)}, bf16[24,3072]{1,0:T(8,128)(2,1)S(1)}, u32[]{:S(2)}, u32[]{:S(2)}) %collective-permute-start.52) | collective-permute-done | bytes 147488 | tf_op jit(solution)/shard_map/ppermute | solution.py:35
  360.7 1.8 collective-permute-start.55
  363.8 3.2 collective-permute-done.56
  367.0 3.9 collective-permute-done.55
  376.1 4.3 %collective-permute-done.57 = bf16[24,3200]{1,0:T(8,128)(2,1)S(1)} collective-permute-done((bf16[24,3200]{1,0:T(8,128)(2,1)S(1)}, bf16[24,3200]{1,0:T(8,128)(2,1)S(1)}, u32[]{:S(2)}, u32[]{:S(2)}) %collective-permute-start.57) | collective-permute-done | bytes 153632 | tf_op jit(solution)/shard_map/ppermute | solution.py:35
  381.6 4.6 %collective-permute-done.58 = bf16[24,3200]{1,0:T(8,128)(2,1)S(1)} collective-permute-done((bf16[24,3200]{1,0:T(8,128)(2,1)S(1)}, bf16[24,3200]{1,0:T(8,128)(2,1)S(1)}, u32[]{:S(2)}, u32[]{:S(2)}) %collective-permute-start.58) | collective-permute-done | bytes 153632 | tf_op jit(solution)/shard_map/ppermute | solution.py:35
  (259 shorter events, 94.2 us)
Async XLA Ops:
  7.2 34.8 %all-gather.5.cloned.1.call-start = ((), (), s32[]{:S(2)}) async-start(), calls=%async_computation.2 | async-start | bytes 1327104 | tf_op jit(solution)/shard_map/all_gather | solution.py:68
  8.0 68.4 %all-gather.7.cloned.1.call-start = ((), (), s32[]{:S(2)}) async-start(), calls=%async_computation.3 | async-start | bytes 2654208 | tf_op jit(solution)/shard_map/all_gather | solution.py:68
  9.8 157.8 %all-gather.9.cloned.1.call-start = ((), (), s32[]{:S(2)}) async-start(), calls=%async_computation.6 | async-start | bytes 10616832 | tf_op jit(solution)/shard_map/all_gather | solution.py:991
  11.6 11.8 %collective-permute-start.2 = (bf16[24,3200]{1,0:T(8,128)(2,1)}, bf16[24,3200]{1,0:T(8,128)(2,1)S(1)}, u32[]{:S(2)}, u32[]{:S(2)}) collective-permute-start(bf16[24,3200]{1,0:T(8,128)(2,1)} %shard_map.365), channel_id=1, source_target_pairs={{0,24},{1,25},{2,26},{3,27},{4,28},{5,29},{6,30},{7,31},{8,0},{9,1... | collective-permute-start | bytes 460808 | tf_op jit(solution)/shard_map/ppermute | solution.py:35
  16.7 20.2 %collective-permute-start.1 = (bf16[24,3200]{1,0:T(8,128)(2,1)}, bf16[24,3200]{1,0:T(8,128)(2,1)S(1)}, u32[]{:S(2)}, u32[]{:S(2)}) collective-permute-start(bf16[24,3200]{1,0:T(8,128)(2,1)} %shard_map.365), channel_id=1, source_target_pairs={{0,16},{1,17},{2,18},{3,19},{4,20},{5,21},{6,22},{7,23},{8,24},{9,... | collective-permute-start | bytes 460808 | tf_op jit(solution)/shard_map/ppermute | solution.py:35
  16.7 20.2 %collective-permute-start = (bf16[24,3200]{1,0:T(8,128)(2,1)}, bf16[24,3200]{1,0:T(8,128)(2,1)S(1)}, u32[]{:S(2)}, u32[]{:S(2)}) collective-permute-start(bf16[24,3200]{1,0:T(8,128)(2,1)} %shard_map.365), channel_id=1, source_target_pairs={{0,8},{1,9},{2,10},{3,11},{4,12},{5,13},{6,14},{7,15},{8,16},{9,17... | collective-permute-start | bytes 460808 | tf_op jit(solution)/shard_map/ppermute | solution.py:35
  36.9 299.3 %reduce-scatter.3.cloned.1.call-start = ((), (), s32[]{:S(2)}) async-start(), calls=%async_computation.4 | async-start | bytes 5308416 | tf_op jit(solution)/shard_map/reduce_scatter | solution.py:1052
  37.1 10.2 %collective-permute-start.3 = (bf16[4,24,3200]{2,1,0:T(8,128)(2,1)S(1)}, bf16[4,24,3200]{2,1,0:T(8,128)(2,1)S(1)}, u32[]{:S(2)}, u32[]{:S(2)}) collective-permute-start(bf16[4,24,3200]{2,1,0:T(8,128)(2,1)S(1)} %pad_maximum_fusion.7), channel_id=1, source_target_pairs={{0,1},{1,0},{2,3},{3,2},{4,6},{5,7},{6,4},{7,5},{8,9},{9,8},{10,11... | collective-permute-start | bytes 1843208 | tf_op jit(solution)/shard_map/ppermute | solution.py:35
  47.4 18.0 %collective-permute-start.5 = (bf16[2,4,24,3200]{3,2,1,0:T(8,128)(2,1)S(1)}, bf16[2,4,24,3200]{3,2,1,0:T(8,128)(2,1)S(1)}, u32[]{:S(2)}, u32[]{:S(2)}) collective-permute-start(bf16[2,4,24,3200]{3,2,1,0:T(8,128)(2,1)S(1)} %pad_maximum_fusion), channel_id=1, source_target_pairs={{0,4},{1,5},{2,6},{3,7},{4,0},{5,1},{6,2},{7,3},{8,12},{9,13},{10,... | collective-permute-start | bytes 3686408 | tf_op jit(solution)/shard_map/ppermute | solution.py:35
  47.5 23.2 %collective-permute-start.4 = (bf16[2,4,24,3200]{3,2,1,0:T(8,128)(2,1)S(1)}, bf16[2,4,24,3200]{3,2,1,0:T(8,128)(2,1)}, u32[]{:S(2)}, u32[]{:S(2)}) collective-permute-start(bf16[2,4,24,3200]{3,2,1,0:T(8,128)(2,1)S(1)} %pad_maximum_fusion), channel_id=1, source_target_pairs={{0,2},{1,3},{2,0},{3,1},{4,5},{5,4},{6,7},{7,6},{8,10},{9,11},{10,... | collective-permute-start | bytes 3686408 | tf_op jit(solution)/shard_map/ppermute | solution.py:35
  49.1 16.4 %collective-permute-start.6 = (bf16[4,96,768]{2,1,0:T(8,128)(2,1)S(1)}, bf16[4,96,768]{2,1,0:T(8,128)(2,1)}, u32[]{:S(2)}, u32[]{:S(2)}) collective-permute-start(bf16[4,96,768]{2,1,0:T(8,128)(2,1)S(1)} %get-tuple-element.219), channel_id=1, source_target_pairs={{0,1},{1,0},{2,3},{3,2},{4,6},{5,7},{6,4},{7,5},{8,9},{9,8},{10,11... | collective-permute-start | bytes 1769480 | tf_op jit(solution)/shard_map/ppermute | solution.py:35
  70.7 22.0 %collective-permute-start.8 = (bf16[4,96,768]{2,1,0:T(8,128)(2,1)}, bf16[4,96,768]{2,1,0:T(8,128)(2,1)S(1)}, u32[]{:S(2)}, u32[]{:S(2)}) collective-permute-start(bf16[4,96,768]{2,1,0:T(8,128)(2,1)} %collective-permute-done.6), channel_id=1, source_target_pairs={{0,4},{1,5},{2,6},{3,7},{4,0},{5,1},{6,2},{7,3},{8,12},{9,13},{10,... | collective-permute-start | bytes 1769480 | tf_op jit(solution)/shard_map/ppermute | solution.py:35
  71.9 20.9 %collective-permute-start.7 = (bf16[2,4,96,768]{3,2,1,0:T(8,128)(2,1)S(1)}, bf16[2,4,96,768]{3,2,1,0:T(8,128)(2,1)}, u32[]{:S(2)}, u32[]{:S(2)}) collective-permute-start(bf16[2,4,96,768]{3,2,1,0:T(8,128)(2,1)S(1)} %pad_maximum_fusion.2), channel_id=1, source_target_pairs={{0,2},{1,3},{2,0},{3,1},{4,5},{5,4},{6,7},{7,6},{8,10},{9,11},{10,... | collective-permute-start | bytes 3538952 | tf_op jit(solution)/shard_map/ppermute | solution.py:35
  80.9 13.3 %collective-permute-start.10 = (bf16[4,24,3072]{2,1,0:T(8,128)(2,1)}, bf16[4,24,3072]{2,1,0:T(8,128)(2,1)}, u32[]{:S(2)}, u32[]{:S(2)}) collective-permute-start(bf16[4,24,3072]{2,1,0:T(8,128)(2,1)} %get-tuple-element.237), channel_id=1, source_target_pairs={{0,1},{1,0},{2,3},{3,2},{4,6},{5,7},{6,4},{7,5},{8,9},{9,8},{10,11... | collective-permute-start | bytes 1769480 | tf_op jit(solution)/shard_map/ppermute | solution.py:35
  82.2 21.1 %collective-permute-start.14 = (bf16[4,24,3072]{2,1,0:T(8,128)(2,1)}, bf16[4,24,3072]{2,1,0:T(8,128)(2,1)}, u32[]{:S(2)}, u32[]{:S(2)}) collective-permute-start(bf16[4,24,3072]{2,1,0:T(8,128)(2,1)} %get-tuple-element.249), channel_id=1, source_target_pairs={{0,1},{1,0},{2,3},{3,2},{4,6},{5,7},{6,4},{7,5},{8,9},{9,8},{10,11... | collective-permute-start | bytes 1769480 | tf_op jit(solution)/shard_map/ppermute | solution.py:35
  95.6 17.8 %collective-permute-start.12 = (bf16[2,4,24,3072]{3,2,1,0:T(8,128)(2,1)S(1)}, bf16[2,4,24,3072]{3,2,1,0:T(8,128)(2,1)S(1)}, u32[]{:S(2)}, u32[]{:S(2)}) collective-permute-start(bf16[2,4,24,3072]{3,2,1,0:T(8,128)(2,1)S(1)} %pad_maximum_fusion.5), channel_id=1, source_target_pairs={{0,2},{1,3},{2,0},{3,1},{4,5},{5,4},{6,7},{7,6},{8,10},{9,11},{10,... | collective-permute-start | bytes 3538952 | tf_op jit(solution)/shard_map/ppermute | solution.py:35
  97.2 16.3 %collective-permute-start.11 = (bf16[2,4,96,768]{3,2,1,0:T(8,128)(2,1)}, bf16[2,4,96,768]{3,2,1,0:T(8,128)(2,1)S(1)}, u32[]{:S(2)}, u32[]{:S(2)}) collective-permute-start(bf16[2,4,96,768]{3,2,1,0:T(8,128)(2,1)} %collective-permute-done.7), channel_id=1, source_target_pairs={{0,4},{1,5},{2,6},{3,7},{4,0},{5,1},{6,2},{7,3},{8,12},{9,13},{10,... | collective-permute-start | bytes 3538952 | tf_op jit(solution)/shard_map/ppermute | solution.py:35
  118.9 16.4 %collective-permute-start.16 = (bf16[2,4,24,3072]{3,2,1,0:T(8,128)(2,1)S(1)}, bf16[2,4,24,3072]{3,2,1,0:T(8,128)(2,1)}, u32[]{:S(2)}, u32[]{:S(2)}) collective-permute-start(bf16[2,4,24,3072]{3,2,1,0:T(8,128)(2,1)S(1)} %pad_maximum_fusion.6), channel_id=1, source_target_pairs={{0,2},{1,3},{2,0},{3,1},{4,5},{5,4},{6,7},{7,6},{8,10},{9,11},{10,... | collective-permute-start | bytes 3538952 | tf_op jit(solution)/shard_map/ppermute | solution.py:35
  120.4 11.6 %collective-permute-start.17 = (bf16[4,24,3072]{2,1,0:T(8,128)(2,1)}, bf16[4,24,3072]{2,1,0:T(8,128)(2,1)S(1)}, u32[]{:S(2)}, u32[]{:S(2)}) collective-permute-start(bf16[4,24,3072]{2,1,0:T(8,128)(2,1)} %collective-permute-done.14), channel_id=1, source_target_pairs={{0,4},{1,5},{2,6},{3,7},{4,0},{5,1},{6,2},{7,3},{8,12},{9,13},{10,... | collective-permute-start | bytes 1769480 | tf_op jit(solution)/shard_map/ppermute | solution.py:35
  152.4 10.2 %collective-permute-start.20 = (bf16[128,768]{1,0:T(8,128)(2,1)}, bf16[128,768]{1,0:T(8,128)(2,1)S(1)}, u32[]{:S(2)}, u32[]{:S(2)}) collective-permute-start(bf16[128,768]{1,0:T(8,128)(2,1)} %get-tuple-element.277), channel_id=1, source_target_pairs={{0,2},{1,3},{2,0},{3,1},{4,6},{5,7},{6,4},{7,5},{8,10},{9,11},{10,... | collective-permute-start | bytes 589832 | tf_op jit(solution)/shard_map/ppermute | solution.py:35
  163.7 18.1 %collective-permute-start.25 = (bf16[128,896]{1,0:T(8,128)(2,1)}, bf16[128,896]{1,0:T(8,128)(2,1)S(1)}, u32[]{:S(2)}, u32[]{:S(2)}) collective-permute-start(bf16[128,896]{1,0:T(8,128)(2,1)} %get-tuple-element.287), channel_id=1, source_target_pairs={{0,1},{1,0},{2,3},{3,2},{4,5},{5,4},{6,7},{7,6},{8,9},{9,8},{10,11... | collective-permute-start | bytes 688136 | tf_op jit(solution)/shard_map/ppermute | solution.py:35
  164.8 17.5 %collective-permute-start.26 = (bf16[128,896]{1,0:T(8,128)(2,1)}, bf16[128,896]{1,0:T(8,128)(2,1)S(1)}, u32[]{:S(2)}, u32[]{:S(2)}) collective-permute-start(bf16[128,896]{1,0:T(8,128)(2,1)} %get-tuple-element.289), channel_id=1, source_target_pairs={{0,2},{1,3},{2,0},{3,1},{4,6},{5,7},{6,4},{7,5},{8,10},{9,11},{10,... | collective-permute-start | bytes 688136 | tf_op jit(solution)/shard_map/ppermute | solution.py:35
  166.1 16.2 %collective-permute-start.27 = (bf16[128,896]{1,0:T(8,128)(2,1)}, bf16[128,896]{1,0:T(8,128)(2,1)S(1)}, u32[]{:S(2)}, u32[]{:S(2)}) collective-permute-start(bf16[128,896]{1,0:T(8,128)(2,1)} %get-tuple-element.291), channel_id=1, source_target_pairs={{0,3},{1,2},{2,1},{3,0},{4,7},{5,6},{6,5},{7,4},{8,11},{9,10},{10,... | collective-permute-start | bytes 688136 | tf_op jit(solution)/shard_map/ppermute | solution.py:35
  178.8 19.7 %collective-permute-start.22 = (bf16[128,768]{1,0:T(8,128)(2,1)}, bf16[128,768]{1,0:T(8,128)(2,1)S(1)}, u32[]{:S(2)}, u32[]{:S(2)}) collective-permute-start(bf16[128,768]{1,0:T(8,128)(2,1)} %get-tuple-element.281.refs_5_), channel_id=1, source_target_pairs={{0,1},{1,0},{2,3},{3,2},{4,5},{5,4},{6,7},{7,6},{8,9},{9,8},{10,11... | collective-permute-start | bytes 589832 | tf_op jit(solution)/shard_map/ppermute | solution.py:35
  180.3 18.2 %collective-permute-start.23 = (bf16[128,768]{1,0:T(8,128)(2,1)}, bf16[128,768]{1,0:T(8,128)(2,1)S(1)}, u32[]{:S(2)}, u32[]{:S(2)}) collective-permute-start(bf16[128,768]{1,0:T(8,128)(2,1)} %get-tuple-element.282.refs_6_), channel_id=1, source_target_pairs={{0,2},{1,3},{2,0},{3,1},{4,6},{5,7},{6,4},{7,5},{8,10},{9,11},{10,... | collective-permute-start | bytes 589832 | tf_op jit(solution)/shard_map/ppermute | solution.py:35
  181.8 16.7 %collective-permute-start.24 = (bf16[128,768]{1,0:T(8,128)(2,1)}, bf16[128,768]{1,0:T(8,128)(2,1)S(1)}, u32[]{:S(2)}, u32[]{:S(2)}) collective-permute-start(bf16[128,768]{1,0:T(8,128)(2,1)} %get-tuple-element.283.refs_7_), channel_id=1, source_target_pairs={{0,3},{1,2},{2,1},{3,0},{4,7},{5,6},{6,5},{7,4},{8,11},{9,10},{10,... | collective-permute-start | bytes 589832 | tf_op jit(solution)/shard_map/ppermute | solution.py:35
  199.3 140.9 %reduce-scatter.5.cloned.1.call-start = ((), (), s32[]{:S(2)}) async-start(), calls=%async_computation.5 | async-start | bytes 5308416 | tf_op jit(solution)/shard_map/reduce_scatter | solution.py:1073
  243.8 16.4 %collective-permute-start.32 = (bf16[192,3072]{1,0:T(8,128)(2,1)}, bf16[192,3072]{1,0:T(8,128)(2,1)S(1)}, u32[]{:S(2)}, u32[]{:S(2)}) collective-permute-start(bf16[192,3072]{1,0:T(8,128)(2,1)} %get-tuple-element.322), channel_id=1, source_target_pairs={{0,2},{1,3},{2,0},{3,1},{4,5},{5,4},{6,7},{7,6},{8,10},{9,11},{10,... | collective-permute-start | bytes 3538952 | tf_op jit(solution)/shard_map/ppermute | solution.py:35
  260.2 13.8 %collective-permute-start.36 = (bf16[1536,768]{1,0:T(8,128)(2,1)}, bf16[1536,768]{1,0:T(8,128)(2,1)}, u32[]{:S(2)}, u32[]{:S(2)}) collective-permute-start(bf16[1536,768]{1,0:T(8,128)(2,1)} %bitcast.229), channel_id=1, source_target_pairs={{0,4},{1,5},{2,6},{3,7},{4,0},{5,1},{6,2},{7,3},{8,12},{9,13},{10,... | collective-permute-start | bytes 7077896 | tf_op jit(solution)/shard_map/ppermute | solution.py:35
  260.4 13.4 %collective-permute-start.34 = (bf16[96,3072]{1,0:T(8,128)(2,1)S(1)}, bf16[96,3072]{1,0:T(8,128)(2,1)S(1)}, u32[]{:S(2)}, u32[]{:S(2)}) collective-permute-start(bf16[96,3072]{1,0:T(8,128)(2,1)S(1)} %add_convert_fusion.18), channel_id=1, source_target_pairs={{0,1},{1,0},{2,3},{3,2},{4,6},{5,7},{6,4},{7,5},{8,9},{9,8},{10,11... | collective-permute-start | bytes 1769480 | tf_op jit(solution)/shard_map/ppermute | solution.py:35
  261.6 12.2 %collective-permute-start.35 = (f32[8,128]{1,0:T(8,128)S(1)}, f32[8,128]{1,0:T(8,128)S(1)}, u32[]{:S(2)}, u32[]{:S(2)}) collective-permute-start(f32[8,128]{1,0:T(8,128)S(1)} %add.405), channel_id=1, source_target_pairs={{0,1},{1,0},{2,3},{3,2},{4,5},{5,4},{6,7},{7,6},{8,9},{9,8},{10,11... | collective-permute-start | bytes 12296 | tf_op jit(solution)/shard_map/ppermute | solution.py:35
  274.0 20.1 %collective-permute-start.37 = (bf16[384,3072]{1,0:T(8,128)(2,1)}, bf16[384,3072]{1,0:T(8,128)(2,1)S(1)}, u32[]{:S(2)}, u32[]{:S(2)}) collective-permute-start(bf16[384,3072]{1,0:T(8,128)(2,1)} %get-tuple-element.341), channel_id=1, source_target_pairs={{0,4},{1,5},{2,6},{3,7},{4,0},{5,1},{6,2},{7,3},{8,12},{9,13},{10,... | collective-permute-start | bytes 7077896 | tf_op jit(solution)/shard_map/ppermute | solution.py:35
  277.8 17.3 %collective-permute-start.38 = (bf16[768,768]{1,0:T(8,128)(2,1)S(1)}, bf16[768,768]{1,0:T(8,128)(2,1)S(1)}, u32[]{:S(2)}, u32[]{:S(2)}) collective-permute-start(bf16[768,768]{1,0:T(8,128)(2,1)S(1)} %get-tuple-element.496), channel_id=1, source_target_pairs={{0,2},{1,3},{2,0},{3,1},{4,5},{5,4},{6,7},{7,6},{8,10},{9,11},{10,... | collective-permute-start | bytes 3538952 | tf_op jit(solution)/shard_map/ppermute | solution.py:35
  279.3 14.8 %collective-permute-start.39 = (f32[8,128]{1,0:T(8,128)S(1)}, f32[8,128]{1,0:T(8,128)S(1)}, u32[]{:S(2)}, u32[]{:S(2)}) collective-permute-start(f32[8,128]{1,0:T(8,128)S(1)} %add.409), channel_id=1, source_target_pairs={{0,2},{1,3},{2,0},{3,1},{4,6},{5,7},{6,4},{7,5},{8,10},{9,11},{10,... | collective-permute-start | bytes 12296 | tf_op jit(solution)/shard_map/ppermute | solution.py:35
  295.1 27.9 %collective-permute-start.43 = (bf16[192,3072]{1,0:T(8,128)(2,1)S(1)}, bf16[192,3072]{1,0:T(8,128)(2,1)}, u32[]{:S(2)}, u32[]{:S(2)}) collective-permute-start(bf16[192,3072]{1,0:T(8,128)(2,1)S(1)} %get-tuple-element.348), channel_id=1, source_target_pairs={{0,2},{1,3},{2,0},{3,1},{4,5},{5,4},{6,7},{7,6},{8,10},{9,11},{10,... | collective-permute-start | bytes 3538952 | tf_op jit(solution)/shard_map/ppermute | solution.py:35
  297.5 24.0 %collective-permute-start.44 = (bf16[384,768]{1,0:T(8,128)(2,1)}, bf16[384,768]{1,0:T(8,128)(2,1)}, u32[]{:S(2)}, u32[]{:S(2)}) collective-permute-start(bf16[384,768]{1,0:T(8,128)(2,1)} %add_convert_fusion.15), channel_id=1, source_target_pairs={{0,1},{1,0},{2,3},{3,2},{4,6},{5,7},{6,4},{7,5},{8,9},{9,8},{10,11... | collective-permute-start | bytes 1769480 | tf_op jit(solution)/shard_map/ppermute | solution.py:35
  298.4 24.6 %collective-permute-start.42 = (bf16[24,3072]{1,0:T(8,128)(2,1)}, bf16[24,3072]{1,0:T(8,128)(2,1)}, u32[]{:S(2)}, u32[]{:S(2)}) collective-permute-start(bf16[24,3072]{1,0:T(8,128)(2,1)} %get-tuple-element.533), channel_id=1, source_target_pairs={{0,8},{1,9},{2,10},{3,11},{4,12},{5,13},{6,14},{7,15},{8,16},{9,17... | collective-permute-start | bytes 442376 | tf_op jit(solution)/shard_map/ppermute | solution.py:35
  299.2 23.8 %collective-permute-start.41 = (bf16[24,3072]{1,0:T(8,128)(2,1)S(1)}, bf16[24,3072]{1,0:T(8,128)(2,1)}, u32[]{:S(2)}, u32[]{:S(2)}) collective-permute-start(bf16[24,3072]{1,0:T(8,128)(2,1)S(1)} %get-tuple-element.534), channel_id=1, source_target_pairs={{0,16},{1,17},{2,18},{3,19},{4,20},{5,21},{6,22},{7,23},{8,24},{9,... | collective-permute-start | bytes 442376 | tf_op jit(solution)/shard_map/ppermute | solution.py:35
  301.3 21.7 %collective-permute-start.40 = (bf16[24,3072]{1,0:T(8,128)(2,1)S(1)}, bf16[24,3072]{1,0:T(8,128)(2,1)}, u32[]{:S(2)}, u32[]{:S(2)}) collective-permute-start(bf16[24,3072]{1,0:T(8,128)(2,1)S(1)} %get-tuple-element.535), channel_id=1, source_target_pairs={{0,24},{1,25},{2,26},{3,27},{4,28},{5,29},{6,30},{7,31},{8,0},{9,1... | collective-permute-start | bytes 442376 | tf_op jit(solution)/shard_map/ppermute | solution.py:35
  323.0 12.5 %collective-permute-start.45 = (bf16[384,3200]{1,0:T(8,128)(2,1)}, bf16[384,3200]{1,0:T(8,128)(2,1)S(1)}, u32[]{:S(2)}, u32[]{:S(2)}) collective-permute-start(bf16[384,3200]{1,0:T(8,128)(2,1)} %get-tuple-element.364), channel_id=1, source_target_pairs={{0,4},{1,5},{2,6},{3,7},{4,0},{5,1},{6,2},{7,3},{8,12},{9,13},{10,... | collective-permute-start | bytes 7372808 | tf_op jit(solution)/shard_map/ppermute | solution.py:35
  327.3 12.8 %collective-permute-start.48 = (bf16[96,768]{1,0:T(8,128)(2,1)}, bf16[96,768]{1,0:T(8,128)(2,1)}, u32[]{:S(2)}, u32[]{:S(2)}) collective-permute-start(bf16[96,768]{1,0:T(8,128)(2,1)} %get-tuple-element.530), channel_id=1, source_target_pairs={{0,16},{1,17},{2,18},{3,19},{4,20},{5,21},{6,22},{7,23},{8,24},{9,... | collective-permute-start | bytes 442376 | tf_op jit(solution)/shard_map/ppermute | solution.py:35
  329.9 10.2 %collective-permute-start.47 = (bf16[96,768]{1,0:T(8,128)(2,1)S(1)}, bf16[96,768]{1,0:T(8,128)(2,1)}, u32[]{:S(2)}, u32[]{:S(2)}) collective-permute-start(bf16[96,768]{1,0:T(8,128)(2,1)S(1)} %get-tuple-element.531), channel_id=1, source_target_pairs={{0,24},{1,25},{2,26},{3,27},{4,28},{5,29},{6,30},{7,31},{8,0},{9,1... | collective-permute-start | bytes 442376 | tf_op jit(solution)/shard_map/ppermute | solution.py:35
  340.1 14.3 %collective-permute-start.54 = (f32[8,128]{1,0:T(8,128)S(1)}, f32[8,128]{1,0:T(8,128)S(1)}, u32[]{:S(2)}, u32[]{:S(2)}) collective-permute-start(f32[8,128]{1,0:T(8,128)S(1)} %add.414), channel_id=1, source_target_pairs={{0,8},{1,9},{2,10},{3,11},{4,12},{5,13},{6,14},{7,15},{8,0},{9,1},... | collective-permute-start | bytes 12296 | tf_op jit(solution)/shard_map/ppermute | solution.py:35
  343.8 16.7 %collective-permute-start.50 = (bf16[192,3200]{1,0:T(8,128)(2,1)S(1)}, bf16[192,3200]{1,0:T(8,128)(2,1)S(1)}, u32[]{:S(2)}, u32[]{:S(2)}) collective-permute-start(bf16[192,3200]{1,0:T(8,128)(2,1)S(1)} %get-tuple-element.376), channel_id=1, source_target_pairs={{0,2},{1,3},{2,0},{3,1},{4,5},{5,4},{6,7},{7,6},{8,10},{9,11},{10,... | collective-permute-start | bytes 3686408 | tf_op jit(solution)/shard_map/ppermute | solution.py:35
  345.3 13.9 %collective-permute-start.52 = (bf16[24,3072]{1,0:T(8,128)(2,1)S(1)}, bf16[24,3072]{1,0:T(8,128)(2,1)S(1)}, u32[]{:S(2)}, u32[]{:S(2)}) collective-permute-start(bf16[24,3072]{1,0:T(8,128)(2,1)S(1)} %get-tuple-element.526), channel_id=1, source_target_pairs={{0,16},{1,17},{2,18},{3,19},{4,20},{5,21},{6,22},{7,23},{8,24},{9,... | collective-permute-start | bytes 442376 | tf_op jit(solution)/shard_map/ppermute | solution.py:35
  346.2 13.0 %collective-permute-start.51 = (bf16[24,3072]{1,0:T(8,128)(2,1)S(1)}, bf16[24,3072]{1,0:T(8,128)(2,1)S(1)}, u32[]{:S(2)}, u32[]{:S(2)}) collective-permute-start(bf16[24,3072]{1,0:T(8,128)(2,1)S(1)} %get-tuple-element.527), channel_id=1, source_target_pairs={{0,24},{1,25},{2,26},{3,27},{4,28},{5,29},{6,30},{7,31},{8,0},{9,1... | collective-permute-start | bytes 442376 | tf_op jit(solution)/shard_map/ppermute | solution.py:35
  360.7 10.2 %collective-permute-start.55 = (bf16[96,3200]{1,0:T(8,128)(2,1)S(1)}, bf16[96,3200]{1,0:T(8,128)(2,1)S(1)}, u32[]{:S(2)}, u32[]{:S(2)}) collective-permute-start(bf16[96,3200]{1,0:T(8,128)(2,1)S(1)} %add_convert_fusion.9), channel_id=1, source_target_pairs={{0,1},{1,0},{2,3},{3,2},{4,6},{5,7},{6,4},{7,5},{8,9},{9,8},{10,11... | collective-permute-start | bytes 1843208 | tf_op jit(solution)/shard_map/ppermute | solution.py:35
  373.2 12.9 %collective-permute-start.58 = (bf16[24,3200]{1,0:T(8,128)(2,1)S(1)}, bf16[24,3200]{1,0:T(8,128)(2,1)S(1)}, u32[]{:S(2)}, u32[]{:S(2)}) collective-permute-start(bf16[24,3200]{1,0:T(8,128)(2,1)S(1)} %get-tuple-element.524), channel_id=1, source_target_pairs={{0,16},{1,17},{2,18},{3,19},{4,20},{5,21},{6,22},{7,23},{8,24},{9,... | collective-permute-start | bytes 460808 | tf_op jit(solution)/shard_map/ppermute | solution.py:35
  (58 other events, 342.2 us)
Sparse Core Ops, SparseCore 0:
  9.7 32.2 all-gather.4
  44.2 32.1 all-gather.6
  78.0 89.4 all-gather.8
  198.7 56.4 reduce-scatter.2
  260.4 64.1 reduce-scatter.4

commit v6 on v5

--- a/solution.py
+++ b/solution.py
@@ -280,14 +280,15 @@
 
 
 def gelu(x):
-    return 0.5 * x * (1.0 + jnp.tanh(ROOT * (x + 0.044715 * (x * x * x))))
+    return x * (0.5 + 0.5 * jnp.tanh(x * (ROOT + 0.044715 * ROOT * (x * x))))
 
 
 def gelu_both(x):
     square = x * x
-    slope = jnp.tanh(ROOT * x * (1.0 + 0.044715 * square))
-    half = 0.5 * (1.0 + slope)
-    return x * half, half + 0.5 * x * (1.0 - slope * slope) * (ROOT * (1.0 + 0.134145 * square))
+    bend = jnp.tanh(x * (ROOT + 0.044715 * ROOT * square))
+    half = 0.5 + 0.5 * bend
+    value = x * half
+    return value, half + value * ((1.0 - bend) * (ROOT + 0.134145 * ROOT * square))
 
 
 def allowed_pair(start, length):
@@ -314,7 +315,7 @@
 def softmax_pair(queries, keys, allowed):
     scores = jnp.where(allowed, dot_nt(queries, keys) * HD ** (-0.5), -1e30)
     exponent = jnp.exp(scores - jnp.max(scores, axis=-1, keepdims=True))
-    return exponent / jnp.sum(exponent, axis=-1, keepdims=True)
+    return exponent * (1.0 / jnp.sum(exponent, axis=-1, keepdims=True))
 
 
 def pack_lower(triple, output, vectors, router, route, valid):

time: 405 us -> 404 us (level)
  no operation moved by 1% of the time
where the time goes in v6:
time: 404 us; the launch traced here: 397 us
  waiting for transfers between devices  130 us (32%)
  Pallas kernels  129 us (32%)
  starting transfers between devices  64.6 us (16%)
  other arithmetic  33.2 us (8%)
  local copies, waits for them, and re-layouts  21.4 us (5%)
  between operations  18.2 us (5%)
    ppermute x60, waiting for transfers between devices, hop(): return lax.ppermute(values, AXES, pairs(target))  123 us
    pallas_call x12, Pallas kernels, call(): pl.pallas_call(kernel, out_shape=outs, grid=grid, in_specs=in_specs or [W...  117 us
    ppermute x60, starting transfers between devices, hop(): return lax.ppermute(values, AXES, pairs(target))  64.3 us
    convert_element_type x12, other arithmetic, add(): return (first.astype(F32) + second.astype(F32)).astype(BF16)  13 us
    pallas_call x1, Pallas kernels, feed_backward_shrink(): pl.pallas_call(kernel, out_shape=outs, grid_spec=pltpu.PrefetchScalarGrid...  11.8 us
  transfers between devices with their start and end apart: 65, of which 29 were waited for; matrix products, arithmetic and copies ran while one was open for 11% of the time, Pallas kernels for 33%

profile of v6, /device:TPU:0, one launch (start us, length us, event | category | flops | bytes accessed | tf_op | source)
XLA Modules:
  0.0 396.8 jit_solution(1159798517086277968)
XLA Ops:
  8.0 1.8 pad_maximum_fusion.10
  9.9 1.8 shard_map.365
  11.6 5.0 %collective-permute-start.2 = (bf16[24,3200]{1,0:T(8,128)(2,1)}, bf16[24,3200]{1,0:T(8,128)(2,1)S(1)}, u32[]{:S(2)}, u32[]{:S(2)}) collective-permute-start(bf16[24,3200]{1,0:T(8,128)(2,1)} %shard_map.365), channel_id=1, source_target_pairs={{0,24},{1,25},{2,26},{3,27},{4,28},{5,29},{6,30},{7,31},{8,0},{9,1... | collective-permute-start | bytes 460808 | tf_op jit(solution)/shard_map/ppermute | solution.py:35
  23.4 13.5 %collective-permute-done.1 = bf16[24,3200]{1,0:T(8,128)(2,1)S(1)} collective-permute-done((bf16[24,3200]{1,0:T(8,128)(2,1)}, bf16[24,3200]{1,0:T(8,128)(2,1)S(1)}, u32[]{:S(2)}, u32[]{:S(2)}) %collective-permute-start.1) | collective-permute-done | bytes 153632 | tf_op jit(solution)/shard_map/ppermute | solution.py:35
  38.6 3.4 all-gather.5.cloned.1.call-done
  44.4 2.9 collective-permute-done.3
  50.6 14.9 %collective-permute-done.6 = bf16[4,96,768]{2,1,0:T(8,128)(2,1)} collective-permute-done((bf16[4,96,768]{2,1,0:T(8,128)(2,1)S(1)}, bf16[4,96,768]{2,1,0:T(8,128)(2,1)}, u32[]{:S(2)}, u32[]{:S(2)}) %collective-permute-start.6) | collective-permute-done | bytes 589856 | tf_op jit(solution)/shard_map/ppermute | solution.py:35
  65.5 5.3 %collective-permute-done.4 = bf16[2,4,24,3200]{3,2,1,0:T(8,128)(2,1)} collective-permute-done((bf16[2,4,24,3200]{3,2,1,0:T(8,128)(2,1)S(1)}, bf16[2,4,24,3200]{3,2,1,0:T(8,128)(2,1)}, u32[]{:S(2)}, u32[]{:S(2)}) %collective-permute-start.4) | collective-permute-done | bytes 1228832 | tf_op jit(solution)/shard_map/ppermute | solution.py:35
  73.5 2.9 all-gather.7.cloned.1.call-done
  76.4 1.7 dynamic-slice_bitcast_fusion.3
  83.0 9.8 %shard_map.366 = (f32[128,768]{1,0:T(8,128)}, f32[256,768]{1,0:T(8,128)}, bf16[256,768]{1,0:T(8,128)(2,1)}, bf16[256,2304]{1,0:T(8,128)(2,1)}, bf16[256,768]{1,0:T(8,128)(2,1)}) custom-call(s32[2]{0:T(128)} %refs_0_.7, bf16[256,768]{1,0:T(8,128)(2,1)} %bitcast.199, bf16[768,768]{1,0:T(8,128)(2,1)} %fusion.refs_2_.refs_11_.refs_6_.refs_5_, ...), custom_call_target="tpu_custom_call" | custom-call | flops 1509949 | bytes 9633 | tf_op jit(solution)/shard_map/pallas_call | solution.py:198
  103.3 10.2 %collective-permute-done.12 = bf16[2,4,24,3072]{3,2,1,0:T(8,128)(2,1)S(1)} collective-permute-done((bf16[2,4,24,3072]{3,2,1,0:T(8,128)(2,1)S(1)}, bf16[2,4,24,3072]{3,2,1,0:T(8,128)(2,1)S(1)}, u32[]{:S(2)}, u32[]{:S(2)}) %collective-permute-start.12) | collective-permute-done | bytes 1179680 | tf_op jit(solution)/shard_map/ppermute | solution.py:35
  113.6 2.8 collective-permute-done.15
  120.4 11.5 %shard_map.367 = (f32[256,768]{1,0:T(8,128)}, bf16[256,768]{1,0:T(8,128)(2,1)}, f32[256,3072]{1,0:T(8,128)}) custom-call(s32[32]{0:T(128)} %get-tuple-element.251.refs_0_.places_ref, bf16[192,3072]{1,0:T(8,128)(2,1)} %bitcast.163, bf16[192,3072]{1,0:T(8,128)(2,1)} %bitcast.177, bf16[96,3072]{1,0:T(8,128)(2,1)} %bitcast.169, ...), custom_call_target="tpu_custom_call" | custom-call | flops 2415919 | bytes 16121 | tf_op jit(solution)/shard_map/pallas_call | solution.py:198
  132.0 3.2 collective-permute-done.16
  136.0 2.3 collective-permute-done.18
  139.4 8.2 %shard_map.368 = (f32[256,768]{1,0:T(8,128)}, bf16[256,768]{1,0:T(8,128)(2,1)}, bf16[256,2304]{1,0:T(8,128)(2,1)}, bf16[256,768]{1,0:T(8,128)(2,1)}) custom-call(s32[2]{0:T(128)} %refs_0_.7, f32[256,768]{1,0:T(8,128)} %get-tuple-element.264.refs_1_.refs_7_, bf16[768,768]{1,0:T(8,128)(2,1)} %fusion.refs_2_.refs_11_.refs_6_.refs_5_, ...), custom_call_target="tpu_custom_call" | custom-call | flops 1509949 | bytes 9830 | tf_op jit(solution)/shard_map/pallas_call | solution.py:198
  147.6 3.6 shard_map.369
  154.7 4.5 %collective-permute-done.19.refs_1_ = bf16[128,768]{1,0:T(8,128)(2,1)S(1)} collective-permute-done((bf16[128,768]{1,0:T(8,128)(2,1)}, bf16[128,768]{1,0:T(8,128)(2,1)S(1)}, u32[]{:S(2)}, u32[]{:S(2)}) %collective-permute-start.19) | collective-permute-done | bytes 196640 | tf_op jit(solution)/shard_map/ppermute | solution.py:35
  159.2 3.5 collective-permute-done.20.refs_2_
  167.6 11.2 %shard_map.370 = (bf16[128,768]{1,0:T(8,128)(2,1)}, bf16[128,768]{1,0:T(8,128)(2,1)}, bf16[128,768]{1,0:T(8,128)(2,1)}, bf16[128,768]{1,0:T(8,128)(2,1)}, bf16[512,768]{1,0:T(8,128)(2,1)}, /*index=5*/f32[512,3072]{1,0:T(8,128)}) custom-call(bf16[128,768]{1,0:T(8,128)(2,1)} %get-tuple-element.275.refs_0_, bf16[128,768]{1,0:T(8,128)(2,1)} %copy-done.26, ...), custom_call_target="tpu_custom_call" | custom-call | flops 4831838208 | bytes 27525120 | tf_op jit(solution)/shard_map/pallas_call | solution.py:198
  183.0 15.0 %shard_map.371 = (bf16[128,768]{1,0:T(8,128)(2,1)}, bf16[128,768]{1,0:T(8,128)(2,1)}, bf16[128,768]{1,0:T(8,128)(2,1)}, bf16[128,768]{1,0:T(8,128)(2,1)}, bf16[5...) custom-call(bf16[128,896]{1,0:T(8,128)(2,1)} %get-tuple-element.285.refs_0_, bf16[128,896]{1,0:T(8,128)(2,1)} %copy-done.23, ...), custom_call_target="tpu_custom_call" | custom-call | flops 7247757 | bytes 35520 | tf_op jit(solution)/shard_map/pallas_call | solution.py:198
  202.7 4.3 %collective-permute-done.28.refs_12_ = bf16[128,768]{1,0:T(8,128)(2,1)S(1)} collective-permute-done((bf16[128,768]{1,0:T(8,128)(2,1)S(1)}, bf16[128,768]{1,0:T(8,128)(2,1)S(1)}, u32[]{:S(2)}, u32[]{:S(2)}) %collective-permute-start.28) | collective-permute-done | bytes 196640 | tf_op jit(solution)/shard_map/ppermute | solution.py:35
  207.0 3.8 collective-permute-done.29.refs_13_
  211.6 5.6 %shard_map.372 = (bf16[256,768]{1,0:T(8,128)(2,1)}, f32[256,768]{1,0:T(8,128)}, f32[128,768]{1,0:T(8,128)}, f32[8,128]{1,0:T(8,128)}) custom-call(f32[256,768]{1,0:T(8,128)} %get-tuple-element.269.stream_ref.refs_0_, f32[128,768]{1,0:T(8,128)} %get-tuple-element.241.refs_13_.refs_8_.rows_ref.refs_1_.refs_7_, f32[8,128]{1,0:T(8,128)} %pad.9.facts_ref.refs_2_, ...), custom_call_target="tpu_custom_call" | custom-call | flops 402653184 | bytes 5254144 | tf_op jit(solution)/shard_map/pallas_call | solution.py:198
  217.2 15.3 %shard_map.373 = (f32[256,768]{1,0:T(8,128)}, bf16[384,3072]{1,0:T(8,128)(2,1)}, bf16[384,3072]{1,0:T(8,128)(2,1)}, f32[8,768]{1,0:T(8,128)}) custom-call(s32[2]{0:T(128)} %refs_0_.7, bf16[192,3072]{1,0:T(8,128)(2,1)} %bitcast.166, bf16[192,3072]{1,0:T(8,128)(2,1)} %bitcast.74.refs_4_.refs_2_, bf16[96,3072]{1,0:T(8,128)(2,1)} %bitcast.172, ...), custom_call_target="tpu_custom_call" | custom-call | flops 3321888 | bytes 15360 | tf_op jit(solution)/shard_map/pallas_call | solution.py:198
  232.6 7.2 %shard_map.374 = bf16[768,3072]{1,0:T(8,128)(2,1)} custom-call(bf16[512,768]{1,0:T(8,128)(2,1)} %get-tuple-element.314.arrived_ref, bf16[512,3072]{1,0:T(8,128)(2,1)} %get-tuple-element.317.inner_grad_ref), custom_call_target="tpu_custom_call" | custom-call | flops 2415919 | bytes 8650 | tf_op jit(solution)/shard_map/pallas_call | solution.py:198
  239.8 3.6 add_convert_fusion.6
  246.0 11.8 %shard_map.375 = (bf16[256,3072]{1,0:T(8,128)(2,1)}, bf16[4,4,96,768]{3,2,1,0:T(8,128)(2,1)}, bf16[4,4,96,768]{3,2,1,0:T(8,128)(2,1)}) custom-call(s32[32]{0:T(128)} %get-tuple-element.251.refs_0_.places_ref, bf16[768,768]{1,0:T(8,128)(2,1)} %bitcast.162, bf16[768,768]{1,0:T(8,128)(2,1)} %bitcast.58.refs_7_.refs_1_, bf16[384,768]{1,0:T(8,128)(2,1)} %bitcast.168, ...), custom_call_target="tpu_custom_call" | custom-call | flops 2415919 | bytes 14942 | tf_op jit(solution)/shard_map/pallas_call | solution.py:587
  257.8 2.0 collective-permute-done.32
  262.1 11.2 %shard_map.376 = (f32[256,768]{1,0:T(8,128)}, bf16[384,3072]{1,0:T(8,128)(2,1)}, bf16[384,3072]{1,0:T(8,128)(2,1)}, f32[8,768]{1,0:T(8,128)}) custom-call(bf16[192,3072]{1,0:T(8,128)(2,1)} %bitcast.164, bf16[192,3072]{1,0:T(8,128)(2,1)} %bitcast.178, bf16[96,3072]{1,0:T(8,128)(2,1)} %bitcast.170, bf16[96,3072]{1,0:T(8,128)(2,1)} %bitcast.69.refs_4_.refs_3_, ...), custom_call_target="tpu_custom_call" | custom-call | flops 2415919 | bytes 15360 | tf_op jit(solution)/shard_map/pallas_call | solution.py:198
  275.1 2.3 add_convert_fusion.2
  279.5 14.3 %collective-permute-done.39 = f32[8,128]{1,0:T(8,128)S(1)} collective-permute-done((f32[8,128]{1,0:T(8,128)S(1)}, f32[8,128]{1,0:T(8,128)S(1)}, u32[]{:S(2)}, u32[]{:S(2)}) %collective-permute-start.39) | collective-permute-done | bytes 4128 | tf_op jit(solution)/shard_map/ppermute | solution.py:35
  298.7 2.2 collective-permute-start.41
  300.9 3.2 collective-permute-start.40
  304.1 17.0 %shard_map.377 = (f32[256,768]{1,0:T(8,128)}, bf16[384,3200]{1,0:T(8,128)(2,1)}, bf16[384,3200]{1,0:T(8,128)(2,1)}, f32[8,768]{1,0:T(8,128)}) custom-call(s32[2]{0:T(128)} %refs_0_.7, bf16[192,3200]{1,0:T(8,128)(2,1)} %bitcast.160, bf16[192,3200]{1,0:T(8,128)(2,1)} %bitcast.54.refs_4_.refs_2_, bf16[192,3200]{1,0:T(8,128)(2,1)} %bitcast.174, ...), custom_call_target="tpu_custom_call" | custom-call | flops 3321888 | bytes 15802 | tf_op jit(solution)/shard_map/pallas_call | solution.py:198
  326.9 2.6 collective-permute-start.48
  329.7 4.2 %collective-permute-done.46 = bf16[96,3072]{1,0:T(8,128)(2,1)S(1)} collective-permute-done((bf16[96,3072]{1,0:T(8,128)(2,1)S(1)}, bf16[96,3072]{1,0:T(8,128)(2,1)S(1)}, u32[]{:S(2)}, u32[]{:S(2)}) %collective-permute-start.46) | collective-permute-done | bytes 589856 | tf_op jit(solution)/shard_map/ppermute | solution.py:35
  335.8 4.0 %collective-permute-done.48 = bf16[96,768]{1,0:T(8,128)(2,1)} collective-permute-done((bf16[96,768]{1,0:T(8,128)(2,1)}, bf16[96,768]{1,0:T(8,128)(2,1)}, u32[]{:S(2)}, u32[]{:S(2)}) %collective-permute-start.48) | collective-permute-done | bytes 147488 | tf_op jit(solution)/shard_map/ppermute | solution.py:35
  339.8 3.7 collective-permute-start.54
  345.8 2.9 collective-permute-start.51
  349.9 1.9 convert_add_fusion.3
  354.0 4.8 %collective-permute-done.52 = bf16[24,3072]{1,0:T(8,128)(2,1)S(1)} collective-permute-done((bf16[24,3072]{1,0:T(8,128)(2,1)S(1)}, bf16[24,3072]{1,0:T(8,128)(2,1)S(1)}, u32[]{:S(2)}, u32[]{:S(2)}) %collective-permute-start.52) | collective-permute-done | bytes 147488 | tf_op jit(solution)/shard_map/ppermute | solution.py:35
  360.3 1.8 collective-permute-start.55
  363.4 3.2 collective-permute-done.56
  366.6 3.9 collective-permute-done.55
  375.7 4.3 %collective-permute-done.57 = bf16[24,3200]{1,0:T(8,128)(2,1)S(1)} collective-permute-done((bf16[24,3200]{1,0:T(8,128)(2,1)S(1)}, bf16[24,3200]{1,0:T(8,128)(2,1)S(1)}, u32[]{:S(2)}, u32[]{:S(2)}) %collective-permute-start.57) | collective-permute-done | bytes 153632 | tf_op jit(solution)/shard_map/ppermute | solution.py:35
  381.2 4.6 %collective-permute-done.58 = bf16[24,3200]{1,0:T(8,128)(2,1)S(1)} collective-permute-done((bf16[24,3200]{1,0:T(8,128)(2,1)S(1)}, bf16[24,3200]{1,0:T(8,128)(2,1)S(1)}, u32[]{:S(2)}, u32[]{:S(2)}) %collective-permute-start.58) | collective-permute-done | bytes 153632 | tf_op jit(solution)/shard_map/ppermute | solution.py:35
  (259 shorter events, 94.2 us)
Async XLA Ops:
  7.2 34.8 %all-gather.5.cloned.1.call-start = ((), (), s32[]{:S(2)}) async-start(), calls=%async_computation.2 | async-start | bytes 1327104 | tf_op jit(solution)/shard_map/all_gather | solution.py:68
  8.0 68.4 %all-gather.7.cloned.1.call-start = ((), (), s32[]{:S(2)}) async-start(), calls=%async_computation.3 | async-start | bytes 2654208 | tf_op jit(solution)/shard_map/all_gather | solution.py:68
  9.8 157.8 %all-gather.9.cloned.1.call-start = ((), (), s32[]{:S(2)}) async-start(), calls=%async_computation.6 | async-start | bytes 10616832 | tf_op jit(solution)/shard_map/all_gather | solution.py:992
  11.6 11.8 %collective-permute-start.2 = (bf16[24,3200]{1,0:T(8,128)(2,1)}, bf16[24,3200]{1,0:T(8,128)(2,1)S(1)}, u32[]{:S(2)}, u32[]{:S(2)}) collective-permute-start(bf16[24,3200]{1,0:T(8,128)(2,1)} %shard_map.365), channel_id=1, source_target_pairs={{0,24},{1,25},{2,26},{3,27},{4,28},{5,29},{6,30},{7,31},{8,0},{9,1... | collective-permute-start | bytes 460808 | tf_op jit(solution)/shard_map/ppermute | solution.py:35
  16.7 20.2 %collective-permute-start.1 = (bf16[24,3200]{1,0:T(8,128)(2,1)}, bf16[24,3200]{1,0:T(8,128)(2,1)S(1)}, u32[]{:S(2)}, u32[]{:S(2)}) collective-permute-start(bf16[24,3200]{1,0:T(8,128)(2,1)} %shard_map.365), channel_id=1, source_target_pairs={{0,16},{1,17},{2,18},{3,19},{4,20},{5,21},{6,22},{7,23},{8,24},{9,... | collective-permute-start | bytes 460808 | tf_op jit(solution)/shard_map/ppermute | solution.py:35
  16.7 20.2 %collective-permute-start = (bf16[24,3200]{1,0:T(8,128)(2,1)}, bf16[24,3200]{1,0:T(8,128)(2,1)S(1)}, u32[]{:S(2)}, u32[]{:S(2)}) collective-permute-start(bf16[24,3200]{1,0:T(8,128)(2,1)} %shard_map.365), channel_id=1, source_target_pairs={{0,8},{1,9},{2,10},{3,11},{4,12},{5,13},{6,14},{7,15},{8,16},{9,17... | collective-permute-start | bytes 460808 | tf_op jit(solution)/shard_map/ppermute | solution.py:35
  36.9 298.8 %reduce-scatter.3.cloned.1.call-start = ((), (), s32[]{:S(2)}) async-start(), calls=%async_computation.4 | async-start | bytes 5308416 | tf_op jit(solution)/shard_map/reduce_scatter | solution.py:1053
  37.1 10.2 %collective-permute-start.3 = (bf16[4,24,3200]{2,1,0:T(8,128)(2,1)S(1)}, bf16[4,24,3200]{2,1,0:T(8,128)(2,1)S(1)}, u32[]{:S(2)}, u32[]{:S(2)}) collective-permute-start(bf16[4,24,3200]{2,1,0:T(8,128)(2,1)S(1)} %pad_maximum_fusion.7), channel_id=1, source_target_pairs={{0,1},{1,0},{2,3},{3,2},{4,6},{5,7},{6,4},{7,5},{8,9},{9,8},{10,11... | collective-permute-start | bytes 1843208 | tf_op jit(solution)/shard_map/ppermute | solution.py:35
  47.4 18.0 %collective-permute-start.5 = (bf16[2,4,24,3200]{3,2,1,0:T(8,128)(2,1)S(1)}, bf16[2,4,24,3200]{3,2,1,0:T(8,128)(2,1)S(1)}, u32[]{:S(2)}, u32[]{:S(2)}) collective-permute-start(bf16[2,4,24,3200]{3,2,1,0:T(8,128)(2,1)S(1)} %pad_maximum_fusion), channel_id=1, source_target_pairs={{0,4},{1,5},{2,6},{3,7},{4,0},{5,1},{6,2},{7,3},{8,12},{9,13},{10,... | collective-permute-start | bytes 3686408 | tf_op jit(solution)/shard_map/ppermute | solution.py:35
  47.5 23.2 %collective-permute-start.4 = (bf16[2,4,24,3200]{3,2,1,0:T(8,128)(2,1)S(1)}, bf16[2,4,24,3200]{3,2,1,0:T(8,128)(2,1)}, u32[]{:S(2)}, u32[]{:S(2)}) collective-permute-start(bf16[2,4,24,3200]{3,2,1,0:T(8,128)(2,1)S(1)} %pad_maximum_fusion), channel_id=1, source_target_pairs={{0,2},{1,3},{2,0},{3,1},{4,5},{5,4},{6,7},{7,6},{8,10},{9,11},{10,... | collective-permute-start | bytes 3686408 | tf_op jit(solution)/shard_map/ppermute | solution.py:35
  49.1 16.4 %collective-permute-start.6 = (bf16[4,96,768]{2,1,0:T(8,128)(2,1)S(1)}, bf16[4,96,768]{2,1,0:T(8,128)(2,1)}, u32[]{:S(2)}, u32[]{:S(2)}) collective-permute-start(bf16[4,96,768]{2,1,0:T(8,128)(2,1)S(1)} %get-tuple-element.219), channel_id=1, source_target_pairs={{0,1},{1,0},{2,3},{3,2},{4,6},{5,7},{6,4},{7,5},{8,9},{9,8},{10,11... | collective-permute-start | bytes 1769480 | tf_op jit(solution)/shard_map/ppermute | solution.py:35
  70.7 22.0 %collective-permute-start.8 = (bf16[4,96,768]{2,1,0:T(8,128)(2,1)}, bf16[4,96,768]{2,1,0:T(8,128)(2,1)S(1)}, u32[]{:S(2)}, u32[]{:S(2)}) collective-permute-start(bf16[4,96,768]{2,1,0:T(8,128)(2,1)} %collective-permute-done.6), channel_id=1, source_target_pairs={{0,4},{1,5},{2,6},{3,7},{4,0},{5,1},{6,2},{7,3},{8,12},{9,13},{10,... | collective-permute-start | bytes 1769480 | tf_op jit(solution)/shard_map/ppermute | solution.py:35
  71.9 20.9 %collective-permute-start.7 = (bf16[2,4,96,768]{3,2,1,0:T(8,128)(2,1)S(1)}, bf16[2,4,96,768]{3,2,1,0:T(8,128)(2,1)}, u32[]{:S(2)}, u32[]{:S(2)}) collective-permute-start(bf16[2,4,96,768]{3,2,1,0:T(8,128)(2,1)S(1)} %pad_maximum_fusion.2), channel_id=1, source_target_pairs={{0,2},{1,3},{2,0},{3,1},{4,5},{5,4},{6,7},{7,6},{8,10},{9,11},{10,... | collective-permute-start | bytes 3538952 | tf_op jit(solution)/shard_map/ppermute | solution.py:35
  80.9 13.3 %collective-permute-start.10 = (bf16[4,24,3072]{2,1,0:T(8,128)(2,1)}, bf16[4,24,3072]{2,1,0:T(8,128)(2,1)}, u32[]{:S(2)}, u32[]{:S(2)}) collective-permute-start(bf16[4,24,3072]{2,1,0:T(8,128)(2,1)} %get-tuple-element.237), channel_id=1, source_target_pairs={{0,1},{1,0},{2,3},{3,2},{4,6},{5,7},{6,4},{7,5},{8,9},{9,8},{10,11... | collective-permute-start | bytes 1769480 | tf_op jit(solution)/shard_map/ppermute | solution.py:35
  82.2 21.1 %collective-permute-start.14 = (bf16[4,24,3072]{2,1,0:T(8,128)(2,1)}, bf16[4,24,3072]{2,1,0:T(8,128)(2,1)}, u32[]{:S(2)}, u32[]{:S(2)}) collective-permute-start(bf16[4,24,3072]{2,1,0:T(8,128)(2,1)} %get-tuple-element.249), channel_id=1, source_target_pairs={{0,1},{1,0},{2,3},{3,2},{4,6},{5,7},{6,4},{7,5},{8,9},{9,8},{10,11... | collective-permute-start | bytes 1769480 | tf_op jit(solution)/shard_map/ppermute | solution.py:35
  95.6 17.8 %collective-permute-start.12 = (bf16[2,4,24,3072]{3,2,1,0:T(8,128)(2,1)S(1)}, bf16[2,4,24,3072]{3,2,1,0:T(8,128)(2,1)S(1)}, u32[]{:S(2)}, u32[]{:S(2)}) collective-permute-start(bf16[2,4,24,3072]{3,2,1,0:T(8,128)(2,1)S(1)} %pad_maximum_fusion.5), channel_id=1, source_target_pairs={{0,2},{1,3},{2,0},{3,1},{4,5},{5,4},{6,7},{7,6},{8,10},{9,11},{10,... | collective-permute-start | bytes 3538952 | tf_op jit(solution)/shard_map/ppermute | solution.py:35
  97.2 16.3 %collective-permute-start.11 = (bf16[2,4,96,768]{3,2,1,0:T(8,128)(2,1)}, bf16[2,4,96,768]{3,2,1,0:T(8,128)(2,1)S(1)}, u32[]{:S(2)}, u32[]{:S(2)}) collective-permute-start(bf16[2,4,96,768]{3,2,1,0:T(8,128)(2,1)} %collective-permute-done.7), channel_id=1, source_target_pairs={{0,4},{1,5},{2,6},{3,7},{4,0},{5,1},{6,2},{7,3},{8,12},{9,13},{10,... | collective-permute-start | bytes 3538952 | tf_op jit(solution)/shard_map/ppermute | solution.py:35
  118.9 16.4 %collective-permute-start.16 = (bf16[2,4,24,3072]{3,2,1,0:T(8,128)(2,1)S(1)}, bf16[2,4,24,3072]{3,2,1,0:T(8,128)(2,1)}, u32[]{:S(2)}, u32[]{:S(2)}) collective-permute-start(bf16[2,4,24,3072]{3,2,1,0:T(8,128)(2,1)S(1)} %pad_maximum_fusion.6), channel_id=1, source_target_pairs={{0,2},{1,3},{2,0},{3,1},{4,5},{5,4},{6,7},{7,6},{8,10},{9,11},{10,... | collective-permute-start | bytes 3538952 | tf_op jit(solution)/shard_map/ppermute | solution.py:35
  120.4 11.5 %collective-permute-start.17 = (bf16[4,24,3072]{2,1,0:T(8,128)(2,1)}, bf16[4,24,3072]{2,1,0:T(8,128)(2,1)S(1)}, u32[]{:S(2)}, u32[]{:S(2)}) collective-permute-start(bf16[4,24,3072]{2,1,0:T(8,128)(2,1)} %collective-permute-done.14), channel_id=1, source_target_pairs={{0,4},{1,5},{2,6},{3,7},{4,0},{5,1},{6,2},{7,3},{8,12},{9,13},{10,... | collective-permute-start | bytes 1769480 | tf_op jit(solution)/shard_map/ppermute | solution.py:35
  152.4 10.2 %collective-permute-start.20 = (bf16[128,768]{1,0:T(8,128)(2,1)}, bf16[128,768]{1,0:T(8,128)(2,1)S(1)}, u32[]{:S(2)}, u32[]{:S(2)}) collective-permute-start(bf16[128,768]{1,0:T(8,128)(2,1)} %get-tuple-element.277), channel_id=1, source_target_pairs={{0,2},{1,3},{2,0},{3,1},{4,6},{5,7},{6,4},{7,5},{8,10},{9,11},{10,... | collective-permute-start | bytes 589832 | tf_op jit(solution)/shard_map/ppermute | solution.py:35
  163.7 18.0 %collective-permute-start.25 = (bf16[128,896]{1,0:T(8,128)(2,1)}, bf16[128,896]{1,0:T(8,128)(2,1)S(1)}, u32[]{:S(2)}, u32[]{:S(2)}) collective-permute-start(bf16[128,896]{1,0:T(8,128)(2,1)} %get-tuple-element.287), channel_id=1, source_target_pairs={{0,1},{1,0},{2,3},{3,2},{4,5},{5,4},{6,7},{7,6},{8,9},{9,8},{10,11... | collective-permute-start | bytes 688136 | tf_op jit(solution)/shard_map/ppermute | solution.py:35
  164.8 17.5 %collective-permute-start.26 = (bf16[128,896]{1,0:T(8,128)(2,1)}, bf16[128,896]{1,0:T(8,128)(2,1)S(1)}, u32[]{:S(2)}, u32[]{:S(2)}) collective-permute-start(bf16[128,896]{1,0:T(8,128)(2,1)} %get-tuple-element.289), channel_id=1, source_target_pairs={{0,2},{1,3},{2,0},{3,1},{4,6},{5,7},{6,4},{7,5},{8,10},{9,11},{10,... | collective-permute-start | bytes 688136 | tf_op jit(solution)/shard_map/ppermute | solution.py:35
  166.1 16.2 %collective-permute-start.27 = (bf16[128,896]{1,0:T(8,128)(2,1)}, bf16[128,896]{1,0:T(8,128)(2,1)S(1)}, u32[]{:S(2)}, u32[]{:S(2)}) collective-permute-start(bf16[128,896]{1,0:T(8,128)(2,1)} %get-tuple-element.291), channel_id=1, source_target_pairs={{0,3},{1,2},{2,1},{3,0},{4,7},{5,6},{6,5},{7,4},{8,11},{9,10},{10,... | collective-permute-start | bytes 688136 | tf_op jit(solution)/shard_map/ppermute | solution.py:35
  178.7 19.3 %collective-permute-start.22 = (bf16[128,768]{1,0:T(8,128)(2,1)}, bf16[128,768]{1,0:T(8,128)(2,1)S(1)}, u32[]{:S(2)}, u32[]{:S(2)}) collective-permute-start(bf16[128,768]{1,0:T(8,128)(2,1)} %get-tuple-element.281.refs_5_), channel_id=1, source_target_pairs={{0,1},{1,0},{2,3},{3,2},{4,5},{5,4},{6,7},{7,6},{8,9},{9,8},{10,11... | collective-permute-start | bytes 589832 | tf_op jit(solution)/shard_map/ppermute | solution.py:35
  180.2 17.8 %collective-permute-start.23 = (bf16[128,768]{1,0:T(8,128)(2,1)}, bf16[128,768]{1,0:T(8,128)(2,1)S(1)}, u32[]{:S(2)}, u32[]{:S(2)}) collective-permute-start(bf16[128,768]{1,0:T(8,128)(2,1)} %get-tuple-element.282.refs_6_), channel_id=1, source_target_pairs={{0,2},{1,3},{2,0},{3,1},{4,6},{5,7},{6,4},{7,5},{8,10},{9,11},{10,... | collective-permute-start | bytes 589832 | tf_op jit(solution)/shard_map/ppermute | solution.py:35
  181.7 16.3 %collective-permute-start.24 = (bf16[128,768]{1,0:T(8,128)(2,1)}, bf16[128,768]{1,0:T(8,128)(2,1)S(1)}, u32[]{:S(2)}, u32[]{:S(2)}) collective-permute-start(bf16[128,768]{1,0:T(8,128)(2,1)} %get-tuple-element.283.refs_7_), channel_id=1, source_target_pairs={{0,3},{1,2},{2,1},{3,0},{4,7},{5,6},{6,5},{7,4},{8,11},{9,10},{10,... | collective-permute-start | bytes 589832 | tf_op jit(solution)/shard_map/ppermute | solution.py:35
  198.8 140.9 %reduce-scatter.5.cloned.1.call-start = ((), (), s32[]{:S(2)}) async-start(), calls=%async_computation.5 | async-start | bytes 5308416 | tf_op jit(solution)/shard_map/reduce_scatter | solution.py:1074
  243.4 16.4 %collective-permute-start.32 = (bf16[192,3072]{1,0:T(8,128)(2,1)}, bf16[192,3072]{1,0:T(8,128)(2,1)S(1)}, u32[]{:S(2)}, u32[]{:S(2)}) collective-permute-start(bf16[192,3072]{1,0:T(8,128)(2,1)} %get-tuple-element.322), channel_id=1, source_target_pairs={{0,2},{1,3},{2,0},{3,1},{4,5},{5,4},{6,7},{7,6},{8,10},{9,11},{10,... | collective-permute-start | bytes 3538952 | tf_op jit(solution)/shard_map/ppermute | solution.py:35
  259.8 13.8 %collective-permute-start.36 = (bf16[1536,768]{1,0:T(8,128)(2,1)}, bf16[1536,768]{1,0:T(8,128)(2,1)}, u32[]{:S(2)}, u32[]{:S(2)}) collective-permute-start(bf16[1536,768]{1,0:T(8,128)(2,1)} %bitcast.229), channel_id=1, source_target_pairs={{0,4},{1,5},{2,6},{3,7},{4,0},{5,1},{6,2},{7,3},{8,12},{9,13},{10,... | collective-permute-start | bytes 7077896 | tf_op jit(solution)/shard_map/ppermute | solution.py:35
  260.0 13.4 %collective-permute-start.34 = (bf16[96,3072]{1,0:T(8,128)(2,1)S(1)}, bf16[96,3072]{1,0:T(8,128)(2,1)S(1)}, u32[]{:S(2)}, u32[]{:S(2)}) collective-permute-start(bf16[96,3072]{1,0:T(8,128)(2,1)S(1)} %add_convert_fusion.18), channel_id=1, source_target_pairs={{0,1},{1,0},{2,3},{3,2},{4,6},{5,7},{6,4},{7,5},{8,9},{9,8},{10,11... | collective-permute-start | bytes 1769480 | tf_op jit(solution)/shard_map/ppermute | solution.py:35
  261.2 12.2 %collective-permute-start.35 = (f32[8,128]{1,0:T(8,128)S(1)}, f32[8,128]{1,0:T(8,128)S(1)}, u32[]{:S(2)}, u32[]{:S(2)}) collective-permute-start(f32[8,128]{1,0:T(8,128)S(1)} %add.405), channel_id=1, source_target_pairs={{0,1},{1,0},{2,3},{3,2},{4,5},{5,4},{6,7},{7,6},{8,9},{9,8},{10,11... | collective-permute-start | bytes 12296 | tf_op jit(solution)/shard_map/ppermute | solution.py:35
  273.6 20.1 %collective-permute-start.37 = (bf16[384,3072]{1,0:T(8,128)(2,1)}, bf16[384,3072]{1,0:T(8,128)(2,1)S(1)}, u32[]{:S(2)}, u32[]{:S(2)}) collective-permute-start(bf16[384,3072]{1,0:T(8,128)(2,1)} %get-tuple-element.341), channel_id=1, source_target_pairs={{0,4},{1,5},{2,6},{3,7},{4,0},{5,1},{6,2},{7,3},{8,12},{9,13},{10,... | collective-permute-start | bytes 7077896 | tf_op jit(solution)/shard_map/ppermute | solution.py:35
  277.4 17.3 %collective-permute-start.38 = (bf16[768,768]{1,0:T(8,128)(2,1)S(1)}, bf16[768,768]{1,0:T(8,128)(2,1)S(1)}, u32[]{:S(2)}, u32[]{:S(2)}) collective-permute-start(bf16[768,768]{1,0:T(8,128)(2,1)S(1)} %get-tuple-element.496), channel_id=1, source_target_pairs={{0,2},{1,3},{2,0},{3,1},{4,5},{5,4},{6,7},{7,6},{8,10},{9,11},{10,... | collective-permute-start | bytes 3538952 | tf_op jit(solution)/shard_map/ppermute | solution.py:35
  278.9 14.8 %collective-permute-start.39 = (f32[8,128]{1,0:T(8,128)S(1)}, f32[8,128]{1,0:T(8,128)S(1)}, u32[]{:S(2)}, u32[]{:S(2)}) collective-permute-start(f32[8,128]{1,0:T(8,128)S(1)} %add.409), channel_id=1, source_target_pairs={{0,2},{1,3},{2,0},{3,1},{4,6},{5,7},{6,4},{7,5},{8,10},{9,11},{10,... | collective-permute-start | bytes 12296 | tf_op jit(solution)/shard_map/ppermute | solution.py:35
  294.7 27.9 %collective-permute-start.43 = (bf16[192,3072]{1,0:T(8,128)(2,1)S(1)}, bf16[192,3072]{1,0:T(8,128)(2,1)}, u32[]{:S(2)}, u32[]{:S(2)}) collective-permute-start(bf16[192,3072]{1,0:T(8,128)(2,1)S(1)} %get-tuple-element.348), channel_id=1, source_target_pairs={{0,2},{1,3},{2,0},{3,1},{4,5},{5,4},{6,7},{7,6},{8,10},{9,11},{10,... | collective-permute-start | bytes 3538952 | tf_op jit(solution)/shard_map/ppermute | solution.py:35
  297.1 24.0 %collective-permute-start.44 = (bf16[384,768]{1,0:T(8,128)(2,1)}, bf16[384,768]{1,0:T(8,128)(2,1)}, u32[]{:S(2)}, u32[]{:S(2)}) collective-permute-start(bf16[384,768]{1,0:T(8,128)(2,1)} %add_convert_fusion.15), channel_id=1, source_target_pairs={{0,1},{1,0},{2,3},{3,2},{4,6},{5,7},{6,4},{7,5},{8,9},{9,8},{10,11... | collective-permute-start | bytes 1769480 | tf_op jit(solution)/shard_map/ppermute | solution.py:35
  298.0 24.6 %collective-permute-start.42 = (bf16[24,3072]{1,0:T(8,128)(2,1)}, bf16[24,3072]{1,0:T(8,128)(2,1)}, u32[]{:S(2)}, u32[]{:S(2)}) collective-permute-start(bf16[24,3072]{1,0:T(8,128)(2,1)} %get-tuple-element.533), channel_id=1, source_target_pairs={{0,8},{1,9},{2,10},{3,11},{4,12},{5,13},{6,14},{7,15},{8,16},{9,17... | collective-permute-start | bytes 442376 | tf_op jit(solution)/shard_map/ppermute | solution.py:35
  298.7 23.8 %collective-permute-start.41 = (bf16[24,3072]{1,0:T(8,128)(2,1)S(1)}, bf16[24,3072]{1,0:T(8,128)(2,1)}, u32[]{:S(2)}, u32[]{:S(2)}) collective-permute-start(bf16[24,3072]{1,0:T(8,128)(2,1)S(1)} %get-tuple-element.534), channel_id=1, source_target_pairs={{0,16},{1,17},{2,18},{3,19},{4,20},{5,21},{6,22},{7,23},{8,24},{9,... | collective-permute-start | bytes 442376 | tf_op jit(solution)/shard_map/ppermute | solution.py:35
  300.9 21.7 %collective-permute-start.40 = (bf16[24,3072]{1,0:T(8,128)(2,1)S(1)}, bf16[24,3072]{1,0:T(8,128)(2,1)}, u32[]{:S(2)}, u32[]{:S(2)}) collective-permute-start(bf16[24,3072]{1,0:T(8,128)(2,1)S(1)} %get-tuple-element.535), channel_id=1, source_target_pairs={{0,24},{1,25},{2,26},{3,27},{4,28},{5,29},{6,30},{7,31},{8,0},{9,1... | collective-permute-start | bytes 442376 | tf_op jit(solution)/shard_map/ppermute | solution.py:35
  322.6 12.5 %collective-permute-start.45 = (bf16[384,3200]{1,0:T(8,128)(2,1)}, bf16[384,3200]{1,0:T(8,128)(2,1)S(1)}, u32[]{:S(2)}, u32[]{:S(2)}) collective-permute-start(bf16[384,3200]{1,0:T(8,128)(2,1)} %get-tuple-element.364), channel_id=1, source_target_pairs={{0,4},{1,5},{2,6},{3,7},{4,0},{5,1},{6,2},{7,3},{8,12},{9,13},{10,... | collective-permute-start | bytes 7372808 | tf_op jit(solution)/shard_map/ppermute | solution.py:35
  326.9 12.9 %collective-permute-start.48 = (bf16[96,768]{1,0:T(8,128)(2,1)}, bf16[96,768]{1,0:T(8,128)(2,1)}, u32[]{:S(2)}, u32[]{:S(2)}) collective-permute-start(bf16[96,768]{1,0:T(8,128)(2,1)} %get-tuple-element.530), channel_id=1, source_target_pairs={{0,16},{1,17},{2,18},{3,19},{4,20},{5,21},{6,22},{7,23},{8,24},{9,... | collective-permute-start | bytes 442376 | tf_op jit(solution)/shard_map/ppermute | solution.py:35
  329.5 10.3 %collective-permute-start.47 = (bf16[96,768]{1,0:T(8,128)(2,1)S(1)}, bf16[96,768]{1,0:T(8,128)(2,1)}, u32[]{:S(2)}, u32[]{:S(2)}) collective-permute-start(bf16[96,768]{1,0:T(8,128)(2,1)S(1)} %get-tuple-element.531), channel_id=1, source_target_pairs={{0,24},{1,25},{2,26},{3,27},{4,28},{5,29},{6,30},{7,31},{8,0},{9,1... | collective-permute-start | bytes 442376 | tf_op jit(solution)/shard_map/ppermute | solution.py:35
  339.8 14.2 %collective-permute-start.54 = (f32[8,128]{1,0:T(8,128)S(1)}, f32[8,128]{1,0:T(8,128)S(1)}, u32[]{:S(2)}, u32[]{:S(2)}) collective-permute-start(f32[8,128]{1,0:T(8,128)S(1)} %add.414), channel_id=1, source_target_pairs={{0,8},{1,9},{2,10},{3,11},{4,12},{5,13},{6,14},{7,15},{8,0},{9,1},... | collective-permute-start | bytes 12296 | tf_op jit(solution)/shard_map/ppermute | solution.py:35
  343.4 16.7 %collective-permute-start.50 = (bf16[192,3200]{1,0:T(8,128)(2,1)S(1)}, bf16[192,3200]{1,0:T(8,128)(2,1)S(1)}, u32[]{:S(2)}, u32[]{:S(2)}) collective-permute-start(bf16[192,3200]{1,0:T(8,128)(2,1)S(1)} %get-tuple-element.376), channel_id=1, source_target_pairs={{0,2},{1,3},{2,0},{3,1},{4,5},{5,4},{6,7},{7,6},{8,10},{9,11},{10,... | collective-permute-start | bytes 3686408 | tf_op jit(solution)/shard_map/ppermute | solution.py:35
  344.9 13.8 %collective-permute-start.52 = (bf16[24,3072]{1,0:T(8,128)(2,1)S(1)}, bf16[24,3072]{1,0:T(8,128)(2,1)S(1)}, u32[]{:S(2)}, u32[]{:S(2)}) collective-permute-start(bf16[24,3072]{1,0:T(8,128)(2,1)S(1)} %get-tuple-element.526), channel_id=1, source_target_pairs={{0,16},{1,17},{2,18},{3,19},{4,20},{5,21},{6,22},{7,23},{8,24},{9,... | collective-permute-start | bytes 442376 | tf_op jit(solution)/shard_map/ppermute | solution.py:35
  345.8 13.0 %collective-permute-start.51 = (bf16[24,3072]{1,0:T(8,128)(2,1)S(1)}, bf16[24,3072]{1,0:T(8,128)(2,1)S(1)}, u32[]{:S(2)}, u32[]{:S(2)}) collective-permute-start(bf16[24,3072]{1,0:T(8,128)(2,1)S(1)} %get-tuple-element.527), channel_id=1, source_target_pairs={{0,24},{1,25},{2,26},{3,27},{4,28},{5,29},{6,30},{7,31},{8,0},{9,1... | collective-permute-start | bytes 442376 | tf_op jit(solution)/shard_map/ppermute | solution.py:35
  360.3 10.2 %collective-permute-start.55 = (bf16[96,3200]{1,0:T(8,128)(2,1)S(1)}, bf16[96,3200]{1,0:T(8,128)(2,1)S(1)}, u32[]{:S(2)}, u32[]{:S(2)}) collective-permute-start(bf16[96,3200]{1,0:T(8,128)(2,1)S(1)} %add_convert_fusion.9), channel_id=1, source_target_pairs={{0,1},{1,0},{2,3},{3,2},{4,6},{5,7},{6,4},{7,5},{8,9},{9,8},{10,11... | collective-permute-start | bytes 1843208 | tf_op jit(solution)/shard_map/ppermute | solution.py:35
  372.9 12.9 %collective-permute-start.58 = (bf16[24,3200]{1,0:T(8,128)(2,1)S(1)}, bf16[24,3200]{1,0:T(8,128)(2,1)S(1)}, u32[]{:S(2)}, u32[]{:S(2)}) collective-permute-start(bf16[24,3200]{1,0:T(8,128)(2,1)S(1)} %get-tuple-element.524), channel_id=1, source_target_pairs={{0,16},{1,17},{2,18},{3,19},{4,20},{5,21},{6,22},{7,23},{8,24},{9,... | collective-permute-start | bytes 460808 | tf_op jit(solution)/shard_map/ppermute | solution.py:35
  (58 other events, 342.2 us)
Sparse Core Ops, SparseCore 0:
  9.7 32.2 all-gather.4
  44.2 32.1 all-gather.6
  78.0 89.4 all-gather.8
  198.3 56.4 reduce-scatter.2
  260.0 64.1 reduce-scatter.4
